TPU v7x, 32 devices: a whole 2x2x4 slice. The times are simulated.
32 devices in a mesh: req: 8 (over y, x, core), head: 4 (over z).
Axes of the slice: x: 2, y: 2, z: 4, core: 2. Of those that a mesh axis runs over, the one named last changes fastest.
Arguments:
- streams: bfloat16 [6144, 4, 2048], P('req', None, 'head'), may hold values from -6 to 6
- hc_in: float32 [2, 4], replicated, may hold values from 0.2 to 1
- hc_mix: float32 [2, 4, 4], replicated, may hold values from -0.4 to 0.4
- hc_out: float32 [2, 4], replicated, may hold values from 0.5 to 1.5
- qkv_weight: bfloat16 [2048, 3, 2048], P(None, None, 'head'), may hold values from -0.125 to 0.125
- out_weight: bfloat16 [2048, 2048], P('head'), may hold values from -0.125 to 0.125
- up_gate: bfloat16 [2048, 2, 8192], P(None, None, 'head'), may hold values from -0.125 to 0.125
- down_weight: bfloat16 [8192, 2048], P('head'), may hold values from -0.0625 to 0.0625
- draft_weight: bfloat16 [2, 2048, 2048], P(None, None, 'head'), may hold values from -0.125 to 0.125
- lm_head: bfloat16 [2048, 50304], P(None, ('req', 'head')), may hold values from -0.125 to 0.125
- k_pages: bfloat16 [384, 128, 16, 128], P('req', None, 'head'), may hold values from -45 to 45
- v_pages: bfloat16 [384, 128, 16, 128], P('req', None, 'head'), may hold values from -6 to 6
- page_owner: int32 [384], P('req'), may hold values from -1 to 127, as said below
- page_fill: int32 [384], P('req'), may hold values from 0 to 128, as said below
- cache_len: int32 [128], P('req'), may hold values from 1 to 16384, as said below
- tree_parent: int32 [128, 48], P('req'), may hold values from 0 to 46, as said below
- accepted_index: int32 [128], P('req'), may hold values from 0 to 47
Outputs:
- new_streams: bfloat16 [6144, 4, 2048], P('req', None, 'head')
- logits: float32 [128, 2, 50304], P(('req', 'head'))
Inputs may be any that keep to these rules, and one draw needn't show every extreme that they name: `page_owner`: each page slot holds one page of the request it names, or -1 where it is empty. Every request owns at least one page and one request owns 128 pages; the live pages of a device's slots vary widely from device to device. `page_fill`: 0 for an empty slot; every page of a request is full except at most one. `cache_len`: equals the valid entries of the pages the request owns; one request has exactly 16384. `tree_parent`: entry i names a smaller position, the parent of position i; position 0 is the root and names itself.
All inputs are finite; a program needn't handle non-finite values.
Results may differ from a plain program's by a relative error of at most 0.027.
Values may be sent and summed in bfloat16 or wider, within the bound.
No kernel may reach another device: no remote copies, remote signals or barrier semaphores. Data moves between devices by JAX's collectives and lax.ppermute only.
A program may use at most 512 MiB of HBM per device.

v0:
```python
import math

import jax
import jax.numpy as jnp
from jax import lax
from jax.sharding import PartitionSpec as P

NEG_FILL = -1e30
PRECISE = lax.Precision.HIGHEST


def layer_norm(values):
    center = jnp.mean(values, axis=-1, keepdims=True)
    square = jnp.mean(values * values, axis=-1, keepdims=True)
    return (values - center) * lax.rsqrt(square - center * center + 1e-05)


def normalize(values, sums, squares, width):
    center = sums / width
    return (values - center) * lax.rsqrt(squares / width - center * center + 1e-05)


def ancestors(parents):
    length = parents.shape[1]
    places = jnp.arange(length, dtype=jnp.int32)
    linked = (parents[:, :, None] == places[None, None, :]) | (places[:, None] == places[None, :])[
        None
    ]
    reach = linked.astype(jnp.float32)
    for repeat in range(max(1, (length - 1).bit_length())):
        reach = jnp.minimum(jnp.einsum("jik,jkl->jil", reach, reach, precision=PRECISE), 1.0)
    return reach


def rotate(values, positions):
    half = values.shape[-1] // 2
    freqs = jnp.exp(
        jnp.arange(half, dtype=jnp.float32) * (-2.0 * math.log(10000.0) / values.shape[-1])
    )
    angles = positions.astype(jnp.float32)[:, None] * freqs[None, :]
    cosine = jnp.cos(angles)[:, None, :]
    sine = jnp.sin(angles)[:, None, :]
    first = values[..., :half]
    second = values[..., half:]
    return jnp.concatenate(
        [first * cosine - second * sine, second * cosine + first * sine], axis=-1
    )


def blend(stream_vals, weights):
    total = weights[0] * stream_vals[:, 0]
    for index in range(1, stream_vals.shape[1]):
        total = total + weights[index] * stream_vals[:, index]
    return total


def remix(stream_vals, mixing, out_scale, delta):
    count = stream_vals.shape[1]
    matrix = jnp.eye(count, dtype=jnp.float32) + mixing
    rows = [
        blend(stream_vals, matrix[:, target]) + out_scale[target] * delta for target in range(count)
    ]
    return jnp.stack(rows, axis=1)


def stream_total(stream_vals):
    total = stream_vals[:, 0]
    for index in range(1, stream_vals.shape[1]):
        total = total + stream_vals[:, index]
    return total


def fold_rows(weight, piece):
    return jnp.dot(piece, weight, preferred_element_type=jnp.float32)


def on_device(
    streams,
    hc_in,
    hc_mix,
    hc_out,
    qkv_weight,
    out_weight,
    up_gate,
    down_weight,
    draft_weight,
    lm_head,
    k_pages,
    v_pages,
    page_owner,
    page_fill,
    cache_len,
    tree_parent,
    accepted_index,
):
    tokens_local = streams.shape[0]
    feature_local = streams.shape[2]
    width = qkv_weight.shape[0]
    req_local = cache_len.shape[0]
    tree_size = tree_parent.shape[1]
    slot_count = k_pages.shape[0]
    page_size = k_pages.shape[1]
    heads_local = k_pages.shape[2]
    head_dim = k_pages.shape[3]
    draft_count = draft_weight.shape[0]
    all_requests = req_local * lax.axis_size("req")
    reach = ancestors(tree_parent)
    depth = (jnp.sum(reach, axis=2) - 1.0).astype(jnp.int32)
    positions = (cache_len[:, None] + depth).reshape(tokens_local)
    stream_vals = streams.astype(jnp.float32)
    mixed_in = blend(stream_vals, hc_in[0])
    stat_sum, stat_square = lax.psum(
        (jnp.sum(mixed_in, axis=1), jnp.sum(mixed_in * mixed_in, axis=1)), "head"
    )
    normed = normalize(mixed_in, stat_sum[:, None], stat_square[:, None], width).astype(
        jnp.bfloat16
    )
    qkv_flat = qkv_weight.reshape(width, -1)
    projected = fold_rows(qkv_flat, lax.all_gather(normed, "head", axis=1, tiled=True))
    projected = projected.reshape(tokens_local, 3, heads_local, head_dim)
    queries = (rotate(projected[:, 0], positions) * head_dim ** (-0.5)).astype(jnp.bfloat16)
    keys_new = rotate(projected[:, 1], positions).astype(jnp.bfloat16)
    values_new = projected[:, 2].astype(jnp.bfloat16)
    gathered = lax.all_gather(
        queries.reshape(req_local, tree_size, heads_local * head_dim), "req", axis=0, tiled=True
    )
    query_all = gathered.reshape(all_requests, tree_size, heads_local, head_dim)
    safe_owner = jnp.maximum(page_owner, 0)
    live = (page_owner >= 0)[:, None] & (
        jnp.arange(page_size, dtype=jnp.int32)[None, :] < page_fill[:, None]
    )
    cache_scores = jnp.einsum(
        "pqhd,pkhd->pqhk", query_all[safe_owner], k_pages, preferred_element_type=jnp.float32
    )
    cache_scores = jnp.where(live[:, None, None, :], cache_scores, NEG_FILL)
    page_top = jnp.max(cache_scores, axis=3)
    owned_mask = page_owner[:, None] == jnp.arange(all_requests, dtype=jnp.int32)[None, :]
    owned = owned_mask.astype(jnp.float32)
    local_top = jnp.max(
        jnp.where(owned_mask[:, :, None, None], page_top[:, None], NEG_FILL), axis=0
    )
    first_request = lax.axis_index("req") * req_local
    global_top = lax.pmax(local_top.astype(jnp.bfloat16), "req").astype(local_top.dtype)
    weights = jnp.where(
        live[:, None, None, :], jnp.exp(cache_scores - global_top[safe_owner][..., None]), 0.0
    )
    page_den = jnp.sum(weights, axis=3)
    page_num = jnp.einsum(
        "pqhk,pkhd->pqhd", weights.astype(jnp.bfloat16), v_pages, preferred_element_type=jnp.float32
    )
    summed = jnp.dot(owned.T, page_num.reshape(slot_count, -1), precision=PRECISE)
    totals = jnp.dot(owned.T, page_den.reshape(slot_count, -1), precision=PRECISE)
    summed, totals = (
        summed.reshape(all_requests, tree_size, heads_local, head_dim),
        totals.reshape(all_requests, tree_size, heads_local),
    )
    own_sum, own_den = (
        lax.psum_scatter(
            summed.astype(jnp.bfloat16), "req", scatter_dimension=0, tiled=True
        ).astype(jnp.float32),
        lax.psum_scatter(
            totals.astype(jnp.bfloat16), "req", scatter_dimension=0, tiled=True
        ).astype(jnp.float32),
    )
    own_top = lax.dynamic_slice_in_dim(global_top, first_request, req_local, 0)
    query_own = queries.reshape(req_local, tree_size, heads_local, head_dim)
    keys_own = keys_new.reshape(req_local, tree_size, heads_local, head_dim)
    values_own = values_new.reshape(req_local, tree_size, heads_local, head_dim)
    tree_scores = jnp.einsum(
        "jqhd,jkhd->jqhk", query_own, keys_own, preferred_element_type=jnp.float32
    )
    tree_mask = (reach > 0)[:, :, None, :]
    tree_scores = jnp.where(tree_mask, tree_scores, NEG_FILL)
    top = jnp.maximum(own_top, jnp.max(tree_scores, axis=3))
    carried = jnp.exp(own_top - top)
    tree_weights = jnp.where(tree_mask, jnp.exp(tree_scores - top[..., None]), 0.0)
    denominator = own_den * carried + jnp.sum(tree_weights, axis=3)
    numerator = own_sum * carried[..., None] + jnp.einsum(
        "jqhk,jkhd->jqhd",
        tree_weights.astype(jnp.bfloat16),
        values_own,
        preferred_element_type=jnp.float32,
    )
    attended = (
        (numerator / denominator[..., None])
        .astype(jnp.bfloat16)
        .reshape(tokens_local, heads_local * head_dim)
    )
    attn_delta = lax.psum_scatter(
        jnp.dot(attended, out_weight, preferred_element_type=jnp.float32).astype(jnp.bfloat16),
        "head",
        scatter_dimension=1,
        tiled=True,
    ).astype(jnp.float32)
    first_streams = remix(stream_vals, hc_mix[0], hc_out[0], attn_delta)
    mixed_mid = blend(first_streams, hc_in[1])
    mid_sum, mid_square = lax.psum(
        (jnp.sum(mixed_mid, axis=1), jnp.sum(mixed_mid * mixed_mid, axis=1)), "head"
    )
    normed_mid = normalize(mixed_mid, mid_sum[:, None], mid_square[:, None], width).astype(
        jnp.bfloat16
    )
    gate_up_flat = up_gate.reshape(width, -1)
    hidden_local = gate_up_flat.shape[1] // 2
    gate_up = fold_rows(gate_up_flat, lax.all_gather(normed_mid, "head", axis=1, tiled=True))
    hidden = (jax.nn.silu(gate_up[:, :hidden_local]) * gate_up[:, hidden_local:]).astype(
        jnp.bfloat16
    )
    mlp_delta = lax.psum_scatter(
        jnp.dot(hidden, down_weight, preferred_element_type=jnp.float32).astype(jnp.bfloat16),
        "head",
        scatter_dimension=1,
        tiled=True,
    ).astype(jnp.float32)
    second_streams = remix(first_streams, hc_mix[1], hc_out[1], mlp_delta)
    new_streams = second_streams.astype(jnp.bfloat16)
    rows_taken = jnp.arange(req_local, dtype=jnp.int32) * tree_size + accepted_index
    final_local = stream_total(second_streams[rows_taken])
    final_full = lax.all_gather(final_local, "head", axis=1, tiled=True)
    final_norm = layer_norm(final_full)
    own_columns = lax.dynamic_slice_in_dim(
        final_norm, lax.axis_index("head") * feature_local, feature_local, 1
    )
    branch = jnp.einsum(
        "jd,kde->jke",
        final_norm.astype(jnp.bfloat16),
        draft_weight,
        preferred_element_type=jnp.float32,
    )
    drafted = (own_columns[:, None, :] + jax.nn.silu(branch)).astype(jnp.bfloat16)
    draft_full = lax.all_gather(drafted, "head", axis=2, tiled=True)
    draft_all = lax.all_gather(draft_full, "req", axis=0, tiled=True)
    logits_local = jnp.dot(
        draft_all.reshape(-1, width), lm_head, preferred_element_type=jnp.float32
    )
    logits_local = logits_local.reshape(all_requests, draft_count, -1)
    logits = lax.all_to_all(
        logits_local.astype(jnp.bfloat16), ("req", "head"), split_axis=0, concat_axis=2, tiled=True
    ).astype(logits_local.dtype)
    return (new_streams, logits)


def solution(mesh):
    in_specs = (
        P("req", None, "head"),
        P(),
        P(),
        P(),
        P(None, None, "head"),
        P("head", None),
        P(None, None, "head"),
        P("head", None),
        P(None, None, "head"),
        P(None, ("req", "head")),
        P("req", None, "head", None),
        P("req", None, "head", None),
        P("req"),
        P("req"),
        P("req"),
        P("req", None),
        P("req"),
    )
    out_specs = (P("req", None, "head"), P(("req", "head"), None, None))
    return jax.shard_map(
        on_device, mesh=mesh, in_specs=in_specs, out_specs=out_specs, check_vma=False
    )
```

profile of v0, /device:TPU:1, one launch (start us, length us, event | category | flops | bytes accessed | tf_op | source)
XLA Modules:
  0.0 699.4 jit_solution(12745890467470610345)
XLA Ops:
  16.3 10.9 %all-reduce.2 = (f32[768]{0:T(1024)S(1)}, f32[768]{0:T(1024)S(1)}) all-reduce(f32[768]{0:T(1024)S(1)} %fusion.51, f32[768]{0:T(1024)S(1)} %get-tuple-element.29), channel_id=1, replica_groups=mesh['req'=8,'head'=4] {'head'}, use_global_device_ids=true, to_apply=%region_3.0 | all-reduce | flops 1536 | bytes 12288 | tf_op jit(solution)/shard_map/psum | solution.py:112
  29.9 8.9 %copy.194 = bf16[2048,3,512]{0,2,1:T(8,128)(2,1)} copy(bf16[2048,3,512]{2,0,1:T(8,128)(2,1)} %param.21) | data formatting | bytes 12582912 | tf_op args[4]
  43.6 50.3 %all-gather.6.cloned.1.call-done = bf16[768,2048]{1,0:T(8,128)(2,1)} async-done(((bf16[768,512]{1,0:T(8,128)(2,1)}), bf16[768,2048]{1,0:T(8,128)(2,1)}) %all-gather.6.cloned.1.call-update) | async-done | bytes 3145744 | tf_op jit(solution)/shard_map/all_gather | solution.py:119
  93.8 8.2 %fusion.16 = f32[768,3,4,128]{0,3,2,1:T(8,128)S(1)} fusion(bf16[3,4,128,2048]{3,2,1,0:T(8,128)(2,1)} %bitcast.197, bf16[768,2048]{1,0:T(8,128)(2,1)} %all-gather.6.cloned.1.call-done), kind=kOutput, calls=%fused_computation.24 | convolution fusion | flops 4831838208 | bytes 14155776 | tf_op jit(solution)/shard_map/dot_general | solution.py:74
  112.5 44.3 %all-gather.8.cloned.1.call-done = bf16[128,48,512]{2,1,0:T(8,128)(2,1)} async-done(((bf16[16,48,512]{2,1,0:T(8,128)(2,1)}), bf16[128,48,512]{2,1,0:T(8,128)(2,1)}) %all-gather.8.cloned.1.call-update) | async-done | bytes 6291472 | tf_op jit(solution)/shard_map/all_gather | solution.py:124
  156.8 9.3 %copy.198 = bf16[128,48,512]{0,2,1:T(8,128)(2,1)} copy(bf16[128,48,512]{2,1,0:T(8,128)(2,1)} %all-gather.8.cloned.1.call-done) | data formatting | bytes 12582912 | tf_op jit(solution)/shard_map/all_gather | solution.py:124
  166.0 9.1 %copy.199 = bf16[128,48,4,128]{3,1,2,0:T(8,128)(2,1)} copy(bf16[128,48,4,128]{0,3,2,1:T(8,128)(2,1)} %bitcast.193) | data formatting | bytes 12582912 | tf_op jit(solution)/shard_map/reshape | solution.py:127
  175.2 5.1 gather_fusion
  180.3 10.1 %bitcast_reduce_fusion = (bf16[48,48,4]{1,2,0:T(4,128)(2,1)S(1)}, f32[48,4,48,128]{3,2,1,0:T(8,128)}) fusion(pred[48,128]{1,0:T(8,128)(4,1)S(1)} %fusion.79, bf16[48,48,4,128]{3,1,2,0:T(8,128)(2,1)} %gather_fusion, bf16[48,128,4,128]{3,2,1,0:T(4,128)(2,1)} %param.27), kind=kOutput, calls=%fused_computation.13 | convolution fusion | flops 304339968 | bytes 13393920 | tf_op jit(solution)/shard_map/pqhd,pkhd->pqhk/dot_general | solution.py:132
  191.8 21.0 %pmax.7 = bf16[128,48,4]{0,1,2:T(8,128)(2,1)S(1)} all-reduce(bf16[128,48,4]{0,1,2:T(8,128)(2,1)S(1)} %select_reduce_fusion), channel_id=1, replica_groups=mesh['req'=8,'head'=4] {'req'}, use_global_device_ids=true, to_apply=%region_7.8 | all-reduce | flops 24576 | bytes 98304 | tf_op jit(solution)/shard_map/pmax | solution.py:143
  213.7 6.0 fusion.28
  223.9 6.6 reshape.384
  230.5 6.7 dot_general.78
  237.2 12.1 %fusion.13 = bf16[128,48,4,128]{3,0,2,1:T(8,128)(2,1)} fusion(f32[48,4,128,48]{2,1,0,3:T(4,128)} %dot_general.78, s32[48]{0:T(128)S(1)} %copy-done.18), kind=kOutput, calls=%fused_computation.21 | convolution fusion | flops 1815091200 | bytes 11010240 | tf_op jit(solution)/shard_map/dot_general | solution.py:151
  274.3 5.1 fusion.102
  286.0 25.4 %all-reduce = bf16[128,48,4]{1,2,0:T(4,128)(2,1)S(1)} all-reduce(bf16[128,48,4]{1,2,0:T(4,128)(2,1)S(1)} %copy.219), channel_id=4, replica_groups=mesh['req'=8,'head'=4] {'req'}, use_global_device_ids=true, to_apply=%region_11.12.clone | all-reduce | flops 24576 | bytes 98304
  326.1 60.5 %reduce-scatter.6.cloned.1.call-done = bf16[768,512]{1,0:T(8,128)(2,1)} async-done(((bf16[768,2048]{1,0:T(8,128)(2,1)}), bf16[768,512]{1,0:T(8,128)(2,1)}) %reduce-scatter.6.cloned.1.call-update) | async-done | bytes 786448 | tf_op jit(solution)/shard_map/reduce_scatter | solution.py:189
  386.6 20.9 %fusion.91 = (f32[768]{0:T(1024)S(1)}, f32[768]{0:T(1024)S(1)}, f32[768,512]{1,0:T(8,128)}, f32[768,512]{1,0:T(8,128)S(1)}, f32[768,512]{1,0:T(8,128)}, /*index=5*/f32[768,512]{1,0:T(8,128)}, f32[768,512]{1,0:T(8,128)}) fusion(f32[]{:T(128)} %bitcast.60, f32[]{:T(128)} %bitcast.59, f32[]{:T(128)} %bitcast.58, f32[]{:T(128)} %bitcast.57, ...), kind=kLoop, calls=%fused_computation.156 | loop fusion | flops 18479616 | bytes 14948448 | tf_op jit(solution)/shard_map/reduce_sum | solution.py:198
  407.5 8.9 %all-reduce.1 = (f32[768]{0:T(1024)S(1)}, f32[768]{0:T(1024)S(1)}) all-reduce(f32[768]{0:T(1024)S(1)} %get-tuple-element.17, f32[768]{0:T(1024)S(1)} %get-tuple-element.16), channel_id=1, replica_groups=mesh['req'=8,'head'=4] {'head'}, use_global_device_ids=true, to_apply=%region_17.18 | all-reduce | flops 1536 | bytes 12288 | tf_op jit(solution)/shard_map/psum | solution.py:197
  419.3 17.5 %copy.236 = bf16[256,8,2,2048]{3,1,2,0:T(8,128)(2,1)} copy(bf16[256,8,2,2048]{3,2,1,0:T(2,128)(2,1)} %bitcast.195) | data formatting | bytes 33554432
  436.8 46.0 %all-gather.10.cloned.1.call-done = bf16[768,2048]{1,0:T(8,128)(2,1)} async-done(((bf16[768,512]{1,0:T(8,128)(2,1)}), bf16[768,2048]{1,0:T(8,128)(2,1)}) %all-gather.10.cloned.1.call-update) | async-done | bytes 3145744 | tf_op jit(solution)/shard_map/all_gather | solution.py:205
  482.9 16.9 %fusion.103 = f32[768,4096]{1,0:T(8,128)S(1)} fusion(bf16[768,2048]{1,0:T(8,128)(2,1)} %all-gather.10.cloned.1.call-done, bf16[2048,4096]{1,0:T(8,128)(2,1)} %bitcast.196), kind=kOutput, calls=%fused_computation.164 | convolution fusion | flops 12884901888 | bytes 32505856 | tf_op jit(solution)/shard_map/dot_general | solution.py:74
  499.8 10.5 %convolution_convert_fusion = bf16[768,2048]{1,0:T(8,128)(2,1)} fusion(bf16[2048,2048]{1,0:T(8,128)(2,1)} %param.24, f32[768,4096]{1,0:T(8,128)S(1)} %fusion.103), kind=kOutput, calls=%fused_computation.22 | convolution fusion | flops 6453460992 | bytes 24117248 | tf_op jit(solution)/shard_map/dot_general | solution.py:210
  511.6 57.6 %reduce-scatter.8.cloned.1.call-done = bf16[768,512]{1,0:T(8,128)(2,1)} async-done(((bf16[768,2048]{1,0:T(8,128)(2,1)}), bf16[768,512]{1,0:T(8,128)(2,1)}) %reduce-scatter.8.cloned.1.call-update) | async-done | bytes 786448 | tf_op jit(solution)/shard_map/reduce_scatter | solution.py:209
  569.2 10.2 %fusion.38 = (f32[768,1,512]{2,0,1:T(8,128)S(1)}, f32[768,1,512]{2,0,1:T(8,128)S(1)}) fusion(bf16[768,512]{1,0:T(8,128)(2,1)} %reduce-scatter.8.cloned.1.call-done, f32[768,512]{1,0:T(8,128)} %get-tuple-element.26, f32[768,512]{1,0:T(8,128)} %get-tuple-element.25, f32[768,512]{1,0:T(8,128)} %get-tuple-element.24, f32[768,512]{1,0:T(8,128)S(1)} %get-tuple-element.23, ...), kind=kLoop, calls=%fused_computation.48 | loop fusion | flops 7471104 | bytes 10223656 | tf_op jit(solution)/shard_map/stack | solution.py:63
  579.5 7.2 %fusion.42 = (f32[768,1,512]{2,0,1:T(8,128)S(1)}, f32[768,1,512]{2,0,1:T(8,128)S(1)}) fusion(bf16[768,512]{1,0:T(8,128)(2,1)S(1)} %copy-done.14, f32[768,512]{1,0:T(8,128)S(1)} %copy-done.5, f32[768,512]{1,0:T(8,128)S(1)} %copy-done.4, f32[768,512]{1,0:T(8,128)S(1)} %copy-done.3, f32[768,512]{1,0:T(8,128)S(1)} %get-tuple-element.23, f32[]{:T(128)} %bitcast.72, ...), kind=kLoop, calls=%fused_computation.52 | loop fusion | flops 7471104 | bytes 10223656 | tf_op jit(solution)/shard_map/stack | solution.py:63
  588.9 6.7 copy.224
  599.1 10.0 %all-gather = f32[16,1,2048]{2,1,0:T(1,128)S(1)} all-gather(f32[16,1,512]{2,1,0:T(1,128)S(1)} %slice_add_fusion), channel_id=2, replica_groups=mesh['req'=8,'head'=4] {'head'}, dimensions={2}, use_global_device_ids=true | all-gather | bytes 163840 | tf_op jit(solution)/shard_map/all_gather | solution.py:219
  612.5 11.4 %all_gather.22 = bf16[16,2,2048]{2,0,1:T(8,128)(2,1)} all-gather(bf16[16,2,512]{2,0,1:T(8,128)(2,1)S(1)} %add_convert_fusion.1), channel_id=1, replica_groups=mesh['req'=8,'head'=4] {'head'}, dimensions={2}, use_global_device_ids=true | all-gather | bytes 163840 | tf_op jit(solution)/shard_map/all_gather | solution.py:231
  623.9 28.2 %all-gather.12.cloned.1.call-done = bf16[128,2,2048]{2,0,1:T(8,128)(2,1)} async-done(((bf16[16,2,2048]{2,0,1:T(8,128)(2,1)}), bf16[128,2,2048]{2,0,1:T(8,128)(2,1)}) %all-gather.12.cloned.1.call-update) | async-done | bytes 1048592 | tf_op jit(solution)/shard_map/all_gather | solution.py:232
  658.6 5.0 all-to-all-start
  670.4 15.3 %all-to-all-done = bf16[128,2,1572]{2,1,0:T(2,128)(2,1)S(1)} async-done(((bf16[128,2,1572]{2,1,0:T(2,128)(2,1)}), bf16[128,2,1572]{2,1,0:T(2,128)(2,1)S(1)}, u32[]{:S(2)}, u32[]{:S(2)}) %all-to-all-start) | async-done | bytes 804896 | tf_op jit(solution)/shard_map/all_to_all | solution.py:237
  (151 shorter events, 111.7 us)
Async XLA Ops:
  7.2 313.4 %copy-start = (bf16[512,2048]{1,0:T(8,128)(2,1)S(1)}, bf16[512,2048]{1,0:T(8,128)(2,1)}, u32[]{:S(2)}) copy-start(bf16[512,2048]{1,0:T(8,128)(2,1)} %param.22) | copy-start | bytes 6291460
  7.2 86.7 %all-gather.6.cloned.1.call-start = ((), (), s32[]{:S(2)}) async-start(), calls=%async_computation.4 | async-start | bytes 3932160 | tf_op jit(solution)/shard_map/all_gather | solution.py:119
  11.8 3.2 copy-start.2
  15.0 1.1 copy-start.11
  29.8 9.0 %copy-start.22 = (s32[16,48]{1,0:T(8,128)S(1)}, s32[16,48]{1,0:T(8,128)}, u32[]{:S(2)}) copy-start(s32[16,48]{1,0:T(8,128)} %param.32) | copy-start | bytes 9220
  29.9 126.9 %all-gather.8.cloned.1.call-start = ((), (), s32[]{:S(2)}) async-start(), calls=%async_computation.5 | async-start | bytes 7077888 | tf_op jit(solution)/shard_map/all_gather | solution.py:124
  40.3 2.4 copy-start.21
  102.0 2.2 copy-start.13
  105.5 0.9 copy-start.12
  109.6 2.7 copy-start.18
  109.6 2.8 copy-start.20
  112.0 205.0 %reduce-scatter.4.cloned.1.call-start = ((), (), s32[]{:S(2)}) async-start(), calls=%async_computation.6 | async-start | bytes 7077888 | tf_op jit(solution)/shard_map/reduce_scatter | solution.py:158
  249.3 1.8 copy-start.24
  249.4 137.2 %reduce-scatter.6.cloned.1.call-start = ((), (), s32[]{:S(2)}) async-start(), calls=%async_computation.7 | async-start | bytes 3932160 | tf_op jit(solution)/shard_map/reduce_scatter | solution.py:189
  274.3 5.2 copy-start.15
  311.5 2.4 copy-start.16
  324.0 0.7 copy-start.17
  324.0 1.4 copy-start.19
  324.0 158.8 %all-gather.10.cloned.1.call-start = ((), (), s32[]{:S(2)}) async-start(), calls=%async_computation.8 | async-start | bytes 3932160 | tf_op jit(solution)/shard_map/all_gather | solution.py:205
  419.0 150.1 %reduce-scatter.8.cloned.1.call-start = ((), (), s32[]{:S(2)}) async-start(), calls=%async_computation.9 | async-start | bytes 3932160 | tf_op jit(solution)/shard_map/reduce_scatter | solution.py:209
  510.2 141.9 %all-gather.12.cloned.1.call-start = ((), (), s32[]{:S(2)}) async-start(), calls=%async_computation.10 | async-start | bytes 1179648 | tf_op jit(solution)/shard_map/all_gather | solution.py:232
  569.1 10.3 %copy-start.3 = (f32[768,512]{1,0:T(8,128)S(1)}, f32[768,512]{1,0:T(8,128)}, u32[]{:S(2)}) copy-start(f32[768,512]{1,0:T(8,128)} %get-tuple-element.24) | copy-start | bytes 4718596
  569.2 10.3 %copy-start.4 = (f32[768,512]{1,0:T(8,128)S(1)}, f32[768,512]{1,0:T(8,128)}, u32[]{:S(2)}) copy-start(f32[768,512]{1,0:T(8,128)} %get-tuple-element.25) | copy-start | bytes 4718596
  569.2 10.3 %copy-start.5 = (f32[768,512]{1,0:T(8,128)S(1)}, f32[768,512]{1,0:T(8,128)}, u32[]{:S(2)}) copy-start(f32[768,512]{1,0:T(8,128)} %get-tuple-element.26) | copy-start | bytes 4718596
  569.2 10.3 %copy-start.14 = (bf16[768,512]{1,0:T(8,128)(2,1)S(1)}, bf16[768,512]{1,0:T(8,128)(2,1)}, u32[]{:S(2)}) copy-start(bf16[768,512]{1,0:T(8,128)(2,1)} %reduce-scatter.8.cloned.1.call-done) | copy-start | bytes 2359300
  579.4 7.3 %copy-start.6 = (f32[768,1,512]{2,0,1:T(8,128)}, f32[768,1,512]{2,0,1:T(8,128)S(1)}, u32[]{:S(2)}) copy-start(f32[768,1,512]{2,0,1:T(8,128)S(1)} %get-tuple-element.31) | copy-start | bytes 4718596
  579.4 7.3 %copy-start.8 = (f32[768,1,512]{2,0,1:T(8,128)}, f32[768,1,512]{2,0,1:T(8,128)S(1)}, u32[]{:S(2)}) copy-start(f32[768,1,512]{2,0,1:T(8,128)S(1)} %get-tuple-element.32) | copy-start | bytes 4718596
  586.6 1.1 copy-start.9
  586.7 1.7 copy-start.10
  656.5 7.1 %copy-start.7 = (f32[768,1,512]{2,0,1:T(8,128)S(1)}, f32[768,1,512]{2,0,1:T(8,128)}, u32[]{:S(2)}) copy-start(f32[768,1,512]{2,0,1:T(8,128)} %copy-done.6) | copy-start | bytes 4718596
  658.6 27.1 %all-to-all-start = ((bf16[128,2,1572]{2,1,0:T(2,128)(2,1)}), bf16[128,2,1572]{2,1,0:T(2,128)(2,1)S(1)}, u32[]{:S(2)}, u32[]{:S(2)}) async-start(bf16[128,2,1572]{2,1,0:T(2,128)(2,1)} %copy.225), calls=%async_computation.3 | async-start | bytes 1703936 | tf_op jit(solution)/shard_map/all_to_all | solution.py:237
  686.3 5.8 copy-start.1
  (1 other events, 0.7 us)
Sparse Core Ops, SparseCore 0:
  30.0 63.8 all-gather.5
  112.1 44.6 all-gather.7
  249.5 65.2 reduce-scatter.3
  324.2 62.3 reduce-scatter.5
  419.2 63.6 all-gather.9
  510.3 58.7 reduce-scatter.7
  624.0 28.0 all-gather.11
where the time goes:
time: 709 us; the launch traced here: 699 us
  waiting for transfers between devices  302 us (43%)
  local copies, waits for them, and re-layouts  130 us (18%)
  blocking collectives  87.6 us (12%)
  matrix products  86.8 us (12%)
  other arithmetic  70.1 us (10%)
  between operations  15.9 us (2%)
    reduce_scatter x1, waiting for transfers between devices, on_device(): lax.psum_scatter(jnp.dot(attended, out_weight, preferred_element_type=jnp...  60.5 us
    reduce_scatter x1, waiting for transfers between devices, on_device(): lax.psum_scatter(jnp.dot(hidden, down_weight, preferred_element_type=jnp....  57.6 us
    all_gather x1, waiting for transfers between devices, on_device(): lax.all_gather(normed, 'head', axis=1, tiled=True)  50.3 us
    all_gather x1, waiting for transfers between devices, on_device(): lax.all_gather(normed_mid, 'head', axis=1, tiled=True)  46 us
    all_gather x1, waiting for transfers between devices, on_device(): lax.all_gather(queries.reshape(req_local, tree_size, heads_local * head_d...  44.3 us
    unnamed x55, local copies, waits for them, and re-layouts  37.7 us
    all_gather x1, waiting for transfers between devices, on_device(): draft_all = lax.all_gather(draft_full, 'req', axis=0, tiled=True)  28.2 us
    unnamed x1, blocking collectives  25.4 us
  transfers between devices with their start and end apart: 8, of which 7 were waited for; matrix products, arithmetic and copies ran while one was open for 12% of the time, Pallas kernels for 0%

commit v1 on v0

v1 whole, which is shorter than its diff:
```python
import functools
import math

import jax
import jax.numpy as jnp
from jax import lax
from jax.experimental import pallas as pl
from jax.experimental.pallas import tpu as pltpu
from jax.sharding import PartitionSpec as P

NEG_FILL = -1e30
EMPTY = -1e29
PRECISE = lax.Precision.HIGHEST
CHUNKS = 2
LANES = 128
VMEM_BYTES = 40 * 1024 * 1024


def params(count=1):
    return pltpu.CompilerParams(
        dimension_semantics=("arbitrary",) * count, vmem_limit_bytes=VMEM_BYTES
    )


def ancestors(parents):
    length = parents.shape[1]
    places = jnp.arange(length, dtype=jnp.int32)
    linked = (parents[:, :, None] == places[None, None, :]) | (places[:, None] == places[None, :])[
        None
    ]
    reach = linked.astype(jnp.float32)
    for repeat in range(max(1, (length - 1).bit_length())):
        reach = jnp.minimum(jnp.einsum("jik,jkl->jil", reach, reach, precision=PRECISE), 1.0)
    return reach


def layer_norm(values):
    center = jnp.mean(values, axis=-1, keepdims=True)
    square = jnp.mean(values * values, axis=-1, keepdims=True)
    return (values - center) * lax.rsqrt(square - center * center + 1e-05)


def blend(stream_vals, weights):
    total = weights[0] * stream_vals[:, 0]
    for index in range(1, stream_vals.shape[1]):
        total = total + weights[index] * stream_vals[:, index]
    return total


def chain_gather(block):
    count = lax.axis_size("head")
    right, left = [block], [block]
    for step in range(1, count):
        right.append(
            lax.ppermute(right[-1], "head", [(z, z + 1) for z in range(step - 1, count - 1)])
        )
        left.append(
            lax.ppermute(left[-1], "head", [(z, z - 1) for z in range(1, count - step + 1)])
        )
    return right, left


def in_order(right, left):
    count = lax.axis_size("head")
    rank = lax.axis_index("head")
    blocks = []
    for source in range(count):
        value = right[0]
        for step in range(1, count):
            if source + step < count:
                value = jnp.where(rank == source + step, right[step], value)
            if source - step >= 0:
                value = jnp.where(rank == source - step, left[step], value)
        blocks.append(value)
    return blocks


def chain_scatter(share):
    count = lax.axis_size("head")
    shares = {}
    for step in range(1, count):
        for key in (step, count - step):
            if key not in shares:
                shares[key] = share(key).astype(jnp.bfloat16)
    from_left = from_right = None
    for step in range(1, count):
        to_right, to_left = shares[step], shares[count - step]
        if step > 1:
            to_right = (to_right.astype(jnp.float32) + from_left.astype(jnp.float32)).astype(
                jnp.bfloat16
            )
            to_left = (to_left.astype(jnp.float32) + from_right.astype(jnp.float32)).astype(
                jnp.bfloat16
            )
        from_left = lax.ppermute(to_right, "head", [(z, z + 1) for z in range(step)])
        from_right = lax.ppermute(
            to_left, "head", [(z, z - 1) for z in range(count - step, count)]
        )
    return share(0) + from_left.astype(jnp.float32) + from_right.astype(jnp.float32)


def shift_gather(small):
    count = lax.axis_size("head")
    rank = lax.axis_index("head")
    parts = [small] + [
        lax.ppermute(small, "head", [(z, (z + step) % count) for z in range(count)])
        for step in range(1, count)
    ]
    stacked = jnp.stack(parts)
    return jnp.stack(
        [
            lax.dynamic_index_in_dim(stacked, (rank - source) % count, 0, keepdims=False)
            for source in range(count)
        ]
    )


def gathered_norm(values, width):
    local = values.shape[1]
    sums = jnp.sum(values, axis=1)
    squares = jnp.sum(values * values, axis=1)
    center = sums / local
    sent = (values - center[:, None]).astype(jnp.bfloat16)
    stats = shift_gather(jnp.stack([sums, squares]))
    right, left = chain_gather(sent)
    mean = jnp.sum(stats[:, 0], axis=0) / width
    variance = jnp.sum(stats[:, 1], axis=0) / width - mean * mean
    scale = lax.rsqrt(variance + 1e-05)
    blocks = in_order(right, left)
    normed = [
        (
            (block.astype(jnp.float32) + (stats[rank, 0] / local - mean)[:, None])
            * scale[:, None]
        ).astype(jnp.bfloat16)
        for rank, block in enumerate(blocks)
    ]
    return jnp.concatenate(normed, axis=1), right[-1]


def columns_for(weight, step):
    count = lax.axis_size("head")
    width = weight.shape[1] // count
    owner = (lax.axis_index("head") - step) % count
    return lax.dynamic_slice_in_dim(weight, owner * width, width, 1)


def swapped(values, bit):
    count = lax.axis_size("req")
    return lax.ppermute(values, "req", [(r, r ^ bit) for r in range(count)])


def bit_orders():
    bits = [1 << index for index in range((lax.axis_size("req") - 1).bit_length())]
    return bits[0], (bits[1:], bits[1:][::-1])


def gather_requests(values):
    half = values.shape[0] // 2
    near, orders = bit_orders()
    parts = []
    for part, order in enumerate(orders):
        blocks = {0: values[part * half : (part + 1) * half]}
        for bit in list(order) + [near]:
            for index in list(blocks):
                blocks[index ^ bit] = swapped(blocks[index], bit)
        parts.append(blocks)
    return [
        jnp.concatenate([blocks[index] for blocks in parts])
        for index in range(lax.axis_size("req"))
    ]


def scatter_requests(sums, logs, merge):
    near, orders = bit_orders()
    count = lax.axis_size("req")
    far = count // 2
    state = []
    mine = [sums[:far], logs[:far]]
    theirs = [swapped(sums[far:], near), swapped(logs[far:], near)]
    merged = merge(mine, theirs)
    half = sums.shape[1] // 2
    done = []
    for part, order in enumerate(orders):
        kept = [value[:, part * half : (part + 1) * half] for value in merged]
        places = list(range(far))
        for place, bit in enumerate(order):
            stay = [at for at, index in enumerate(places) if not index & (bit >> 1)]
            leave = [at for at, index in enumerate(places) if index & (bit >> 1)]
            pick = lambda value, which: jnp.concatenate([value[at : at + 1] for at in which])
            ours = [pick(value, stay) for value in kept]
            got = [swapped(pick(value, leave), bit) for value in kept]
            places = [places[at] for at in stay]
            kept = merge(ours, got) if place < len(order) - 1 else (ours, got)
        done.append(kept)
    return done


def rotate_kernel(heads, size, scale, x_ref, cos_ref, sin_ref, q_ref, k_ref, v_ref):
    width = heads * size
    cosine, sine = cos_ref[...], sin_ref[...]
    for head in range(heads):
        at = head * size
        for base, out_ref, factor in ((0, q_ref, scale), (width, k_ref, 1.0)):
            values = x_ref[:, base + at : base + at + size]
            turned = values * cosine + pltpu.roll(values, size // 2, 1) * sine
            out_ref[:, at : at + size] = (turned * factor).astype(out_ref.dtype)
    v_ref[...] = x_ref[:, 2 * width :].astype(v_ref.dtype)


def rotate_all(projected, cosine, sine, heads, size, rows):
    tokens = projected.shape[0]
    out = jax.ShapeDtypeStruct((tokens, heads * size), jnp.bfloat16)
    block = lambda width: pl.BlockSpec((rows, width), lambda i: (i, 0))
    return pl.pallas_call(
        functools.partial(rotate_kernel, heads, size, size ** (-0.5)),
        grid=(tokens // rows,),
        in_specs=[block(3 * heads * size), block(size), block(size)],
        out_specs=[block(heads * size)] * 3,
        out_shape=[out] * 3,
        compiler_params=params(),
        name="rotate",
    )(projected, cosine, sine)


def lay_logs(columns, rows):
    lane = lax.broadcasted_iota(jnp.int32, (LANES, LANES), 1)
    table = jnp.full((LANES, LANES), NEG_FILL, jnp.float32)
    for head, column in enumerate(columns):
        tall = jnp.concatenate(
            [column, jnp.full((LANES - rows, 1), NEG_FILL, jnp.float32)], axis=0
        )
        table = jnp.where(lane == head, tall, table)
    return jnp.transpose(table)[:8]


def tree_kernel(heads, size, q_ref, k_ref, v_ref, reach_ref, out_ref, log_ref):
    seen = reach_ref[0] > 0
    logs = []
    for head in range(heads):
        at = slice(head * size, (head + 1) * size)
        scores = lax.dot_general(
            q_ref[0, :, at],
            k_ref[0, :, at],
            (((1,), (1,)), ((), ())),
            preferred_element_type=jnp.float32,
        )
        scores = jnp.where(seen, scores, NEG_FILL)
        top = jnp.max(scores, axis=1, keepdims=True)
        weights = jnp.where(seen, jnp.exp(scores - top), 0.0)
        total = jnp.sum(weights, axis=1, keepdims=True)
        summed = jnp.dot(
            weights.astype(jnp.bfloat16), v_ref[0, :, at], preferred_element_type=jnp.float32
        )
        out_ref[0, :, at] = summed / total
        logs.append(top + jnp.log(total))
    log_ref[0] = lay_logs(logs, q_ref.shape[1])


def tree_attention(queries, keys, values, reach, heads, size):
    requests, tree, width = queries.shape
    block = pl.BlockSpec((1, tree, width), lambda j: (j, 0, 0))
    return pl.pallas_call(
        functools.partial(tree_kernel, heads, size),
        grid=(requests,),
        in_specs=[block] * 3 + [pl.BlockSpec((1, tree, tree), lambda j: (j, 0, 0))],
        out_specs=[block, pl.BlockSpec((1, 8, LANES), lambda j: (j, 0, 0))],
        out_shape=[
            jax.ShapeDtypeStruct((requests, tree, width), jnp.float32),
            jax.ShapeDtypeStruct((requests, 8, LANES), jnp.float32),
        ],
        compiler_params=params(),
        name="tree_attention",
    )(queries, keys, values, reach)


def page_kernel(
    heads,
    size,
    page_ref,
    place_ref,
    fill_ref,
    first_ref,
    last_ref,
    live_ref,
    q_ref,
    k_ref,
    v_ref,
    out_ref,
    log_ref,
    acc_ref,
    top_ref,
    total_ref,
):
    step = pl.program_id(0)
    tree = q_ref.shape[1]

    @pl.when(step == 0)
    def _():
        log_ref[...] = jnp.full(log_ref.shape, NEG_FILL, jnp.float32)

    @pl.when(step < live_ref[0])
    def _():
        @pl.when(first_ref[step] == 1)
        def _():
            acc_ref[...] = jnp.zeros(acc_ref.shape, jnp.float32)
            top_ref[...] = jnp.full(top_ref.shape, NEG_FILL, jnp.float32)
            total_ref[...] = jnp.zeros(total_ref.shape, jnp.float32)

        entries = k_ref.shape[2]
        valid = lax.broadcasted_iota(jnp.int32, (tree, entries), 1) < fill_ref[step]
        for head in range(heads):
            at = slice(head * size, (head + 1) * size)
            scores = lax.dot_general(
                q_ref[0, :, at],
                k_ref[0, head],
                (((1,), (1,)), ((), ())),
                preferred_element_type=jnp.float32,
            )
            scores = jnp.where(valid, scores, NEG_FILL)
            before = top_ref[head]
            top = jnp.maximum(before, jnp.max(scores, axis=1, keepdims=True))
            weights = jnp.where(valid, jnp.exp(scores - top), 0.0)
            decay = jnp.exp(before - top)
            top_ref[head] = top
            total_ref[head] = total_ref[head] * decay + jnp.sum(weights, axis=1, keepdims=True)
            acc_ref[:, at] = acc_ref[:, at] * decay + jnp.dot(
                weights.astype(jnp.bfloat16), v_ref[0, head], preferred_element_type=jnp.float32
            )

        @pl.when(last_ref[step] == 1)
        def _():
            logs = []
            for head in range(heads):
                at = slice(head * size, (head + 1) * size)
                total = total_ref[head]
                some = total > 0
                safe = jnp.where(some, total, 1.0)
                out_ref[0, :, at] = (acc_ref[:, at] / safe).astype(out_ref.dtype)
                logs.append(jnp.where(some, top_ref[head] + jnp.log(safe), NEG_FILL)[:, :1])
            log_ref[place_ref[step]] = lay_logs(logs, tree)


def page_attention(queries, k_pages, v_pages, plan, heads, size):
    requests, tree, width = queries.shape
    entries = k_pages.shape[2]
    row = pl.BlockSpec((1, tree, width), lambda p, page, place, *rest: (place[p], 0, 0))
    leaf = pl.BlockSpec(
        (1, heads, entries, size), lambda p, page, place, *rest: (page[p], 0, 0, 0)
    )
    grid_spec = pltpu.PrefetchScalarGridSpec(
        num_scalar_prefetch=6,
        grid=(k_pages.shape[0],),
        in_specs=[row, leaf, leaf],
        out_specs=[
            row,
            pl.BlockSpec((requests, 8, LANES), lambda p, *rest: (0, 0, 0)),
        ],
        scratch_shapes=[
            pltpu.VMEM((tree, width), jnp.float32),
            pltpu.VMEM((heads, tree, size), jnp.float32),
            pltpu.VMEM((heads, tree, size), jnp.float32),
        ],
    )
    return pl.pallas_call(
        functools.partial(page_kernel, heads, size),
        grid_spec=grid_spec,
        out_shape=[
            jax.ShapeDtypeStruct((requests, tree, width), jnp.bfloat16),
            jax.ShapeDtypeStruct((requests, 8, LANES), jnp.float32),
        ],
        compiler_params=params(),
        name="page_attention",
    )(*plan, queries, k_pages, v_pages)


def merge_kernel(heads, size, count, *refs):
    sums, logs, out_ref = refs[:count], refs[count : 2 * count], refs[2 * count]
    log_ref = refs[2 * count + 1] if len(refs) > 2 * count + 1 else None
    tree = out_ref.shape[1]
    for request in range(out_ref.shape[0]):
        tables = [ref[request] for ref in logs]
        top = functools.reduce(jnp.maximum, tables)
        total = functools.reduce(lambda a, b: a + b, [jnp.exp(table - top) for table in tables])
        merged = top + jnp.log(total)
        if log_ref is not None:
            log_ref[request] = merged
        shares = [
            jnp.transpose(jnp.where(table > EMPTY, jnp.exp(table - merged), 0.0))
            for table in tables
        ]
        for head in range(heads):
            at = slice(head * size, (head + 1) * size)
            value = jnp.zeros((tree, size), jnp.float32)
            for ref, share in zip(sums, shares):
                factor = share[:tree, head : head + 1]
                term = ref[request, :, at].astype(jnp.float32)
                value = value + jnp.where(factor > 0, term * factor, 0.0)
            out_ref[request, :, at] = value.astype(out_ref.dtype)


def merge_partials(pairs, heads, size, with_logs=True):
    requests, tree, width = pairs[0][0].shape
    group = max(size for size in (1, 2, 4, 8) if requests % size == 0)
    big = pl.BlockSpec((group, tree, width), lambda j: (j, 0, 0))
    small = pl.BlockSpec((group, 8, LANES), lambda j: (j, 0, 0))
    out_specs = [big, small] if with_logs else [big]
    out_shape = [
        jax.ShapeDtypeStruct((requests, tree, width), jnp.bfloat16),
        jax.ShapeDtypeStruct((requests, 8, LANES), jnp.float32),
    ][: len(out_specs)]
    return pl.pallas_call(
        functools.partial(merge_kernel, heads, size, len(pairs)),
        grid=(requests // group,),
        in_specs=[big] * len(pairs) + [small] * len(pairs),
        out_specs=out_specs,
        out_shape=out_shape,
        compiler_params=params(),
        name="merge_partials",
    )(*[pair[0] for pair in pairs], *[pair[1] for pair in pairs])


def page_plan(owner, fill, first_request, requests, all_local, count):
    slots = owner.shape[0]
    me = lax.axis_index("req")
    source = owner // all_local
    local = owner % all_local - first_request
    mine = (owner >= 0) & (local >= 0) & (local < requests)
    index = source ^ me
    index = (index & 1) * (count // 2) + (index >> 1)
    place = jnp.where(mine, index * requests + local, count * requests)
    spot = jnp.arange(slots, dtype=jnp.int32)
    ahead = (place[None, :] < place[:, None]) | (
        (place[None, :] == place[:, None]) & (spot[None, :] < spot[:, None])
    )
    rank = jnp.sum(ahead.astype(jnp.int32), axis=1)
    live = jnp.sum(mine.astype(jnp.int32))
    wanted = jnp.minimum(spot, jnp.maximum(live - 1, 0))
    chosen = rank[None, :] == wanted[:, None]
    take = lambda values: jnp.sum(jnp.where(chosen, values[None, :], 0), axis=1)
    pages, places, fills = take(spot), take(jnp.where(mine, place, 0)), take(fill)
    changed = (places[1:] != places[:-1]).astype(jnp.int32)
    one = jnp.ones((1,), jnp.int32)
    first = jnp.concatenate([one, changed])
    last = jnp.concatenate([changed, one])
    last = jnp.where(spot == live - 1, 1, last)
    return (pages, places, fills, first, last, live[None])


def on_device(
    streams,
    hc_in,
    hc_mix,
    hc_out,
    qkv_weight,
    out_weight,
    up_gate,
    down_weight,
    draft_weight,
    lm_head,
    k_pages,
    v_pages,
    page_owner,
    page_fill,
    cache_len,
    tree_parent,
    accepted_index,
):
    tokens_local = streams.shape[0]
    stream_count = streams.shape[1]
    feature_local = streams.shape[2]
    width = qkv_weight.shape[0]
    req_local = cache_len.shape[0]
    tree_size = tree_parent.shape[1]
    heads = k_pages.shape[2]
    size = k_pages.shape[3]
    draft_count = draft_weight.shape[0]
    parts = lax.axis_size("req")
    all_requests = req_local * parts

    identity = jnp.eye(stream_count, dtype=jnp.float32)
    first_mix, second_mix = identity + hc_mix[0], identity + hc_mix[1]
    mid_in = jnp.sum(first_mix * hc_in[1][None, :], axis=1)
    mid_out = jnp.sum(hc_out[0] * hc_in[1])
    both_mix = jnp.sum(first_mix[:, :, None] * second_mix[None, :, :], axis=1)
    both_out = jnp.sum(hc_out[0][:, None] * second_mix, axis=0)

    reach = ancestors(tree_parent)
    depth = (jnp.sum(reach, axis=2) - 1.0).astype(jnp.int32)
    positions = (cache_len[:, None] + depth).reshape(tokens_local)
    half = size // 2
    freqs = jnp.exp(jnp.arange(half, dtype=jnp.float32) * (-2.0 * math.log(10000.0) / size))
    angles = positions.astype(jnp.float32)[:, None] * freqs[None, :]
    cosine, sine = jnp.cos(angles), jnp.sin(angles)
    cosine = jnp.concatenate([cosine, cosine], axis=1)
    sine = jnp.concatenate([-sine, sine], axis=1)

    k_heads = jnp.transpose(k_pages, (0, 2, 1, 3))
    v_heads = jnp.transpose(v_pages, (0, 2, 1, 3))
    hidden_local = up_gate.shape[2]
    gate_weight, up_weight = up_gate[:, 0], up_gate[:, 1]

    step_requests = req_local // CHUNKS
    step_tokens = step_requests * tree_size
    merge = lambda ours, got: merge_flat(ours, got, heads, size)

    token = None
    attended_in = []
    for chunk in range(CHUNKS):
        rows = slice(chunk * step_tokens, (chunk + 1) * step_tokens)
        stream_vals = streams[rows].astype(jnp.float32)
        mixed_in = blend(stream_vals, hc_in[0])
        if token is not None:
            mixed_in, token = lax.optimization_barrier((mixed_in, token))
        normed, token = gathered_norm(mixed_in, width)
        attended_in.append(normed)

    attn_parts, mlp_parts = [], []
    for chunk in range(CHUNKS):
        rows = slice(chunk * step_tokens, (chunk + 1) * step_tokens)
        asked = slice(chunk * step_requests, (chunk + 1) * step_requests)
        normed = attended_in[chunk]
        projected = jnp.concatenate(
            [
                jnp.dot(normed, qkv_weight[:, third], preferred_element_type=jnp.float32)
                for third in range(3)
            ],
            axis=1,
        )
        queries, keys, values = rotate_all(
            projected, cosine[rows], sine[rows], heads, size, 2 * tree_size
        )
        shape = (step_requests, tree_size, heads * size)
        queries, keys, values = (item.reshape(shape) for item in (queries, keys, values))
        blocks = gather_requests(queries)
        near_last = [index for low in (0, 1) for index in range(parts) if index & 1 == low]
        query_all = jnp.concatenate([blocks[index] for index in near_last])
        plan = page_plan(
            page_owner, page_fill, chunk * step_requests, step_requests, req_local, parts
        )
        sums, logs = page_attention(query_all, k_heads, v_heads, plan, heads, size)
        tree_pair = tree_attention(queries, keys, values, reach[asked], heads, size)
        done = scatter_requests(
            sums.reshape(parts, step_requests, tree_size, heads * size),
            logs.reshape(parts, step_requests, 8, LANES),
            merge,
        )
        part_requests = step_requests // 2
        attended = []
        for part, (ours, got) in enumerate(done):
            own = slice(part * part_requests, (part + 1) * part_requests)
            pairs = [
                tuple(value.reshape((-1,) + value.shape[2:]) for value in pair)
                for pair in (ours, got)
            ] + [(tree_pair[0][own], tree_pair[1][own])]
            attended.append(merge_partials(pairs, heads, size, with_logs=False)[0])
        attended = jnp.concatenate(attended).reshape(step_tokens, heads * size)
        attn_delta = chain_scatter(
            lambda step: jnp.dot(
                attended, columns_for(out_weight, step), preferred_element_type=jnp.float32
            )
        )
        attn_parts.append(attn_delta)

        stream_vals = streams[rows].astype(jnp.float32)
        mixed_mid = blend(stream_vals, mid_in) + mid_out * attn_delta
        normed_mid, token = gathered_norm(mixed_mid, width)
        gate = jnp.dot(normed_mid, gate_weight, preferred_element_type=jnp.float32)
        up = jnp.dot(normed_mid, up_weight, preferred_element_type=jnp.float32)
        hidden = (jax.nn.silu(gate) * up).astype(jnp.bfloat16)
        mlp_parts.append(
            chain_scatter(
                lambda step: jnp.dot(
                    hidden, columns_for(down_weight, step), preferred_element_type=jnp.float32
                )
            )
        )

    attn_delta = jnp.concatenate(attn_parts)
    mlp_delta = jnp.concatenate(mlp_parts)
    stream_vals = streams.astype(jnp.float32)
    new_streams = both_out[None, :, None] * attn_delta[:, None] + (
        hc_out[1][None, :, None] * mlp_delta[:, None]
    )
    for index in range(stream_count):
        new_streams = (
            new_streams + both_mix[index][None, :, None] * stream_vals[:, index : index + 1]
        )
    new_streams = new_streams.astype(jnp.bfloat16)

    rows_taken = jnp.arange(req_local, dtype=jnp.int32) * tree_size + accepted_index
    final_local = (
        jnp.sum(both_out) * attn_delta[rows_taken] + jnp.sum(hc_out[1]) * mlp_delta[rows_taken]
    ) + blend(stream_vals[rows_taken], jnp.sum(both_mix, axis=1))
    final_full = lax.all_gather(final_local, "head", axis=1, tiled=True)
    final_norm = layer_norm(final_full)
    own_columns = lax.dynamic_slice_in_dim(
        final_norm, lax.axis_index("head") * feature_local, feature_local, 1
    )
    branch = jnp.einsum(
        "jd,kde->jke",
        final_norm.astype(jnp.bfloat16),
        draft_weight,
        preferred_element_type=jnp.float32,
    )
    drafted = (own_columns[:, None, :] + jax.nn.silu(branch)).astype(jnp.bfloat16)
    draft_full = lax.all_gather(drafted, "head", axis=2, tiled=True)
    draft_all = lax.all_gather(draft_full, "req", axis=0, tiled=True)
    logits_local = jnp.dot(
        draft_all.reshape(-1, width), lm_head, preferred_element_type=jnp.float32
    )
    logits_local = logits_local.reshape(all_requests, draft_count, -1)
    logits = lax.all_to_all(
        logits_local.astype(jnp.bfloat16), ("req", "head"), split_axis=0, concat_axis=2, tiled=True
    ).astype(logits_local.dtype)
    return (new_streams, logits)


def merge_flat(ours, got, heads, size):
    lead = ours[0].shape[:2]
    pairs = [
        tuple(value.reshape((-1,) + value.shape[2:]) for value in pair) for pair in (ours, got)
    ]
    merged = merge_partials(pairs, heads, size)
    return [value.reshape(lead + value.shape[1:]) for value in merged]


def solution(mesh):
    in_specs = (
        P("req", None, "head"),
        P(),
        P(),
        P(),
        P(None, None, "head"),
        P("head", None),
        P(None, None, "head"),
        P("head", None),
        P(None, None, "head"),
        P(None, ("req", "head")),
        P("req", None, "head", None),
        P("req", None, "head", None),
        P("req"),
        P("req"),
        P("req"),
        P("req", None),
        P("req"),
    )
    out_specs = (P("req", None, "head"), P(("req", "head"), None, None))
    return jax.shard_map(
        on_device, mesh=mesh, in_specs=in_specs, out_specs=out_specs, check_vma=False
    )
```

time: 709 us -> 680 us (0.959); the launches traced: 699 us -> 678 us
  starting transfers between devices: 6.35 us -> 202 us
  waiting for transfers between devices: 302 us -> 124 us
  Pallas kernels: 0 us -> 68.3 us
  blocking collectives: 87.6 us -> 24.6 us
  local copies, waits for them, and re-layouts: 130 us -> 84.2 us
  other arithmetic: 70.1 us -> 62.2 us
  matrix products: 86.8 us -> 94.1 us
    ppermute x0 -> x108, starting transfers between devices: none -> 197 us  [the longest x48 91.4 us: swapped(): return lax.ppermute(values, 'req', [(r, r ^ bit) for r in range(count)])]
    all_gather x3 -> x0, waiting for transfers between devices: 141 us -> none  [the longest x1 50.3 us: on_device(): lax.all_gather(normed, 'head', axis=1, tiled=True)]
    reduce_scatter x3 -> x0, waiting for transfers between devices: 118 us -> none  [the longest x1 60.5 us: on_device(): lax.psum_scatter(jnp.dot(attended, out_weight, preferred_element_type=jnp...]
    ppermute x0 -> x108, waiting for transfers between devices: none -> 71.6 us  [the longest x48 27.4 us: swapped(): return lax.ppermute(values, 'req', [(r, r ^ bit) for r in range(count)])]
    pallas_call x0 -> x16, Pallas kernels: none -> 68.3 us  [the longest x2 38.3 us: page_attention(): pl.pallas_call(functools.partial(page_kernel, heads, size), grid_spec=gri...]
    slice x3 -> x26, local copies, waits for them, and re-layouts: 4.22 us -> 42.7 us  [the longest x1 32.3 us: on_device(): gate_weight, up_weight = (up_gate[:, 0], up_gate[:, 1])]
    unnamed x55 -> x142, local copies, waits for them, and re-layouts: 37.7 us -> 8.67 us
    unnamed x1 -> x0, blocking collectives: 25.4 us -> none
  transfers between devices with their start and end apart: 8 -> 110, of which waited for: 7 -> 29; matrix products, arithmetic and copies ran while one was open for 12% -> 28% of each run, Pallas kernels for 0% -> 10%
where the time goes in v1:
time: 680 us; the launch traced here: 678 us
  starting transfers between devices  202 us (30%)
  waiting for transfers between devices  124 us (18%)
  matrix products  94.1 us (14%)
  local copies, waits for them, and re-layouts  84.2 us (12%)
  Pallas kernels  68.3 us (10%)
  other arithmetic  62.2 us (9%)
  blocking collectives  24.6 us (4%)
  between operations  18.5 us (3%)
    ppermute x48, starting transfers between devices, swapped(): return lax.ppermute(values, 'req', [(r, r ^ bit) for r in range(count)])  91.4 us
    all_gather x1, waiting for transfers between devices, on_device(): draft_all = lax.all_gather(draft_full, 'req', axis=0, tiled=True)  40 us
    pallas_call x2, Pallas kernels, page_attention(): pl.pallas_call(functools.partial(page_kernel, heads, size), grid_spec=gri...  38.3 us
    ppermute x12, starting transfers between devices, chain_scatter(): lax.ppermute(to_right, 'head', [(z, z + 1) for z in range(step)])  36.7 us
    slice x1, local copies, waits for them, and re-layouts, on_device(): gate_weight, up_weight = (up_gate[:, 0], up_gate[:, 1])  32.3 us
    ppermute x48, waiting for transfers between devices, swapped(): return lax.ppermute(values, 'req', [(r, r ^ bit) for r in range(count)])  27.4 us
    ppermute x12, waiting for transfers between devices, chain_gather(): lax.ppermute(left[-1], 'head', [(z, z - 1) for z in range(1, count - step...  27.2 us
    dot_general x2, matrix products, on_device(): up = jnp.dot(normed_mid, up_weight, preferred_element_type=jnp.float32)  26.9 us
  transfers between devices with their start and end apart: 110, of which 29 were waited for; matrix products, arithmetic and copies ran while one was open for 28% of the time, Pallas kernels for 10%

profile of v1, /device:TPU:1, one launch (start us, length us, event | category | flops | bytes accessed | tf_op | source)
XLA Modules:
  0.0 677.9 jit_solution(12673878213673102908)
XLA Ops:
  31.2 5.4 convert_element_type.516
  47.8 32.3 %fusion.171 = (bf16[2048,1,2048]{2,1,0:T(2,128)(2,1)}, bf16[2048,1,2048]{2,1,0:T(2,128)(2,1)}) fusion(bf16[2048,2,2048]{2,1,0:T(2,128)(2,1)} %param.23), kind=kLoop, calls=%fused_computation.435 | loop fusion | bytes 33554432 | tf_op jit(solution)/shard_map/slice | solution.py:500
  87.1 11.9 %copy_bitcast_fusion.2 = (bf16[48,4,128,128]{3,2,1,0:T(8,128)(2,1)}, bf16[48,4,128,128]{3,2,1,0:T(8,128)(2,1)}) fusion(bf16[48,128,4,128]{3,2,1,0:T(4,128)(2,1)} %param.28, bf16[48,128,4,128]{3,2,1,0:T(4,128)(2,1)} %param.27), kind=kLoop, calls=%fused_computation.7 | loop fusion | bytes 25165824 | tf_op jit(solution)/shard_map/transpose | solution.py:498
  112.0 5.9 collective-permute-done.7
  119.3 8.6 %collective-permute-done.8 = bf16[384,512]{1,0:T(8,128)(2,1)S(1)} collective-permute-done((bf16[384,512]{1,0:T(8,128)(2,1)}, bf16[384,512]{1,0:T(8,128)(2,1)S(1)}, u32[]{:S(2)}, u32[]{:S(2)}) %collective-permute-start.8) | collective-permute-done | bytes 393248 | tf_op jit(solution)/shard_map/ppermute | solution.py:58
  141.2 5.9 tree_attention.2
  149.0 5.3 collective-permute-start.15
  168.5 5.4 collective-permute-done.45
  175.4 23.7 %page_attention.2 = (bf16[64,48,512]{2,1,0:T(8,128)(2,1)S(1)}, f32[64,8,128]{2,1,0:T(8,128)S(1)}) custom-call(s32[48]{0:T(128)S(1)} %get-tuple-element.95.page_ref, s32[48]{0:T(128)S(1)} %get-tuple-element.94.place_ref, s32[48]{0:T(128)S(1)} %get-tuple-element.93.fill_ref, s32[48]{0:T(128)S(1)} %get-tuple-element.284.first_ref, ...), custom_call_target="tpu_custom_call" | custom-call | tf_op jit(solution)/shard_map/page_attention/pallas_call | solution.py:364
  201.3 28.0 %collective-permute-start.23 = (bf16[4,8,48,512]{3,2,1,0:T(8,128)(2,1)S(1)}, bf16[4,8,48,512]{3,2,1,0:T(8,128)(2,1)S(1)}, u32[]{:S(2)}, u32[]{:S(2)}) collective-permute-start(bf16[4,8,48,512]{3,2,1,0:T(8,128)(2,1)S(1)} %bitcast.284), channel_id=1, source_target_pairs={{0,4},{4,0},{8,12},{12,8},{16,20},{20,16},{24,28},{28,24},{1,5},{5... | collective-permute-start | bytes 4718600 | tf_op jit(solution)/shard_map/ppermute | solution.py:149
  235.7 5.9 tree_attention.3
  243.4 9.1 %collective-permute-start.54 = (bf16[4,48,512]{2,1,0:T(8,128)(2,1)S(1)}, bf16[4,48,512]{2,1,0:T(8,128)(2,1)S(1)}, u32[]{:S(2)}, u32[]{:S(2)}) collective-permute-start(bf16[4,48,512]{2,1,0:T(8,128)(2,1)S(1)} %bitcast.301), channel_id=1, source_target_pairs={{0,4},{4,0},{8,12},{12,8},{16,20},{20,16},{24,28},{28,24},{1,5},{5... | collective-permute-start | bytes 589832 | tf_op jit(solution)/shard_map/ppermute | solution.py:149
  252.8 6.8 %collective-permute-done.52 = bf16[4,48,512]{2,1,0:T(8,128)(2,1)S(1)} collective-permute-done((bf16[4,48,512]{2,1,0:T(8,128)(2,1)S(1)}, bf16[4,48,512]{2,1,0:T(8,128)(2,1)S(1)}, u32[]{:S(2)}, u32[]{:S(2)}) %collective-permute-start.52) | collective-permute-done | bytes 196640 | tf_op jit(solution)/shard_map/ppermute | solution.py:149
  266.6 14.6 %page_attention.3 = (bf16[64,48,512]{2,1,0:T(8,128)(2,1)S(1)}, f32[64,8,128]{2,1,0:T(8,128)S(1)}) custom-call(s32[48]{0:T(128)S(1)} %get-tuple-element.99.page_ref, s32[48]{0:T(128)S(1)} %get-tuple-element.100.place_ref, s32[48]{0:T(128)S(1)} %get-tuple-element.101.fill_ref, s32[48]{0:T(128)S(1)} %get-tuple-element.286.first_ref, ...), custom_call_target="tpu_custom_call" | custom-call | tf_op jit(solution)/shard_map/page_attention/pallas_call | solution.py:364
  281.6 4.4 merge_partials.10
  286.2 16.6 %collective-permute-start.26 = (f32[2,4,8,128]{3,2,1,0:T(8,128)S(1)}, f32[2,4,8,128]{3,2,1,0:T(8,128)S(1)}, u32[]{:S(2)}, u32[]{:S(2)}) collective-permute-start(f32[2,4,8,128]{3,2,1,0:T(8,128)S(1)} %pad_maximum_fusion.21), channel_id=1, source_target_pairs={{0,8},{4,12},{8,0},{12,4},{16,24},{20,28},{24,16},{28,20},{1,9},{5... | collective-permute-start | bytes 98312 | tf_op jit(solution)/shard_map/ppermute | solution.py:149
  304.5 8.3 %collective-permute-done.25 = bf16[2,4,48,512]{3,2,1,0:T(8,128)(2,1)S(1)} collective-permute-done((bf16[2,4,48,512]{3,2,1,0:T(8,128)(2,1)S(1)}, bf16[2,4,48,512]{3,2,1,0:T(8,128)(2,1)S(1)}, u32[]{:S(2)}, u32[]{:S(2)}) %collective-permute-start.25) | collective-permute-done | bytes 393248 | tf_op jit(solution)/shard_map/ppermute | solution.py:149
  410.1 7.0 %collective-permute-start.93 = (bf16[384,512]{1,0:T(8,128)(2,1)}, bf16[384,512]{1,0:T(8,128)(2,1)S(1)}, u32[]{:S(2)}, u32[]{:S(2)}) collective-permute-start(bf16[384,512]{1,0:T(8,128)(2,1)} %subtract_convert_fusion), channel_id=1, source_target_pairs={{0,1},{1,2},{2,3},{4,5},{5,6},{6,7},{8,9},{9,10},{10,11},{12,13},{... | collective-permute-start | bytes 1179656 | tf_op jit(solution)/shard_map/ppermute | solution.py:55
  424.0 8.8 %fusion.3 = f32[384,2048]{1,0:T(8,128)} fusion(bf16[2048,1,2048]{2,1,0:T(2,128)(2,1)S(1)} %bitcast.273, bf16[384,512]{1,0:T(8,128)(2,1)} %get-tuple-element.143, bf16[384,512]{1,0:T(8,128)(2,1)} %get-tuple-element.142, bf16[384,512]{1,0:T(8,128)(2,1)S(1)} %get-tuple-element.141, bf16[384,512]{1,0:T(8,128)(2,1)S(1)} %get-tuple-element.140), kind=kOutput, calls=%fused_computation.11 | convolution fusion | flops 3227516928 | bytes 13107200 | tf_op jit(solution)/shard_map/dot_general | solution.py:567
  432.8 14.1 %multiply_convert_fusion.1 = bf16[384,2048]{1,0:T(8,128)(2,1)} fusion(f32[384,2048]{1,0:T(8,128)} %fusion.3, bf16[2048,1,2048]{2,1,0:T(2,128)(2,1)} %get-tuple-element.116, bf16[384,512]{1,0:T(8,128)(2,1)S(1)} %copy-done.17, bf16[384,512]{1,0:T(8,128)(2,1)S(1)} %copy-done.16, bf16[384,512]{1,0:T(8,128)(2,1)S(1)} %get-tuple-element.141, ...), kind=kOutput, calls=%fused_computation.15 | convolution fusion | flops 3232235520 | bytes 14680064 | tf_op jit(solution)/shard_map/dot_general | solution.py:568
  460.4 5.4 collective-permute-start.87
  468.0 7.3 %collective-permute-done.101 = bf16[384,512]{1,0:T(8,128)(2,1)S(1)} collective-permute-done((bf16[384,512]{1,0:T(8,128)(2,1)S(1)}, bf16[384,512]{1,0:T(8,128)(2,1)S(1)}, u32[]{:S(2)}, u32[]{:S(2)}) %collective-permute-start.101) | collective-permute-done | bytes 393248 | tf_op jit(solution)/shard_map/ppermute | solution.py:58
  477.7 8.6 %fusion.2 = f32[384,2048]{1,0:T(8,128)} fusion(bf16[2048,1,2048]{2,1,0:T(2,128)(2,1)S(1)} %bitcast.275, bf16[384,512]{1,0:T(8,128)(2,1)} %get-tuple-element.151, bf16[384,512]{1,0:T(8,128)(2,1)S(1)} %get-tuple-element.150, bf16[384,512]{1,0:T(8,128)(2,1)S(1)} %get-tuple-element.149, bf16[384,512]{1,0:T(8,128)(2,1)S(1)} %get-tuple-element.148), kind=kOutput, calls=%fused_computation.10 | convolution fusion | flops 3227516928 | bytes 13107200 | tf_op jit(solution)/shard_map/dot_general | solution.py:567
  486.3 12.9 %multiply_convert_fusion = bf16[384,2048]{1,0:T(8,128)(2,1)S(1)} fusion(f32[384,2048]{1,0:T(8,128)} %fusion.2, bf16[2048,1,2048]{2,1,0:T(2,128)(2,1)} %get-tuple-element.116, bf16[384,512]{1,0:T(8,128)(2,1)S(1)} %copy-done.15, bf16[384,512]{1,0:T(8,128)(2,1)} %copy-done.14, bf16[384,512]{1,0:T(8,128)(2,1)S(1)} %get-tuple-element.149, ...), kind=kOutput, calls=%fused_computation.14 | convolution fusion | flops 3232235520 | bytes 14680064 | tf_op jit(solution)/shard_map/dot_general | solution.py:568
  551.7 13.4 %all_gather.9 = f32[16,2048]{1,0:T(8,128)S(1)} all-gather(f32[16,512]{1,0:T(8,128)S(1)} %fusion.95), channel_id=1, replica_groups=mesh['req'=8,'head'=4] {'head'}, dimensions={1}, use_global_device_ids=true | all-gather | bytes 163840 | tf_op jit(solution)/shard_map/all_gather | solution.py:594
  568.3 11.2 %all_gather.10 = bf16[16,2,2048]{2,0,1:T(8,128)(2,1)} all-gather(bf16[16,2,512]{2,0,1:T(8,128)(2,1)S(1)} %add_convert_fusion.17), channel_id=1, replica_groups=mesh['req'=8,'head'=4] {'head'}, dimensions={2}, use_global_device_ids=true | all-gather | bytes 163840 | tf_op jit(solution)/shard_map/all_gather | solution.py:606
  579.5 5.3 fusion.175
  586.8 40.0 %all-gather.2.cloned.1.call-done = bf16[128,2,2048]{2,0,1:T(8,128)(2,1)} async-done(((bf16[16,2,2048]{2,0,1:T(8,128)(2,1)}), bf16[128,2,2048]{2,0,1:T(8,128)(2,1)}) %all-gather.2.cloned.1.call-update) | async-done | bytes 1048592 | tf_op jit(solution)/shard_map/all_gather | solution.py:607
  626.8 6.8 %fusion.6 = bf16[128,2,1572]{0,2,1:T(8,128)(2,1)S(1)} fusion(bf16[128,2,2048]{2,0,1:T(8,128)(2,1)} %all-gather.2.cloned.1.call-done, bf16[2048,1572]{0,1:T(8,128)(2,1)} %param.26), kind=kOutput, calls=%fused_computation.16 | convolution fusion | flops 1648763904 | bytes 8292352 | tf_op jit(solution)/shard_map/dot_general | solution.py:608
  635.8 5.1 all-to-all-start
  644.6 6.4 add_convert_fusion
  651.0 11.9 %all-to-all-done = bf16[128,2,1572]{2,1,0:T(2,128)(2,1)} async-done(((bf16[128,2,1572]{2,1,0:T(2,128)(2,1)}), bf16[128,2,1572]{2,1,0:T(2,128)(2,1)}, u32[]{:S(2)}, u32[]{:S(2)}) %all-to-all-start) | async-done | bytes 804896 | tf_op jit(solution)/shard_map/all_to_all | solution.py:612
  (562 shorter events, 297.1 us)
Async XLA Ops:
  7.2 619.6 %all-gather.2.cloned.1.call-start = ((), (), s32[]{:S(2)}) async-start(), calls=%async_computation.1 | async-start | bytes 1179648 | tf_op jit(solution)/shard_map/all_gather | solution.py:607
  18.6 90.3 %collective-permute-start.3 = (f32[2,384]{1,0:T(2,128)}, f32[2,384]{1,0:T(2,128)}, u32[]{:S(2)}, u32[]{:S(2)}) collective-permute-start(f32[2,384]{1,0:T(2,128)} %get-tuple-element.241), channel_id=1, source_target_pairs={{0,1},{1,2},{2,3},{3,0},{4,5},{5,6},{6,7},{7,4},{8,9},{9,10},{10,1... | collective-permute-start | bytes 9224 | tf_op jit(solution)/shard_map/ppermute | solution.py:106
  20.7 88.8 %collective-permute-start.4 = (f32[2,384]{1,0:T(2,128)}, f32[2,384]{1,0:T(2,128)}, u32[]{:S(2)}, u32[]{:S(2)}) collective-permute-start(f32[2,384]{1,0:T(2,128)} %get-tuple-element.241), channel_id=1, source_target_pairs={{0,2},{1,3},{2,0},{3,1},{4,6},{5,7},{6,4},{7,5},{8,10},{9,11},{10,... | collective-permute-start | bytes 9224 | tf_op jit(solution)/shard_map/ppermute | solution.py:106
  23.0 87.2 %collective-permute-start.5 = (f32[2,384]{1,0:T(2,128)}, f32[2,384]{1,0:T(2,128)}, u32[]{:S(2)}, u32[]{:S(2)}) collective-permute-start(f32[2,384]{1,0:T(2,128)} %get-tuple-element.241), channel_id=1, source_target_pairs={{0,3},{1,0},{2,1},{3,2},{4,7},{5,4},{6,5},{7,6},{8,11},{9,8},{10,9... | collective-permute-start | bytes 9224 | tf_op jit(solution)/shard_map/ppermute | solution.py:106
  24.9 79.2 %collective-permute-start = (bf16[384,512]{1,0:T(8,128)(2,1)}, bf16[384,512]{1,0:T(8,128)(2,1)}, u32[]{:S(2)}, u32[]{:S(2)}) collective-permute-start(bf16[384,512]{1,0:T(8,128)(2,1)} %fusion.69), channel_id=1, source_target_pairs={{0,1},{1,2},{2,3},{4,5},{5,6},{6,7},{8,9},{9,10},{10,11},{12,13},{... | collective-permute-start | bytes 1179656 | tf_op jit(solution)/shard_map/ppermute | solution.py:55
  28.0 77.6 %collective-permute-start.6 = (bf16[384,512]{1,0:T(8,128)(2,1)}, bf16[384,512]{1,0:T(8,128)(2,1)}, u32[]{:S(2)}, u32[]{:S(2)}) collective-permute-start(bf16[384,512]{1,0:T(8,128)(2,1)} %fusion.69), channel_id=1, source_target_pairs={{1,0},{2,1},{3,2},{5,4},{6,5},{7,6},{9,8},{10,9},{11,10},{13,12},{... | collective-permute-start | bytes 1179656 | tf_op jit(solution)/shard_map/ppermute | solution.py:58
  136.1 18.3 %collective-permute-start.9 = (bf16[4,48,512]{2,1,0:T(8,128)(2,1)S(1)}, bf16[4,48,512]{2,1,0:T(8,128)(2,1)S(1)}, u32[]{:S(2)}, u32[]{:S(2)}) collective-permute-start(bf16[4,48,512]{2,1,0:T(8,128)(2,1)S(1)} %bitcast.291), channel_id=1, source_target_pairs={{0,8},{4,12},{8,0},{12,4},{16,24},{20,28},{24,16},{28,20},{1,9},{5... | collective-permute-start | bytes 589832 | tf_op jit(solution)/shard_map/ppermute | solution.py:149
  149.0 16.7 %collective-permute-start.15 = (bf16[4,48,512]{2,1,0:T(8,128)(2,1)S(1)}, bf16[4,48,512]{2,1,0:T(8,128)(2,1)S(1)}, u32[]{:S(2)}, u32[]{:S(2)}) collective-permute-start(bf16[4,48,512]{2,1,0:T(8,128)(2,1)S(1)} %bitcast.293), channel_id=1, source_target_pairs={{0,4},{4,0},{8,12},{12,8},{16,20},{20,16},{24,28},{28,24},{1,5},{5... | collective-permute-start | bytes 589832 | tf_op jit(solution)/shard_map/ppermute | solution.py:149
  167.9 31.2 %collective-permute-start.40 = (bf16[384,512]{1,0:T(8,128)(2,1)S(1)}, bf16[384,512]{1,0:T(8,128)(2,1)S(1)}, u32[]{:S(2)}, u32[]{:S(2)}) collective-permute-start(bf16[384,512]{1,0:T(8,128)(2,1)S(1)} %collective-permute-done.39), channel_id=1, source_target_pairs={{1,2},{2,3},{5,6},{6,7},{9,10},{10,11},{13,14},{14,15},{17,18},{18... | collective-permute-start | bytes 1179656 | tf_op jit(solution)/shard_map/ppermute | solution.py:55
  173.9 25.8 %collective-permute-start.46 = (bf16[384,512]{1,0:T(8,128)(2,1)S(1)}, bf16[384,512]{1,0:T(8,128)(2,1)S(1)}, u32[]{:S(2)}, u32[]{:S(2)}) collective-permute-start(bf16[384,512]{1,0:T(8,128)(2,1)S(1)} %collective-permute-done.45), channel_id=1, source_target_pairs={{1,0},{2,1},{5,4},{6,5},{9,8},{10,9},{13,12},{14,13},{17,16},{18,1... | collective-permute-start | bytes 1179656 | tf_op jit(solution)/shard_map/ppermute | solution.py:58
  199.1 30.4 %collective-permute-start.41 = (bf16[384,512]{1,0:T(8,128)(2,1)S(1)}, bf16[384,512]{1,0:T(8,128)(2,1)S(1)}, u32[]{:S(2)}, u32[]{:S(2)}) collective-permute-start(bf16[384,512]{1,0:T(8,128)(2,1)S(1)} %collective-permute-done.40), channel_id=1, source_target_pairs={{2,3},{6,7},{10,11},{14,15},{18,19},{22,23},{26,27},{30,31}} | collective-permute-start | bytes 1179656 | tf_op jit(solution)/shard_map/ppermute | solution.py:55
  199.8 29.7 %collective-permute-start.47 = (bf16[384,512]{1,0:T(8,128)(2,1)S(1)}, bf16[384,512]{1,0:T(8,128)(2,1)S(1)}, u32[]{:S(2)}, u32[]{:S(2)}) collective-permute-start(bf16[384,512]{1,0:T(8,128)(2,1)S(1)} %collective-permute-done.46), channel_id=1, source_target_pairs={{1,0},{5,4},{9,8},{13,12},{17,16},{21,20},{25,24},{29,28}} | collective-permute-start | bytes 1179656 | tf_op jit(solution)/shard_map/ppermute | solution.py:58
  201.3 80.3 %collective-permute-start.23 = (bf16[4,8,48,512]{3,2,1,0:T(8,128)(2,1)S(1)}, bf16[4,8,48,512]{3,2,1,0:T(8,128)(2,1)S(1)}, u32[]{:S(2)}, u32[]{:S(2)}) collective-permute-start(bf16[4,8,48,512]{3,2,1,0:T(8,128)(2,1)S(1)} %bitcast.284), channel_id=1, source_target_pairs={{0,4},{4,0},{8,12},{12,8},{16,20},{20,16},{24,28},{28,24},{1,5},{5... | collective-permute-start | bytes 4718600 | tf_op jit(solution)/shard_map/ppermute | solution.py:149
  229.4 52.2 %collective-permute-start.24 = (f32[4,8,8,128]{3,2,1,0:T(8,128)S(1)}, f32[4,8,8,128]{3,2,1,0:T(8,128)S(1)}, u32[]{:S(2)}, u32[]{:S(2)}) collective-permute-start(f32[4,8,8,128]{3,2,1,0:T(8,128)S(1)} %bitcast.302), channel_id=1, source_target_pairs={{0,4},{4,0},{8,12},{12,8},{16,20},{20,16},{24,28},{28,24},{1,5},{5... | collective-permute-start | bytes 393224 | tf_op jit(solution)/shard_map/ppermute | solution.py:149
  234.3 18.2 %collective-permute-start.50 = (bf16[4,48,512]{2,1,0:T(8,128)(2,1)S(1)}, bf16[4,48,512]{2,1,0:T(8,128)(2,1)S(1)}, u32[]{:S(2)}, u32[]{:S(2)}) collective-permute-start(bf16[4,48,512]{2,1,0:T(8,128)(2,1)S(1)} %bitcast.299), channel_id=1, source_target_pairs={{0,16},{4,20},{8,24},{12,28},{16,0},{20,4},{24,8},{28,12},{1,17},{... | collective-permute-start | bytes 589832 | tf_op jit(solution)/shard_map/ppermute | solution.py:149
  243.4 20.0 %collective-permute-start.54 = (bf16[4,48,512]{2,1,0:T(8,128)(2,1)S(1)}, bf16[4,48,512]{2,1,0:T(8,128)(2,1)S(1)}, u32[]{:S(2)}, u32[]{:S(2)}) collective-permute-start(bf16[4,48,512]{2,1,0:T(8,128)(2,1)S(1)} %bitcast.301), channel_id=1, source_target_pairs={{0,4},{4,0},{8,12},{12,8},{16,20},{20,16},{24,28},{28,24},{1,5},{5... | collective-permute-start | bytes 589832 | tf_op jit(solution)/shard_map/ppermute | solution.py:149
  281.5 54.0 %collective-permute-start.62 = (bf16[4,8,48,512]{3,2,1,0:T(8,128)(2,1)S(1)}, bf16[4,8,48,512]{3,2,1,0:T(8,128)(2,1)S(1)}, u32[]{:S(2)}, u32[]{:S(2)}) collective-permute-start(bf16[4,8,48,512]{3,2,1,0:T(8,128)(2,1)S(1)} %bitcast.285), channel_id=1, source_target_pairs={{0,4},{4,0},{8,12},{12,8},{16,20},{20,16},{24,28},{28,24},{1,5},{5... | collective-permute-start | bytes 4718600 | tf_op jit(solution)/shard_map/ppermute | solution.py:149
  286.2 18.3 %collective-permute-start.26 = (f32[2,4,8,128]{3,2,1,0:T(8,128)S(1)}, f32[2,4,8,128]{3,2,1,0:T(8,128)S(1)}, u32[]{:S(2)}, u32[]{:S(2)}) collective-permute-start(f32[2,4,8,128]{3,2,1,0:T(8,128)S(1)} %pad_maximum_fusion.21), channel_id=1, source_target_pairs={{0,8},{4,12},{8,0},{12,4},{16,24},{20,28},{24,16},{28,20},{1,9},{5... | collective-permute-start | bytes 98312 | tf_op jit(solution)/shard_map/ppermute | solution.py:149
  334.8 17.9 %collective-permute-start.37 = (bf16[384,512]{1,0:T(8,128)(2,1)S(1)}, bf16[384,512]{1,0:T(8,128)(2,1)S(1)}, u32[]{:S(2)}, u32[]{:S(2)}) collective-permute-start(bf16[384,512]{1,0:T(8,128)(2,1)S(1)} %get-tuple-element.159), channel_id=1, source_target_pairs={{2,1},{3,2},{6,5},{7,6},{10,9},{11,10},{14,13},{15,14},{18,17},{19... | collective-permute-start | bytes 1179656 | tf_op jit(solution)/shard_map/ppermute | solution.py:96
  343.5 21.5 %collective-permute-start.35 = (bf16[384,512]{1,0:T(8,128)(2,1)S(1)}, bf16[384,512]{1,0:T(8,128)(2,1)S(1)}, u32[]{:S(2)}, u32[]{:S(2)}) collective-permute-start(bf16[384,512]{1,0:T(8,128)(2,1)S(1)} %add_convert_fusion.15), channel_id=1, source_target_pairs={{0,1},{1,2},{2,3},{4,5},{5,6},{6,7},{8,9},{9,10},{10,11},{12,13},{... | collective-permute-start | bytes 1179656 | tf_op jit(solution)/shard_map/ppermute | solution.py:95
  361.0 16.5 %collective-permute-start.72 = (bf16[384,512]{1,0:T(8,128)(2,1)S(1)}, bf16[384,512]{1,0:T(8,128)(2,1)S(1)}, u32[]{:S(2)}, u32[]{:S(2)}) collective-permute-start(bf16[384,512]{1,0:T(8,128)(2,1)S(1)} %convolution_convert_fusion), channel_id=1, source_target_pairs={{0,1},{4,5},{8,9},{12,13},{16,17},{20,21},{24,25},{28,29}} | collective-permute-start | bytes 1179656 | tf_op jit(solution)/shard_map/ppermute | solution.py:95
  369.3 17.4 %collective-permute-start.78 = (bf16[384,512]{1,0:T(8,128)(2,1)S(1)}, bf16[384,512]{1,0:T(8,128)(2,1)S(1)}, u32[]{:S(2)}, u32[]{:S(2)}) collective-permute-start(bf16[384,512]{1,0:T(8,128)(2,1)S(1)} %subtract_convert_fusion.1), channel_id=1, source_target_pairs={{0,1},{1,2},{2,3},{4,5},{5,6},{6,7},{8,9},{9,10},{10,11},{12,13},{... | collective-permute-start | bytes 1179656 | tf_op jit(solution)/shard_map/ppermute | solution.py:55
  396.4 22.2 %collective-permute-start.80 = (bf16[384,512]{1,0:T(8,128)(2,1)S(1)}, bf16[384,512]{1,0:T(8,128)(2,1)S(1)}, u32[]{:S(2)}, u32[]{:S(2)}) collective-permute-start(bf16[384,512]{1,0:T(8,128)(2,1)S(1)} %collective-permute-done.79), channel_id=1, source_target_pairs={{2,3},{6,7},{10,11},{14,15},{18,19},{22,23},{26,27},{30,31}} | collective-permute-start | bytes 1179656 | tf_op jit(solution)/shard_map/ppermute | solution.py:55
  397.1 22.4 %collective-permute-start.86 = (bf16[384,512]{1,0:T(8,128)(2,1)S(1)}, bf16[384,512]{1,0:T(8,128)(2,1)S(1)}, u32[]{:S(2)}, u32[]{:S(2)}) collective-permute-start(bf16[384,512]{1,0:T(8,128)(2,1)S(1)} %collective-permute-done.85), channel_id=1, source_target_pairs={{1,0},{5,4},{9,8},{13,12},{17,16},{21,20},{25,24},{29,28}} | collective-permute-start | bytes 1179656 | tf_op jit(solution)/shard_map/ppermute | solution.py:58
  408.8 45.6 %collective-permute-start.99 = (bf16[384,512]{1,0:T(8,128)(2,1)}, bf16[384,512]{1,0:T(8,128)(2,1)S(1)}, u32[]{:S(2)}, u32[]{:S(2)}) collective-permute-start(bf16[384,512]{1,0:T(8,128)(2,1)} %subtract_convert_fusion), channel_id=1, source_target_pairs={{1,0},{2,1},{3,2},{5,4},{6,5},{7,6},{9,8},{10,9},{11,10},{13,12},{... | collective-permute-start | bytes 1179656 | tf_op jit(solution)/shard_map/ppermute | solution.py:58
  410.1 45.6 %collective-permute-start.93 = (bf16[384,512]{1,0:T(8,128)(2,1)}, bf16[384,512]{1,0:T(8,128)(2,1)S(1)}, u32[]{:S(2)}, u32[]{:S(2)}) collective-permute-start(bf16[384,512]{1,0:T(8,128)(2,1)} %subtract_convert_fusion), channel_id=1, source_target_pairs={{0,1},{1,2},{2,3},{4,5},{5,6},{6,7},{8,9},{9,10},{10,11},{12,13},{... | collective-permute-start | bytes 1179656 | tf_op jit(solution)/shard_map/ppermute | solution.py:55
  417.1 41.9 %collective-permute-start.96 = (f32[2,384]{1,0:T(2,128)S(1)}, f32[2,384]{1,0:T(2,128)S(1)}, u32[]{:S(2)}, u32[]{:S(2)}) collective-permute-start(f32[2,384]{1,0:T(2,128)S(1)} %get-tuple-element.243), channel_id=1, source_target_pairs={{0,1},{1,2},{2,3},{3,0},{4,5},{5,6},{6,7},{7,4},{8,9},{9,10},{10,1... | collective-permute-start | bytes 9224 | tf_op jit(solution)/shard_map/ppermute | solution.py:106
  418.6 41.8 %collective-permute-start.97 = (f32[2,384]{1,0:T(2,128)S(1)}, f32[2,384]{1,0:T(2,128)S(1)}, u32[]{:S(2)}, u32[]{:S(2)}) collective-permute-start(f32[2,384]{1,0:T(2,128)S(1)} %get-tuple-element.243), channel_id=1, source_target_pairs={{0,2},{1,3},{2,0},{3,1},{4,6},{5,7},{6,4},{7,5},{8,10},{9,11},{10,... | collective-permute-start | bytes 9224 | tf_op jit(solution)/shard_map/ppermute | solution.py:106
  419.5 46.3 %collective-permute-start.98 = (f32[2,384]{1,0:T(2,128)S(1)}, f32[2,384]{1,0:T(2,128)S(1)}, u32[]{:S(2)}, u32[]{:S(2)}) collective-permute-start(f32[2,384]{1,0:T(2,128)S(1)} %get-tuple-element.243), channel_id=1, source_target_pairs={{0,3},{1,0},{2,1},{3,2},{4,7},{5,4},{6,5},{7,6},{8,11},{9,8},{10,9... | collective-permute-start | bytes 9224 | tf_op jit(solution)/shard_map/ppermute | solution.py:106
  459.0 50.5 %collective-permute-start.90 = (bf16[384,512]{1,0:T(8,128)(2,1)}, bf16[384,512]{1,0:T(8,128)(2,1)}, u32[]{:S(2)}, u32[]{:S(2)}) collective-permute-start(bf16[384,512]{1,0:T(8,128)(2,1)} %fusion.45), channel_id=1, source_target_pairs={{3,2},{7,6},{11,10},{15,14},{19,18},{23,22},{27,26},{31,30}} | collective-permute-start | bytes 1179656 | tf_op jit(solution)/shard_map/ppermute | solution.py:96
  460.4 49.0 %collective-permute-start.87 = (bf16[384,512]{1,0:T(8,128)(2,1)}, bf16[384,512]{1,0:T(8,128)(2,1)}, u32[]{:S(2)}, u32[]{:S(2)}) collective-permute-start(bf16[384,512]{1,0:T(8,128)(2,1)} %fusion.63), channel_id=1, source_target_pairs={{0,1},{4,5},{8,9},{12,13},{16,17},{20,21},{24,25},{28,29}} | collective-permute-start | bytes 1179656 | tf_op jit(solution)/shard_map/ppermute | solution.py:95
  635.8 27.1 %all-to-all-start = ((bf16[128,2,1572]{2,1,0:T(2,128)(2,1)}), bf16[128,2,1572]{2,1,0:T(2,128)(2,1)}, u32[]{:S(2)}, u32[]{:S(2)}) async-start(bf16[128,2,1572]{2,1,0:T(2,128)(2,1)} %copy.91), calls=%async_computation | async-start | bytes 1703936 | tf_op jit(solution)/shard_map/all_to_all | solution.py:612
  (133 other events, 1939.4 us)
Sparse Core Ops, SparseCore 0:
  579.6 47.1 all-gather.1

commit v2 on v1

--- a/solution.py
+++ b/solution.py
@@ -75,13 +75,8 @@
     return blocks
 
 
-def chain_scatter(share):
+def chain_scatter(shares):
     count = lax.axis_size("head")
-    shares = {}
-    for step in range(1, count):
-        for key in (step, count - step):
-            if key not in shares:
-                shares[key] = share(key).astype(jnp.bfloat16)
     from_left = from_right = None
     for step in range(1, count):
         to_right, to_left = shares[step], shares[count - step]
@@ -96,7 +91,8 @@
         from_right = lax.ppermute(
             to_left, "head", [(z, z - 1) for z in range(count - step, count)]
         )
-    return share(0) + from_left.astype(jnp.float32) + from_right.astype(jnp.float32)
+    own = shares[0].astype(jnp.float32)
+    return own + from_left.astype(jnp.float32) + from_right.astype(jnp.float32)
 
 
 def shift_gather(small):
@@ -137,13 +133,6 @@
     return jnp.concatenate(normed, axis=1), right[-1]
 
 
-def columns_for(weight, step):
-    count = lax.axis_size("head")
-    width = weight.shape[1] // count
-    owner = (lax.axis_index("head") - step) % count
-    return lax.dynamic_slice_in_dim(weight, owner * width, width, 1)
-
-
 def swapped(values, bit):
     count = lax.axis_size("req")
     return lax.ppermute(values, "req", [(r, r ^ bit) for r in range(count)])
@@ -160,14 +149,12 @@
     parts = []
     for part, order in enumerate(orders):
         blocks = {0: values[part * half : (part + 1) * half]}
-        for bit in list(order) + [near]:
+        for bit in order:
             for index in list(blocks):
                 blocks[index ^ bit] = swapped(blocks[index], bit)
         parts.append(blocks)
-    return [
-        jnp.concatenate([blocks[index] for blocks in parts])
-        for index in range(lax.axis_size("req"))
-    ]
+    even = jnp.concatenate([blocks[index] for index in sorted(parts[0]) for blocks in parts])
+    return even, swapped(even, near)
 
 
 def scatter_requests(sums, logs, merge):
@@ -177,7 +164,7 @@
     state = []
     mine = [sums[:far], logs[:far]]
     theirs = [swapped(sums[far:], near), swapped(logs[far:], near)]
-    merged = merge(mine, theirs)
+    merged = first_merged = merge(mine, theirs)
     half = sums.shape[1] // 2
     done = []
     for part, order in enumerate(orders):
@@ -192,7 +179,7 @@
             places = [places[at] for at in stay]
             kept = merge(ours, got) if place < len(order) - 1 else (ours, got)
         done.append(kept)
-    return done
+    return done, first_merged[1]
 
 
 def rotate_kernel(heads, size, scale, x_ref, cos_ref, sin_ref, q_ref, k_ref, v_ref):
@@ -282,7 +269,8 @@
     first_ref,
     last_ref,
     live_ref,
-    q_ref,
+    even_ref,
+    odd_ref,
     k_ref,
     v_ref,
     out_ref,
@@ -292,7 +280,8 @@
     total_ref,
 ):
     step = pl.program_id(0)
-    tree = q_ref.shape[1]
+    tree = even_ref.shape[1]
+    spans = [slice(head * size, (head + 1) * size) for head in range(heads)]
 
     @pl.when(step == 0)
     def _():
@@ -307,52 +296,72 @@
             total_ref[...] = jnp.zeros(total_ref.shape, jnp.float32)
 
         entries = k_ref.shape[2]
+        is_even = place_ref[step] < log_ref.shape[0] // 2
+        asked = jnp.where(is_even, even_ref[0], odd_ref[0])
         valid = lax.broadcasted_iota(jnp.int32, (tree, entries), 1) < fill_ref[step]
-        for head in range(heads):
-            at = slice(head * size, (head + 1) * size)
-            scores = lax.dot_general(
-                q_ref[0, :, at],
+        scores = [
+            lax.dot_general(
+                asked[:, span],
                 k_ref[0, head],
                 (((1,), (1,)), ((), ())),
                 preferred_element_type=jnp.float32,
             )
-            scores = jnp.where(valid, scores, NEG_FILL)
-            before = top_ref[head]
-            top = jnp.maximum(before, jnp.max(scores, axis=1, keepdims=True))
-            weights = jnp.where(valid, jnp.exp(scores - top), 0.0)
-            decay = jnp.exp(before - top)
-            top_ref[head] = top
-            total_ref[head] = total_ref[head] * decay + jnp.sum(weights, axis=1, keepdims=True)
-            acc_ref[:, at] = acc_ref[:, at] * decay + jnp.dot(
-                weights.astype(jnp.bfloat16), v_ref[0, head], preferred_element_type=jnp.float32
+            for head, span in enumerate(spans)
+        ]
+        scores = [jnp.where(valid, score, NEG_FILL) for score in scores]
+        before = [top_ref[head] for head in range(heads)]
+        tops = [
+            jnp.maximum(old, jnp.max(score, axis=1, keepdims=True))
+            for old, score in zip(before, scores)
+        ]
+        weights = [
+            jnp.where(valid, jnp.exp(score - top), 0.0) for score, top in zip(scores, tops)
+        ]
+        decays = [jnp.exp(old - top) for old, top in zip(before, tops)]
+        sums = [
+            jnp.dot(
+                weight.astype(jnp.bfloat16), v_ref[0, head], preferred_element_type=jnp.float32
             )
+            for head, weight in enumerate(weights)
+        ]
+        totals = [
+            total_ref[head] * decays[head] + jnp.sum(weights[head], axis=1, keepdims=True)
+            for head in range(heads)
+        ]
+        news = [acc_ref[:, span] * decays[head] + sums[head] for head, span in enumerate(spans)]
+        for head, span in enumerate(spans):
+            top_ref[head] = tops[head]
+            total_ref[head] = totals[head]
+            acc_ref[:, span] = news[head]
 
         @pl.when(last_ref[step] == 1)
         def _():
             logs = []
-            for head in range(heads):
-                at = slice(head * size, (head + 1) * size)
+            for head, span in enumerate(spans):
                 total = total_ref[head]
                 some = total > 0
                 safe = jnp.where(some, total, 1.0)
-                out_ref[0, :, at] = (acc_ref[:, at] / safe).astype(out_ref.dtype)
+                out_ref[0, :, span] = (acc_ref[:, span] / safe).astype(out_ref.dtype)
                 logs.append(jnp.where(some, top_ref[head] + jnp.log(safe), NEG_FILL)[:, :1])
             log_ref[place_ref[step]] = lay_logs(logs, tree)
 
 
-def page_attention(queries, k_pages, v_pages, plan, heads, size):
-    requests, tree, width = queries.shape
+def page_attention(even, odd, k_pages, v_pages, plan, heads, size):
+    half, tree, width = even.shape
+    requests = 2 * half
     entries = k_pages.shape[2]
-    row = pl.BlockSpec((1, tree, width), lambda p, page, place, *rest: (place[p], 0, 0))
+    low = lambda p, page, place, *rest: (jnp.minimum(place[p], half - 1), 0, 0)
+    high = lambda p, page, place, *rest: (jnp.maximum(place[p] - half, 0), 0, 0)
+    row = lambda at: pl.BlockSpec((1, tree, width), at)
     leaf = pl.BlockSpec(
         (1, heads, entries, size), lambda p, page, place, *rest: (page[p], 0, 0, 0)
     )
     grid_spec = pltpu.PrefetchScalarGridSpec(
         num_scalar_prefetch=6,
         grid=(k_pages.shape[0],),
-        in_specs=[row, leaf, leaf],
+        in_specs=[row(low), row(high), leaf, leaf],
         out_specs=[
-            row,
+            row(lambda p, page, place, *rest: (place[p], 0, 0)),
             pl.BlockSpec((requests, 8, LANES), lambda p, *rest: (0, 0, 0)),
         ],
         scratch_shapes=[
@@ -370,7 +379,98 @@
         ],
         compiler_params=params(),
         name="page_attention",
-    )(*plan, queries, k_pages, v_pages)
+    )(*plan, even, odd, k_pages, v_pages)
+
+
+def owned_tile(index, rank, per, count):
+    owner = lax.rem(rank - lax.div(index, per) + count, count)
+    return owner * per + lax.rem(index, per)
+
+
+def project_kernel(rank_ref, x_ref, w_ref, out_ref):
+    out_ref[0] = jnp.dot(x_ref[...], w_ref[...], preferred_element_type=jnp.float32).astype(
+        out_ref.dtype
+    )
+
+
+def project(values, weight, rank):
+    count = lax.axis_size("head")
+    rows, depth = values.shape
+    columns = weight.shape[1] // count
+    tile = min(columns, 256)
+    per = columns // tile
+    grid_spec = pltpu.PrefetchScalarGridSpec(
+        num_scalar_prefetch=1,
+        grid=(count * per,),
+        in_specs=[
+            pl.BlockSpec((rows, depth), lambda i, z: (0, 0)),
+            pl.BlockSpec(
+                (depth, tile), lambda i, z: (0, owned_tile(i, z[0], per, count))
+            ),
+        ],
+        out_specs=pl.BlockSpec((1, rows, tile), lambda i, z: (lax.div(i, per), 0, lax.rem(i, per))),
+    )
+    return pl.pallas_call(
+        project_kernel,
+        grid_spec=grid_spec,
+        out_shape=jax.ShapeDtypeStruct((count, rows, columns), jnp.bfloat16),
+        compiler_params=params(),
+        name="project",
+    )(rank, values, weight)
+
+
+def mlp_kernel(steps, tile, rank_ref, x_ref, gate_ref, up_ref, down_ref, out_ref, hidden_ref):
+    step = pl.program_id(0)
+
+    @pl.when(step < steps)
+    def _():
+        gate = jnp.dot(x_ref[...], gate_ref[...], preferred_element_type=jnp.float32)
+        up = jnp.dot(x_ref[...], up_ref[...], preferred_element_type=jnp.float32)
+        at = pl.ds(pl.multiple_of(step * tile, tile), tile)
+        hidden_ref[:, at] = (jax.nn.silu(gate) * up).astype(hidden_ref.dtype)
+
+    @pl.when(step >= steps)
+    def _():
+        out_ref[0] = jnp.dot(
+            hidden_ref[...], down_ref[...], preferred_element_type=jnp.float32
+        ).astype(out_ref.dtype)
+
+
+def mlp(values, gate_up, down, rank):
+    count = lax.axis_size("head")
+    rows, width = values.shape
+    hidden = down.shape[0]
+    tile = min(hidden, 256)
+    steps = hidden // tile
+    columns = down.shape[1] // count
+    out_tile = min(columns, 256)
+    per = columns // out_tile
+    late = lambda i: jnp.maximum(i - steps, 0)
+    early = lambda i: jnp.minimum(i, steps - 1)
+    grid_spec = pltpu.PrefetchScalarGridSpec(
+        num_scalar_prefetch=1,
+        grid=(steps + count * per,),
+        in_specs=[
+            pl.BlockSpec((rows, width), lambda i, z: (0, 0)),
+            pl.BlockSpec((width, tile), lambda i, z: (0, early(i))),
+            pl.BlockSpec((width, tile), lambda i, z: (0, steps + early(i))),
+            pl.BlockSpec(
+                (hidden, out_tile),
+                lambda i, z: (0, owned_tile(late(i), z[0], per, count)),
+            ),
+        ],
+        out_specs=pl.BlockSpec(
+            (1, rows, out_tile), lambda i, z: (lax.div(late(i), per), 0, lax.rem(late(i), per))
+        ),
+        scratch_shapes=[pltpu.VMEM((rows, hidden), jnp.bfloat16)],
+    )
+    return pl.pallas_call(
+        functools.partial(mlp_kernel, steps, tile),
+        grid_spec=grid_spec,
+        out_shape=jax.ShapeDtypeStruct((count, rows, columns), jnp.bfloat16),
+        compiler_params=params(),
+        name="mlp",
+    )(rank, values, gate_up, gate_up, down)
 
 
 def merge_kernel(heads, size, count, *refs):
@@ -496,8 +596,7 @@
 
     k_heads = jnp.transpose(k_pages, (0, 2, 1, 3))
     v_heads = jnp.transpose(v_pages, (0, 2, 1, 3))
-    hidden_local = up_gate.shape[2]
-    gate_weight, up_weight = up_gate[:, 0], up_gate[:, 1]
+    rank = lax.axis_index("head").astype(jnp.int32)[None]
 
     step_requests = req_local // CHUNKS
     step_tokens = step_requests * tree_size
@@ -514,6 +613,9 @@
         normed, token = gathered_norm(mixed_in, width)
         attended_in.append(normed)
 
+    all_shape = (step_requests, tree_size, heads * size)
+    gate_up = None
+    before_pages = None
     attn_parts, mlp_parts = [], []
     for chunk in range(CHUNKS):
         rows = slice(chunk * step_tokens, (chunk + 1) * step_tokens)
@@ -526,21 +628,23 @@
             ],
             axis=1,
         )
+        if gate_up is None:
+            projected, gate_up = lax.optimization_barrier((projected, up_gate))
+            gate_up = gate_up.reshape(width, -1)
         queries, keys, values = rotate_all(
             projected, cosine[rows], sine[rows], heads, size, 2 * tree_size
         )
-        shape = (step_requests, tree_size, heads * size)
-        queries, keys, values = (item.reshape(shape) for item in (queries, keys, values))
-        blocks = gather_requests(queries)
-        near_last = [index for low in (0, 1) for index in range(parts) if index & 1 == low]
-        query_all = jnp.concatenate([blocks[index] for index in near_last])
+        queries, keys, values = (item.reshape(all_shape) for item in (queries, keys, values))
+        even, odd = gather_requests(queries)
         plan = page_plan(
             page_owner, page_fill, chunk * step_requests, step_requests, req_local, parts
         )
-        sums, logs = page_attention(query_all, k_heads, v_heads, plan, heads, size)
+        if before_pages is not None:
+            even, odd, before_pages = lax.optimization_barrier((even, odd, before_pages))
+        sums, logs = page_attention(even, odd, k_heads, v_heads, plan, heads, size)
         tree_pair = tree_attention(queries, keys, values, reach[asked], heads, size)
-        done = scatter_requests(
-            sums.reshape(parts, step_requests, tree_size, heads * size),
+        done, before_pages = scatter_requests(
+            sums.reshape((parts,) + all_shape),
             logs.reshape(parts, step_requests, 8, LANES),
             merge,
         )
@@ -554,26 +658,13 @@
             ] + [(tree_pair[0][own], tree_pair[1][own])]
             attended.append(merge_partials(pairs, heads, size, with_logs=False)[0])
         attended = jnp.concatenate(attended).reshape(step_tokens, heads * size)
-        attn_delta = chain_scatter(
-            lambda step: jnp.dot(
-                attended, columns_for(out_weight, step), preferred_element_type=jnp.float32
-            )
-        )
+        attn_delta = chain_scatter(project(attended, out_weight, rank))
         attn_parts.append(attn_delta)
 
         stream_vals = streams[rows].astype(jnp.float32)
         mixed_mid = blend(stream_vals, mid_in) + mid_out * attn_delta
         normed_mid, token = gathered_norm(mixed_mid, width)
-        gate = jnp.dot(normed_mid, gate_weight, preferred_element_type=jnp.float32)
-        up = jnp.dot(normed_mid, up_weight, preferred_element_type=jnp.float32)
-        hidden = (jax.nn.silu(gate) * up).astype(jnp.bfloat16)
-        mlp_parts.append(
-            chain_scatter(
-                lambda step: jnp.dot(
-                    hidden, columns_for(down_weight, step), preferred_element_type=jnp.float32
-                )
-            )
-        )
+        mlp_parts.append(chain_scatter(mlp(normed_mid, gate_up, down_weight, rank)))
 
     attn_delta = jnp.concatenate(attn_parts)
     mlp_delta = jnp.concatenate(mlp_parts)
@@ -591,7 +682,7 @@
     final_local = (
         jnp.sum(both_out) * attn_delta[rows_taken] + jnp.sum(hc_out[1]) * mlp_delta[rows_taken]
     ) + blend(stream_vals[rows_taken], jnp.sum(both_mix, axis=1))
-    final_full = lax.all_gather(final_local, "head", axis=1, tiled=True)
+    final_full = jnp.concatenate(list(shift_gather(final_local)), axis=1)
     final_norm = layer_norm(final_full)
     own_columns = lax.dynamic_slice_in_dim(
         final_norm, lax.axis_index("head") * feature_local, feature_local, 1
@@ -603,8 +694,8 @@
         preferred_element_type=jnp.float32,
     )
     drafted = (own_columns[:, None, :] + jax.nn.silu(branch)).astype(jnp.bfloat16)
-    draft_full = lax.all_gather(drafted, "head", axis=2, tiled=True)
-    draft_all = lax.all_gather(draft_full, "req", axis=0, tiled=True)
+    draft_all = lax.all_gather(drafted, ("req", "head"), axis=0, tiled=False)
+    draft_all = draft_all.reshape((parts, -1) + drafted.shape).transpose(0, 2, 3, 1, 4)
     logits_local = jnp.dot(
         draft_all.reshape(-1, width), lm_head, preferred_element_type=jnp.float32
     )

time: 680 us -> 622 us (0.915); the launches traced: 678 us -> 613 us
  matrix products: 94.1 us -> 19.4 us
  waiting for transfers between devices: 124 us -> 154 us
  Pallas kernels: 68.3 us -> 97.4 us
  blocking collectives: 24.6 us -> 0 us
  starting transfers between devices: 202 us -> 190 us
  local copies, waits for them, and re-layouts: 84.2 us -> 75.5 us
    dot_general x20 -> x0, matrix products: 73.8 us -> none  [the longest x2 26.9 us: on_device(): up = jnp.dot(normed_mid, up_weight, preferred_element_type=jnp.float32)]
    pallas_call x0 -> x4, Pallas kernels: none -> 42 us  [the longest x2 36.2 us: mlp(): pl.pallas_call(functools.partial(mlp_kernel, steps, tile), grid_spec=grid...]
    slice x1 -> x0, local copies, waits for them, and re-layouts: 32.3 us -> none  [on_device(): gate_weight, up_weight = (up_gate[:, 0], up_gate[:, 1])]
    all_gather x1, waiting for transfers between devices: 40 us -> 65 us  [on_device(): draft_all = lax.all_gather(drafted, ('req', 'head'), axis=0, tiled=False)]
    all_gather x2 -> x0, blocking collectives: 24.6 us -> none  [the longest x1 13.4 us: on_device(): final_full = lax.all_gather(final_local, 'head', axis=1, tiled=True)]
    ppermute x48 -> x34, starting transfers between devices: 91.4 us -> 67.2 us  [swapped(): return lax.ppermute(values, 'req', [(r, r ^ bit) for r in range(count)])]
    unnamed x142 -> x117, local copies, waits for them, and re-layouts: 8.67 us -> 27.5 us
    pallas_call x2, Pallas kernels: 38.3 us -> 24.5 us  [page_attention(): pl.pallas_call(functools.partial(page_kernel, heads, size), grid_spec=gri...]
  transfers between devices with their start and end apart: 110 -> 99, of which waited for: 29 -> 24; matrix products, arithmetic and copies ran while one was open for 28% -> 18% of each run, Pallas kernels for 10% -> 12%
where the time goes in v2:
time: 622 us; the launch traced here: 613 us
  starting transfers between devices  190 us (31%)
  waiting for transfers between devices  154 us (25%)
  Pallas kernels  97.4 us (16%)
  local copies, waits for them, and re-layouts  75.5 us (12%)
  other arithmetic  58.5 us (9%)
  matrix products  19.4 us (3%)
  between operations  18.3 us (3%)
    ppermute x34, starting transfers between devices, swapped(): return lax.ppermute(values, 'req', [(r, r ^ bit) for r in range(count)])  67.2 us
    all_gather x1, waiting for transfers between devices, on_device(): draft_all = lax.all_gather(drafted, ('req', 'head'), axis=0, tiled=False)  65 us
    ppermute x12, starting transfers between devices, chain_scatter(): lax.ppermute(to_right, 'head', [(z, z + 1) for z in range(step)])  38.3 us
    pallas_call x2, Pallas kernels, mlp(): pl.pallas_call(functools.partial(mlp_kernel, steps, tile), grid_spec=grid...  36.2 us
    ppermute x15, starting transfers between devices, shift_gather(): lax.ppermute(small, 'head', [(z, (z + step) % count) for z in range(count)])  29.1 us
    unnamed x117, local copies, waits for them, and re-layouts  27.5 us
    pallas_call x2, Pallas kernels, page_attention(): pl.pallas_call(functools.partial(page_kernel, heads, size), grid_spec=gri...  24.5 us
    ppermute x34, waiting for transfers between devices, swapped(): return lax.ppermute(values, 'req', [(r, r ^ bit) for r in range(count)])  24.3 us
  transfers between devices with their start and end apart: 99, of which 24 were waited for; matrix products, arithmetic and copies ran while one was open for 18% of the time, Pallas kernels for 12%

profile of v2, /device:TPU:1, one launch (start us, length us, event | category | flops | bytes accessed | tf_op | source)
XLA Modules:
  0.0 612.8 jit_solution(3508354392801197015)
XLA Ops:
  37.5 11.8 %copy_bitcast_fusion = (bf16[48,4,128,128]{3,2,1,0:T(8,128)(2,1)}, bf16[48,4,128,128]{3,2,1,0:T(8,128)(2,1)}) fusion(bf16[48,128,4,128]{3,2,1,0:T(4,128)(2,1)} %param.28, bf16[48,128,4,128]{3,2,1,0:T(4,128)(2,1)} %param.27), kind=kLoop, calls=%fused_computation.5 | loop fusion | bytes 25165824 | tf_op jit(solution)/shard_map/transpose | solution.py:598
  57.9 4.6 add_bitcast_fusion
  90.8 6.0 tree_attention.2
  103.3 5.8 collective-permute-done.39
  110.5 8.5 %collective-permute-start.15 = (bf16[32,48,512]{2,1,0:T(8,128)(2,1)S(1)}, bf16[32,48,512]{2,1,0:T(8,128)(2,1)S(1)}, u32[]{:S(2)}, u32[]{:S(2)}) collective-permute-start(bf16[32,48,512]{2,1,0:T(8,128)(2,1)S(1)} %constant_dynamic-update-slice_fusion.even_ref), channel_id=1, source_target_pairs={{0,4},{4,0},{8,12},{12,8},{16,20},{20,16},{24,28},{28,24},{1,5},{5... | collective-permute-start | bytes 4718600 | tf_op jit(solution)/shard_map/ppermute | solution.py:138
  125.7 18.0 %page_attention.2 = (bf16[64,48,512]{2,1,0:T(8,128)(2,1)S(1)}, f32[64,8,128]{2,1,0:T(8,128)S(1)}) custom-call(s32[48]{0:T(128)S(1)} %get-tuple-element.105.page_ref, s32[48]{0:T(128)S(1)} %get-tuple-element.104.place_ref, s32[48]{0:T(128)S(1)} %get-tuple-element.103.fill_ref, s32[48]{0:T(128)S(1)} %get-tuple-element.314.first_ref, ...), custom_call_target="tpu_custom_call" | custom-call | tf_op jit(solution)/shard_map/page_attention/pallas_call | solution.py:373
  144.0 11.2 %collective-permute-start.16 = (bf16[4,8,48,512]{3,2,1,0:T(8,128)(2,1)S(1)}, bf16[4,8,48,512]{3,2,1,0:T(8,128)(2,1)S(1)}, u32[]{:S(2)}, u32[]{:S(2)}) collective-permute-start(bf16[4,8,48,512]{3,2,1,0:T(8,128)(2,1)S(1)} %bitcast.355), channel_id=1, source_target_pairs={{0,4},{4,0},{8,12},{12,8},{16,20},{20,16},{24,28},{28,24},{1,5},{5... | collective-permute-start | bytes 4718600 | tf_op jit(solution)/shard_map/ppermute | solution.py:138
  155.2 9.4 %collective-permute-start.41 = (bf16[4,48,512]{2,1,0:T(8,128)(2,1)S(1)}, bf16[4,48,512]{2,1,0:T(8,128)(2,1)S(1)}, u32[]{:S(2)}, u32[]{:S(2)}) collective-permute-start(bf16[4,48,512]{2,1,0:T(8,128)(2,1)S(1)} %bitcast.363), channel_id=1, source_target_pairs={{0,8},{4,12},{8,0},{12,4},{16,24},{20,28},{24,16},{28,20},{1,9},{5... | collective-permute-start | bytes 589832 | tf_op jit(solution)/shard_map/ppermute | solution.py:138
  169.8 5.1 collective-permute-done.44
  185.8 4.4 merge_partials.10
  193.6 6.4 %page_attention.3 = (bf16[64,48,512]{2,1,0:T(8,128)(2,1)S(1)}, f32[64,8,128]{2,1,0:T(8,128)S(1)}) custom-call(s32[48]{0:T(128)S(1)} %get-tuple-element.109.page_ref, s32[48]{0:T(128)S(1)} %get-tuple-element.110.place_ref, s32[48]{0:T(128)S(1)} %get-tuple-element.111.fill_ref, s32[48]{0:T(128)S(1)} %get-tuple-element.316.first_ref, ...), custom_call_target="tpu_custom_call" | custom-call | tf_op jit(solution)/shard_map/page_attention/pallas_call | solution.py:373
  208.5 14.5 %collective-permute-start.48 = (bf16[4,8,48,512]{3,2,1,0:T(8,128)(2,1)}, bf16[4,8,48,512]{3,2,1,0:T(8,128)(2,1)}, u32[]{:S(2)}, u32[]{:S(2)}) collective-permute-start(bf16[4,8,48,512]{3,2,1,0:T(8,128)(2,1)} %bitcast.57), channel_id=1, source_target_pairs={{0,4},{4,0},{8,12},{12,8},{16,20},{20,16},{24,28},{28,24},{1,5},{5... | collective-permute-start | bytes 4718600 | tf_op jit(solution)/shard_map/ppermute | solution.py:138
  230.7 9.9 %collective-permute-start.29 = (bf16[384,512]{1,0:T(8,128)(2,1)}, bf16[384,512]{1,0:T(8,128)(2,1)}, u32[]{:S(2)}, u32[]{:S(2)}) collective-permute-start(bf16[384,512]{1,0:T(8,128)(2,1)} %get-tuple-element.151), channel_id=1, source_target_pairs={{3,2},{7,6},{11,10},{15,14},{19,18},{23,22},{27,26},{31,30}} | collective-permute-start | bytes 1179656 | tf_op jit(solution)/shard_map/ppermute | solution.py:91
  251.8 5.9 tree_attention.3
  267.6 5.1 collective-permute-start.28
  274.1 5.4 merge_partials.15
  282.9 5.4 collective-permute-done.50
  314.8 7.9 %collective-permute-done.67 = f32[2,384]{1,0:T(2,128)S(1)} collective-permute-done((f32[2,384]{1,0:T(2,128)S(1)}, f32[2,384]{1,0:T(2,128)S(1)}, u32[]{:S(2)}, u32[]{:S(2)}) %collective-permute-start.67) | collective-permute-done | bytes 3104 | tf_op jit(solution)/shard_map/ppermute | solution.py:102
  325.4 17.9 %copy.102 = bf16[256,8,2,2048]{3,1,2,0:T(8,128)(2,1)} copy(bf16[256,8,2,2048]{3,2,1,0:T(2,128)(2,1)} %bitcast.354) | data formatting | bytes 33554432
  345.7 5.5 collective-permute-start.60
  355.9 7.3 %collective-permute-done.63 = bf16[384,512]{1,0:T(8,128)(2,1)S(1)} collective-permute-done((bf16[384,512]{1,0:T(8,128)(2,1)S(1)}, bf16[384,512]{1,0:T(8,128)(2,1)S(1)}, u32[]{:S(2)}, u32[]{:S(2)}) %collective-permute-start.63) | collective-permute-done | bytes 393248 | tf_op jit(solution)/shard_map/ppermute | solution.py:91
  372.7 18.1 %mlp.2 = bf16[4,384,512]{2,1,0:T(8,128)(2,1)S(1)} custom-call(s32[1]{0:T(128)} %bitcast.2.rank_ref, bf16[384,2048]{1,0:T(8,128)(2,1)S(1)} %pad_maximum_fusion.5.x_ref, bf16[2048,4096]{1,0:T(8,128)(2,1)} %bitcast.350, bf16[2048,4096]{1,0:T(8,128)(2,1)} %bitcast.351, bf16[2048,2048]{1,0:T(8,128)(2,1)S(1)} %bitcast.306), custom_call_target="tpu_custom_call" | custom-call | tf_op jit(solution)/shard_map/mlp/pallas_call | solution.py:467
  397.0 4.9 collective-permute-start.73
  406.7 11.3 %collective-permute-done.87 = bf16[384,512]{1,0:T(8,128)(2,1)S(1)} collective-permute-done((bf16[384,512]{1,0:T(8,128)(2,1)S(1)}, bf16[384,512]{1,0:T(8,128)(2,1)S(1)}, u32[]{:S(2)}, u32[]{:S(2)}) %collective-permute-start.87) | collective-permute-done | bytes 393248 | tf_op jit(solution)/shard_map/ppermute | solution.py:58
  419.1 18.1 %mlp.3 = bf16[4,384,512]{2,1,0:T(8,128)(2,1)S(1)} custom-call(s32[1]{0:T(128)} %bitcast.2.rank_ref, bf16[384,2048]{1,0:T(8,128)(2,1)S(1)} %pad_maximum_fusion.6.x_ref, bf16[2048,4096]{1,0:T(8,128)(2,1)} %bitcast.352, bf16[2048,4096]{1,0:T(8,128)(2,1)} %bitcast.353, bf16[2048,2048]{1,0:T(8,128)(2,1)S(1)} %bitcast.306), custom_call_target="tpu_custom_call" | custom-call | tf_op jit(solution)/shard_map/mlp/pallas_call | solution.py:467
  455.5 4.7 collective-permute-start.90
  466.8 4.4 collective-permute-done.90
  490.4 5.3 fusion.110
  497.8 65.0 %all-gather.3.cloned.1.call-done = bf16[512,2,512]{2,0,1:T(8,128)(2,1)} async-done(((bf16[16,2,512]{2,0,1:T(8,128)(2,1)}), bf16[512,2,512]{2,0,1:T(8,128)(2,1)}) %all-gather.3.cloned.1.call-update) | async-done | bytes 1048592 | tf_op jit(solution)/shard_map/all_gather | solution.py:697
  565.7 5.1 fusion.2
  580.9 6.4 %add_convert_fusion = bf16[768,4,512]{2,1,0:T(4,128)(2,1)} fusion(f32[768,512]{1,0:T(8,128)S(1)} %get-tuple-element.323, f32[4]{0:T(128)S(1)} %get-tuple-element.299, f32[768,512]{1,0:T(8,128)S(1)} %get-tuple-element.324, f32[4]{0:T(128)S(1)} %get-tuple-element.300, f32[768,512]{1,0:T(8,128)S(1)} %copy-done.21, f32[4]{0:T(128)S(1)} %get-tuple-element.301, ...), kind=kLoop, calls=%fused_computation.7 | loop fusion | flops 18874368 | bytes 12583008 | tf_op jit(solution)/shard_map/convert_element_type | solution.py:679
  587.3 13.0 %all-to-all-done = bf16[128,2,1572]{2,1,0:T(2,128)(2,1)} async-done(((bf16[128,2,1572]{2,1,0:T(2,128)(2,1)}), bf16[128,2,1572]{2,1,0:T(2,128)(2,1)}, u32[]{:S(2)}, u32[]{:S(2)}) %all-to-all-start) | async-done | bytes 804896 | tf_op jit(solution)/shard_map/all_to_all | solution.py:703
  (504 shorter events, 261.7 us)
Async XLA Ops:
  7.2 555.6 %all-gather.3.cloned.1.call-start = ((), (), s32[]{:S(2)}) async-start(), calls=%async_computation.1 | async-start | bytes 1081344 | tf_op jit(solution)/shard_map/all_gather | solution.py:697
  16.7 45.9 %collective-permute-start.3 = (f32[2,384]{1,0:T(2,128)}, f32[2,384]{1,0:T(2,128)S(1)}, u32[]{:S(2)}, u32[]{:S(2)}) collective-permute-start(f32[2,384]{1,0:T(2,128)} %get-tuple-element.275), channel_id=1, source_target_pairs={{0,1},{1,2},{2,3},{3,0},{4,5},{5,6},{6,7},{7,4},{8,9},{9,10},{10,1... | collective-permute-start | bytes 9224 | tf_op jit(solution)/shard_map/ppermute | solution.py:102
  18.9 43.8 %collective-permute-start.4 = (f32[2,384]{1,0:T(2,128)}, f32[2,384]{1,0:T(2,128)S(1)}, u32[]{:S(2)}, u32[]{:S(2)}) collective-permute-start(f32[2,384]{1,0:T(2,128)} %get-tuple-element.275), channel_id=1, source_target_pairs={{0,2},{1,3},{2,0},{3,1},{4,6},{5,7},{6,4},{7,5},{8,10},{9,11},{10,... | collective-permute-start | bytes 9224 | tf_op jit(solution)/shard_map/ppermute | solution.py:102
  21.2 41.5 %collective-permute-start.5 = (f32[2,384]{1,0:T(2,128)}, f32[2,384]{1,0:T(2,128)}, u32[]{:S(2)}, u32[]{:S(2)}) collective-permute-start(f32[2,384]{1,0:T(2,128)} %get-tuple-element.275), channel_id=1, source_target_pairs={{0,3},{1,0},{2,1},{3,2},{4,7},{5,4},{6,5},{7,6},{8,11},{9,8},{10,9... | collective-permute-start | bytes 9224 | tf_op jit(solution)/shard_map/ppermute | solution.py:102
  23.1 29.1 %collective-permute-start = (bf16[384,512]{1,0:T(8,128)(2,1)}, bf16[384,512]{1,0:T(8,128)(2,1)}, u32[]{:S(2)}, u32[]{:S(2)}) collective-permute-start(bf16[384,512]{1,0:T(8,128)(2,1)} %fusion.35), channel_id=1, source_target_pairs={{0,1},{1,2},{2,3},{4,5},{5,6},{6,7},{8,9},{9,10},{10,11},{12,13},{... | collective-permute-start | bytes 1179656 | tf_op jit(solution)/shard_map/ppermute | solution.py:55
  26.2 28.9 %collective-permute-start.6 = (bf16[384,512]{1,0:T(8,128)(2,1)}, bf16[384,512]{1,0:T(8,128)(2,1)}, u32[]{:S(2)}, u32[]{:S(2)}) collective-permute-start(bf16[384,512]{1,0:T(8,128)(2,1)} %fusion.35), channel_id=1, source_target_pairs={{1,0},{2,1},{3,2},{5,4},{6,5},{7,6},{9,8},{10,9},{11,10},{13,12},{... | collective-permute-start | bytes 1179656 | tf_op jit(solution)/shard_map/ppermute | solution.py:58
  76.7 20.9 %collective-permute-start.32 = (bf16[384,512]{1,0:T(8,128)(2,1)S(1)}, bf16[384,512]{1,0:T(8,128)(2,1)S(1)}, u32[]{:S(2)}, u32[]{:S(2)}) collective-permute-start(bf16[384,512]{1,0:T(8,128)(2,1)S(1)} %subtract_convert_fusion.2), channel_id=1, source_target_pairs={{0,1},{1,2},{2,3},{4,5},{5,6},{6,7},{8,9},{9,10},{10,11},{12,13},{... | collective-permute-start | bytes 1179656 | tf_op jit(solution)/shard_map/ppermute | solution.py:55
  78.4 19.9 %collective-permute-start.38 = (bf16[384,512]{1,0:T(8,128)(2,1)S(1)}, bf16[384,512]{1,0:T(8,128)(2,1)S(1)}, u32[]{:S(2)}, u32[]{:S(2)}) collective-permute-start(bf16[384,512]{1,0:T(8,128)(2,1)S(1)} %subtract_convert_fusion.2), channel_id=1, source_target_pairs={{1,0},{2,1},{3,2},{5,4},{6,5},{7,6},{9,8},{10,9},{11,10},{13,12},{... | collective-permute-start | bytes 1179656 | tf_op jit(solution)/shard_map/ppermute | solution.py:58
  102.6 16.5 %collective-permute-start.34 = (bf16[384,512]{1,0:T(8,128)(2,1)S(1)}, bf16[384,512]{1,0:T(8,128)(2,1)S(1)}, u32[]{:S(2)}, u32[]{:S(2)}) collective-permute-start(bf16[384,512]{1,0:T(8,128)(2,1)S(1)} %collective-permute-done.33), channel_id=1, source_target_pairs={{2,3},{6,7},{10,11},{14,15},{18,19},{22,23},{26,27},{30,31}} | collective-permute-start | bytes 1179656 | tf_op jit(solution)/shard_map/ppermute | solution.py:55
  144.0 41.8 %collective-permute-start.16 = (bf16[4,8,48,512]{3,2,1,0:T(8,128)(2,1)S(1)}, bf16[4,8,48,512]{3,2,1,0:T(8,128)(2,1)S(1)}, u32[]{:S(2)}, u32[]{:S(2)}) collective-permute-start(bf16[4,8,48,512]{3,2,1,0:T(8,128)(2,1)S(1)} %bitcast.355), channel_id=1, source_target_pairs={{0,4},{4,0},{8,12},{12,8},{16,20},{20,16},{24,28},{28,24},{1,5},{5... | collective-permute-start | bytes 4718600 | tf_op jit(solution)/shard_map/ppermute | solution.py:138
  202.5 20.5 %collective-permute-start.20 = (bf16[1,4,48,512]{3,2,1,0:T(8,128)(2,1)S(1)}, bf16[1,4,48,512]{3,2,1,0:T(8,128)(2,1)S(1)}, u32[]{:S(2)}, u32[]{:S(2)}) collective-permute-start(bf16[1,4,48,512]{3,2,1,0:T(8,128)(2,1)S(1)} %get-tuple-element.198), channel_id=1, source_target_pairs={{0,16},{4,20},{8,24},{12,28},{16,0},{20,4},{24,8},{28,12},{1,17},{... | collective-permute-start | bytes 589832 | tf_op jit(solution)/shard_map/ppermute | solution.py:138
  202.8 20.2 %collective-permute-start.21 = (f32[1,4,8,128]{3,2,1,0:T(8,128)S(1)}, f32[1,4,8,128]{3,2,1,0:T(8,128)S(1)}, u32[]{:S(2)}, u32[]{:S(2)}) collective-permute-start(f32[1,4,8,128]{3,2,1,0:T(8,128)S(1)} %get-tuple-element.240), channel_id=1, source_target_pairs={{0,16},{4,20},{8,24},{12,28},{16,0},{20,4},{24,8},{28,12},{1,17},{... | collective-permute-start | bytes 49160 | tf_op jit(solution)/shard_map/ppermute | solution.py:138
  205.2 18.7 %collective-permute-start.24 = (bf16[1,4,48,512]{3,2,1,0:T(8,128)(2,1)S(1)}, bf16[1,4,48,512]{3,2,1,0:T(8,128)(2,1)S(1)}, u32[]{:S(2)}, u32[]{:S(2)}) collective-permute-start(bf16[1,4,48,512]{3,2,1,0:T(8,128)(2,1)S(1)} %get-tuple-element.202), channel_id=1, source_target_pairs={{0,8},{4,12},{8,0},{12,4},{16,24},{20,28},{24,16},{28,20},{1,9},{5... | collective-permute-start | bytes 589832 | tf_op jit(solution)/shard_map/ppermute | solution.py:138
  207.0 16.9 %collective-permute-start.25 = (f32[1,4,8,128]{3,2,1,0:T(8,128)S(1)}, f32[1,4,8,128]{3,2,1,0:T(8,128)S(1)}, u32[]{:S(2)}, u32[]{:S(2)}) collective-permute-start(f32[1,4,8,128]{3,2,1,0:T(8,128)S(1)} %get-tuple-element.242), channel_id=1, source_target_pairs={{0,8},{4,12},{8,0},{12,4},{16,24},{20,28},{24,16},{28,20},{1,9},{5... | collective-permute-start | bytes 49160 | tf_op jit(solution)/shard_map/ppermute | solution.py:138
  208.5 65.6 %collective-permute-start.48 = (bf16[4,8,48,512]{3,2,1,0:T(8,128)(2,1)}, bf16[4,8,48,512]{3,2,1,0:T(8,128)(2,1)}, u32[]{:S(2)}, u32[]{:S(2)}) collective-permute-start(bf16[4,8,48,512]{3,2,1,0:T(8,128)(2,1)} %bitcast.57), channel_id=1, source_target_pairs={{0,4},{4,0},{8,12},{12,8},{16,20},{20,16},{24,28},{28,24},{1,5},{5... | collective-permute-start | bytes 4718600 | tf_op jit(solution)/shard_map/ppermute | solution.py:138
  228.6 29.2 %collective-permute-start.26 = (bf16[384,512]{1,0:T(8,128)(2,1)}, bf16[384,512]{1,0:T(8,128)(2,1)}, u32[]{:S(2)}, u32[]{:S(2)}) collective-permute-start(bf16[384,512]{1,0:T(8,128)(2,1)} %get-tuple-element.150), channel_id=1, source_target_pairs={{0,1},{4,5},{8,9},{12,13},{16,17},{20,21},{24,25},{28,29}} | collective-permute-start | bytes 1179656 | tf_op jit(solution)/shard_map/ppermute | solution.py:90
  230.7 27.2 %collective-permute-start.29 = (bf16[384,512]{1,0:T(8,128)(2,1)}, bf16[384,512]{1,0:T(8,128)(2,1)}, u32[]{:S(2)}, u32[]{:S(2)}) collective-permute-start(bf16[384,512]{1,0:T(8,128)(2,1)} %get-tuple-element.151), channel_id=1, source_target_pairs={{3,2},{7,6},{11,10},{15,14},{19,18},{23,22},{27,26},{31,30}} | collective-permute-start | bytes 1179656 | tf_op jit(solution)/shard_map/ppermute | solution.py:91
  267.6 25.8 %collective-permute-start.28 = (bf16[384,512]{1,0:T(8,128)(2,1)S(1)}, bf16[384,512]{1,0:T(8,128)(2,1)S(1)}, u32[]{:S(2)}, u32[]{:S(2)}) collective-permute-start(bf16[384,512]{1,0:T(8,128)(2,1)S(1)} %get-tuple-element.146), channel_id=1, source_target_pairs={{0,1},{1,2},{2,3},{4,5},{5,6},{6,7},{8,9},{9,10},{10,11},{12,13},{... | collective-permute-start | bytes 1179656 | tf_op jit(solution)/shard_map/ppermute | solution.py:90
  272.7 20.9 %collective-permute-start.31 = (bf16[384,512]{1,0:T(8,128)(2,1)S(1)}, bf16[384,512]{1,0:T(8,128)(2,1)S(1)}, u32[]{:S(2)}, u32[]{:S(2)}) collective-permute-start(bf16[384,512]{1,0:T(8,128)(2,1)S(1)} %get-tuple-element.147), channel_id=1, source_target_pairs={{1,0},{2,1},{3,2},{5,4},{6,5},{7,6},{9,8},{10,9},{11,10},{13,12},{... | collective-permute-start | bytes 1179656 | tf_op jit(solution)/shard_map/ppermute | solution.py:91
  306.6 36.8 %collective-permute-start.64 = (bf16[384,512]{1,0:T(8,128)(2,1)S(1)}, bf16[384,512]{1,0:T(8,128)(2,1)S(1)}, u32[]{:S(2)}, u32[]{:S(2)}) collective-permute-start(bf16[384,512]{1,0:T(8,128)(2,1)S(1)} %subtract_convert_fusion.1), channel_id=1, source_target_pairs={{0,1},{1,2},{2,3},{4,5},{5,6},{6,7},{8,9},{9,10},{10,11},{12,13},{... | collective-permute-start | bytes 1179656 | tf_op jit(solution)/shard_map/ppermute | solution.py:55
  308.3 35.9 %collective-permute-start.70 = (bf16[384,512]{1,0:T(8,128)(2,1)S(1)}, bf16[384,512]{1,0:T(8,128)(2,1)S(1)}, u32[]{:S(2)}, u32[]{:S(2)}) collective-permute-start(bf16[384,512]{1,0:T(8,128)(2,1)S(1)} %subtract_convert_fusion.1), channel_id=1, source_target_pairs={{1,0},{2,1},{3,2},{5,4},{6,5},{7,6},{9,8},{10,9},{11,10},{13,12},{... | collective-permute-start | bytes 1179656 | tf_op jit(solution)/shard_map/ppermute | solution.py:58
  313.7 29.6 %collective-permute-start.69 = (f32[2,384]{1,0:T(2,128)S(1)}, f32[2,384]{1,0:T(2,128)S(1)}, u32[]{:S(2)}, u32[]{:S(2)}) collective-permute-start(f32[2,384]{1,0:T(2,128)S(1)} %get-tuple-element.271), channel_id=1, source_target_pairs={{0,3},{1,0},{2,1},{3,2},{4,7},{5,4},{6,5},{7,6},{8,11},{9,8},{10,9... | collective-permute-start | bytes 9224 | tf_op jit(solution)/shard_map/ppermute | solution.py:102
  322.7 22.8 %collective-permute-start.59 = (bf16[384,512]{1,0:T(8,128)(2,1)S(1)}, bf16[384,512]{1,0:T(8,128)(2,1)S(1)}, u32[]{:S(2)}, u32[]{:S(2)}) collective-permute-start(bf16[384,512]{1,0:T(8,128)(2,1)S(1)} %get-tuple-element.166), channel_id=1, source_target_pairs={{0,1},{1,2},{4,5},{5,6},{8,9},{9,10},{12,13},{13,14},{16,17},{17,1... | collective-permute-start | bytes 1179656 | tf_op jit(solution)/shard_map/ppermute | solution.py:90
  324.0 21.5 %collective-permute-start.62 = (bf16[384,512]{1,0:T(8,128)(2,1)S(1)}, bf16[384,512]{1,0:T(8,128)(2,1)S(1)}, u32[]{:S(2)}, u32[]{:S(2)}) collective-permute-start(bf16[384,512]{1,0:T(8,128)(2,1)S(1)} %get-tuple-element.167), channel_id=1, source_target_pairs={{2,1},{3,2},{6,5},{7,6},{10,9},{11,10},{14,13},{15,14},{18,17},{19... | collective-permute-start | bytes 1179656 | tf_op jit(solution)/shard_map/ppermute | solution.py:91
  352.8 18.5 %collective-permute-start.66 = (bf16[384,512]{1,0:T(8,128)(2,1)S(1)}, bf16[384,512]{1,0:T(8,128)(2,1)S(1)}, u32[]{:S(2)}, u32[]{:S(2)}) collective-permute-start(bf16[384,512]{1,0:T(8,128)(2,1)S(1)} %collective-permute-done.65), channel_id=1, source_target_pairs={{2,3},{6,7},{10,11},{14,15},{18,19},{22,23},{26,27},{30,31}} | collective-permute-start | bytes 1179656 | tf_op jit(solution)/shard_map/ppermute | solution.py:55
  354.2 17.5 %collective-permute-start.72 = (bf16[384,512]{1,0:T(8,128)(2,1)S(1)}, bf16[384,512]{1,0:T(8,128)(2,1)S(1)}, u32[]{:S(2)}, u32[]{:S(2)}) collective-permute-start(bf16[384,512]{1,0:T(8,128)(2,1)S(1)} %collective-permute-done.71), channel_id=1, source_target_pairs={{1,0},{5,4},{9,8},{13,12},{17,16},{21,20},{25,24},{29,28}} | collective-permute-start | bytes 1179656 | tf_op jit(solution)/shard_map/ppermute | solution.py:58
  367.0 27.9 %collective-permute-start.79 = (bf16[384,512]{1,0:T(8,128)(2,1)S(1)}, bf16[384,512]{1,0:T(8,128)(2,1)S(1)}, u32[]{:S(2)}, u32[]{:S(2)}) collective-permute-start(bf16[384,512]{1,0:T(8,128)(2,1)S(1)} %subtract_convert_fusion), channel_id=1, source_target_pairs={{0,1},{1,2},{2,3},{4,5},{5,6},{6,7},{8,9},{9,10},{10,11},{12,13},{... | collective-permute-start | bytes 1179656 | tf_op jit(solution)/shard_map/ppermute | solution.py:55
  370.0 25.5 %collective-permute-start.85 = (bf16[384,512]{1,0:T(8,128)(2,1)S(1)}, bf16[384,512]{1,0:T(8,128)(2,1)S(1)}, u32[]{:S(2)}, u32[]{:S(2)}) collective-permute-start(bf16[384,512]{1,0:T(8,128)(2,1)S(1)} %subtract_convert_fusion), channel_id=1, source_target_pairs={{1,0},{2,1},{3,2},{5,4},{6,5},{7,6},{9,8},{10,9},{11,10},{13,12},{... | collective-permute-start | bytes 1179656 | tf_op jit(solution)/shard_map/ppermute | solution.py:58
  397.0 42.4 %collective-permute-start.73 = (bf16[384,512]{1,0:T(8,128)(2,1)S(1)}, bf16[384,512]{1,0:T(8,128)(2,1)S(1)}, u32[]{:S(2)}, u32[]{:S(2)}) collective-permute-start(bf16[384,512]{1,0:T(8,128)(2,1)S(1)} %get-tuple-element.144), channel_id=1, source_target_pairs={{0,1},{4,5},{8,9},{12,13},{16,17},{20,21},{24,25},{28,29}} | collective-permute-start | bytes 1179656 | tf_op jit(solution)/shard_map/ppermute | solution.py:90
  401.9 37.5 %collective-permute-start.76 = (bf16[384,512]{1,0:T(8,128)(2,1)S(1)}, bf16[384,512]{1,0:T(8,128)(2,1)S(1)}, u32[]{:S(2)}, u32[]{:S(2)}) collective-permute-start(bf16[384,512]{1,0:T(8,128)(2,1)S(1)} %get-tuple-element.145), channel_id=1, source_target_pairs={{3,2},{7,6},{11,10},{15,14},{19,18},{23,22},{27,26},{31,30}} | collective-permute-start | bytes 1179656 | tf_op jit(solution)/shard_map/ppermute | solution.py:91
  449.9 15.6 %collective-permute-start.75 = (bf16[384,512]{1,0:T(8,128)(2,1)}, bf16[384,512]{1,0:T(8,128)(2,1)}, u32[]{:S(2)}, u32[]{:S(2)}) collective-permute-start(bf16[384,512]{1,0:T(8,128)(2,1)} %get-tuple-element.140), channel_id=1, source_target_pairs={{0,1},{1,2},{2,3},{4,5},{5,6},{6,7},{8,9},{9,10},{10,11},{12,13},{... | collective-permute-start | bytes 1179656 | tf_op jit(solution)/shard_map/ppermute | solution.py:90
  574.4 25.8 %all-to-all-start = ((bf16[128,2,1572]{2,1,0:T(2,128)(2,1)}), bf16[128,2,1572]{2,1,0:T(2,128)(2,1)}, u32[]{:S(2)}, u32[]{:S(2)}) async-start(bf16[128,2,1572]{2,1,0:T(2,128)(2,1)} %copy.88), calls=%async_computation | async-start | bytes 1703936 | tf_op jit(solution)/shard_map/all_to_all | solution.py:703
  (117 other events, 1047.3 us)
Sparse Core Ops, SparseCore 0:
  490.6 72.2 all-gather.2

commit v3 on v2

--- a/solution.py
+++ b/solution.py
@@ -45,54 +45,6 @@
     for index in range(1, stream_vals.shape[1]):
         total = total + weights[index] * stream_vals[:, index]
     return total
-
-
-def chain_gather(block):
-    count = lax.axis_size("head")
-    right, left = [block], [block]
-    for step in range(1, count):
-        right.append(
-            lax.ppermute(right[-1], "head", [(z, z + 1) for z in range(step - 1, count - 1)])
-        )
-        left.append(
-            lax.ppermute(left[-1], "head", [(z, z - 1) for z in range(1, count - step + 1)])
-        )
-    return right, left
-
-
-def in_order(right, left):
-    count = lax.axis_size("head")
-    rank = lax.axis_index("head")
-    blocks = []
-    for source in range(count):
-        value = right[0]
-        for step in range(1, count):
-            if source + step < count:
-                value = jnp.where(rank == source + step, right[step], value)
-            if source - step >= 0:
-                value = jnp.where(rank == source - step, left[step], value)
-        blocks.append(value)
-    return blocks
-
-
-def chain_scatter(shares):
-    count = lax.axis_size("head")
-    from_left = from_right = None
-    for step in range(1, count):
-        to_right, to_left = shares[step], shares[count - step]
-        if step > 1:
-            to_right = (to_right.astype(jnp.float32) + from_left.astype(jnp.float32)).astype(
-                jnp.bfloat16
-            )
-            to_left = (to_left.astype(jnp.float32) + from_right.astype(jnp.float32)).astype(
-                jnp.bfloat16
-            )
-        from_left = lax.ppermute(to_right, "head", [(z, z + 1) for z in range(step)])
-        from_right = lax.ppermute(
-            to_left, "head", [(z, z - 1) for z in range(count - step, count)]
-        )
-    own = shares[0].astype(jnp.float32)
-    return own + from_left.astype(jnp.float32) + from_right.astype(jnp.float32)
 
 
 def shift_gather(small):
@@ -111,26 +63,34 @@
     )
 
 
-def gathered_norm(values, width):
+def gathered_norm(values, width, after=None):
     local = values.shape[1]
     sums = jnp.sum(values, axis=1)
     squares = jnp.sum(values * values, axis=1)
     center = sums / local
     sent = (values - center[:, None]).astype(jnp.bfloat16)
     stats = shift_gather(jnp.stack([sums, squares]))
-    right, left = chain_gather(sent)
+    if after is not None:
+        sent, after = lax.optimization_barrier((sent, after))
+    gathered = lax.all_gather(sent, "head", axis=1, tiled=True)
     mean = jnp.sum(stats[:, 0], axis=0) / width
     variance = jnp.sum(stats[:, 1], axis=0) / width - mean * mean
     scale = lax.rsqrt(variance + 1e-05)
-    blocks = in_order(right, left)
     normed = [
         (
-            (block.astype(jnp.float32) + (stats[rank, 0] / local - mean)[:, None])
+            (
+                gathered[:, rank * local : (rank + 1) * local].astype(jnp.float32)
+                + (stats[rank, 0] / local - mean)[:, None]
+            )
             * scale[:, None]
         ).astype(jnp.bfloat16)
-        for rank, block in enumerate(blocks)
+        for rank in range(lax.axis_size("head"))
     ]
-    return jnp.concatenate(normed, axis=1), right[-1]
+    return jnp.concatenate(normed, axis=1), gathered
+
+
+def scatter_columns(shares):
+    return lax.psum_scatter(shares, "head", scatter_dimension=1, tiled=True).astype(jnp.float32)
 
 
 def swapped(values, bit):
@@ -382,44 +342,31 @@
     )(*plan, even, odd, k_pages, v_pages)
 
 
-def owned_tile(index, rank, per, count):
-    owner = lax.rem(rank - lax.div(index, per) + count, count)
-    return owner * per + lax.rem(index, per)
-
-
-def project_kernel(rank_ref, x_ref, w_ref, out_ref):
-    out_ref[0] = jnp.dot(x_ref[...], w_ref[...], preferred_element_type=jnp.float32).astype(
+def project_kernel(x_ref, w_ref, out_ref):
+    out_ref[...] = jnp.dot(x_ref[...], w_ref[...], preferred_element_type=jnp.float32).astype(
         out_ref.dtype
     )
 
 
-def project(values, weight, rank):
-    count = lax.axis_size("head")
+def project(values, weight):
     rows, depth = values.shape
-    columns = weight.shape[1] // count
-    tile = min(columns, 256)
-    per = columns // tile
-    grid_spec = pltpu.PrefetchScalarGridSpec(
-        num_scalar_prefetch=1,
-        grid=(count * per,),
-        in_specs=[
-            pl.BlockSpec((rows, depth), lambda i, z: (0, 0)),
-            pl.BlockSpec(
-                (depth, tile), lambda i, z: (0, owned_tile(i, z[0], per, count))
-            ),
-        ],
-        out_specs=pl.BlockSpec((1, rows, tile), lambda i, z: (lax.div(i, per), 0, lax.rem(i, per))),
-    )
+    columns = weight.shape[1]
+    tile = min(columns, 512)
     return pl.pallas_call(
         project_kernel,
-        grid_spec=grid_spec,
-        out_shape=jax.ShapeDtypeStruct((count, rows, columns), jnp.bfloat16),
+        grid=(columns // tile,),
+        in_specs=[
+            pl.BlockSpec((rows, depth), lambda i: (0, 0)),
+            pl.BlockSpec((depth, tile), lambda i: (0, i)),
+        ],
+        out_specs=pl.BlockSpec((rows, tile), lambda i: (0, i)),
+        out_shape=jax.ShapeDtypeStruct((rows, columns), jnp.bfloat16),
         compiler_params=params(),
         name="project",
-    )(rank, values, weight)
-
-
-def mlp_kernel(steps, tile, rank_ref, x_ref, gate_ref, up_ref, down_ref, out_ref, hidden_ref):
+    )(values, weight)
+
+
+def mlp_kernel(steps, tile, x_ref, gate_ref, up_ref, down_ref, out_ref, hidden_ref):
     step = pl.program_id(0)
 
     @pl.when(step < steps)
@@ -431,46 +378,34 @@
 
     @pl.when(step >= steps)
     def _():
-        out_ref[0] = jnp.dot(
+        out_ref[...] = jnp.dot(
             hidden_ref[...], down_ref[...], preferred_element_type=jnp.float32
         ).astype(out_ref.dtype)
 
 
-def mlp(values, gate_up, down, rank):
-    count = lax.axis_size("head")
+def mlp(values, gate_up, down):
     rows, width = values.shape
-    hidden = down.shape[0]
+    hidden, columns = down.shape
     tile = min(hidden, 256)
     steps = hidden // tile
-    columns = down.shape[1] // count
     out_tile = min(columns, 256)
-    per = columns // out_tile
     late = lambda i: jnp.maximum(i - steps, 0)
     early = lambda i: jnp.minimum(i, steps - 1)
-    grid_spec = pltpu.PrefetchScalarGridSpec(
-        num_scalar_prefetch=1,
-        grid=(steps + count * per,),
-        in_specs=[
-            pl.BlockSpec((rows, width), lambda i, z: (0, 0)),
-            pl.BlockSpec((width, tile), lambda i, z: (0, early(i))),
-            pl.BlockSpec((width, tile), lambda i, z: (0, steps + early(i))),
-            pl.BlockSpec(
-                (hidden, out_tile),
-                lambda i, z: (0, owned_tile(late(i), z[0], per, count)),
-            ),
-        ],
-        out_specs=pl.BlockSpec(
-            (1, rows, out_tile), lambda i, z: (lax.div(late(i), per), 0, lax.rem(late(i), per))
-        ),
-        scratch_shapes=[pltpu.VMEM((rows, hidden), jnp.bfloat16)],
-    )
     return pl.pallas_call(
         functools.partial(mlp_kernel, steps, tile),
-        grid_spec=grid_spec,
-        out_shape=jax.ShapeDtypeStruct((count, rows, columns), jnp.bfloat16),
+        grid=(steps + columns // out_tile,),
+        in_specs=[
+            pl.BlockSpec((rows, width), lambda i: (0, 0)),
+            pl.BlockSpec((width, tile), lambda i: (0, early(i))),
+            pl.BlockSpec((width, tile), lambda i: (0, steps + early(i))),
+            pl.BlockSpec((hidden, out_tile), lambda i: (0, late(i))),
+        ],
+        out_specs=pl.BlockSpec((rows, out_tile), lambda i: (0, late(i))),
+        out_shape=jax.ShapeDtypeStruct((rows, columns), jnp.bfloat16),
+        scratch_shapes=[pltpu.VMEM((rows, hidden), jnp.bfloat16)],
         compiler_params=params(),
         name="mlp",
-    )(rank, values, gate_up, gate_up, down)
+    )(values, gate_up, gate_up, down)
 
 
 def merge_kernel(heads, size, count, *refs):
@@ -596,7 +531,6 @@
 
     k_heads = jnp.transpose(k_pages, (0, 2, 1, 3))
     v_heads = jnp.transpose(v_pages, (0, 2, 1, 3))
-    rank = lax.axis_index("head").astype(jnp.int32)[None]
 
     step_requests = req_local // CHUNKS
     step_tokens = step_requests * tree_size
@@ -608,9 +542,7 @@
         rows = slice(chunk * step_tokens, (chunk + 1) * step_tokens)
         stream_vals = streams[rows].astype(jnp.float32)
         mixed_in = blend(stream_vals, hc_in[0])
-        if token is not None:
-            mixed_in, token = lax.optimization_barrier((mixed_in, token))
-        normed, token = gathered_norm(mixed_in, width)
+        normed, token = gathered_norm(mixed_in, width, token)
         attended_in.append(normed)
 
     all_shape = (step_requests, tree_size, heads * size)
@@ -658,13 +590,13 @@
             ] + [(tree_pair[0][own], tree_pair[1][own])]
             attended.append(merge_partials(pairs, heads, size, with_logs=False)[0])
         attended = jnp.concatenate(attended).reshape(step_tokens, heads * size)
-        attn_delta = chain_scatter(project(attended, out_weight, rank))
+        attn_delta = scatter_columns(project(attended, out_weight))
         attn_parts.append(attn_delta)
 
         stream_vals = streams[rows].astype(jnp.float32)
         mixed_mid = blend(stream_vals, mid_in) + mid_out * attn_delta
-        normed_mid, token = gathered_norm(mixed_mid, width)
-        mlp_parts.append(chain_scatter(mlp(normed_mid, gate_up, down_weight, rank)))
+        normed_mid = gathered_norm(mixed_mid, width)[0]
+        mlp_parts.append(scatter_columns(mlp(normed_mid, gate_up, down_weight)))
 
     attn_delta = jnp.concatenate(attn_parts)
     mlp_delta = jnp.concatenate(mlp_parts)
@@ -694,8 +626,8 @@
         preferred_element_type=jnp.float32,
     )
     drafted = (own_columns[:, None, :] + jax.nn.silu(branch)).astype(jnp.bfloat16)
-    draft_all = lax.all_gather(drafted, ("req", "head"), axis=0, tiled=False)
-    draft_all = draft_all.reshape((parts, -1) + drafted.shape).transpose(0, 2, 3, 1, 4)
+    draft_full = jnp.concatenate(list(shift_gather(drafted)), axis=2)
+    draft_all = lax.all_gather(draft_full, "req", axis=0, tiled=True)
     logits_local = jnp.dot(
         draft_all.reshape(-1, width), lm_head, preferred_element_type=jnp.float32
     )

time: 622 us -> 574 us (0.923)
  starting transfers between devices: 190 us -> 85.3 us
  waiting for transfers between devices: 154 us -> 205 us
  local copies, waits for them, and re-layouts: 75.5 us -> 84.2 us
    ppermute x48 -> x0, starting transfers between devices: 89.8 us -> none  [the longest x12 38.3 us: chain_scatter(): lax.ppermute(to_right, 'head', [(z, z + 1) for z in range(step)])]
    reduce_scatter x0 -> x4, waiting for transfers between devices: none -> 71.1 us  [scatter_columns(): lax.psum_scatter(shares, 'head', scatter_dimension=1, tiled=True)]
    ppermute x48 -> x0, waiting for transfers between devices: 42.6 us -> none  [the longest x12 24.3 us: chain_gather(): lax.ppermute(left[-1], 'head', [(z, z - 1) for z in range(1, count - step...]
    unnamed x117 -> x113, local copies, waits for them, and re-layouts: 27.5 us -> 49.8 us
    ppermute x34, waiting for transfers between devices: 24.3 us -> 44.6 us  [swapped(): return lax.ppermute(values, 'req', [(r, r ^ bit) for r in range(count)])]
    ppermute x34, starting transfers between devices: 67.2 us -> 47.4 us  [swapped(): return lax.ppermute(values, 'req', [(r, r ^ bit) for r in range(count)])]
    transpose x2 -> x0, local copies, waits for them, and re-layouts: 13.9 us -> none  [the longest x1 11.8 us: on_device(): v_heads = jnp.transpose(v_pages, (0, 2, 1, 3))]
    reduce_sum x1 -> x3, other arithmetic: 2.73 us -> 12.5 us  [gathered_norm(): squares = jnp.sum(values * values, axis=1)]
  transfers between devices with their start and end apart: 99 -> 62, of which waited for: 24 -> 26; matrix products, arithmetic and copies ran while one was open for 18% -> 18% of each run, Pallas kernels for 12% -> 17%
where the time goes in v3:
time: 574 us; the launch traced here: 568 us
  waiting for transfers between devices  205 us (36%)
  Pallas kernels  97.3 us (17%)
  starting transfers between devices  85.3 us (15%)
  local copies, waits for them, and re-layouts  84.2 us (15%)
  other arithmetic  57 us (10%)
  matrix products  22.9 us (4%)
  between operations  17.1 us (3%)
    reduce_scatter x4, waiting for transfers between devices, scatter_columns(): lax.psum_scatter(shares, 'head', scatter_dimension=1, tiled=True)  71.1 us
    all_gather x4, waiting for transfers between devices, gathered_norm(): gathered = lax.all_gather(sent, 'head', axis=1, tiled=True)  50.6 us
    unnamed x113, local copies, waits for them, and re-layouts  49.8 us
    ppermute x34, starting transfers between devices, swapped(): return lax.ppermute(values, 'req', [(r, r ^ bit) for r in range(count)])  47.4 us
    ppermute x34, waiting for transfers between devices, swapped(): return lax.ppermute(values, 'req', [(r, r ^ bit) for r in range(count)])  44.6 us
    pallas_call x2, Pallas kernels, mlp(): pl.pallas_call(functools.partial(mlp_kernel, steps, tile), grid=(steps +...  37.4 us
    ppermute x18, starting transfers between devices, shift_gather(): lax.ppermute(small, 'head', [(z, (z + step) % count) for z in range(count)])  32.9 us
    pallas_call x2, Pallas kernels, page_attention(): pl.pallas_call(functools.partial(page_kernel, heads, size), grid_spec=gri...  24.2 us
  transfers between devices with their start and end apart: 62, of which 26 were waited for; matrix products, arithmetic and copies ran while one was open for 18% of the time, Pallas kernels for 17%

profile of v3, /device:TPU:1, one launch (start us, length us, event | category | flops | bytes accessed | tf_op | source)
XLA Modules:
  0.0 568.3 jit_solution(297505283101143979)
XLA Ops:
  40.2 27.8 %all-gather.6.cloned.1.call-done = bf16[384,2048]{1,0:T(8,128)(2,1)} async-done(((bf16[384,512]{1,0:T(8,128)(2,1)}), bf16[384,2048]{1,0:T(8,128)(2,1)}) %all-gather.6.cloned.1.call-update) | async-done | bytes 1572880 | tf_op jit(solution)/shard_map/all_gather | solution.py:75
  85.0 12.0 %collective-permute-start.22 = (f32[2,384]{1,0:T(2,128)}, f32[2,384]{1,0:T(2,128)S(1)}, u32[]{:S(2)}, u32[]{:S(2)}) collective-permute-start(f32[2,384]{1,0:T(2,128)} %get-tuple-element.255), channel_id=1, source_target_pairs={{0,3},{1,0},{2,1},{3,2},{4,7},{5,4},{6,5},{7,6},{8,11},{9,8},{10,9... | collective-permute-start | bytes 9224 | tf_op jit(solution)/shard_map/ppermute | solution.py:54
  106.6 7.3 %copy.126 = bf16[48,128,4,128]{3,1,2,0:T(8,128)(2,1)} copy(bf16[48,128,4,128]{3,2,1,0:T(4,128)(2,1)} %param.28) | data formatting | bytes 12582912 | tf_op args[11]
  113.8 4.5 copy.127
  121.0 5.9 %tree_attention.2 = (f32[8,48,512]{2,1,0:T(8,128)S(1)}, f32[8,8,128]{2,1,0:T(8,128)S(1)}) custom-call(bf16[8,48,512]{2,1,0:T(8,128)(2,1)S(1)} %bitcast.241, bf16[8,48,512]{2,1,0:T(8,128)(2,1)S(1)} %bitcast.251, bf16[8,48,512]{2,1,0:T(8,128)(2,1)S(1)} %bitcast.252, f32[8,48,48]{2,1,0:T(8,128)S(1)} %get-tuple-element.174.reach_ref), custom_call_target="tpu_custom_call" | custom-call | tf_op jit(solution)/shard_map/tree_attention/pallas_call | solution.py:209
  127.9 17.8 %page_attention.2 = (bf16[64,48,512]{2,1,0:T(8,128)(2,1)S(1)}, f32[64,8,128]{2,1,0:T(8,128)S(1)}) custom-call(s32[48]{0:T(128)S(1)} %get-tuple-element.103.page_ref, s32[48]{0:T(128)S(1)} %get-tuple-element.102.place_ref, s32[48]{0:T(128)S(1)} %get-tuple-element.101.fill_ref, s32[48]{0:T(128)S(1)} %get-tuple-element.296.first_ref, ...), custom_call_target="tpu_custom_call" | custom-call | tf_op jit(solution)/shard_map/page_attention/pallas_call | solution.py:333
  147.1 6.2 %collective-permute-start.10 = (bf16[4,8,48,512]{3,2,1,0:T(8,128)(2,1)}, bf16[4,8,48,512]{3,2,1,0:T(8,128)(2,1)S(1)}, u32[]{:S(2)}, u32[]{:S(2)}) collective-permute-start(bf16[4,8,48,512]{3,2,1,0:T(8,128)(2,1)} %bitcast.18), channel_id=1, source_target_pairs={{0,4},{4,0},{8,12},{12,8},{16,20},{20,16},{24,28},{28,24},{1,5},{5... | collective-permute-start | bytes 4718600 | tf_op jit(solution)/shard_map/ppermute | solution.py:98
  163.9 8.7 %collective-permute-done.23 = bf16[4,48,512]{2,1,0:T(8,128)(2,1)S(1)} collective-permute-done((bf16[4,48,512]{2,1,0:T(8,128)(2,1)S(1)}, bf16[4,48,512]{2,1,0:T(8,128)(2,1)S(1)}, u32[]{:S(2)}, u32[]{:S(2)}) %collective-permute-start.23) | collective-permute-done | bytes 196640 | tf_op jit(solution)/shard_map/ppermute | solution.py:98
  177.7 4.2 collective-permute-done.27
  184.3 5.3 merge_partials.10
  193.1 8.2 %collective-permute-done.12 = bf16[2,4,48,512]{3,2,1,0:T(8,128)(2,1)S(1)} collective-permute-done((bf16[2,4,48,512]{3,2,1,0:T(8,128)(2,1)S(1)}, bf16[2,4,48,512]{3,2,1,0:T(8,128)(2,1)S(1)}, u32[]{:S(2)}, u32[]{:S(2)}) %collective-permute-start.12) | collective-permute-done | bytes 393248 | tf_op jit(solution)/shard_map/ppermute | solution.py:98
  202.5 6.5 %page_attention.3 = (bf16[64,48,512]{2,1,0:T(8,128)(2,1)S(1)}, f32[64,8,128]{2,1,0:T(8,128)S(1)}) custom-call(s32[48]{0:T(128)S(1)} %get-tuple-element.107.page_ref, s32[48]{0:T(128)S(1)} %get-tuple-element.108.place_ref, s32[48]{0:T(128)S(1)} %copy-done.15, s32[48]{0:T(128)S(1)} %get-tuple-element.298.first_ref, s32[48]{0:T(128)S(1)} %get-tuple-element.297.last_ref, ...), custom_call_target="tpu_custom_call" | custom-call | tf_op jit(solution)/shard_map/page_attention/pallas_call | solution.py:333
  215.8 10.5 %collective-permute-start.18 = (bf16[1,4,48,512]{3,2,1,0:T(8,128)(2,1)S(1)}, bf16[1,4,48,512]{3,2,1,0:T(8,128)(2,1)S(1)}, u32[]{:S(2)}, u32[]{:S(2)}) collective-permute-start(bf16[1,4,48,512]{3,2,1,0:T(8,128)(2,1)S(1)} %get-tuple-element.176), channel_id=1, source_target_pairs={{0,8},{4,12},{8,0},{12,4},{16,24},{20,28},{24,16},{28,20},{1,9},{5... | collective-permute-start | bytes 589832 | tf_op jit(solution)/shard_map/ppermute | solution.py:98
  226.4 5.9 %tree_attention.3 = (f32[8,48,512]{2,1,0:T(8,128)S(1)}, f32[8,8,128]{2,1,0:T(8,128)S(1)}) custom-call(bf16[8,48,512]{2,1,0:T(8,128)(2,1)S(1)} %bitcast.240, bf16[8,48,512]{2,1,0:T(8,128)(2,1)S(1)} %bitcast.249, bf16[8,48,512]{2,1,0:T(8,128)(2,1)S(1)} %bitcast.250, f32[8,48,48]{2,1,0:T(8,128)S(1)} %get-tuple-element.175.reach_ref), custom_call_target="tpu_custom_call" | custom-call | tf_op jit(solution)/shard_map/tree_attention/pallas_call | solution.py:209
  240.2 5.8 %merge_partials.15 = (bf16[32,48,512]{2,1,0:T(8,128)(2,1)S(1)}, f32[32,8,128]{2,1,0:T(8,128)S(1)}) custom-call(bf16[32,48,512]{2,1,0:T(8,128)(2,1)S(1)} %copy-done.6, bf16[32,48,512]{2,1,0:T(8,128)(2,1)} %bitcast.52.refs_1_, f32[32,8,128]{2,1,0:T(8,128)S(1)} %get-tuple-element.189.refs_2_, f32[32,8,128]{2,1,0:T(8,128)S(1)} %bitcast.269), custom_call_target="tpu_custom_call" | custom-call | tf_op jit(solution)/shard_map/merge_partials/pallas_call | solution.py:446
  249.9 8.2 %collective-permute-done.32 = bf16[2,4,48,512]{3,2,1,0:T(8,128)(2,1)S(1)} collective-permute-done((bf16[2,4,48,512]{3,2,1,0:T(8,128)(2,1)S(1)}, bf16[2,4,48,512]{3,2,1,0:T(8,128)(2,1)S(1)}, u32[]{:S(2)}, u32[]{:S(2)}) %collective-permute-start.32) | collective-permute-done | bytes 393248 | tf_op jit(solution)/shard_map/ppermute | solution.py:98
  274.5 35.1 %reduce-scatter.7.cloned.1.call-done = bf16[384,512]{1,0:T(8,128)(2,1)} async-done(((bf16[384,2048]{1,0:T(8,128)(2,1)}), bf16[384,512]{1,0:T(8,128)(2,1)}) %reduce-scatter.7.cloned.1.call-update) | async-done | bytes 393232 | tf_op jit(solution)/shard_map/reduce_scatter | solution.py:93
  309.6 7.0 %multiply_reduce_fusion = (f32[384]{0:T(512)S(1)}, f32[384]{0:T(512)S(1)}, f32[384,512]{1,0:T(8,128)S(1)}, f32[384]{0:T(512)S(1)}, f32[384]{0:T(512)S(1)}, /*index=5*/f32[384,512]{1,0:T(8,128)S(1)}) fusion(bf16[384,512]{1,0:T(8,128)(2,1)} %reduce-scatter.7.cloned.1.call-done, f32[]{:T(128)} %multiply_reduce_fusion.6, f32[384,4,512]{2,0,1:T(8,128)} %copy-done.18, ...), kind=kLoop, calls=%fused_computation.62 | loop fusion | flops 5110272 | bytes 8656916 | tf_op jit(solution)/shard_map/reduce_sum | solution.py:69
  322.3 17.3 %copy.97 = bf16[256,8,2,2048]{3,1,2,0:T(8,128)(2,1)} copy(bf16[256,8,2,2048]{3,2,1,0:T(2,128)(2,1)} %bitcast.284) | data formatting | bytes 33554432
  339.9 13.9 %all-gather.10.cloned.1.call-done = bf16[384,2048]{1,0:T(8,128)(2,1)} async-done(((bf16[384,512]{1,0:T(8,128)(2,1)}), bf16[384,2048]{1,0:T(8,128)(2,1)}) %all-gather.10.cloned.1.call-update) | async-done | bytes 1572880 | tf_op jit(solution)/shard_map/all_gather | solution.py:75
  359.1 18.6 %mlp.2 = bf16[384,2048]{1,0:T(8,128)(2,1)} custom-call(bf16[384,2048]{1,0:T(8,128)(2,1)S(1)} %pad_maximum_fusion.5.x_ref, bf16[2048,4096]{1,0:T(8,128)(2,1)} %bitcast.278, bf16[2048,4096]{1,0:T(8,128)(2,1)} %bitcast.279, bf16[2048,2048]{1,0:T(8,128)(2,1)S(1)} %copy-done.1), custom_call_target="tpu_custom_call" | custom-call | tf_op jit(solution)/shard_map/mlp/pallas_call | solution.py:394
  383.0 8.9 %all-gather.12.cloned.1.call-done = bf16[384,2048]{1,0:T(8,128)(2,1)} async-done(((bf16[384,512]{1,0:T(8,128)(2,1)}), bf16[384,2048]{1,0:T(8,128)(2,1)}) %all-gather.12.cloned.1.call-update) | async-done | bytes 1572880 | tf_op jit(solution)/shard_map/all_gather | solution.py:75
  397.3 18.8 %mlp.3 = bf16[384,2048]{1,0:T(8,128)(2,1)} custom-call(bf16[384,2048]{1,0:T(8,128)(2,1)S(1)} %pad_maximum_fusion.6.x_ref, bf16[2048,4096]{1,0:T(8,128)(2,1)} %bitcast.280, bf16[2048,4096]{1,0:T(8,128)(2,1)} %bitcast.281, bf16[2048,2048]{1,0:T(8,128)(2,1)S(1)} %copy-done.2), custom_call_target="tpu_custom_call" | custom-call | tf_op jit(solution)/shard_map/mlp/pallas_call | solution.py:394
  419.8 4.0 gather_fusion.2
  430.2 36.0 %reduce-scatter.11.cloned.1.call-done = bf16[384,512]{1,0:T(8,128)(2,1)} async-done(((bf16[384,2048]{1,0:T(8,128)(2,1)}), bf16[384,512]{1,0:T(8,128)(2,1)}) %reduce-scatter.11.cloned.1.call-update) | async-done | bytes 393232 | tf_op jit(solution)/shard_map/reduce_scatter | solution.py:93
  470.7 3.8 bitcast_add_fusion.3
  491.5 5.3 fusion.95
  498.8 19.6 %all-gather.14.cloned.1.call-done = bf16[128,2,2048]{2,0,1:T(8,128)(2,1)} async-done(((bf16[16,2,2048]{2,0,1:T(8,128)(2,1)}), bf16[128,2,2048]{2,0,1:T(8,128)(2,1)}) %all-gather.14.cloned.1.call-update) | async-done | bytes 1048592 | tf_op jit(solution)/shard_map/all_gather | solution.py:630
  518.4 7.6 %fusion.2 = bf16[128,2,1572]{0,2,1:T(8,128)(2,1)} fusion(bf16[128,2,2048]{2,0,1:T(8,128)(2,1)} %all-gather.14.cloned.1.call-done, bf16[2048,1572]{0,1:T(8,128)(2,1)} %param.26), kind=kOutput, calls=%fused_computation.8 | convolution fusion | flops 1648763904 | bytes 8292352 | tf_op jit(solution)/shard_map/dot_general | solution.py:631
  529.5 4.6 all-to-all-start
  537.0 6.4 %add_convert_fusion = bf16[768,4,512]{2,1,0:T(4,128)(2,1)} fusion(f32[768,512]{1,0:T(8,128)S(1)} %get-tuple-element.301, f32[4]{0:T(128)S(1)} %get-tuple-element.277, f32[768,512]{1,0:T(8,128)S(1)} %get-tuple-element.302, f32[4]{0:T(128)S(1)} %get-tuple-element.278, f32[768,512]{1,0:T(8,128)S(1)} %copy-done.23, f32[4]{0:T(128)S(1)} %get-tuple-element.279, ...), kind=kLoop, calls=%fused_computation.7 | loop fusion | flops 18874368 | bytes 12583008 | tf_op jit(solution)/shard_map/convert_element_type | solution.py:611
  543.4 13.0 %all-to-all-done = bf16[128,2,1572]{2,1,0:T(2,128)(2,1)} async-done(((bf16[128,2,1572]{2,1,0:T(2,128)(2,1)}), bf16[128,2,1572]{2,1,0:T(2,128)(2,1)}, u32[]{:S(2)}, u32[]{:S(2)}) %all-to-all-start) | async-done | bytes 804896 | tf_op jit(solution)/shard_map/all_to_all | solution.py:635
  (424 shorter events, 186.5 us)
Async XLA Ops:
  7.2 60.8 %all-gather.6.cloned.1.call-start = ((), (), s32[]{:S(2)}) async-start(), calls=%async_computation.5 | async-start | bytes 1966080 | tf_op jit(solution)/shard_map/all_gather | solution.py:75
  16.7 23.3 %collective-permute-start = (f32[2,384]{1,0:T(2,128)S(1)}, f32[2,384]{1,0:T(2,128)S(1)}, u32[]{:S(2)}, u32[]{:S(2)}) collective-permute-start(f32[2,384]{1,0:T(2,128)S(1)} %get-tuple-element.253), channel_id=1, source_target_pairs={{0,1},{1,2},{2,3},{3,0},{4,5},{5,6},{6,7},{7,4},{8,9},{9,10},{10,1... | collective-permute-start | bytes 9224 | tf_op jit(solution)/shard_map/ppermute | solution.py:54
  18.8 21.1 %collective-permute-start.1 = (f32[2,384]{1,0:T(2,128)S(1)}, f32[2,384]{1,0:T(2,128)S(1)}, u32[]{:S(2)}, u32[]{:S(2)}) collective-permute-start(f32[2,384]{1,0:T(2,128)S(1)} %get-tuple-element.253), channel_id=1, source_target_pairs={{0,2},{1,3},{2,0},{3,1},{4,6},{5,7},{6,4},{7,5},{8,10},{9,11},{10,... | collective-permute-start | bytes 9224 | tf_op jit(solution)/shard_map/ppermute | solution.py:54
  21.2 18.8 %collective-permute-start.2 = (f32[2,384]{1,0:T(2,128)S(1)}, f32[2,384]{1,0:T(2,128)S(1)}, u32[]{:S(2)}, u32[]{:S(2)}) collective-permute-start(f32[2,384]{1,0:T(2,128)S(1)} %get-tuple-element.253), channel_id=1, source_target_pairs={{0,3},{1,0},{2,1},{3,2},{4,7},{5,4},{6,5},{7,6},{8,11},{9,8},{10,9... | collective-permute-start | bytes 9224 | tf_op jit(solution)/shard_map/ppermute | solution.py:54
  27.9 90.5 %collective-permute-start.20 = (f32[2,384]{1,0:T(2,128)}, f32[2,384]{1,0:T(2,128)}, u32[]{:S(2)}, u32[]{:S(2)}) collective-permute-start(f32[2,384]{1,0:T(2,128)} %get-tuple-element.255), channel_id=1, source_target_pairs={{0,1},{1,2},{2,3},{3,0},{4,5},{5,6},{6,7},{7,4},{8,9},{9,10},{10,1... | collective-permute-start | bytes 9224 | tf_op jit(solution)/shard_map/ppermute | solution.py:54
  28.3 90.8 %collective-permute-start.21 = (f32[2,384]{1,0:T(2,128)}, f32[2,384]{1,0:T(2,128)}, u32[]{:S(2)}, u32[]{:S(2)}) collective-permute-start(f32[2,384]{1,0:T(2,128)} %get-tuple-element.255), channel_id=1, source_target_pairs={{0,2},{1,3},{2,0},{3,1},{4,6},{5,7},{6,4},{7,5},{8,10},{9,11},{10,... | collective-permute-start | bytes 9224 | tf_op jit(solution)/shard_map/ppermute | solution.py:54
  29.3 124.7 %all-gather.8.cloned.1.call-start = ((), (), s32[]{:S(2)}) async-start(), calls=%async_computation.7 | async-start | bytes 1966080 | tf_op jit(solution)/shard_map/all_gather | solution.py:75
  77.0 20.0 %collective-permute-start.5 = (bf16[4,48,512]{2,1,0:T(8,128)(2,1)S(1)}, bf16[4,48,512]{2,1,0:T(8,128)(2,1)S(1)}, u32[]{:S(2)}, u32[]{:S(2)}) collective-permute-start(bf16[4,48,512]{2,1,0:T(8,128)(2,1)S(1)} %bitcast.289), channel_id=1, source_target_pairs={{0,16},{4,20},{8,24},{12,28},{16,0},{20,4},{24,8},{28,12},{1,17},{... | collective-permute-start | bytes 589832 | tf_op jit(solution)/shard_map/ppermute | solution.py:98
  78.5 196.0 %reduce-scatter.5.cloned.1.call-start = ((), (), s32[]{:S(2)}) async-start(), calls=%async_computation.6 | async-start | bytes 1966080 | tf_op jit(solution)/shard_map/reduce_scatter | solution.py:93
  80.2 18.4 %collective-permute-start.6 = (bf16[4,48,512]{2,1,0:T(8,128)(2,1)S(1)}, bf16[4,48,512]{2,1,0:T(8,128)(2,1)S(1)}, u32[]{:S(2)}, u32[]{:S(2)}) collective-permute-start(bf16[4,48,512]{2,1,0:T(8,128)(2,1)S(1)} %bitcast.287), channel_id=1, source_target_pairs={{0,16},{4,20},{8,24},{12,28},{16,0},{20,4},{24,8},{28,12},{1,17},{... | collective-permute-start | bytes 589832 | tf_op jit(solution)/shard_map/ppermute | solution.py:98
  85.0 34.8 %collective-permute-start.22 = (f32[2,384]{1,0:T(2,128)}, f32[2,384]{1,0:T(2,128)S(1)}, u32[]{:S(2)}, u32[]{:S(2)}) collective-permute-start(f32[2,384]{1,0:T(2,128)} %get-tuple-element.255), channel_id=1, source_target_pairs={{0,3},{1,0},{2,1},{3,2},{4,7},{5,4},{6,5},{7,6},{8,11},{9,8},{10,9... | collective-permute-start | bytes 9224 | tf_op jit(solution)/shard_map/ppermute | solution.py:54
  103.5 24.4 %collective-permute-start.9 = (bf16[32,48,512]{2,1,0:T(8,128)(2,1)S(1)}, bf16[32,48,512]{2,1,0:T(8,128)(2,1)S(1)}, u32[]{:S(2)}, u32[]{:S(2)}) collective-permute-start(bf16[32,48,512]{2,1,0:T(8,128)(2,1)S(1)} %constant_dynamic-update-slice_fusion.even_ref), channel_id=1, source_target_pairs={{0,4},{4,0},{8,12},{12,8},{16,20},{20,16},{24,28},{28,24},{1,5},{5... | collective-permute-start | bytes 4718600 | tf_op jit(solution)/shard_map/ppermute | solution.py:98
  147.1 37.2 %collective-permute-start.10 = (bf16[4,8,48,512]{3,2,1,0:T(8,128)(2,1)}, bf16[4,8,48,512]{3,2,1,0:T(8,128)(2,1)S(1)}, u32[]{:S(2)}, u32[]{:S(2)}) collective-permute-start(bf16[4,8,48,512]{3,2,1,0:T(8,128)(2,1)} %bitcast.18), channel_id=1, source_target_pairs={{0,4},{4,0},{8,12},{12,8},{16,20},{20,16},{24,28},{28,24},{1,5},{5... | collective-permute-start | bytes 4718600 | tf_op jit(solution)/shard_map/ppermute | solution.py:98
  154.0 30.3 %collective-permute-start.11 = (f32[4,8,8,128]{3,2,1,0:T(8,128)}, f32[4,8,8,128]{3,2,1,0:T(8,128)}, u32[]{:S(2)}, u32[]{:S(2)}) collective-permute-start(f32[4,8,8,128]{3,2,1,0:T(8,128)} %bitcast.20), channel_id=1, source_target_pairs={{0,4},{4,0},{8,12},{12,8},{16,20},{20,16},{24,28},{28,24},{1,5},{5... | collective-permute-start | bytes 393224 | tf_op jit(solution)/shard_map/ppermute | solution.py:98
  181.9 20.5 %collective-permute-start.29 = (bf16[32,48,512]{2,1,0:T(8,128)(2,1)S(1)}, bf16[32,48,512]{2,1,0:T(8,128)(2,1)S(1)}, u32[]{:S(2)}, u32[]{:S(2)}) collective-permute-start(bf16[32,48,512]{2,1,0:T(8,128)(2,1)S(1)} %constant_dynamic-update-slice_fusion.8.even_ref), channel_id=1, source_target_pairs={{0,4},{4,0},{8,12},{12,8},{16,20},{20,16},{24,28},{28,24},{1,5},{5... | collective-permute-start | bytes 4718600 | tf_op jit(solution)/shard_map/ppermute | solution.py:98
  191.5 23.2 %collective-permute-start.16 = (bf16[2,4,48,512]{3,2,1,0:T(8,128)(2,1)S(1)}, bf16[2,4,48,512]{3,2,1,0:T(8,128)(2,1)S(1)}, u32[]{:S(2)}, u32[]{:S(2)}) collective-permute-start(bf16[2,4,48,512]{3,2,1,0:T(8,128)(2,1)S(1)} %get-tuple-element.158), channel_id=1, source_target_pairs={{0,16},{4,20},{8,24},{12,28},{16,0},{20,4},{24,8},{28,12},{1,17},{... | collective-permute-start | bytes 1179656 | tf_op jit(solution)/shard_map/ppermute | solution.py:98
  191.6 23.1 %collective-permute-start.17 = (f32[2,4,8,128]{3,2,1,0:T(8,128)S(1)}, f32[2,4,8,128]{3,2,1,0:T(8,128)S(1)}, u32[]{:S(2)}, u32[]{:S(2)}) collective-permute-start(f32[2,4,8,128]{3,2,1,0:T(8,128)S(1)} %get-tuple-element.208), channel_id=1, source_target_pairs={{0,16},{4,20},{8,24},{12,28},{16,0},{20,4},{24,8},{28,12},{1,17},{... | collective-permute-start | bytes 98312 | tf_op jit(solution)/shard_map/ppermute | solution.py:98
  210.9 29.3 %collective-permute-start.30 = (bf16[4,8,48,512]{3,2,1,0:T(8,128)(2,1)}, bf16[4,8,48,512]{3,2,1,0:T(8,128)(2,1)}, u32[]{:S(2)}, u32[]{:S(2)}) collective-permute-start(bf16[4,8,48,512]{3,2,1,0:T(8,128)(2,1)} %bitcast.51), channel_id=1, source_target_pairs={{0,4},{4,0},{8,12},{12,8},{16,20},{20,16},{24,28},{28,24},{1,5},{5... | collective-permute-start | bytes 4718600 | tf_op jit(solution)/shard_map/ppermute | solution.py:98
  213.1 19.3 %collective-permute-start.14 = (bf16[1,4,48,512]{3,2,1,0:T(8,128)(2,1)S(1)}, bf16[1,4,48,512]{3,2,1,0:T(8,128)(2,1)S(1)}, u32[]{:S(2)}, u32[]{:S(2)}) collective-permute-start(bf16[1,4,48,512]{3,2,1,0:T(8,128)(2,1)S(1)} %get-tuple-element.172), channel_id=1, source_target_pairs={{0,16},{4,20},{8,24},{12,28},{16,0},{20,4},{24,8},{28,12},{1,17},{... | collective-permute-start | bytes 589832 | tf_op jit(solution)/shard_map/ppermute | solution.py:98
  213.2 19.2 %collective-permute-start.15 = (f32[1,4,8,128]{3,2,1,0:T(8,128)S(1)}, f32[1,4,8,128]{3,2,1,0:T(8,128)S(1)}, u32[]{:S(2)}, u32[]{:S(2)}) collective-permute-start(f32[1,4,8,128]{3,2,1,0:T(8,128)S(1)} %get-tuple-element.218), channel_id=1, source_target_pairs={{0,16},{4,20},{8,24},{12,28},{16,0},{20,4},{24,8},{28,12},{1,17},{... | collective-permute-start | bytes 49160 | tf_op jit(solution)/shard_map/ppermute | solution.py:98
  215.8 17.4 %collective-permute-start.18 = (bf16[1,4,48,512]{3,2,1,0:T(8,128)(2,1)S(1)}, bf16[1,4,48,512]{3,2,1,0:T(8,128)(2,1)S(1)}, u32[]{:S(2)}, u32[]{:S(2)}) collective-permute-start(bf16[1,4,48,512]{3,2,1,0:T(8,128)(2,1)S(1)} %get-tuple-element.176), channel_id=1, source_target_pairs={{0,8},{4,12},{8,0},{12,4},{16,24},{20,28},{24,16},{28,20},{1,9},{5... | collective-permute-start | bytes 589832 | tf_op jit(solution)/shard_map/ppermute | solution.py:98
  237.1 72.5 %reduce-scatter.7.cloned.1.call-start = ((), (), s32[]{:S(2)}) async-start(), calls=%async_computation.8 | async-start | bytes 1966080 | tf_op jit(solution)/shard_map/reduce_scatter | solution.py:93
  248.0 13.0 %collective-permute-start.36 = (bf16[2,4,48,512]{3,2,1,0:T(8,128)(2,1)S(1)}, bf16[2,4,48,512]{3,2,1,0:T(8,128)(2,1)S(1)}, u32[]{:S(2)}, u32[]{:S(2)}) collective-permute-start(bf16[2,4,48,512]{3,2,1,0:T(8,128)(2,1)S(1)} %get-tuple-element.164), channel_id=1, source_target_pairs={{0,16},{4,20},{8,24},{12,28},{16,0},{20,4},{24,8},{28,12},{1,17},{... | collective-permute-start | bytes 1179656 | tf_op jit(solution)/shard_map/ppermute | solution.py:98
  271.2 82.5 %all-gather.10.cloned.1.call-start = ((), (), s32[]{:S(2)}) async-start(), calls=%async_computation.9 | async-start | bytes 1966080 | tf_op jit(solution)/shard_map/all_gather | solution.py:75
  317.5 74.4 %all-gather.12.cloned.1.call-start = ((), (), s32[]{:S(2)}) async-start(), calls=%async_computation.11 | async-start | bytes 1966080 | tf_op jit(solution)/shard_map/all_gather | solution.py:75
  318.5 111.7 %reduce-scatter.9.cloned.1.call-start = ((), (), s32[]{:S(2)}) async-start(), calls=%async_computation.10 | async-start | bytes 1966080 | tf_op jit(solution)/shard_map/reduce_scatter | solution.py:93
  318.5 21.1 %collective-permute-start.40 = (f32[2,384]{1,0:T(2,128)S(1)}, f32[2,384]{1,0:T(2,128)S(1)}, u32[]{:S(2)}, u32[]{:S(2)}) collective-permute-start(f32[2,384]{1,0:T(2,128)S(1)} %get-tuple-element.249), channel_id=1, source_target_pairs={{0,1},{1,2},{2,3},{3,0},{4,5},{5,6},{6,7},{7,4},{8,9},{9,10},{10,1... | collective-permute-start | bytes 9224 | tf_op jit(solution)/shard_map/ppermute | solution.py:54
  318.6 21.0 %collective-permute-start.41 = (f32[2,384]{1,0:T(2,128)S(1)}, f32[2,384]{1,0:T(2,128)S(1)}, u32[]{:S(2)}, u32[]{:S(2)}) collective-permute-start(f32[2,384]{1,0:T(2,128)S(1)} %get-tuple-element.249), channel_id=1, source_target_pairs={{0,2},{1,3},{2,0},{3,1},{4,6},{5,7},{6,4},{7,5},{8,10},{9,11},{10,... | collective-permute-start | bytes 9224 | tf_op jit(solution)/shard_map/ppermute | solution.py:54
  320.1 19.5 %collective-permute-start.42 = (f32[2,384]{1,0:T(2,128)S(1)}, f32[2,384]{1,0:T(2,128)S(1)}, u32[]{:S(2)}, u32[]{:S(2)}) collective-permute-start(f32[2,384]{1,0:T(2,128)S(1)} %get-tuple-element.249), channel_id=1, source_target_pairs={{0,3},{1,0},{2,1},{3,2},{4,7},{5,4},{6,5},{7,6},{8,11},{9,8},{10,9... | collective-permute-start | bytes 9224 | tf_op jit(solution)/shard_map/ppermute | solution.py:54
  377.7 88.4 %reduce-scatter.11.cloned.1.call-start = ((), (), s32[]{:S(2)}) async-start(), calls=%async_computation.12 | async-start | bytes 1966080 | tf_op jit(solution)/shard_map/reduce_scatter | solution.py:93
  416.1 102.3 %all-gather.14.cloned.1.call-start = ((), (), s32[]{:S(2)}) async-start(), calls=%async_computation.13 | async-start | bytes 1179648 | tf_op jit(solution)/shard_map/all_gather | solution.py:630
  529.5 26.9 %all-to-all-start = ((bf16[128,2,1572]{2,1,0:T(2,128)(2,1)}), bf16[128,2,1572]{2,1,0:T(2,128)(2,1)}, u32[]{:S(2)}, u32[]{:S(2)}) async-start(bf16[128,2,1572]{2,1,0:T(2,128)(2,1)} %copy.83), calls=%async_computation.4 | async-start | bytes 1703936 | tf_op jit(solution)/shard_map/all_to_all | solution.py:635
  (77 other events, 618.6 us)
Sparse Core Ops, SparseCore 0:
  29.4 38.5 all-gather.5
  78.6 36.6 all-gather.7
  237.2 35.3 reduce-scatter.4
  275.3 34.2 reduce-scatter.6
  317.6 36.0 all-gather.9
  355.7 36.1 all-gather.11
  394.8 34.1 reduce-scatter.8
  431.8 34.2 reduce-scatter.10
  491.6 26.7 all-gather.13

commit v4 on v3

--- a/solution.py
+++ b/solution.py
@@ -13,6 +13,7 @@
 PRECISE = lax.Precision.HIGHEST
 CHUNKS = 2
 LANES = 128
+PAGES_A_STEP = 2
 VMEM_BYTES = 40 * 1024 * 1024
 
 
@@ -61,6 +62,20 @@
             for source in range(count)
         ]
     )
+
+
+def shift_scatter(shares):
+    count = lax.axis_size("head")
+    rank = lax.axis_index("head")
+    width = shares.shape[1] // count
+    total = None
+    for step in range(count):
+        block = lax.dynamic_slice_in_dim(shares, (rank + step) % count * width, width, 1)
+        if step:
+            block = lax.ppermute(block, "head", [(z, (z + step) % count) for z in range(count)])
+        block = block.astype(jnp.float32)
+        total = block if total is None else total + block
+    return total
 
 
 def gathered_norm(values, width, after=None):
@@ -86,7 +101,7 @@
         ).astype(jnp.bfloat16)
         for rank in range(lax.axis_size("head"))
     ]
-    return jnp.concatenate(normed, axis=1), gathered
+    return jnp.concatenate(normed, axis=1), gathered, sent
 
 
 def scatter_columns(shares):
@@ -117,6 +132,21 @@
     return even, swapped(even, near)
 
 
+def gather_small(values):
+    count = lax.axis_size("req")
+    near, orders = bit_orders()
+    stacked = values[None]
+    bits = []
+    for bit in list(orders[0]) + [near]:
+        stacked = jnp.concatenate([stacked, swapped(stacked, bit)])
+        bits.append(bit)
+    index = lax.axis_index("req") ^ jnp.arange(count, dtype=jnp.int32)
+    place = jnp.zeros_like(index)
+    for spot, bit in enumerate(bits):
+        place = place + jnp.where((index & bit) != 0, 1 << spot, 0)
+    return stacked[place]
+
+
 def scatter_requests(sums, logs, merge):
     near, orders = bit_orders()
     count = lax.axis_size("req")
@@ -124,7 +154,7 @@
     state = []
     mine = [sums[:far], logs[:far]]
     theirs = [swapped(sums[far:], near), swapped(logs[far:], near)]
-    merged = first_merged = merge(mine, theirs)
+    merged = merge(mine, theirs)
     half = sums.shape[1] // 2
     done = []
     for part, order in enumerate(orders):
@@ -139,7 +169,7 @@
             places = [places[at] for at in stay]
             kept = merge(ours, got) if place < len(order) - 1 else (ours, got)
         done.append(kept)
-    return done, first_merged[1]
+    return done
 
 
 def rotate_kernel(heads, size, scale, x_ref, cos_ref, sin_ref, q_ref, k_ref, v_ref):
@@ -231,99 +261,158 @@
     live_ref,
     even_ref,
     odd_ref,
-    k_ref,
-    v_ref,
+    *refs,
+):
+    leaves = refs[: 2 * PAGES_A_STEP]
+    out_ref, log_ref, acc_ref, top_ref, total_ref = refs[2 * PAGES_A_STEP :]
+    step = pl.program_id(0)
+    half, tree = even_ref.shape[:2]
+    spans = [slice(head * size, (head + 1) * size) for head in range(heads)]
+    entries = leaves[0].shape[2]
+
+    @pl.when(step == 0)
+    def _():
+        log_ref[...] = jnp.full(log_ref.shape, NEG_FILL, jnp.float32)
+
+    @pl.when(step * PAGES_A_STEP < live_ref[0])
+    def _():
+        column = lax.broadcasted_iota(jnp.int32, (tree, entries), 1)
+        units = [(part, head) for part in range(PAGES_A_STEP) for head in range(heads)]
+        asked, valid = [], []
+        for part in range(PAGES_A_STEP):
+            visit = step * PAGES_A_STEP + part
+            place = place_ref[visit]
+            asked.append(
+                jnp.where(
+                    place < half,
+                    even_ref[jnp.minimum(place, half - 1)],
+                    odd_ref[jnp.maximum(place - half, 0)],
+                )
+            )
+            valid.append(column < fill_ref[visit])
+        scores = [
+            lax.dot_general(
+                asked[part][:, spans[head]],
+                leaves[2 * part][0, head],
+                (((1,), (1,)), ((), ())),
+                preferred_element_type=jnp.float32,
+            )
+            for part, head in units
+        ]
+        scores = [
+            jnp.where(valid[part], score, NEG_FILL) for (part, head), score in zip(units, scores)
+        ]
+        tops = [jnp.max(score, axis=1, keepdims=True) for score in scores]
+        weights = [
+            jnp.where(valid[part], jnp.exp(score - top), 0.0)
+            for (part, head), score, top in zip(units, scores, tops)
+        ]
+        totals = [jnp.sum(weight, axis=1, keepdims=True) for weight in weights]
+        sums = [
+            jnp.dot(
+                weight.astype(jnp.bfloat16),
+                leaves[2 * part + 1][0, head],
+                preferred_element_type=jnp.float32,
+            )
+            for (part, head), weight in zip(units, weights)
+        ]
+        for part in range(PAGES_A_STEP):
+            visit = step * PAGES_A_STEP + part
+            merge_page(
+                visit,
+                spans,
+                tops[part * heads : (part + 1) * heads],
+                totals[part * heads : (part + 1) * heads],
+                sums[part * heads : (part + 1) * heads],
+                place_ref,
+                first_ref,
+                last_ref,
+                live_ref,
+                out_ref,
+                log_ref,
+                acc_ref,
+                top_ref,
+                total_ref,
+            )
+
+
+def merge_page(
+    visit,
+    spans,
+    tops,
+    totals,
+    sums,
+    place_ref,
+    first_ref,
+    last_ref,
+    live_ref,
     out_ref,
     log_ref,
     acc_ref,
     top_ref,
     total_ref,
 ):
-    step = pl.program_id(0)
-    tree = even_ref.shape[1]
-    spans = [slice(head * size, (head + 1) * size) for head in range(heads)]
-
-    @pl.when(step == 0)
+    tree = acc_ref.shape[0]
+    live = visit < live_ref[0]
+    alone = (first_ref[visit] == 1) & (last_ref[visit] == 1)
+
+    def write(tops, totals, sums):
+        logs = []
+        for span, top, total, value in zip(spans, tops, totals, sums):
+            some = total > 0
+            safe = jnp.where(some, total, 1.0)
+            out_ref[place_ref[visit], :, span] = (value / safe).astype(out_ref.dtype)
+            logs.append(jnp.where(some, top + jnp.log(safe), NEG_FILL)[:, :1])
+        log_ref[place_ref[visit]] = lay_logs(logs, tree)
+
+    @pl.when(live & alone)
     def _():
-        log_ref[...] = jnp.full(log_ref.shape, NEG_FILL, jnp.float32)
-
-    @pl.when(step < live_ref[0])
+        write(tops, totals, sums)
+
+    @pl.when(live & jnp.logical_not(alone))
     def _():
-        @pl.when(first_ref[step] == 1)
+        @pl.when(first_ref[visit] == 1)
         def _():
             acc_ref[...] = jnp.zeros(acc_ref.shape, jnp.float32)
             top_ref[...] = jnp.full(top_ref.shape, NEG_FILL, jnp.float32)
             total_ref[...] = jnp.zeros(total_ref.shape, jnp.float32)
 
-        entries = k_ref.shape[2]
-        is_even = place_ref[step] < log_ref.shape[0] // 2
-        asked = jnp.where(is_even, even_ref[0], odd_ref[0])
-        valid = lax.broadcasted_iota(jnp.int32, (tree, entries), 1) < fill_ref[step]
-        scores = [
-            lax.dot_general(
-                asked[:, span],
-                k_ref[0, head],
-                (((1,), (1,)), ((), ())),
-                preferred_element_type=jnp.float32,
+        for head, span in enumerate(spans):
+            before = top_ref[head]
+            top = jnp.maximum(before, tops[head])
+            decay, gain = jnp.exp(before - top), jnp.exp(tops[head] - top)
+            top_ref[head] = top
+            total_ref[head] = total_ref[head] * decay + totals[head] * gain
+            acc_ref[:, span] = acc_ref[:, span] * decay + sums[head] * gain
+
+        @pl.when(last_ref[visit] == 1)
+        def _():
+            heads = range(len(spans))
+            write(
+                [top_ref[head] for head in heads],
+                [total_ref[head] for head in heads],
+                [acc_ref[:, span] for span in spans],
             )
-            for head, span in enumerate(spans)
-        ]
-        scores = [jnp.where(valid, score, NEG_FILL) for score in scores]
-        before = [top_ref[head] for head in range(heads)]
-        tops = [
-            jnp.maximum(old, jnp.max(score, axis=1, keepdims=True))
-            for old, score in zip(before, scores)
-        ]
-        weights = [
-            jnp.where(valid, jnp.exp(score - top), 0.0) for score, top in zip(scores, tops)
-        ]
-        decays = [jnp.exp(old - top) for old, top in zip(before, tops)]
-        sums = [
-            jnp.dot(
-                weight.astype(jnp.bfloat16), v_ref[0, head], preferred_element_type=jnp.float32
-            )
-            for head, weight in enumerate(weights)
-        ]
-        totals = [
-            total_ref[head] * decays[head] + jnp.sum(weights[head], axis=1, keepdims=True)
-            for head in range(heads)
-        ]
-        news = [acc_ref[:, span] * decays[head] + sums[head] for head, span in enumerate(spans)]
-        for head, span in enumerate(spans):
-            top_ref[head] = tops[head]
-            total_ref[head] = totals[head]
-            acc_ref[:, span] = news[head]
-
-        @pl.when(last_ref[step] == 1)
-        def _():
-            logs = []
-            for head, span in enumerate(spans):
-                total = total_ref[head]
-                some = total > 0
-                safe = jnp.where(some, total, 1.0)
-                out_ref[0, :, span] = (acc_ref[:, span] / safe).astype(out_ref.dtype)
-                logs.append(jnp.where(some, top_ref[head] + jnp.log(safe), NEG_FILL)[:, :1])
-            log_ref[place_ref[step]] = lay_logs(logs, tree)
 
 
 def page_attention(even, odd, k_pages, v_pages, plan, heads, size):
     half, tree, width = even.shape
     requests = 2 * half
-    entries = k_pages.shape[2]
-    low = lambda p, page, place, *rest: (jnp.minimum(place[p], half - 1), 0, 0)
-    high = lambda p, page, place, *rest: (jnp.maximum(place[p] - half, 0), 0, 0)
-    row = lambda at: pl.BlockSpec((1, tree, width), at)
-    leaf = pl.BlockSpec(
-        (1, heads, entries, size), lambda p, page, place, *rest: (page[p], 0, 0, 0)
-    )
+    slots, entries = k_pages.shape[0], k_pages.shape[2]
+    whole = lambda shape: pl.BlockSpec(shape, lambda p, *rest: (0, 0, 0))
+
+    def leaf(part):
+        return pl.BlockSpec(
+            (1, heads, entries, size),
+            lambda p, page, *rest: (page[p * PAGES_A_STEP + part], 0, 0, 0),
+        )
+
     grid_spec = pltpu.PrefetchScalarGridSpec(
         num_scalar_prefetch=6,
-        grid=(k_pages.shape[0],),
-        in_specs=[row(low), row(high), leaf, leaf],
-        out_specs=[
-            row(lambda p, page, place, *rest: (place[p], 0, 0)),
-            pl.BlockSpec((requests, 8, LANES), lambda p, *rest: (0, 0, 0)),
-        ],
+        grid=(slots // PAGES_A_STEP,),
+        in_specs=[whole(even.shape), whole(odd.shape)]
+        + [leaf(part) for part in range(PAGES_A_STEP) for _ in range(2)],
+        out_specs=[whole((requests, tree, width)), whole((requests, 8, LANES))],
         scratch_shapes=[
             pltpu.VMEM((tree, width), jnp.float32),
             pltpu.VMEM((heads, tree, size), jnp.float32),
@@ -339,7 +428,7 @@
         ],
         compiler_params=params(),
         name="page_attention",
-    )(*plan, even, odd, k_pages, v_pages)
+    )(*plan, even, odd, *([k_pages, v_pages] * PAGES_A_STEP))
 
 
 def project_kernel(x_ref, w_ref, out_ref):
@@ -536,18 +625,23 @@
     step_tokens = step_requests * tree_size
     merge = lambda ours, got: merge_flat(ours, got, heads, size)
 
+    gate_up = up_gate.reshape(width, -1)
     token = None
+    sent_mid = None
     attended_in = []
     for chunk in range(CHUNKS):
         rows = slice(chunk * step_tokens, (chunk + 1) * step_tokens)
         stream_vals = streams[rows].astype(jnp.float32)
         mixed_in = blend(stream_vals, hc_in[0])
-        normed, token = gathered_norm(mixed_in, width, token)
+        normed, token, sent = gathered_norm(mixed_in, width, token)
+        if chunk == 0:
+            normed, k_heads, v_heads, gate_up = lax.optimization_barrier(
+                (normed, k_heads, v_heads, gate_up)
+            )
         attended_in.append(normed)
 
     all_shape = (step_requests, tree_size, heads * size)
-    gate_up = None
-    before_pages = None
+    before_queries = None
     attn_parts, mlp_parts = [], []
     for chunk in range(CHUNKS):
         rows = slice(chunk * step_tokens, (chunk + 1) * step_tokens)
@@ -560,22 +654,20 @@
             ],
             axis=1,
         )
-        if gate_up is None:
-            projected, gate_up = lax.optimization_barrier((projected, up_gate))
-            gate_up = gate_up.reshape(width, -1)
         queries, keys, values = rotate_all(
             projected, cosine[rows], sine[rows], heads, size, 2 * tree_size
         )
         queries, keys, values = (item.reshape(all_shape) for item in (queries, keys, values))
+        if before_queries is not None:
+            queries, before_queries = lax.optimization_barrier((queries, before_queries))
         even, odd = gather_requests(queries)
         plan = page_plan(
             page_owner, page_fill, chunk * step_requests, step_requests, req_local, parts
         )
-        if before_pages is not None:
-            even, odd, before_pages = lax.optimization_barrier((even, odd, before_pages))
         sums, logs = page_attention(even, odd, k_heads, v_heads, plan, heads, size)
+        keys, sums, logs = lax.optimization_barrier((keys, sums, logs))
         tree_pair = tree_attention(queries, keys, values, reach[asked], heads, size)
-        done, before_pages = scatter_requests(
+        done = scatter_requests(
             sums.reshape((parts,) + all_shape),
             logs.reshape(parts, step_requests, 8, LANES),
             merge,
@@ -590,13 +682,18 @@
             ] + [(tree_pair[0][own], tree_pair[1][own])]
             attended.append(merge_partials(pairs, heads, size, with_logs=False)[0])
         attended = jnp.concatenate(attended).reshape(step_tokens, heads * size)
+        before_queries = attended
         attn_delta = scatter_columns(project(attended, out_weight))
+        if sent_mid is not None:
+            attn_delta, sent_mid = lax.optimization_barrier((attn_delta, sent_mid))
         attn_parts.append(attn_delta)
 
         stream_vals = streams[rows].astype(jnp.float32)
         mixed_mid = blend(stream_vals, mid_in) + mid_out * attn_delta
-        normed_mid = gathered_norm(mixed_mid, width)[0]
-        mlp_parts.append(scatter_columns(mlp(normed_mid, gate_up, down_weight)))
+        normed_mid, gathered, sent_mid = gathered_norm(mixed_mid, width)
+        shares = mlp(normed_mid, gate_up, down_weight)
+        first_shares = shares if chunk == 0 else first_shares
+        mlp_parts.append(scatter_columns(shares))
 
     attn_delta = jnp.concatenate(attn_parts)
     mlp_delta = jnp.concatenate(mlp_parts)
@@ -611,9 +708,30 @@
     new_streams = new_streams.astype(jnp.bfloat16)
 
     rows_taken = jnp.arange(req_local, dtype=jnp.int32) * tree_size + accepted_index
+    stream_rows = streams[rows_taken].astype(jnp.float32)
+    is_taken = jnp.arange(tree_size, dtype=jnp.int32)[None, :] == accepted_index[:, None]
+    attn_rows = jnp.concatenate(
+        [
+            jnp.sum(
+                jnp.where(
+                    is_taken[chunk * step_requests : (chunk + 1) * step_requests, :, None],
+                    part.reshape(step_requests, tree_size, feature_local),
+                    0.0,
+                ),
+                axis=1,
+            )
+            for chunk, part in enumerate(attn_parts)
+        ]
+    )
+    mid_rows = blend(stream_rows, mid_in) + mid_out * attn_rows
+    mid_full = jnp.concatenate(list(shift_gather(mid_rows)), axis=1)
+    mid_full, first_shares = lax.optimization_barrier((mid_full, first_shares))
+    mlp_rows = shift_scatter(
+        mlp(layer_norm(mid_full).astype(jnp.bfloat16), gate_up, down_weight)
+    )
     final_local = (
-        jnp.sum(both_out) * attn_delta[rows_taken] + jnp.sum(hc_out[1]) * mlp_delta[rows_taken]
-    ) + blend(stream_vals[rows_taken], jnp.sum(both_mix, axis=1))
+        jnp.sum(both_out) * attn_rows + jnp.sum(hc_out[1]) * mlp_rows
+    ) + blend(stream_rows, jnp.sum(both_mix, axis=1))
     final_full = jnp.concatenate(list(shift_gather(final_local)), axis=1)
     final_norm = layer_norm(final_full)
     own_columns = lax.dynamic_slice_in_dim(
@@ -627,7 +745,7 @@
     )
     drafted = (own_columns[:, None, :] + jax.nn.silu(branch)).astype(jnp.bfloat16)
     draft_full = jnp.concatenate(list(shift_gather(drafted)), axis=2)
-    draft_all = lax.all_gather(draft_full, "req", axis=0, tiled=True)
+    draft_all = gather_small(draft_full)
     logits_local = jnp.dot(
         draft_all.reshape(-1, width), lm_head, preferred_element_type=jnp.float32
     )

time: 574 us -> 506 us (0.88)
  waiting for transfers between devices: 205 us -> 122 us
  other arithmetic: 57 us -> 70.9 us
  starting transfers between devices: 85.3 us -> 93.2 us
  local copies, waits for them, and re-layouts: 84.2 us -> 77.3 us
    all_gather x4, waiting for transfers between devices: 50.6 us -> 1.54 us  [gathered_norm(): gathered = lax.all_gather(sent, 'head', axis=1, tiled=True)]
    reduce_scatter x4, waiting for transfers between devices: 71.1 us -> 31.1 us  [scatter_columns(): lax.psum_scatter(shares, 'head', scatter_dimension=1, tiled=True)]
    all_to_all x1, waiting for transfers between devices: 13 us -> 33.6 us  [on_device(): lax.all_to_all(logits_local.astype(jnp.bfloat16), ('req', 'head'), split_...]
    all_gather x1 -> x0, waiting for transfers between devices: 19.6 us -> none  [on_device(): draft_all = lax.all_gather(draft_full, 'req', axis=0, tiled=True)]
    ppermute x34 -> x37, starting transfers between devices: 47.4 us -> 61.6 us  [swapped(): return lax.ppermute(values, 'req', [(r, r ^ bit) for r in range(count)])]
    pallas_call x2 -> x3, Pallas kernels: 37.4 us -> 49.2 us  [mlp(): pl.pallas_call(functools.partial(mlp_kernel, steps, tile), grid=(steps +...]
    transpose x0 -> x1, local copies, waits for them, and re-layouts: none -> 11.7 us  [on_device(): v_heads = jnp.transpose(v_pages, (0, 2, 1, 3))]
    unnamed x113 -> x130, local copies, waits for them, and re-layouts: 49.8 us -> 39.5 us
  transfers between devices with their start and end apart: 62 -> 70, of which waited for: 26 -> 28; matrix products, arithmetic and copies ran while one was open for 18% -> 24% of each run, Pallas kernels for 17% -> 18%
where the time goes in v4:
time: 506 us; the launch traced here: 502 us
  waiting for transfers between devices  122 us (24%)
  Pallas kernels  98.8 us (20%)
  starting transfers between devices  93.2 us (18%)
  local copies, waits for them, and re-layouts  77.3 us (15%)
  other arithmetic  70.9 us (14%)
  matrix products  23.1 us (5%)
  between operations  17.5 us (3%)
    ppermute x37, starting transfers between devices, swapped(): return lax.ppermute(values, 'req', [(r, r ^ bit) for r in range(count)])  61.6 us
    pallas_call x3, Pallas kernels, mlp(): pl.pallas_call(functools.partial(mlp_kernel, steps, tile), grid=(steps +...  49.2 us
    ppermute x37, waiting for transfers between devices, swapped(): return lax.ppermute(values, 'req', [(r, r ^ bit) for r in range(count)])  42.8 us
    unnamed x130, local copies, waits for them, and re-layouts  39.5 us
    all_to_all x1, waiting for transfers between devices, on_device(): lax.all_to_all(logits_local.astype(jnp.bfloat16), ('req', 'head'), split_...  33.6 us
    reduce_scatter x4, waiting for transfers between devices, scatter_columns(): lax.psum_scatter(shares, 'head', scatter_dimension=1, tiled=True)  31.1 us
    ppermute x21, starting transfers between devices, shift_gather(): lax.ppermute(small, 'head', [(z, (z + step) % count) for z in range(count)])  23.8 us
    pallas_call x10, Pallas kernels, merge_partials(): pl.pallas_call(functools.partial(merge_kernel, heads, size, len(pairs)),...  18.3 us
  transfers between devices with their start and end apart: 70, of which 28 were waited for; matrix products, arithmetic and copies ran while one was open for 24% of the time, Pallas kernels for 18%

profile of v4, /device:TPU:1, one launch (start us, length us, event | category | flops | bytes accessed | tf_op | source)
XLA Modules:
  0.0 502.4 jit_solution(15071708198891463295)
XLA Ops:
  7.2 5.8 %fusion.95 = (bf16[768,4,512]{2,0,1:T(8,128)(2,1)S(1)}, f32[768,4,512]{2,0,1:T(8,128)}) fusion(bf16[768,4,512]{2,1,0:T(4,128)(2,1)} %param.17), kind=kLoop, calls=%fused_computation.370 | loop fusion | flops 1572864 | bytes 12582912 | tf_op args[0]
  18.8 4.2 collective-permute-start.22
  40.9 11.7 %copy_bitcast_fusion = (bf16[48,4,128,128]{3,2,1,0:T(8,128)(2,1)}, bf16[48,4,128,128]{3,2,1,0:T(8,128)(2,1)}) fusion(bf16[48,128,4,128]{3,2,1,0:T(4,128)(2,1)} %param.28, bf16[48,128,4,128]{3,2,1,0:T(4,128)(2,1)} %param.27), kind=kLoop, calls=%fused_computation.4 | loop fusion | bytes 25165824 | tf_op jit(solution)/shard_map/transpose | solution.py:622
  52.6 17.3 %copy.82 = bf16[256,8,2,2048]{3,1,2,0:T(8,128)(2,1)} copy(bf16[256,8,2,2048]{3,2,1,0:T(2,128)(2,1)} %bitcast.302) | data formatting | bytes 33554432
  92.4 4.3 collective-permute-done.7
  96.8 6.8 %collective-permute-start.9 = (bf16[32,48,512]{2,1,0:T(8,128)(2,1)S(1)}, bf16[32,48,512]{2,1,0:T(8,128)(2,1)S(1)}, u32[]{:S(2)}, u32[]{:S(2)}) collective-permute-start(bf16[32,48,512]{2,1,0:T(8,128)(2,1)S(1)} %constant_dynamic-update-slice_fusion.even_ref), channel_id=1, source_target_pairs={{0,4},{4,0},{8,12},{12,8},{16,20},{20,16},{24,28},{28,24},{1,5},{5... | collective-permute-start | bytes 4718600 | tf_op jit(solution)/shard_map/ppermute | solution.py:113
  112.5 8.7 %page_attention.2 = (bf16[64,48,512]{2,1,0:T(8,128)(2,1)S(1)}, f32[64,8,128]{2,1,0:T(8,128)S(1)}) custom-call(s32[48]{0:T(128)S(1)} %get-tuple-element.123.page_ref, s32[48]{0:T(128)S(1)} %get-tuple-element.122.place_ref, s32[48]{0:T(128)S(1)} %get-tuple-element.121.fill_ref, s32[48]{0:T(128)S(1)} %get-tuple-element.325.first_ref, ...), custom_call_target="tpu_custom_call" | custom-call | tf_op jit(solution)/shard_map/page_attention/pallas_call | solution.py:422
  122.7 8.8 %collective-permute-start.10 = (bf16[4,8,48,512]{3,2,1,0:T(8,128)(2,1)}, bf16[4,8,48,512]{3,2,1,0:T(8,128)(2,1)S(1)}, u32[]{:S(2)}, u32[]{:S(2)}) collective-permute-start(bf16[4,8,48,512]{3,2,1,0:T(8,128)(2,1)} %bitcast.19), channel_id=1, source_target_pairs={{0,4},{4,0},{8,12},{12,8},{16,20},{20,16},{24,28},{28,24},{1,5},{5... | collective-permute-start | bytes 4718600 | tf_op jit(solution)/shard_map/ppermute | solution.py:113
  132.2 6.0 %tree_attention.2 = (f32[8,48,512]{2,1,0:T(8,128)S(1)}, f32[8,8,128]{2,1,0:T(8,128)S(1)}) custom-call(bf16[8,48,512]{2,1,0:T(8,128)(2,1)S(1)} %bitcast.259, bf16[8,48,512]{2,1,0:T(8,128)(2,1)S(1)} %bitcast.267, bf16[8,48,512]{2,1,0:T(8,128)(2,1)S(1)} %bitcast.268, f32[8,48,48]{2,1,0:T(8,128)S(1)} %get-tuple-element.197.reach_ref), custom_call_target="tpu_custom_call" | custom-call | tf_op jit(solution)/shard_map/tree_attention/pallas_call | solution.py:239
  147.9 5.2 %merge_partials.10 = (bf16[32,48,512]{2,1,0:T(8,128)(2,1)S(1)}, f32[32,8,128]{2,1,0:T(8,128)S(1)}) custom-call(bf16[32,48,512]{2,1,0:T(8,128)(2,1)S(1)} %get-tuple-element.155.refs_0_, bf16[32,48,512]{2,1,0:T(8,128)(2,1)S(1)} %bitcast.262, f32[32,8,128]{2,1,0:T(8,128)S(1)} %copy-done.13, f32[32,8,128]{2,1,0:T(8,128)} %bitcast.22.refs_3_), custom_call_target="tpu_custom_call" | custom-call | tf_op jit(solution)/shard_map/merge_partials/pallas_call | solution.py:535
  154.8 3.8 collective-permute-start.12
  158.8 5.1 %collective-permute-done.17 = f32[2,4,8,128]{3,2,1,0:T(8,128)S(1)} collective-permute-done((f32[2,4,8,128]{3,2,1,0:T(8,128)S(1)}, f32[2,4,8,128]{3,2,1,0:T(8,128)S(1)}, u32[]{:S(2)}, u32[]{:S(2)}) %collective-permute-start.17) | collective-permute-done | bytes 32800 | tf_op jit(solution)/shard_map/ppermute | solution.py:113
  164.9 4.2 collective-permute-start.18
  185.6 5.1 %collective-permute-done.27 = bf16[4,48,512]{2,1,0:T(8,128)(2,1)S(1)} collective-permute-done((bf16[4,48,512]{2,1,0:T(8,128)(2,1)S(1)}, bf16[4,48,512]{2,1,0:T(8,128)(2,1)S(1)}, u32[]{:S(2)}, u32[]{:S(2)}) %collective-permute-start.27) | collective-permute-done | bytes 196640 | tf_op jit(solution)/shard_map/ppermute | solution.py:113
  200.2 5.7 %page_attention.3 = (bf16[64,48,512]{2,1,0:T(8,128)(2,1)S(1)}, f32[64,8,128]{2,1,0:T(8,128)S(1)}) custom-call(s32[48]{0:T(128)S(1)} %copy-done.23, s32[48]{0:T(128)S(1)} %copy-done.24, s32[48]{0:T(128)S(1)} %copy-done.25, s32[48]{0:T(128)S(1)} %get-tuple-element.327.first_ref, s32[48]{0:T(128)S(1)} %get-tuple-element.326.last_ref, s32[1]{0:T(128)} %bitcast.49.live_ref, ...), custom_call_target="tpu_custom_call" | custom-call | tf_op jit(solution)/shard_map/page_attention/pallas_call | solution.py:422
  209.7 6.0 %tree_attention.3 = (f32[8,48,512]{2,1,0:T(8,128)S(1)}, f32[8,8,128]{2,1,0:T(8,128)S(1)}) custom-call(bf16[8,48,512]{2,1,0:T(8,128)(2,1)S(1)} %bitcast.254, bf16[8,48,512]{2,1,0:T(8,128)(2,1)S(1)} %bitcast.269, bf16[8,48,512]{2,1,0:T(8,128)(2,1)S(1)} %bitcast.270, f32[8,48,48]{2,1,0:T(8,128)S(1)} %copy-done.10), custom_call_target="tpu_custom_call" | custom-call | tf_op jit(solution)/shard_map/tree_attention/pallas_call | solution.py:239
  215.8 5.5 %reduce-scatter.5.cloned.1.call-done = bf16[384,512]{1,0:T(8,128)(2,1)} async-done(((bf16[384,2048]{1,0:T(8,128)(2,1)}), bf16[384,512]{1,0:T(8,128)(2,1)}) %reduce-scatter.5.cloned.1.call-update) | async-done | bytes 393232 | tf_op jit(solution)/shard_map/reduce_scatter | solution.py:108
  221.2 5.4 %multiply_reduce_fusion.1 = (f32[384]{0:T(512)S(1)}, f32[384]{0:T(512)S(1)}, f32[384,512]{1,0:T(8,128)S(1)}) fusion(bf16[384,512]{1,0:T(8,128)(2,1)} %reduce-scatter.5.cloned.1.call-done, f32[]{:T(128)} %multiply_reduce_fusion.7, f32[384,4,512]{2,0,1:T(8,128)} %copy-done.28, f32[]{:T(128)} %bitcast.80, f32[]{:T(128)} %bitcast.79, f32[]{:T(128)} %bitcast.78, ...), kind=kLoop, calls=%fused_computation.70 | loop fusion | flops 2555136 | bytes 4328468 | tf_op jit(solution)/shard_map/reduce_sum | solution.py:84
  229.1 5.4 %merge_partials.15 = (bf16[32,48,512]{2,1,0:T(8,128)(2,1)S(1)}, f32[32,8,128]{2,1,0:T(8,128)S(1)}) custom-call(bf16[32,48,512]{2,1,0:T(8,128)(2,1)S(1)} %copy-done.8, bf16[32,48,512]{2,1,0:T(8,128)(2,1)} %bitcast.52.refs_1_, f32[32,8,128]{2,1,0:T(8,128)S(1)} %get-tuple-element.211.refs_2_, f32[32,8,128]{2,1,0:T(8,128)S(1)} %bitcast.287), custom_call_target="tpu_custom_call" | custom-call | tf_op jit(solution)/shard_map/merge_partials/pallas_call | solution.py:535
  239.8 8.5 %collective-permute-done.37 = f32[2,4,8,128]{3,2,1,0:T(8,128)S(1)} collective-permute-done((f32[2,4,8,128]{3,2,1,0:T(8,128)S(1)}, f32[2,4,8,128]{3,2,1,0:T(8,128)S(1)}, u32[]{:S(2)}, u32[]{:S(2)}) %collective-permute-start.37) | collective-permute-done | bytes 32800 | tf_op jit(solution)/shard_map/ppermute | solution.py:113
  277.3 25.6 %reduce-scatter.7.cloned.1.call-done = bf16[384,512]{1,0:T(8,128)(2,1)} async-done(((bf16[384,2048]{1,0:T(8,128)(2,1)}), bf16[384,512]{1,0:T(8,128)(2,1)}) %reduce-scatter.7.cloned.1.call-update) | async-done | bytes 393232 | tf_op jit(solution)/shard_map/reduce_scatter | solution.py:108
  304.0 4.0 multiply_reduce_fusion
  321.0 18.5 %mlp.3 = bf16[384,2048]{1,0:T(8,128)(2,1)} custom-call(bf16[384,2048]{1,0:T(8,128)(2,1)S(1)} %pad_maximum_fusion.5.x_ref, bf16[2048,4096]{1,0:T(8,128)(2,1)} %bitcast.296, bf16[2048,4096]{1,0:T(8,128)(2,1)} %bitcast.297, bf16[2048,2048]{1,0:T(8,128)(2,1)S(1)} %copy-done.2), custom_call_target="tpu_custom_call" | custom-call | tf_op jit(solution)/shard_map/mlp/pallas_call | solution.py:483
  343.3 12.2 %mlp.5 = bf16[16,2048]{1,0:T(8,128)(2,1)S(1)} custom-call(bf16[16,2048]{1,0:T(8,128)(2,1)S(1)} %multiply_convert_fusion.16.x_ref, bf16[2048,4096]{1,0:T(8,128)(2,1)} %bitcast.298, bf16[2048,4096]{1,0:T(8,128)(2,1)} %bitcast.299, bf16[2048,2048]{1,0:T(8,128)(2,1)S(1)} %copy-done.3), custom_call_target="tpu_custom_call" | custom-call | tf_op jit(solution)/shard_map/mlp/pallas_call | solution.py:483
  390.9 4.3 collective-permute-done.59
  395.3 10.2 %collective-permute-start.60 = (bf16[4,16,2,2048]{3,1,2,0:T(8,128)(2,1)S(1)}, bf16[4,16,2,2048]{3,1,2,0:T(8,128)(2,1)S(1)}, u32[]{:S(2)}, u32[]{:S(2)}) collective-permute-start(bf16[4,16,2,2048]{3,1,2,0:T(8,128)(2,1)S(1)} %pad_maximum_fusion.8), channel_id=1, source_target_pairs={{0,4},{4,0},{8,12},{12,8},{16,20},{20,16},{24,28},{28,24},{1,5},{5... | collective-permute-start | bytes 1572872 | tf_op jit(solution)/shard_map/ppermute | solution.py:113
  410.9 18.4 %mlp.4 = bf16[384,2048]{1,0:T(8,128)(2,1)} custom-call(bf16[384,2048]{1,0:T(8,128)(2,1)S(1)} %pad_maximum_fusion.6.x_ref, bf16[2048,4096]{1,0:T(8,128)(2,1)} %bitcast.300, bf16[2048,4096]{1,0:T(8,128)(2,1)} %bitcast.301, bf16[2048,2048]{1,0:T(8,128)(2,1)S(1)} %copy-done.4), custom_call_target="tpu_custom_call" | custom-call | tf_op jit(solution)/shard_map/mlp/pallas_call | solution.py:483
  430.2 4.1 fusion.2
  436.5 3.8 all-to-all-start
  440.4 5.3 %slice_bitcast_fusion.3 = (f32[768,512]{1,0:T(8,128)S(1)}, f32[768,512]{1,0:T(8,128)}, f32[768,512]{1,0:T(8,128)}, f32[768,512]{1,0:T(8,128)}) fusion(f32[768,4,512]{2,0,1:T(8,128)} %get-tuple-element.159), kind=kLoop, calls=%fused_computation.32 | loop fusion | bytes 12582912 | tf_op jit(solution)/shard_map/mul | solution.py:706
  446.9 33.6 %all-to-all-done = bf16[128,2,1572]{2,1,0:T(2,128)(2,1)S(1)} async-done(((bf16[128,2,1572]{2,1,0:T(2,128)(2,1)}), bf16[128,2,1572]{2,1,0:T(2,128)(2,1)S(1)}, u32[]{:S(2)}, u32[]{:S(2)}) %all-to-all-start) | async-done | bytes 804896 | tf_op jit(solution)/shard_map/all_to_all | solution.py:753
  486.3 9.1 %add_convert_fusion = bf16[768,4,512]{2,1,0:T(4,128)(2,1)} fusion(f32[768,512]{1,0:T(8,128)S(1)} %copy-done.35, f32[4]{0:T(128)S(1)} %get-tuple-element.304, f32[768,512]{1,0:T(8,128)} %get-tuple-element.150, f32[4]{0:T(128)S(1)} %get-tuple-element.305, f32[768,512]{1,0:T(8,128)} %get-tuple-element.151, f32[4]{0:T(128)S(1)} %get-tuple-element.306, ...), kind=kLoop, calls=%fused_computation.6 | loop fusion | flops 18874368 | bytes 12583008 | tf_op jit(solution)/shard_map/convert_element_type | solution.py:708
  (470 shorter events, 202.4 us)
Async XLA Ops:
  7.2 63.0 %all-gather.5.cloned.1.call-start = ((), (), s32[]{:S(2)}) async-start(), calls=%async_computation.5 | async-start | bytes 1966080 | tf_op jit(solution)/shard_map/all_gather | solution.py:90
  18.8 90.0 %collective-permute-start.22 = (f32[2,384]{1,0:T(2,128)}, f32[2,384]{1,0:T(2,128)S(1)}, u32[]{:S(2)}, u32[]{:S(2)}) collective-permute-start(f32[2,384]{1,0:T(2,128)} %get-tuple-element.280), channel_id=1, source_target_pairs={{0,3},{1,0},{2,1},{3,2},{4,7},{5,4},{6,5},{7,6},{8,11},{9,8},{10,9... | collective-permute-start | bytes 9224 | tf_op jit(solution)/shard_map/ppermute | solution.py:55
  22.9 85.2 %collective-permute-start.21 = (f32[2,384]{1,0:T(2,128)}, f32[2,384]{1,0:T(2,128)S(1)}, u32[]{:S(2)}, u32[]{:S(2)}) collective-permute-start(f32[2,384]{1,0:T(2,128)} %get-tuple-element.280), channel_id=1, source_target_pairs={{0,2},{1,3},{2,0},{3,1},{4,6},{5,7},{6,4},{7,5},{8,10},{9,11},{10,... | collective-permute-start | bytes 9224 | tf_op jit(solution)/shard_map/ppermute | solution.py:55
  23.1 46.9 %collective-permute-start.2 = (f32[2,384]{1,0:T(2,128)S(1)}, f32[2,384]{1,0:T(2,128)S(1)}, u32[]{:S(2)}, u32[]{:S(2)}) collective-permute-start(f32[2,384]{1,0:T(2,128)S(1)} %get-tuple-element.278), channel_id=1, source_target_pairs={{0,3},{1,0},{2,1},{3,2},{4,7},{5,4},{6,5},{7,6},{8,11},{9,8},{10,9... | collective-permute-start | bytes 9224 | tf_op jit(solution)/shard_map/ppermute | solution.py:55
  23.3 46.6 %collective-permute-start.1 = (f32[2,384]{1,0:T(2,128)S(1)}, f32[2,384]{1,0:T(2,128)S(1)}, u32[]{:S(2)}, u32[]{:S(2)}) collective-permute-start(f32[2,384]{1,0:T(2,128)S(1)} %get-tuple-element.278), channel_id=1, source_target_pairs={{0,2},{1,3},{2,0},{3,1},{4,6},{5,7},{6,4},{7,5},{8,10},{9,11},{10,... | collective-permute-start | bytes 9224 | tf_op jit(solution)/shard_map/ppermute | solution.py:55
  25.6 44.3 %collective-permute-start = (f32[2,384]{1,0:T(2,128)S(1)}, f32[2,384]{1,0:T(2,128)S(1)}, u32[]{:S(2)}, u32[]{:S(2)}) collective-permute-start(f32[2,384]{1,0:T(2,128)S(1)} %get-tuple-element.278), channel_id=1, source_target_pairs={{0,1},{1,2},{2,3},{3,0},{4,5},{5,6},{6,7},{7,4},{8,9},{9,10},{10,1... | collective-permute-start | bytes 9224 | tf_op jit(solution)/shard_map/ppermute | solution.py:55
  27.9 113.3 %all-gather.7.cloned.1.call-start = ((), (), s32[]{:S(2)}) async-start(), calls=%async_computation.7 | async-start | bytes 1966080 | tf_op jit(solution)/shard_map/all_gather | solution.py:90
  90.3 17.8 %collective-permute-start.20 = (f32[2,384]{1,0:T(2,128)}, f32[2,384]{1,0:T(2,128)}, u32[]{:S(2)}, u32[]{:S(2)}) collective-permute-start(f32[2,384]{1,0:T(2,128)} %get-tuple-element.280), channel_id=1, source_target_pairs={{0,1},{1,2},{2,3},{3,0},{4,5},{5,6},{6,7},{7,4},{8,9},{9,10},{10,1... | collective-permute-start | bytes 9224 | tf_op jit(solution)/shard_map/ppermute | solution.py:55
  96.8 12.8 %collective-permute-start.9 = (bf16[32,48,512]{2,1,0:T(8,128)(2,1)S(1)}, bf16[32,48,512]{2,1,0:T(8,128)(2,1)S(1)}, u32[]{:S(2)}, u32[]{:S(2)}) collective-permute-start(bf16[32,48,512]{2,1,0:T(8,128)(2,1)S(1)} %constant_dynamic-update-slice_fusion.even_ref), channel_id=1, source_target_pairs={{0,4},{4,0},{8,12},{12,8},{16,20},{20,16},{24,28},{28,24},{1,5},{5... | collective-permute-start | bytes 4718600 | tf_op jit(solution)/shard_map/ppermute | solution.py:113
  104.4 116.8 %reduce-scatter.5.cloned.1.call-start = ((), (), s32[]{:S(2)}) async-start(), calls=%async_computation.6 | async-start | bytes 1966080 | tf_op jit(solution)/shard_map/reduce_scatter | solution.py:108
  122.7 25.2 %collective-permute-start.10 = (bf16[4,8,48,512]{3,2,1,0:T(8,128)(2,1)}, bf16[4,8,48,512]{3,2,1,0:T(8,128)(2,1)S(1)}, u32[]{:S(2)}, u32[]{:S(2)}) collective-permute-start(bf16[4,8,48,512]{3,2,1,0:T(8,128)(2,1)} %bitcast.19), channel_id=1, source_target_pairs={{0,4},{4,0},{8,12},{12,8},{16,20},{20,16},{24,28},{28,24},{1,5},{5... | collective-permute-start | bytes 4718600 | tf_op jit(solution)/shard_map/ppermute | solution.py:113
  132.2 15.6 %collective-permute-start.11 = (f32[4,8,8,128]{3,2,1,0:T(8,128)}, f32[4,8,8,128]{3,2,1,0:T(8,128)}, u32[]{:S(2)}, u32[]{:S(2)}) collective-permute-start(f32[4,8,8,128]{3,2,1,0:T(8,128)} %bitcast.21), channel_id=1, source_target_pairs={{0,4},{4,0},{8,12},{12,8},{16,20},{20,16},{24,28},{28,24},{1,5},{5... | collective-permute-start | bytes 393224 | tf_op jit(solution)/shard_map/ppermute | solution.py:113
  153.2 10.6 %collective-permute-start.16 = (bf16[2,4,48,512]{3,2,1,0:T(8,128)(2,1)S(1)}, bf16[2,4,48,512]{3,2,1,0:T(8,128)(2,1)S(1)}, u32[]{:S(2)}, u32[]{:S(2)}) collective-permute-start(bf16[2,4,48,512]{3,2,1,0:T(8,128)(2,1)S(1)} %get-tuple-element.186), channel_id=1, source_target_pairs={{0,16},{4,20},{8,24},{12,28},{16,0},{20,4},{24,8},{28,12},{1,17},{... | collective-permute-start | bytes 1179656 | tf_op jit(solution)/shard_map/ppermute | solution.py:113
  154.5 9.3 %collective-permute-start.17 = (f32[2,4,8,128]{3,2,1,0:T(8,128)S(1)}, f32[2,4,8,128]{3,2,1,0:T(8,128)S(1)}, u32[]{:S(2)}, u32[]{:S(2)}) collective-permute-start(f32[2,4,8,128]{3,2,1,0:T(8,128)S(1)} %get-tuple-element.236), channel_id=1, source_target_pairs={{0,16},{4,20},{8,24},{12,28},{16,0},{20,4},{24,8},{28,12},{1,17},{... | collective-permute-start | bytes 98312 | tf_op jit(solution)/shard_map/ppermute | solution.py:113
  154.8 14.4 %collective-permute-start.12 = (bf16[2,4,48,512]{3,2,1,0:T(8,128)(2,1)S(1)}, bf16[2,4,48,512]{3,2,1,0:T(8,128)(2,1)S(1)}, u32[]{:S(2)}, u32[]{:S(2)}) collective-permute-start(bf16[2,4,48,512]{3,2,1,0:T(8,128)(2,1)S(1)} %pad_maximum_fusion.10), channel_id=1, source_target_pairs={{0,8},{4,12},{8,0},{12,4},{16,24},{20,28},{24,16},{28,20},{1,9},{5... | collective-permute-start | bytes 1179656 | tf_op jit(solution)/shard_map/ppermute | solution.py:113
  158.6 10.6 %collective-permute-start.13 = (f32[2,4,8,128]{3,2,1,0:T(8,128)S(1)}, f32[2,4,8,128]{3,2,1,0:T(8,128)S(1)}, u32[]{:S(2)}, u32[]{:S(2)}) collective-permute-start(f32[2,4,8,128]{3,2,1,0:T(8,128)S(1)} %pad_maximum_fusion.24), channel_id=1, source_target_pairs={{0,8},{4,12},{8,0},{12,4},{16,24},{20,28},{24,16},{28,20},{1,9},{5... | collective-permute-start | bytes 98312 | tf_op jit(solution)/shard_map/ppermute | solution.py:113
  183.1 91.1 %all-gather.9.cloned.1.call-start = ((), (), s32[]{:S(2)}) async-start(), calls=%async_computation.9 | async-start | bytes 1966080 | tf_op jit(solution)/shard_map/all_gather | solution.py:90
  207.8 19.9 %collective-permute-start.30 = (bf16[4,8,48,512]{3,2,1,0:T(8,128)(2,1)}, bf16[4,8,48,512]{3,2,1,0:T(8,128)(2,1)}, u32[]{:S(2)}, u32[]{:S(2)}) collective-permute-start(bf16[4,8,48,512]{3,2,1,0:T(8,128)(2,1)} %bitcast.51), channel_id=1, source_target_pairs={{0,4},{4,0},{8,12},{12,8},{16,20},{20,16},{24,28},{28,24},{1,5},{5... | collective-permute-start | bytes 4718600 | tf_op jit(solution)/shard_map/ppermute | solution.py:113
  209.5 18.1 %collective-permute-start.31 = (f32[4,8,8,128]{3,2,1,0:T(8,128)S(1)}, f32[4,8,8,128]{3,2,1,0:T(8,128)S(1)}, u32[]{:S(2)}, u32[]{:S(2)}) collective-permute-start(f32[4,8,8,128]{3,2,1,0:T(8,128)S(1)} %bitcast.316), channel_id=1, source_target_pairs={{0,4},{4,0},{8,12},{12,8},{16,20},{20,16},{24,28},{28,24},{1,5},{5... | collective-permute-start | bytes 393224 | tf_op jit(solution)/shard_map/ppermute | solution.py:113
  227.6 75.2 %reduce-scatter.7.cloned.1.call-start = ((), (), s32[]{:S(2)}) async-start(), calls=%async_computation.8 | async-start | bytes 1966080 | tf_op jit(solution)/shard_map/reduce_scatter | solution.py:108
  234.6 13.6 %collective-permute-start.36 = (bf16[2,4,48,512]{3,2,1,0:T(8,128)(2,1)S(1)}, bf16[2,4,48,512]{3,2,1,0:T(8,128)(2,1)S(1)}, u32[]{:S(2)}, u32[]{:S(2)}) collective-permute-start(bf16[2,4,48,512]{3,2,1,0:T(8,128)(2,1)S(1)} %get-tuple-element.180), channel_id=1, source_target_pairs={{0,16},{4,20},{8,24},{12,28},{16,0},{20,4},{24,8},{28,12},{1,17},{... | collective-permute-start | bytes 1179656 | tf_op jit(solution)/shard_map/ppermute | solution.py:113
  238.0 10.3 %collective-permute-start.37 = (f32[2,4,8,128]{3,2,1,0:T(8,128)S(1)}, f32[2,4,8,128]{3,2,1,0:T(8,128)S(1)}, u32[]{:S(2)}, u32[]{:S(2)}) collective-permute-start(f32[2,4,8,128]{3,2,1,0:T(8,128)S(1)} %get-tuple-element.230), channel_id=1, source_target_pairs={{0,16},{4,20},{8,24},{12,28},{16,0},{20,4},{24,8},{28,12},{1,17},{... | collective-permute-start | bytes 98312 | tf_op jit(solution)/shard_map/ppermute | solution.py:113
  238.2 12.7 %collective-permute-start.32 = (bf16[2,4,48,512]{3,2,1,0:T(8,128)(2,1)S(1)}, bf16[2,4,48,512]{3,2,1,0:T(8,128)(2,1)S(1)}, u32[]{:S(2)}, u32[]{:S(2)}) collective-permute-start(bf16[2,4,48,512]{3,2,1,0:T(8,128)(2,1)S(1)} %pad_maximum_fusion.13), channel_id=1, source_target_pairs={{0,8},{4,12},{8,0},{12,4},{16,24},{20,28},{24,16},{28,20},{1,9},{5... | collective-permute-start | bytes 1179656 | tf_op jit(solution)/shard_map/ppermute | solution.py:113
  238.3 12.6 %collective-permute-start.33 = (f32[2,4,8,128]{3,2,1,0:T(8,128)S(1)}, f32[2,4,8,128]{3,2,1,0:T(8,128)S(1)}, u32[]{:S(2)}, u32[]{:S(2)}) collective-permute-start(f32[2,4,8,128]{3,2,1,0:T(8,128)S(1)} %pad_maximum_fusion.26), channel_id=1, source_target_pairs={{0,8},{4,12},{8,0},{12,4},{16,24},{20,28},{24,16},{28,20},{1,9},{5... | collective-permute-start | bytes 98312 | tf_op jit(solution)/shard_map/ppermute | solution.py:113
  261.7 143.7 %all-gather.11.cloned.1.call-start = ((), (), s32[]{:S(2)}) async-start(), calls=%async_computation.11 | async-start | bytes 1966080 | tf_op jit(solution)/shard_map/all_gather | solution.py:90
  309.5 175.2 %reduce-scatter.9.cloned.1.call-start = ((), (), s32[]{:S(2)}) async-start(), calls=%async_computation.10 | async-start | bytes 1966080 | tf_op jit(solution)/shard_map/reduce_scatter | solution.py:108
  314.4 25.1 %collective-permute-start.48 = (f32[16,512]{1,0:T(8,128)S(1)}, f32[16,512]{1,0:T(8,128)S(1)}, u32[]{:S(2)}, u32[]{:S(2)}) collective-permute-start(f32[16,512]{1,0:T(8,128)S(1)} %bitcast_add_fusion.3), channel_id=1, source_target_pairs={{0,3},{1,0},{2,1},{3,2},{4,7},{5,4},{6,5},{7,6},{8,11},{9,8},{10,9... | collective-permute-start | bytes 98312 | tf_op jit(solution)/shard_map/ppermute | solution.py:55
  315.7 23.9 %collective-permute-start.47 = (f32[16,512]{1,0:T(8,128)S(1)}, f32[16,512]{1,0:T(8,128)S(1)}, u32[]{:S(2)}, u32[]{:S(2)}) collective-permute-start(f32[16,512]{1,0:T(8,128)S(1)} %bitcast_add_fusion.3), channel_id=1, source_target_pairs={{0,2},{1,3},{2,0},{3,1},{4,6},{5,7},{6,4},{7,5},{8,10},{9,11},{10,... | collective-permute-start | bytes 98312 | tf_op jit(solution)/shard_map/ppermute | solution.py:55
  315.9 23.7 %collective-permute-start.46 = (f32[16,512]{1,0:T(8,128)S(1)}, f32[16,512]{1,0:T(8,128)S(1)}, u32[]{:S(2)}, u32[]{:S(2)}) collective-permute-start(f32[16,512]{1,0:T(8,128)S(1)} %bitcast_add_fusion.3), channel_id=1, source_target_pairs={{0,1},{1,2},{2,3},{3,0},{4,5},{5,6},{6,7},{7,4},{8,9},{9,10},{10,1... | collective-permute-start | bytes 98312 | tf_op jit(solution)/shard_map/ppermute | solution.py:55
  373.0 111.7 %reduce-scatter.11.cloned.1.call-start = ((), (), s32[]{:S(2)}) async-start(), calls=%async_computation.12 | async-start | bytes 1966080 | tf_op jit(solution)/shard_map/reduce_scatter | solution.py:108
  395.3 34.1 %collective-permute-start.60 = (bf16[4,16,2,2048]{3,1,2,0:T(8,128)(2,1)S(1)}, bf16[4,16,2,2048]{3,1,2,0:T(8,128)(2,1)S(1)}, u32[]{:S(2)}, u32[]{:S(2)}) collective-permute-start(bf16[4,16,2,2048]{3,1,2,0:T(8,128)(2,1)S(1)} %pad_maximum_fusion.8), channel_id=1, source_target_pairs={{0,4},{4,0},{8,12},{12,8},{16,20},{20,16},{24,28},{28,24},{1,5},{5... | collective-permute-start | bytes 1572872 | tf_op jit(solution)/shard_map/ppermute | solution.py:113
  436.5 44.1 %all-to-all-start = ((bf16[128,2,1572]{2,1,0:T(2,128)(2,1)}), bf16[128,2,1572]{2,1,0:T(2,128)(2,1)S(1)}, u32[]{:S(2)}, u32[]{:S(2)}) async-start(bf16[128,2,1572]{2,1,0:T(2,128)(2,1)} %copy.78), calls=%async_computation.4 | async-start | bytes 1703936 | tf_op jit(solution)/shard_map/all_to_all | solution.py:753
  (96 other events, 575.0 us)
Sparse Core Ops, SparseCore 0:
  28.0 37.8 all-gather.4
  104.6 36.5 all-gather.6
  183.2 37.9 reduce-scatter.4
  227.7 38.1 all-gather.8
  268.7 34.1 reduce-scatter.6
  309.6 37.8 all-gather.10
  373.1 40.1 reduce-scatter.8
  429.5 47.3 reduce-scatter.10

commit v5 on v4

--- a/solution.py
+++ b/solution.py
@@ -14,7 +14,7 @@
 CHUNKS = 2
 LANES = 128
 PAGES_A_STEP = 2
-VMEM_BYTES = 40 * 1024 * 1024
+VMEM_BYTES = 56 * 1024 * 1024
 
 
 def params(count=1):
@@ -154,7 +154,7 @@
     state = []
     mine = [sums[:far], logs[:far]]
     theirs = [swapped(sums[far:], near), swapped(logs[far:], near)]
-    merged = merge(mine, theirs)
+    merged = first_merged = merge(mine, theirs)
     half = sums.shape[1] // 2
     done = []
     for part, order in enumerate(orders):
@@ -169,7 +169,7 @@
             places = [places[at] for at in stay]
             kept = merge(ours, got) if place < len(order) - 1 else (ours, got)
         done.append(kept)
-    return done
+    return done, first_merged[1]
 
 
 def rotate_kernel(heads, size, scale, x_ref, cos_ref, sin_ref, q_ref, k_ref, v_ref):
@@ -475,9 +475,9 @@
 def mlp(values, gate_up, down):
     rows, width = values.shape
     hidden, columns = down.shape
-    tile = min(hidden, 256)
+    tile = min(hidden, 512)
     steps = hidden // tile
-    out_tile = min(columns, 256)
+    out_tile = min(columns, 512)
     late = lambda i: jnp.maximum(i - steps, 0)
     early = lambda i: jnp.minimum(i, steps - 1)
     return pl.pallas_call(
@@ -627,7 +627,8 @@
 
     gate_up = up_gate.reshape(width, -1)
     token = None
-    sent_mid = None
+    first_shares = None
+    before_normed = None
     attended_in = []
     for chunk in range(CHUNKS):
         rows = slice(chunk * step_tokens, (chunk + 1) * step_tokens)
@@ -647,6 +648,8 @@
         rows = slice(chunk * step_tokens, (chunk + 1) * step_tokens)
         asked = slice(chunk * step_requests, (chunk + 1) * step_requests)
         normed = attended_in[chunk]
+        if before_normed is not None:
+            normed, before_normed = lax.optimization_barrier((normed, before_normed))
         projected = jnp.concatenate(
             [
                 jnp.dot(normed, qkv_weight[:, third], preferred_element_type=jnp.float32)
@@ -667,7 +670,7 @@
         sums, logs = page_attention(even, odd, k_heads, v_heads, plan, heads, size)
         keys, sums, logs = lax.optimization_barrier((keys, sums, logs))
         tree_pair = tree_attention(queries, keys, values, reach[asked], heads, size)
-        done = scatter_requests(
+        done, before_normed = scatter_requests(
             sums.reshape((parts,) + all_shape),
             logs.reshape(parts, step_requests, 8, LANES),
             merge,
@@ -684,16 +687,20 @@
         attended = jnp.concatenate(attended).reshape(step_tokens, heads * size)
         before_queries = attended
         attn_delta = scatter_columns(project(attended, out_weight))
-        if sent_mid is not None:
-            attn_delta, sent_mid = lax.optimization_barrier((attn_delta, sent_mid))
+        if first_shares is not None:
+            attn_delta, first_shares = lax.optimization_barrier((attn_delta, first_shares))
         attn_parts.append(attn_delta)
 
         stream_vals = streams[rows].astype(jnp.float32)
         mixed_mid = blend(stream_vals, mid_in) + mid_out * attn_delta
         normed_mid, gathered, sent_mid = gathered_norm(mixed_mid, width)
         shares = mlp(normed_mid, gate_up, down_weight)
-        first_shares = shares if chunk == 0 else first_shares
-        mlp_parts.append(scatter_columns(shares))
+        if first_shares is None:
+            first_shares = shares
+        else:
+            first_shares, sent_mid = lax.optimization_barrier((first_shares, sent_mid))
+            mlp_parts.append(scatter_columns(first_shares))
+            mlp_parts.append(scatter_columns(shares))
 
     attn_delta = jnp.concatenate(attn_parts)
     mlp_delta = jnp.concatenate(mlp_parts)

time: 506 us -> 557 us (1.10)
  waiting for transfers between devices: 122 us -> 74.6 us
  Pallas kernels: 98.8 us -> 144 us
  local copies, waits for them, and re-layouts: 77.3 us -> 106 us
  other arithmetic: 70.9 us -> 95.2 us
    reduce_scatter x4, waiting for transfers between devices: 31.1 us -> 0.03 us  [scatter_columns(): lax.psum_scatter(shares, 'head', scatter_dimension=1, tiled=True)]
    ppermute x37, waiting for transfers between devices: 42.8 us -> 24.8 us  [swapped(): return lax.ppermute(values, 'req', [(r, r ^ bit) for r in range(count)])]
    pallas_call x10, Pallas kernels: 18.3 us -> 35.8 us  [merge_partials(): pl.pallas_call(functools.partial(merge_kernel, heads, size, len(pairs)),...]
    slice x12, local copies, waits for them, and re-layouts: 0.27 us -> 12.4 us  [scatter_requests(): value[at:at + 1]]
    pallas_call x2, Pallas kernels: 14.4 us -> 26.5 us  [page_attention(): pl.pallas_call(functools.partial(page_kernel, heads, size), grid_spec=gri...]
    pallas_call x2, Pallas kernels: 1.49 us -> 7.93 us  [rotate_all(): pl.pallas_call(functools.partial(rotate_kernel, heads, size, size ** (-0....]
    unnamed x130 -> x116, local copies, waits for them, and re-layouts: 39.5 us -> 36.2 us
  transfers between devices with their start and end apart: 70 -> 70, of which waited for: 28 -> 24; matrix products, arithmetic and copies ran while one was open for 24% -> 32% of each run, Pallas kernels for 18% -> 24%
where the time goes in v5:
time: 557 us; the launch traced here: 551 us
  Pallas kernels  144 us (26%)
  local copies, waits for them, and re-layouts  106 us (19%)
  other arithmetic  95.2 us (17%)
  starting transfers between devices  88.9 us (16%)
  waiting for transfers between devices  74.6 us (13%)
  matrix products  25.7 us (5%)
  between operations  16.8 us (3%)
    ppermute x37, starting transfers between devices, swapped(): return lax.ppermute(values, 'req', [(r, r ^ bit) for r in range(count)])  59.4 us
    pallas_call x3, Pallas kernels, mlp(): pl.pallas_call(functools.partial(mlp_kernel, steps, tile), grid=(steps +...  49.2 us
    unnamed x116, local copies, waits for them, and re-layouts  36.2 us
    pallas_call x10, Pallas kernels, merge_partials(): pl.pallas_call(functools.partial(merge_kernel, heads, size, len(pairs)),...  35.8 us
    all_to_all x1, waiting for transfers between devices, on_device(): lax.all_to_all(logits_local.astype(jnp.bfloat16), ('req', 'head'), split_...  33.7 us
    pallas_call x2, Pallas kernels, page_attention(): pl.pallas_call(functools.partial(page_kernel, heads, size), grid_spec=gri...  26.5 us
    ppermute x37, waiting for transfers between devices, swapped(): return lax.ppermute(values, 'req', [(r, r ^ bit) for r in range(count)])  24.8 us
    ppermute x21, starting transfers between devices, shift_gather(): lax.ppermute(small, 'head', [(z, (z + step) % count) for z in range(count)])  23.4 us
  transfers between devices with their start and end apart: 70, of which 24 were waited for; matrix products, arithmetic and copies ran while one was open for 32% of the time, Pallas kernels for 24%

profile of v5, /device:TPU:1, one launch (start us, length us, event | category | flops | bytes accessed | tf_op | source)
XLA Modules:
  0.0 550.7 jit_solution(10235225822503887454)
XLA Ops:
  7.2 5.8 %fusion.95 = (bf16[768,4,512]{2,0,1:T(8,128)(2,1)S(1)}, f32[768,4,512]{2,0,1:T(8,128)}) fusion(bf16[768,4,512]{2,1,0:T(4,128)(2,1)} %param.17), kind=kLoop, calls=%fused_computation.370 | loop fusion | flops 1572864 | bytes 12582912 | tf_op args[0]
  14.7 4.2 fusion.24
  20.8 4.2 collective-permute-start.22
  48.6 11.8 %copy_bitcast_fusion = (bf16[48,4,128,128]{3,2,1,0:T(8,128)(2,1)}, bf16[48,4,128,128]{3,2,1,0:T(8,128)(2,1)}) fusion(bf16[48,128,4,128]{3,2,1,0:T(4,128)(2,1)} %param.28, bf16[48,128,4,128]{3,2,1,0:T(4,128)(2,1)} %param.27), kind=kLoop, calls=%fused_computation.4 | loop fusion | bytes 25165824 | tf_op jit(solution)/shard_map/transpose | solution.py:622
  60.3 17.3 %copy.82 = bf16[256,8,2,2048]{3,1,2,0:T(8,128)(2,1)} copy(bf16[256,8,2,2048]{3,2,1,0:T(2,128)(2,1)} %bitcast.261) | data formatting | bytes 33554432
  92.4 4.0 rotate.2
  115.7 5.5 %collective-permute-start.9 = (bf16[32,48,512]{2,1,0:T(8,128)(2,1)}, bf16[32,48,512]{2,1,0:T(8,128)(2,1)}, u32[]{:S(2)}, u32[]{:S(2)}) collective-permute-start(bf16[32,48,512]{2,1,0:T(8,128)(2,1)} %constant_dynamic-update-slice_fusion.even_ref), channel_id=1, source_target_pairs={{0,4},{4,0},{8,12},{12,8},{16,20},{20,16},{24,28},{28,24},{1,5},{5... | collective-permute-start | bytes 4718600 | tf_op jit(solution)/shard_map/ppermute | solution.py:113
  127.6 16.9 %page_attention.2 = (bf16[64,48,512]{2,1,0:T(8,128)(2,1)}, f32[64,8,128]{2,1,0:T(8,128)}) custom-call(s32[48]{0:T(128)} %get-tuple-element.133.page_ref, s32[48]{0:T(128)} %copy-done.40, s32[48]{0:T(128)} %get-tuple-element.135.fill_ref, s32[48]{0:T(128)} %get-tuple-element.333.first_ref, s32[48]{0:T(128)} %get-tuple-element.332.last_ref, ...), custom_call_target="tpu_custom_call" | custom-call | tf_op jit(solution)/shard_map/page_attention/pallas_call | solution.py:422
  144.5 3.9 fusion.94
  149.6 7.8 %tree_attention.2 = (f32[8,48,512]{2,1,0:T(8,128)}, f32[8,8,128]{2,1,0:T(8,128)}) custom-call(bf16[8,48,512]{2,1,0:T(8,128)(2,1)} %bitcast.272, bf16[8,48,512]{2,1,0:T(8,128)(2,1)} %bitcast.286, bf16[8,48,512]{2,1,0:T(8,128)(2,1)} %bitcast.287, f32[8,48,48]{2,1,0:T(8,128)} %get-tuple-element.203.reach_ref), custom_call_target="tpu_custom_call" | custom-call | tf_op jit(solution)/shard_map/tree_attention/pallas_call | solution.py:239
  163.4 6.5 %merge_partials.10 = (bf16[32,48,512]{2,1,0:T(8,128)(2,1)}, f32[32,8,128]{2,1,0:T(8,128)}) custom-call(bf16[32,48,512]{2,1,0:T(8,128)(2,1)} %get-tuple-element.161.refs_0_, bf16[32,48,512]{2,1,0:T(8,128)(2,1)} %bitcast.20.refs_1_, f32[32,8,128]{2,1,0:T(8,128)} %get-tuple-element.219.refs_2_, f32[32,8,128]{2,1,0:T(8,128)} %bitcast.312), custom_call_target="tpu_custom_call" | custom-call | tf_op jit(solution)/shard_map/merge_partials/pallas_call | solution.py:535
  176.7 5.3 collective-permute-start.16
  182.2 3.7 collective-permute-start.12
  213.0 4.0 rotate.3
  229.3 4.5 project.2
  248.2 9.5 %page_attention.3 = (bf16[64,48,512]{2,1,0:T(8,128)(2,1)}, f32[64,8,128]{2,1,0:T(8,128)}) custom-call(s32[48]{0:T(128)} %get-tuple-element.129.page_ref, s32[48]{0:T(128)} %copy-done.39, s32[48]{0:T(128)} %get-tuple-element.127.fill_ref, s32[48]{0:T(128)} %get-tuple-element.331.first_ref, s32[48]{0:T(128)} %get-tuple-element.330.last_ref, ...), custom_call_target="tpu_custom_call" | custom-call | tf_op jit(solution)/shard_map/page_attention/pallas_call | solution.py:422
  257.7 3.8 fusion.93
  265.9 7.8 %tree_attention.3 = (f32[8,48,512]{2,1,0:T(8,128)}, f32[8,8,128]{2,1,0:T(8,128)}) custom-call(bf16[8,48,512]{2,1,0:T(8,128)(2,1)} %bitcast.264, bf16[8,48,512]{2,1,0:T(8,128)(2,1)} %bitcast.288, bf16[8,48,512]{2,1,0:T(8,128)(2,1)} %bitcast.289, f32[8,48,48]{2,1,0:T(8,128)} %get-tuple-element.202.reach_ref), custom_call_target="tpu_custom_call" | custom-call | tf_op jit(solution)/shard_map/tree_attention/pallas_call | solution.py:239
  275.8 5.4 multiply_reduce_fusion.1
  282.9 6.5 %merge_partials.15 = (bf16[32,48,512]{2,1,0:T(8,128)(2,1)}, f32[32,8,128]{2,1,0:T(8,128)}) custom-call(bf16[32,48,512]{2,1,0:T(8,128)(2,1)} %get-tuple-element.159.refs_0_, bf16[32,48,512]{2,1,0:T(8,128)(2,1)} %bitcast.52.refs_1_, f32[32,8,128]{2,1,0:T(8,128)} %get-tuple-element.217.refs_2_, f32[32,8,128]{2,1,0:T(8,128)} %bitcast.313), custom_call_target="tpu_custom_call" | custom-call | tf_op jit(solution)/shard_map/merge_partials/pallas_call | solution.py:535
  299.5 5.8 %collective-permute-done.37 = f32[2,4,8,128]{3,2,1,0:T(8,128)S(1)} collective-permute-done((f32[2,4,8,128]{3,2,1,0:T(8,128)S(1)}, f32[2,4,8,128]{3,2,1,0:T(8,128)S(1)}, u32[]{:S(2)}, u32[]{:S(2)}) %collective-permute-start.37) | collective-permute-done | bytes 32800 | tf_op jit(solution)/shard_map/ppermute | solution.py:113
  331.2 4.5 project.3
  353.5 18.1 %mlp.3 = bf16[384,2048]{1,0:T(8,128)(2,1)} custom-call(bf16[384,2048]{1,0:T(8,128)(2,1)} %pad_maximum_fusion.4.x_ref, bf16[2048,4096]{1,0:T(8,128)(2,1)} %bitcast.255, bf16[2048,4096]{1,0:T(8,128)(2,1)} %bitcast.256, bf16[2048,2048]{1,0:T(8,128)(2,1)} %down_ref.5), custom_call_target="tpu_custom_call" | custom-call | tf_op jit(solution)/shard_map/mlp/pallas_call | solution.py:483
  388.0 13.1 %mlp.5 = bf16[16,2048]{1,0:T(8,128)(2,1)} custom-call(bf16[16,2048]{1,0:T(8,128)(2,1)} %multiply_convert_fusion.16.x_ref, bf16[2048,4096]{1,0:T(8,128)(2,1)} %bitcast.257, bf16[2048,4096]{1,0:T(8,128)(2,1)} %bitcast.258, bf16[2048,2048]{1,0:T(8,128)(2,1)} %down_ref.5), custom_call_target="tpu_custom_call" | custom-call | tf_op jit(solution)/shard_map/mlp/pallas_call | solution.py:483
  407.6 4.5 bitcast_add_fusion.2
  438.1 4.4 collective-permute-done.59
  442.5 14.4 %collective-permute-start.60 = (bf16[4,16,2,2048]{3,1,2,0:T(8,128)(2,1)S(1)}, bf16[4,16,2,2048]{3,1,2,0:T(8,128)(2,1)S(1)}, u32[]{:S(2)}, u32[]{:S(2)}) collective-permute-start(bf16[4,16,2,2048]{3,1,2,0:T(8,128)(2,1)S(1)} %pad_maximum_fusion.8), channel_id=1, source_target_pairs={{0,4},{4,0},{8,12},{12,8},{16,20},{20,16},{24,28},{28,24},{1,5},{5... | collective-permute-start | bytes 1572872 | tf_op jit(solution)/shard_map/ppermute | solution.py:113
  460.1 18.0 %mlp.4 = bf16[384,2048]{1,0:T(8,128)(2,1)} custom-call(bf16[384,2048]{1,0:T(8,128)(2,1)} %pad_maximum_fusion.6.x_ref, bf16[2048,4096]{1,0:T(8,128)(2,1)} %bitcast.259, bf16[2048,4096]{1,0:T(8,128)(2,1)} %bitcast.260, bf16[2048,2048]{1,0:T(8,128)(2,1)} %down_ref.5), custom_call_target="tpu_custom_call" | custom-call | tf_op jit(solution)/shard_map/mlp/pallas_call | solution.py:483
  479.0 4.1 fusion.2
  488.6 5.3 slice_bitcast_fusion.3
  495.1 33.7 %all-to-all-done = bf16[128,2,1572]{2,1,0:T(2,128)(2,1)S(1)} async-done(((bf16[128,2,1572]{2,1,0:T(2,128)(2,1)}), bf16[128,2,1572]{2,1,0:T(2,128)(2,1)S(1)}, u32[]{:S(2)}, u32[]{:S(2)}) %all-to-all-start) | async-done | bytes 804896 | tf_op jit(solution)/shard_map/all_to_all | solution.py:760
  534.6 9.1 %add_convert_fusion = bf16[768,4,512]{2,1,0:T(4,128)(2,1)} fusion(f32[768,512]{1,0:T(8,128)S(1)} %copy-done.6, f32[4]{0:T(128)S(1)} %get-tuple-element.310, f32[768,512]{1,0:T(8,128)} %get-tuple-element.156, f32[4]{0:T(128)S(1)} %get-tuple-element.311, f32[768,512]{1,0:T(8,128)} %get-tuple-element.157, f32[4]{0:T(128)S(1)} %get-tuple-element.312, ...), kind=kLoop, calls=%fused_computation.6 | loop fusion | flops 18874368 | bytes 12583008 | tf_op jit(solution)/shard_map/convert_element_type | solution.py:715
  (456 shorter events, 260.4 us)
Async XLA Ops:
  7.2 73.9 %all-gather.5.cloned.1.call-start = ((), (), s32[]{:S(2)}) async-start(), calls=%async_computation.5 | async-start | bytes 1966080 | tf_op jit(solution)/shard_map/all_gather | solution.py:90
  20.8 105.9 %collective-permute-start.22 = (f32[2,384]{1,0:T(2,128)}, f32[2,384]{1,0:T(2,128)}, u32[]{:S(2)}, u32[]{:S(2)}) collective-permute-start(f32[2,384]{1,0:T(2,128)} %get-tuple-element.286), channel_id=1, source_target_pairs={{0,3},{1,0},{2,1},{3,2},{4,7},{5,4},{6,5},{7,6},{8,11},{9,8},{10,9... | collective-permute-start | bytes 9224 | tf_op jit(solution)/shard_map/ppermute | solution.py:55
  25.0 101.0 %collective-permute-start.21 = (f32[2,384]{1,0:T(2,128)}, f32[2,384]{1,0:T(2,128)}, u32[]{:S(2)}, u32[]{:S(2)}) collective-permute-start(f32[2,384]{1,0:T(2,128)} %get-tuple-element.286), channel_id=1, source_target_pairs={{0,2},{1,3},{2,0},{3,1},{4,6},{5,7},{6,4},{7,5},{8,10},{9,11},{10,... | collective-permute-start | bytes 9224 | tf_op jit(solution)/shard_map/ppermute | solution.py:55
  26.9 52.7 %collective-permute-start.2 = (f32[2,384]{1,0:T(2,128)}, f32[2,384]{1,0:T(2,128)}, u32[]{:S(2)}, u32[]{:S(2)}) collective-permute-start(f32[2,384]{1,0:T(2,128)} %get-tuple-element.284), channel_id=1, source_target_pairs={{0,3},{1,0},{2,1},{3,2},{4,7},{5,4},{6,5},{7,6},{8,11},{9,8},{10,9... | collective-permute-start | bytes 9224 | tf_op jit(solution)/shard_map/ppermute | solution.py:55
  27.1 51.2 %collective-permute-start.1 = (f32[2,384]{1,0:T(2,128)}, f32[2,384]{1,0:T(2,128)}, u32[]{:S(2)}, u32[]{:S(2)}) collective-permute-start(f32[2,384]{1,0:T(2,128)} %get-tuple-element.284), channel_id=1, source_target_pairs={{0,2},{1,3},{2,0},{3,1},{4,6},{5,7},{6,4},{7,5},{8,10},{9,11},{10,... | collective-permute-start | bytes 9224 | tf_op jit(solution)/shard_map/ppermute | solution.py:55
  29.3 49.7 %collective-permute-start = (f32[2,384]{1,0:T(2,128)}, f32[2,384]{1,0:T(2,128)}, u32[]{:S(2)}, u32[]{:S(2)}) collective-permute-start(f32[2,384]{1,0:T(2,128)} %get-tuple-element.284), channel_id=1, source_target_pairs={{0,1},{1,2},{2,3},{3,0},{4,5},{5,6},{6,7},{7,4},{8,9},{9,10},{10,1... | collective-permute-start | bytes 9224 | tf_op jit(solution)/shard_map/ppermute | solution.py:55
  32.8 128.0 %all-gather.7.cloned.1.call-start = ((), (), s32[]{:S(2)}) async-start(), calls=%async_computation.7 | async-start | bytes 1966080 | tf_op jit(solution)/shard_map/all_gather | solution.py:90
  106.8 20.0 %collective-permute-start.20 = (f32[2,384]{1,0:T(2,128)}, f32[2,384]{1,0:T(2,128)S(1)}, u32[]{:S(2)}, u32[]{:S(2)}) collective-permute-start(f32[2,384]{1,0:T(2,128)} %get-tuple-element.286), channel_id=1, source_target_pairs={{0,1},{1,2},{2,3},{3,0},{4,5},{5,6},{6,7},{7,4},{8,9},{9,10},{10,1... | collective-permute-start | bytes 9224 | tf_op jit(solution)/shard_map/ppermute | solution.py:55
  115.7 11.8 %collective-permute-start.9 = (bf16[32,48,512]{2,1,0:T(8,128)(2,1)}, bf16[32,48,512]{2,1,0:T(8,128)(2,1)}, u32[]{:S(2)}, u32[]{:S(2)}) collective-permute-start(bf16[32,48,512]{2,1,0:T(8,128)(2,1)} %constant_dynamic-update-slice_fusion.even_ref), channel_id=1, source_target_pairs={{0,4},{4,0},{8,12},{12,8},{16,20},{20,16},{24,28},{28,24},{1,5},{5... | collective-permute-start | bytes 4718600 | tf_op jit(solution)/shard_map/ppermute | solution.py:113
  122.7 153.1 %reduce-scatter.5.cloned.1.call-start = ((), (), s32[]{:S(2)}) async-start(), calls=%async_computation.6 | async-start | bytes 1966080 | tf_op jit(solution)/shard_map/reduce_scatter | solution.py:108
  148.4 14.4 %collective-permute-start.10 = (bf16[4,8,48,512]{3,2,1,0:T(8,128)(2,1)}, bf16[4,8,48,512]{3,2,1,0:T(8,128)(2,1)}, u32[]{:S(2)}, u32[]{:S(2)}) collective-permute-start(bf16[4,8,48,512]{3,2,1,0:T(8,128)(2,1)} %bitcast.19), channel_id=1, source_target_pairs={{0,4},{4,0},{8,12},{12,8},{16,20},{20,16},{24,28},{28,24},{1,5},{5... | collective-permute-start | bytes 4718600 | tf_op jit(solution)/shard_map/ppermute | solution.py:113
  149.1 13.7 %collective-permute-start.11 = (f32[4,8,8,128]{3,2,1,0:T(8,128)S(1)}, f32[4,8,8,128]{3,2,1,0:T(8,128)S(1)}, u32[]{:S(2)}, u32[]{:S(2)}) collective-permute-start(f32[4,8,8,128]{3,2,1,0:T(8,128)S(1)} %bitcast.305), channel_id=1, source_target_pairs={{0,4},{4,0},{8,12},{12,8},{16,20},{20,16},{24,28},{28,24},{1,5},{5... | collective-permute-start | bytes 393224 | tf_op jit(solution)/shard_map/ppermute | solution.py:113
  176.7 15.5 %collective-permute-start.16 = (bf16[2,4,48,512]{3,2,1,0:T(8,128)(2,1)S(1)}, bf16[2,4,48,512]{3,2,1,0:T(8,128)(2,1)S(1)}, u32[]{:S(2)}, u32[]{:S(2)}) collective-permute-start(bf16[2,4,48,512]{3,2,1,0:T(8,128)(2,1)S(1)} %get-tuple-element.192), channel_id=1, source_target_pairs={{0,16},{4,20},{8,24},{12,28},{16,0},{20,4},{24,8},{28,12},{1,17},{... | collective-permute-start | bytes 1179656 | tf_op jit(solution)/shard_map/ppermute | solution.py:113
  182.2 21.0 %collective-permute-start.12 = (bf16[2,4,48,512]{3,2,1,0:T(8,128)(2,1)S(1)}, bf16[2,4,48,512]{3,2,1,0:T(8,128)(2,1)S(1)}, u32[]{:S(2)}, u32[]{:S(2)}) collective-permute-start(bf16[2,4,48,512]{3,2,1,0:T(8,128)(2,1)S(1)} %pad_maximum_fusion.10), channel_id=1, source_target_pairs={{0,8},{4,12},{8,0},{12,4},{16,24},{20,28},{24,16},{28,20},{1,9},{5... | collective-permute-start | bytes 1179656 | tf_op jit(solution)/shard_map/ppermute | solution.py:113
  186.5 16.6 %collective-permute-start.13 = (f32[2,4,8,128]{3,2,1,0:T(8,128)}, f32[2,4,8,128]{3,2,1,0:T(8,128)}, u32[]{:S(2)}, u32[]{:S(2)}) collective-permute-start(f32[2,4,8,128]{3,2,1,0:T(8,128)} %pad_maximum_fusion.24), channel_id=1, source_target_pairs={{0,8},{4,12},{8,0},{12,4},{16,24},{20,28},{24,16},{28,20},{1,9},{5... | collective-permute-start | bytes 98312 | tf_op jit(solution)/shard_map/ppermute | solution.py:113
  198.3 18.7 %collective-permute-start.18 = (bf16[1,4,48,512]{3,2,1,0:T(8,128)(2,1)S(1)}, bf16[1,4,48,512]{3,2,1,0:T(8,128)(2,1)S(1)}, u32[]{:S(2)}, u32[]{:S(2)}) collective-permute-start(bf16[1,4,48,512]{3,2,1,0:T(8,128)(2,1)S(1)} %get-tuple-element.210), channel_id=1, source_target_pairs={{0,8},{4,12},{8,0},{12,4},{16,24},{20,28},{24,16},{28,20},{1,9},{5... | collective-permute-start | bytes 589832 | tf_op jit(solution)/shard_map/ppermute | solution.py:113
  203.2 13.8 %collective-permute-start.19 = (f32[1,4,8,128]{3,2,1,0:T(8,128)S(1)}, f32[1,4,8,128]{3,2,1,0:T(8,128)S(1)}, u32[]{:S(2)}, u32[]{:S(2)}) collective-permute-start(f32[1,4,8,128]{3,2,1,0:T(8,128)S(1)} %get-tuple-element.257), channel_id=1, source_target_pairs={{0,8},{4,12},{8,0},{12,4},{16,24},{20,28},{24,16},{28,20},{1,9},{5... | collective-permute-start | bytes 49160 | tf_op jit(solution)/shard_map/ppermute | solution.py:113
  208.6 11.8 %collective-permute-start.14 = (bf16[1,4,48,512]{3,2,1,0:T(8,128)(2,1)S(1)}, bf16[1,4,48,512]{3,2,1,0:T(8,128)(2,1)S(1)}, u32[]{:S(2)}, u32[]{:S(2)}) collective-permute-start(bf16[1,4,48,512]{3,2,1,0:T(8,128)(2,1)S(1)} %get-tuple-element.208), channel_id=1, source_target_pairs={{0,16},{4,20},{8,24},{12,28},{16,0},{20,4},{24,8},{28,12},{1,17},{... | collective-permute-start | bytes 589832 | tf_op jit(solution)/shard_map/ppermute | solution.py:113
  233.9 116.4 %all-gather.9.cloned.1.call-start = ((), (), s32[]{:S(2)}) async-start(), calls=%async_computation.9 | async-start | bytes 1966080 | tf_op jit(solution)/shard_map/all_gather | solution.py:90
  261.6 20.7 %collective-permute-start.30 = (bf16[4,8,48,512]{3,2,1,0:T(8,128)(2,1)}, bf16[4,8,48,512]{3,2,1,0:T(8,128)(2,1)}, u32[]{:S(2)}, u32[]{:S(2)}) collective-permute-start(bf16[4,8,48,512]{3,2,1,0:T(8,128)(2,1)} %bitcast.51), channel_id=1, source_target_pairs={{0,4},{4,0},{8,12},{12,8},{16,20},{20,16},{24,28},{28,24},{1,5},{5... | collective-permute-start | bytes 4718600 | tf_op jit(solution)/shard_map/ppermute | solution.py:113
  265.9 16.3 %collective-permute-start.31 = (f32[4,8,8,128]{3,2,1,0:T(8,128)S(1)}, f32[4,8,8,128]{3,2,1,0:T(8,128)S(1)}, u32[]{:S(2)}, u32[]{:S(2)}) collective-permute-start(f32[4,8,8,128]{3,2,1,0:T(8,128)S(1)} %bitcast.306), channel_id=1, source_target_pairs={{0,4},{4,0},{8,12},{12,8},{16,20},{20,16},{24,28},{28,24},{1,5},{5... | collective-permute-start | bytes 393224 | tf_op jit(solution)/shard_map/ppermute | solution.py:113
  282.1 89.4 %reduce-scatter.7.cloned.1.call-start = ((), (), s32[]{:S(2)}) async-start(), calls=%async_computation.8 | async-start | bytes 1966080 | tf_op jit(solution)/shard_map/reduce_scatter | solution.py:108
  291.5 13.9 %collective-permute-start.36 = (bf16[2,4,48,512]{3,2,1,0:T(8,128)(2,1)S(1)}, bf16[2,4,48,512]{3,2,1,0:T(8,128)(2,1)S(1)}, u32[]{:S(2)}, u32[]{:S(2)}) collective-permute-start(bf16[2,4,48,512]{3,2,1,0:T(8,128)(2,1)S(1)} %get-tuple-element.186), channel_id=1, source_target_pairs={{0,16},{4,20},{8,24},{12,28},{16,0},{20,4},{24,8},{28,12},{1,17},{... | collective-permute-start | bytes 1179656 | tf_op jit(solution)/shard_map/ppermute | solution.py:113
  296.6 17.0 %collective-permute-start.32 = (bf16[2,4,48,512]{3,2,1,0:T(8,128)(2,1)S(1)}, bf16[2,4,48,512]{3,2,1,0:T(8,128)(2,1)S(1)}, u32[]{:S(2)}, u32[]{:S(2)}) collective-permute-start(bf16[2,4,48,512]{3,2,1,0:T(8,128)(2,1)S(1)} %pad_maximum_fusion.13), channel_id=1, source_target_pairs={{0,8},{4,12},{8,0},{12,4},{16,24},{20,28},{24,16},{28,20},{1,9},{5... | collective-permute-start | bytes 1179656 | tf_op jit(solution)/shard_map/ppermute | solution.py:113
  296.7 16.9 %collective-permute-start.33 = (f32[2,4,8,128]{3,2,1,0:T(8,128)S(1)}, f32[2,4,8,128]{3,2,1,0:T(8,128)S(1)}, u32[]{:S(2)}, u32[]{:S(2)}) collective-permute-start(f32[2,4,8,128]{3,2,1,0:T(8,128)S(1)} %pad_maximum_fusion.26), channel_id=1, source_target_pairs={{0,8},{4,12},{8,0},{12,4},{16,24},{20,28},{24,16},{28,20},{1,9},{5... | collective-permute-start | bytes 98312 | tf_op jit(solution)/shard_map/ppermute | solution.py:113
  310.8 11.7 %collective-permute-start.38 = (bf16[1,4,48,512]{3,2,1,0:T(8,128)(2,1)S(1)}, bf16[1,4,48,512]{3,2,1,0:T(8,128)(2,1)S(1)}, u32[]{:S(2)}, u32[]{:S(2)}) collective-permute-start(bf16[1,4,48,512]{3,2,1,0:T(8,128)(2,1)S(1)} %get-tuple-element.204), channel_id=1, source_target_pairs={{0,8},{4,12},{8,0},{12,4},{16,24},{20,28},{24,16},{28,20},{1,9},{5... | collective-permute-start | bytes 589832 | tf_op jit(solution)/shard_map/ppermute | solution.py:113
  312.2 10.3 %collective-permute-start.39 = (f32[1,4,8,128]{3,2,1,0:T(8,128)S(1)}, f32[1,4,8,128]{3,2,1,0:T(8,128)S(1)}, u32[]{:S(2)}, u32[]{:S(2)}) collective-permute-start(f32[1,4,8,128]{3,2,1,0:T(8,128)S(1)} %get-tuple-element.251), channel_id=1, source_target_pairs={{0,8},{4,12},{8,0},{12,4},{16,24},{20,28},{24,16},{28,20},{1,9},{5... | collective-permute-start | bytes 49160 | tf_op jit(solution)/shard_map/ppermute | solution.py:113
  335.7 121.3 %all-gather.11.cloned.1.call-start = ((), (), s32[]{:S(2)}) async-start(), calls=%async_computation.11 | async-start | bytes 1966080 | tf_op jit(solution)/shard_map/all_gather | solution.py:90
  377.0 155.9 %reduce-scatter.9.cloned.1.call-start = ((), (), s32[]{:S(2)}) async-start(), calls=%async_computation.10 | async-start | bytes 1966080 | tf_op jit(solution)/shard_map/reduce_scatter | solution.py:108
  420.2 112.7 %reduce-scatter.11.cloned.1.call-start = ((), (), s32[]{:S(2)}) async-start(), calls=%async_computation.12 | async-start | bytes 1966080 | tf_op jit(solution)/shard_map/reduce_scatter | solution.py:108
  442.5 35.6 %collective-permute-start.60 = (bf16[4,16,2,2048]{3,1,2,0:T(8,128)(2,1)S(1)}, bf16[4,16,2,2048]{3,1,2,0:T(8,128)(2,1)S(1)}, u32[]{:S(2)}, u32[]{:S(2)}) collective-permute-start(bf16[4,16,2,2048]{3,1,2,0:T(8,128)(2,1)S(1)} %pad_maximum_fusion.8), channel_id=1, source_target_pairs={{0,4},{4,0},{8,12},{12,8},{16,20},{20,16},{24,28},{28,24},{1,5},{5... | collective-permute-start | bytes 1572872 | tf_op jit(solution)/shard_map/ppermute | solution.py:113
  485.2 43.7 %all-to-all-start = ((bf16[128,2,1572]{2,1,0:T(2,128)(2,1)}), bf16[128,2,1572]{2,1,0:T(2,128)(2,1)S(1)}, u32[]{:S(2)}, u32[]{:S(2)}) async-start(bf16[128,2,1572]{2,1,0:T(2,128)(2,1)} %copy.78), calls=%async_computation.4 | async-start | bytes 1703936 | tf_op jit(solution)/shard_map/all_to_all | solution.py:760
  (89 other events, 464.5 us)
Sparse Core Ops, SparseCore 0:
  32.9 37.7 all-gather.4
  122.8 35.1 all-gather.6
  234.0 35.9 reduce-scatter.4
  282.3 37.0 all-gather.8
  335.8 34.7 reduce-scatter.6
  377.2 39.8 all-gather.10
  420.3 42.8 reduce-scatter.8
  478.2 46.9 reduce-scatter.10

commit v6 on v5

--- a/solution.py
+++ b/solution.py
@@ -14,12 +14,12 @@
 CHUNKS = 2
 LANES = 128
 PAGES_A_STEP = 2
-VMEM_BYTES = 56 * 1024 * 1024
-
-
-def params(count=1):
+MIB = 1024 * 1024
+
+
+def params(mebibytes):
     return pltpu.CompilerParams(
-        dimension_semantics=("arbitrary",) * count, vmem_limit_bytes=VMEM_BYTES
+        dimension_semantics=("arbitrary",), vmem_limit_bytes=mebibytes * MIB
     )
 
 
@@ -172,31 +172,30 @@
     return done, first_merged[1]
 
 
-def rotate_kernel(heads, size, scale, x_ref, cos_ref, sin_ref, q_ref, k_ref, v_ref):
-    width = heads * size
+def rotate_kernel(heads, size, scale, x_ref, y_ref, z_ref, cos_ref, sin_ref, q_ref, k_ref, v_ref):
     cosine, sine = cos_ref[...], sin_ref[...]
     for head in range(heads):
-        at = head * size
-        for base, out_ref, factor in ((0, q_ref, scale), (width, k_ref, 1.0)):
-            values = x_ref[:, base + at : base + at + size]
+        at = slice(head * size, (head + 1) * size)
+        for in_ref, out_ref, factor in ((x_ref, q_ref, scale), (y_ref, k_ref, 1.0)):
+            values = in_ref[:, at]
             turned = values * cosine + pltpu.roll(values, size // 2, 1) * sine
-            out_ref[:, at : at + size] = (turned * factor).astype(out_ref.dtype)
-    v_ref[...] = x_ref[:, 2 * width :].astype(v_ref.dtype)
-
-
-def rotate_all(projected, cosine, sine, heads, size, rows):
-    tokens = projected.shape[0]
-    out = jax.ShapeDtypeStruct((tokens, heads * size), jnp.bfloat16)
-    block = lambda width: pl.BlockSpec((rows, width), lambda i: (i, 0))
+            out_ref[:, at] = (turned * factor).astype(out_ref.dtype)
+    v_ref[...] = z_ref[...].astype(v_ref.dtype)
+
+
+def rotate_all(thirds, cosine, sine, heads, size, rows):
+    tokens, width = thirds[0].shape
+    out = jax.ShapeDtypeStruct((tokens, width), jnp.bfloat16)
+    block = lambda lanes: pl.BlockSpec((rows, lanes), lambda i: (i, 0))
     return pl.pallas_call(
         functools.partial(rotate_kernel, heads, size, size ** (-0.5)),
         grid=(tokens // rows,),
-        in_specs=[block(3 * heads * size), block(size), block(size)],
-        out_specs=[block(heads * size)] * 3,
+        in_specs=[block(width)] * 3 + [block(size)] * 2,
+        out_specs=[block(width)] * 3,
         out_shape=[out] * 3,
-        compiler_params=params(),
+        compiler_params=params(8),
         name="rotate",
-    )(projected, cosine, sine)
+    )(*thirds, cosine, sine)
 
 
 def lay_logs(columns, rows):
@@ -245,7 +244,7 @@
             jax.ShapeDtypeStruct((requests, tree, width), jnp.float32),
             jax.ShapeDtypeStruct((requests, 8, LANES), jnp.float32),
         ],
-        compiler_params=params(),
+        compiler_params=params(8),
         name="tree_attention",
     )(queries, keys, values, reach)
 
@@ -426,7 +425,7 @@
             jax.ShapeDtypeStruct((requests, tree, width), jnp.bfloat16),
             jax.ShapeDtypeStruct((requests, 8, LANES), jnp.float32),
         ],
-        compiler_params=params(),
+        compiler_params=params(20),
         name="page_attention",
     )(*plan, even, odd, *([k_pages, v_pages] * PAGES_A_STEP))
 
@@ -450,7 +449,7 @@
         ],
         out_specs=pl.BlockSpec((rows, tile), lambda i: (0, i)),
         out_shape=jax.ShapeDtypeStruct((rows, columns), jnp.bfloat16),
-        compiler_params=params(),
+        compiler_params=params(8),
         name="project",
     )(values, weight)
 
@@ -475,9 +474,9 @@
 def mlp(values, gate_up, down):
     rows, width = values.shape
     hidden, columns = down.shape
-    tile = min(hidden, 512)
+    tile = min(hidden, 256)
     steps = hidden // tile
-    out_tile = min(columns, 512)
+    out_tile = min(columns, 256)
     late = lambda i: jnp.maximum(i - steps, 0)
     early = lambda i: jnp.minimum(i, steps - 1)
     return pl.pallas_call(
@@ -492,7 +491,7 @@
         out_specs=pl.BlockSpec((rows, out_tile), lambda i: (0, late(i))),
         out_shape=jax.ShapeDtypeStruct((rows, columns), jnp.bfloat16),
         scratch_shapes=[pltpu.VMEM((rows, hidden), jnp.bfloat16)],
-        compiler_params=params(),
+        compiler_params=params(16),
         name="mlp",
     )(values, gate_up, gate_up, down)
 
@@ -538,7 +537,7 @@
         in_specs=[big] * len(pairs) + [small] * len(pairs),
         out_specs=out_specs,
         out_shape=out_shape,
-        compiler_params=params(),
+        compiler_params=params(10),
         name="merge_partials",
     )(*[pair[0] for pair in pairs], *[pair[1] for pair in pairs])
 
@@ -650,15 +649,12 @@
         normed = attended_in[chunk]
         if before_normed is not None:
             normed, before_normed = lax.optimization_barrier((normed, before_normed))
-        projected = jnp.concatenate(
-            [
-                jnp.dot(normed, qkv_weight[:, third], preferred_element_type=jnp.float32)
-                for third in range(3)
-            ],
-            axis=1,
-        )
+        thirds = [
+            jnp.dot(normed, qkv_weight[:, third], preferred_element_type=jnp.float32)
+            for third in range(3)
+        ]
         queries, keys, values = rotate_all(
-            projected, cosine[rows], sine[rows], heads, size, 2 * tree_size
+            thirds, cosine[rows], sine[rows], heads, size, 2 * tree_size
         )
         queries, keys, values = (item.reshape(all_shape) for item in (queries, keys, values))
         if before_queries is not None:
@@ -700,19 +696,8 @@
         else:
             first_shares, sent_mid = lax.optimization_barrier((first_shares, sent_mid))
             mlp_parts.append(scatter_columns(first_shares))
+            last_shares = shares
             mlp_parts.append(scatter_columns(shares))
-
-    attn_delta = jnp.concatenate(attn_parts)
-    mlp_delta = jnp.concatenate(mlp_parts)
-    stream_vals = streams.astype(jnp.float32)
-    new_streams = both_out[None, :, None] * attn_delta[:, None] + (
-        hc_out[1][None, :, None] * mlp_delta[:, None]
-    )
-    for index in range(stream_count):
-        new_streams = (
-            new_streams + both_mix[index][None, :, None] * stream_vals[:, index : index + 1]
-        )
-    new_streams = new_streams.astype(jnp.bfloat16)
 
     rows_taken = jnp.arange(req_local, dtype=jnp.int32) * tree_size + accepted_index
     stream_rows = streams[rows_taken].astype(jnp.float32)
@@ -740,7 +725,20 @@
         jnp.sum(both_out) * attn_rows + jnp.sum(hc_out[1]) * mlp_rows
     ) + blend(stream_rows, jnp.sum(both_mix, axis=1))
     final_full = jnp.concatenate(list(shift_gather(final_local)), axis=1)
+    final_full, last_shares = lax.optimization_barrier((final_full, last_shares))
     final_norm = layer_norm(final_full)
+    attn_delta = jnp.concatenate(attn_parts)
+    mlp_delta = jnp.concatenate(mlp_parts)
+    stream_vals = streams.astype(jnp.float32)
+    new_streams = both_out[None, :, None] * attn_delta[:, None] + (
+        hc_out[1][None, :, None] * mlp_delta[:, None]
+    )
+    for index in range(stream_count):
+        new_streams = (
+            new_streams + both_mix[index][None, :, None] * stream_vals[:, index : index + 1]
+        )
+    new_streams = new_streams.astype(jnp.bfloat16)
+
     own_columns = lax.dynamic_slice_in_dim(
         final_norm, lax.axis_index("head") * feature_local, feature_local, 1
     )

time: 557 us -> 495 us (0.89)
  Pallas kernels: 144 us -> 101 us
  other arithmetic: 95.2 us -> 68.3 us
  waiting for transfers between devices: 74.6 us -> 99.2 us
  starting transfers between devices: 88.9 us -> 77.4 us
    unnamed x116 -> x120, local copies, waits for them, and re-layouts: 36.2 us -> 63.2 us
    ppermute x37, waiting for transfers between devices: 24.8 us -> 42.8 us  [swapped(): return lax.ppermute(values, 'req', [(r, r ^ bit) for r in range(count)])]
    pallas_call x10, Pallas kernels: 35.8 us -> 18.5 us  [merge_partials(): pl.pallas_call(functools.partial(merge_kernel, heads, size, len(pairs)),...]
    ppermute x37, starting transfers between devices: 59.4 us -> 46.6 us  [swapped(): return lax.ppermute(values, 'req', [(r, r ^ bit) for r in range(count)])]
    slice x12, local copies, waits for them, and re-layouts: 12.4 us -> 0.26 us  [scatter_requests(): value[at:at + 1]]
    pallas_call x2, Pallas kernels: 7.93 us -> 1.57 us  [rotate_all(): pl.pallas_call(functools.partial(rotate_kernel, heads, size, size ** (-0....]
    reduce_scatter x4, waiting for transfers between devices: 0.03 us -> 5.7 us  [scatter_columns(): lax.psum_scatter(shares, 'head', scatter_dimension=1, tiled=True)]
  transfers between devices with their start and end apart: 70 -> 70, of which waited for: 24 -> 32; matrix products, arithmetic and copies ran while one was open for 32% -> 24% of each run, Pallas kernels for 24% -> 19%
where the time goes in v6:
time: 495 us; the launch traced here: 489 us
  local copies, waits for them, and re-layouts  102 us (21%)
  Pallas kernels  101 us (20%)
  waiting for transfers between devices  99.2 us (20%)
  starting transfers between devices  77.4 us (16%)
  other arithmetic  68.3 us (14%)
  matrix products  23.2 us (5%)
  between operations  17.6 us (4%)
    unnamed x120, local copies, waits for them, and re-layouts  63.2 us
    ppermute x37, starting transfers between devices, swapped(): return lax.ppermute(values, 'req', [(r, r ^ bit) for r in range(count)])  46.6 us
    pallas_call x3, Pallas kernels, mlp(): pl.pallas_call(functools.partial(mlp_kernel, steps, tile), grid=(steps +...  43.8 us
    ppermute x37, waiting for transfers between devices, swapped(): return lax.ppermute(values, 'req', [(r, r ^ bit) for r in range(count)])  42.8 us
    all_to_all x1, waiting for transfers between devices, on_device(): lax.all_to_all(logits_local.astype(jnp.bfloat16), ('req', 'head'), split_...  28.7 us
    ppermute x21, starting transfers between devices, shift_gather(): lax.ppermute(small, 'head', [(z, (z + step) % count) for z in range(count)])  22 us
    pallas_call x2, Pallas kernels, page_attention(): pl.pallas_call(functools.partial(page_kernel, heads, size), grid_spec=gri...  21.6 us
    pallas_call x10, Pallas kernels, merge_partials(): pl.pallas_call(functools.partial(merge_kernel, heads, size, len(pairs)),...  18.5 us
  transfers between devices with their start and end apart: 70, of which 32 were waited for; matrix products, arithmetic and copies ran while one was open for 24% of the time, Pallas kernels for 19%

profile of v6, /device:TPU:1, one launch (start us, length us, event | category | flops | bytes accessed | tf_op | source)
XLA Modules:
  0.0 489.2 jit_solution(12490527954497663004)
XLA Ops:
  7.2 5.8 %fusion.96 = (bf16[768,4,512]{2,0,1:T(8,128)(2,1)S(1)}, f32[768,4,512]{2,0,1:T(8,128)}) fusion(bf16[768,4,512]{2,1,0:T(4,128)(2,1)} %param.17), kind=kLoop, calls=%fused_computation.365 | loop fusion | flops 1572864 | bytes 12582912 | tf_op args[0]
  18.7 4.2 collective-permute-start.22
  39.8 11.7 %copy_bitcast_fusion = (bf16[48,4,128,128]{3,2,1,0:T(8,128)(2,1)}, bf16[48,4,128,128]{3,2,1,0:T(8,128)(2,1)}) fusion(bf16[48,128,4,128]{3,2,1,0:T(4,128)(2,1)} %param.28, bf16[48,128,4,128]{3,2,1,0:T(4,128)(2,1)} %param.27), kind=kLoop, calls=%fused_computation.4 | loop fusion | bytes 25165824 | tf_op jit(solution)/shard_map/transpose | solution.py:621
  51.5 17.3 %copy.82 = bf16[256,8,2,2048]{3,1,2,0:T(8,128)(2,1)} copy(bf16[256,8,2,2048]{3,2,1,0:T(2,128)(2,1)} %bitcast.305) | data formatting | bytes 33554432
  91.7 4.3 collective-permute-done.7
  96.2 6.7 %collective-permute-start.9 = (bf16[32,48,512]{2,1,0:T(8,128)(2,1)S(1)}, bf16[32,48,512]{2,1,0:T(8,128)(2,1)S(1)}, u32[]{:S(2)}, u32[]{:S(2)}) collective-permute-start(bf16[32,48,512]{2,1,0:T(8,128)(2,1)S(1)} %constant_dynamic-update-slice_fusion.even_ref), channel_id=1, source_target_pairs={{0,4},{4,0},{8,12},{12,8},{16,20},{20,16},{24,28},{28,24},{1,5},{5... | collective-permute-start | bytes 4718600 | tf_op jit(solution)/shard_map/ppermute | solution.py:113
  115.2 13.4 %page_attention.2 = (bf16[64,48,512]{2,1,0:T(8,128)(2,1)S(1)}, f32[64,8,128]{2,1,0:T(8,128)S(1)}) custom-call(s32[48]{0:T(128)S(1)} %get-tuple-element.133.page_ref, s32[48]{0:T(128)S(1)} %get-tuple-element.134.place_ref, s32[48]{0:T(128)S(1)} %get-tuple-element.135.fill_ref, s32[48]{0:T(128)S(1)} %get-tuple-element.333.first_ref, ...), custom_call_target="tpu_custom_call" | custom-call | tf_op jit(solution)/shard_map/page_attention/pallas_call | solution.py:421
  131.9 5.9 %tree_attention.2 = (f32[8,48,512]{2,1,0:T(8,128)S(1)}, f32[8,8,128]{2,1,0:T(8,128)S(1)}) custom-call(bf16[8,48,512]{2,1,0:T(8,128)(2,1)S(1)} %bitcast.268, bf16[8,48,512]{2,1,0:T(8,128)(2,1)S(1)} %bitcast.276, bf16[8,48,512]{2,1,0:T(8,128)(2,1)S(1)} %bitcast.277, f32[8,48,48]{2,1,0:T(8,128)S(1)} %get-tuple-element.201.reach_ref), custom_call_target="tpu_custom_call" | custom-call | tf_op jit(solution)/shard_map/tree_attention/pallas_call | solution.py:238
  143.8 5.3 %merge_partials.10 = (bf16[32,48,512]{2,1,0:T(8,128)(2,1)S(1)}, f32[32,8,128]{2,1,0:T(8,128)S(1)}) custom-call(bf16[32,48,512]{2,1,0:T(8,128)(2,1)S(1)} %get-tuple-element.159.refs_0_, bf16[32,48,512]{2,1,0:T(8,128)(2,1)S(1)} %bitcast.271, f32[32,8,128]{2,1,0:T(8,128)S(1)} %copy-done.18, f32[32,8,128]{2,1,0:T(8,128)} %bitcast.22.refs_3_), custom_call_target="tpu_custom_call" | custom-call | tf_op jit(solution)/shard_map/merge_partials/pallas_call | solution.py:534
  156.2 6.4 %collective-permute-done.17 = f32[2,4,8,128]{3,2,1,0:T(8,128)S(1)} collective-permute-done((f32[2,4,8,128]{3,2,1,0:T(8,128)S(1)}, f32[2,4,8,128]{3,2,1,0:T(8,128)S(1)}, u32[]{:S(2)}, u32[]{:S(2)}) %collective-permute-start.17) | collective-permute-done | bytes 32800 | tf_op jit(solution)/shard_map/ppermute | solution.py:113
  183.0 4.2 collective-permute-done.27
  187.6 4.4 collective-permute-start.29
  200.7 8.2 %page_attention.3 = (bf16[64,48,512]{2,1,0:T(8,128)(2,1)S(1)}, f32[64,8,128]{2,1,0:T(8,128)S(1)}) custom-call(s32[48]{0:T(128)S(1)} %copy-done.31, s32[48]{0:T(128)S(1)} %copy-done.29, s32[48]{0:T(128)S(1)} %copy-done.30, s32[48]{0:T(128)S(1)} %get-tuple-element.331.first_ref, s32[48]{0:T(128)S(1)} %get-tuple-element.330.last_ref, s32[1]{0:T(128)} %bitcast.49.live_ref, ...), custom_call_target="tpu_custom_call" | custom-call | tf_op jit(solution)/shard_map/page_attention/pallas_call | solution.py:421
  212.7 6.0 %tree_attention.3 = (f32[8,48,512]{2,1,0:T(8,128)S(1)}, f32[8,8,128]{2,1,0:T(8,128)S(1)}) custom-call(bf16[8,48,512]{2,1,0:T(8,128)(2,1)S(1)} %bitcast.263, bf16[8,48,512]{2,1,0:T(8,128)(2,1)S(1)} %bitcast.278, bf16[8,48,512]{2,1,0:T(8,128)(2,1)S(1)} %bitcast.279, f32[8,48,48]{2,1,0:T(8,128)S(1)} %copy-done.15), custom_call_target="tpu_custom_call" | custom-call | tf_op jit(solution)/shard_map/tree_attention/pallas_call | solution.py:238
  218.8 5.4 %multiply_reduce_fusion.1 = (f32[384]{0:T(512)S(1)}, f32[384]{0:T(512)S(1)}, f32[384,512]{1,0:T(8,128)S(1)}) fusion(bf16[384,512]{1,0:T(8,128)(2,1)} %reduce-scatter.5.cloned.1.call-done, f32[]{:T(128)} %multiply_reduce_fusion.7, f32[384,4,512]{2,0,1:T(8,128)} %copy-done.34, f32[]{:T(128)} %bitcast.80, f32[]{:T(128)} %bitcast.79, f32[]{:T(128)} %bitcast.78, ...), kind=kLoop, calls=%fused_computation.68 | loop fusion | flops 2555136 | bytes 4328468 | tf_op jit(solution)/shard_map/reduce_sum | solution.py:84
  226.6 5.4 %merge_partials.15 = (bf16[32,48,512]{2,1,0:T(8,128)(2,1)S(1)}, f32[32,8,128]{2,1,0:T(8,128)S(1)}) custom-call(bf16[32,48,512]{2,1,0:T(8,128)(2,1)S(1)} %copy-done.13, bf16[32,48,512]{2,1,0:T(8,128)(2,1)} %bitcast.52.refs_1_, f32[32,8,128]{2,1,0:T(8,128)S(1)} %get-tuple-element.215.refs_2_, f32[32,8,128]{2,1,0:T(8,128)S(1)} %bitcast.296), custom_call_target="tpu_custom_call" | custom-call | tf_op jit(solution)/shard_map/merge_partials/pallas_call | solution.py:534
  235.4 8.0 %collective-permute-done.37 = f32[2,4,8,128]{3,2,1,0:T(8,128)S(1)} collective-permute-done((f32[2,4,8,128]{3,2,1,0:T(8,128)S(1)}, f32[2,4,8,128]{3,2,1,0:T(8,128)S(1)}, u32[]{:S(2)}, u32[]{:S(2)}) %collective-permute-start.37) | collective-permute-done | bytes 32800 | tf_op jit(solution)/shard_map/ppermute | solution.py:113
  265.2 6.1 %copy-done = bf16[256,8,2,2048]{3,1,2,0:T(8,128)(2,1)S(1)} copy-done((bf16[256,8,2,2048]{3,1,2,0:T(8,128)(2,1)S(1)}, bf16[256,8,2,2048]{3,1,2,0:T(8,128)(2,1)}, u32[]{:S(2)}) %copy-start) | copy-done | bytes 16777240
  274.7 17.5 %mlp.3 = bf16[384,2048]{1,0:T(8,128)(2,1)} custom-call(bf16[384,2048]{1,0:T(8,128)(2,1)S(1)} %pad_maximum_fusion.2.x_ref, bf16[2048,4096]{1,0:T(8,128)(2,1)S(1)} %bitcast.255, bf16[2048,4096]{1,0:T(8,128)(2,1)S(1)} %bitcast.256, bf16[2048,2048]{1,0:T(8,128)(2,1)S(1)} %copy-done.7), custom_call_target="tpu_custom_call" | custom-call | tf_op jit(solution)/shard_map/mlp/pallas_call | solution.py:482
  292.1 5.7 %reduce-scatter.7.cloned.1.call-done = bf16[384,512]{1,0:T(8,128)(2,1)} async-done(((bf16[384,2048]{1,0:T(8,128)(2,1)}), bf16[384,512]{1,0:T(8,128)(2,1)}) %reduce-scatter.7.cloned.1.call-update) | async-done | bytes 393232 | tf_op jit(solution)/shard_map/reduce_scatter | solution.py:108
  318.7 4.3 collective-permute-done.47
  323.3 5.8 %copy-done.1 = bf16[256,8,2,2048]{3,1,2,0:T(8,128)(2,1)S(1)} copy-done((bf16[256,8,2,2048]{3,1,2,0:T(8,128)(2,1)S(1)}, bf16[256,8,2,2048]{3,1,2,0:T(8,128)(2,1)}, u32[]{:S(2)}) %copy-start.1) | copy-done | bytes 16777240
  332.6 8.9 %mlp.5 = bf16[16,2048]{1,0:T(8,128)(2,1)S(1)} custom-call(bf16[16,2048]{1,0:T(8,128)(2,1)S(1)} %multiply_convert_fusion.16.x_ref, bf16[2048,4096]{1,0:T(8,128)(2,1)S(1)} %bitcast.257, bf16[2048,4096]{1,0:T(8,128)(2,1)S(1)} %bitcast.258, bf16[2048,2048]{1,0:T(8,128)(2,1)S(1)} %copy-done.8), custom_call_target="tpu_custom_call" | custom-call | tf_op jit(solution)/shard_map/mlp/pallas_call | solution.py:482
  352.9 4.2 collective-permute-done.54
  360.3 5.9 %copy-done.2 = bf16[256,8,2,2048]{3,1,2,0:T(8,128)(2,1)S(1)} copy-done((bf16[256,8,2,2048]{3,1,2,0:T(8,128)(2,1)S(1)}, bf16[256,8,2,2048]{3,1,2,0:T(8,128)(2,1)}, u32[]{:S(2)}) %copy-start.2) | copy-done | bytes 16777240
  369.6 17.5 %mlp.4 = bf16[384,2048]{1,0:T(8,128)(2,1)} custom-call(bf16[384,2048]{1,0:T(8,128)(2,1)S(1)} %pad_maximum_fusion.4.x_ref, bf16[2048,4096]{1,0:T(8,128)(2,1)S(1)} %bitcast.259, bf16[2048,4096]{1,0:T(8,128)(2,1)S(1)} %bitcast.260, bf16[2048,2048]{1,0:T(8,128)(2,1)S(1)} %copy-done.9), custom_call_target="tpu_custom_call" | custom-call | tf_op jit(solution)/shard_map/mlp/pallas_call | solution.py:482
  405.7 8.9 %collective-permute-start.60 = (bf16[4,16,2,2048]{3,1,2,0:T(8,128)(2,1)S(1)}, bf16[4,16,2,2048]{3,1,2,0:T(8,128)(2,1)}, u32[]{:S(2)}, u32[]{:S(2)}) collective-permute-start(bf16[4,16,2,2048]{3,1,2,0:T(8,128)(2,1)S(1)} %pad_maximum_fusion.6), channel_id=1, source_target_pairs={{0,4},{4,0},{8,12},{12,8},{16,20},{20,16},{24,28},{28,24},{1,5},{5... | collective-permute-start | bytes 1572872 | tf_op jit(solution)/shard_map/ppermute | solution.py:113
  420.4 4.2 fusion.2
  426.6 4.1 all-to-all-start
  430.8 5.2 %slice_bitcast_fusion.3 = (f32[768,512]{1,0:T(8,128)S(1)}, f32[768,512]{1,0:T(8,128)}, f32[768,512]{1,0:T(8,128)}, f32[768,512]{1,0:T(8,128)}) fusion(f32[768,4,512]{2,0,1:T(8,128)} %get-tuple-element.163), kind=kLoop, calls=%fused_computation.30 | loop fusion | bytes 12582912 | tf_op jit(solution)/shard_map/mul | solution.py:738
  437.2 28.7 %all-to-all-done = bf16[128,2,1572]{2,1,0:T(2,128)(2,1)} async-done(((bf16[128,2,1572]{2,1,0:T(2,128)(2,1)}), bf16[128,2,1572]{2,1,0:T(2,128)(2,1)}, u32[]{:S(2)}, u32[]{:S(2)}) %all-to-all-start) | async-done | bytes 804896 | tf_op jit(solution)/shard_map/all_to_all | solution.py:758
  472.8 9.1 %add_convert_fusion = bf16[768,4,512]{2,1,0:T(4,128)(2,1)} fusion(f32[768,512]{1,0:T(8,128)S(1)} %copy-done.39, f32[4]{0:T(128)S(1)} %get-tuple-element.308, f32[768,512]{1,0:T(8,128)} %get-tuple-element.154, f32[4]{0:T(128)S(1)} %get-tuple-element.309, f32[768,512]{1,0:T(8,128)} %get-tuple-element.155, f32[4]{0:T(128)S(1)} %get-tuple-element.310, ...), kind=kLoop, calls=%fused_computation.6 | loop fusion | flops 18874368 | bytes 12583008 | tf_op jit(solution)/shard_map/convert_element_type | solution.py:740
  (460 shorter events, 213.0 us)
Async XLA Ops:
  7.2 62.5 %all-gather.5.cloned.1.call-start = ((), (), s32[]{:S(2)}) async-start(), calls=%async_computation.5 | async-start | bytes 1966080 | tf_op jit(solution)/shard_map/all_gather | solution.py:90
  18.7 90.4 %collective-permute-start.22 = (f32[2,384]{1,0:T(2,128)}, f32[2,384]{1,0:T(2,128)S(1)}, u32[]{:S(2)}, u32[]{:S(2)}) collective-permute-start(f32[2,384]{1,0:T(2,128)} %get-tuple-element.284), channel_id=1, source_target_pairs={{0,3},{1,0},{2,1},{3,2},{4,7},{5,4},{6,5},{7,6},{8,11},{9,8},{10,9... | collective-permute-start | bytes 9224 | tf_op jit(solution)/shard_map/ppermute | solution.py:55
  22.9 85.6 %collective-permute-start.21 = (f32[2,384]{1,0:T(2,128)}, f32[2,384]{1,0:T(2,128)S(1)}, u32[]{:S(2)}, u32[]{:S(2)}) collective-permute-start(f32[2,384]{1,0:T(2,128)} %get-tuple-element.284), channel_id=1, source_target_pairs={{0,2},{1,3},{2,0},{3,1},{4,6},{5,7},{6,4},{7,5},{8,10},{9,11},{10,... | collective-permute-start | bytes 9224 | tf_op jit(solution)/shard_map/ppermute | solution.py:55
  23.1 46.3 %collective-permute-start.2 = (f32[2,384]{1,0:T(2,128)S(1)}, f32[2,384]{1,0:T(2,128)S(1)}, u32[]{:S(2)}, u32[]{:S(2)}) collective-permute-start(f32[2,384]{1,0:T(2,128)S(1)} %get-tuple-element.282), channel_id=1, source_target_pairs={{0,3},{1,0},{2,1},{3,2},{4,7},{5,4},{6,5},{7,6},{8,11},{9,8},{10,9... | collective-permute-start | bytes 9224 | tf_op jit(solution)/shard_map/ppermute | solution.py:55
  23.3 46.1 %collective-permute-start.1 = (f32[2,384]{1,0:T(2,128)S(1)}, f32[2,384]{1,0:T(2,128)S(1)}, u32[]{:S(2)}, u32[]{:S(2)}) collective-permute-start(f32[2,384]{1,0:T(2,128)S(1)} %get-tuple-element.282), channel_id=1, source_target_pairs={{0,2},{1,3},{2,0},{3,1},{4,6},{5,7},{6,4},{7,5},{8,10},{9,11},{10,... | collective-permute-start | bytes 9224 | tf_op jit(solution)/shard_map/ppermute | solution.py:55
  25.6 43.8 %collective-permute-start = (f32[2,384]{1,0:T(2,128)S(1)}, f32[2,384]{1,0:T(2,128)S(1)}, u32[]{:S(2)}, u32[]{:S(2)}) collective-permute-start(f32[2,384]{1,0:T(2,128)S(1)} %get-tuple-element.282), channel_id=1, source_target_pairs={{0,1},{1,2},{2,3},{3,0},{4,5},{5,6},{6,7},{7,4},{8,9},{9,10},{10,1... | collective-permute-start | bytes 9224 | tf_op jit(solution)/shard_map/ppermute | solution.py:55
  27.9 113.2 %all-gather.7.cloned.1.call-start = ((), (), s32[]{:S(2)}) async-start(), calls=%async_computation.7 | async-start | bytes 1966080 | tf_op jit(solution)/shard_map/all_gather | solution.py:90
  81.6 8.2 %collective-permute-start.5 = (bf16[4,48,512]{2,1,0:T(8,128)(2,1)S(1)}, bf16[4,48,512]{2,1,0:T(8,128)(2,1)S(1)}, u32[]{:S(2)}, u32[]{:S(2)}) collective-permute-start(bf16[4,48,512]{2,1,0:T(8,128)(2,1)S(1)} %bitcast.313), channel_id=1, source_target_pairs={{0,16},{4,20},{8,24},{12,28},{16,0},{20,4},{24,8},{28,12},{1,17},{... | collective-permute-start | bytes 589832 | tf_op jit(solution)/shard_map/ppermute | solution.py:113
  89.7 18.8 %collective-permute-start.20 = (f32[2,384]{1,0:T(2,128)}, f32[2,384]{1,0:T(2,128)}, u32[]{:S(2)}, u32[]{:S(2)}) collective-permute-start(f32[2,384]{1,0:T(2,128)} %get-tuple-element.284), channel_id=1, source_target_pairs={{0,1},{1,2},{2,3},{3,0},{4,5},{5,6},{6,7},{7,4},{8,9},{9,10},{10,1... | collective-permute-start | bytes 9224 | tf_op jit(solution)/shard_map/ppermute | solution.py:55
  96.2 13.1 %collective-permute-start.9 = (bf16[32,48,512]{2,1,0:T(8,128)(2,1)S(1)}, bf16[32,48,512]{2,1,0:T(8,128)(2,1)S(1)}, u32[]{:S(2)}, u32[]{:S(2)}) collective-permute-start(bf16[32,48,512]{2,1,0:T(8,128)(2,1)S(1)} %constant_dynamic-update-slice_fusion.even_ref), channel_id=1, source_target_pairs={{0,4},{4,0},{8,12},{12,8},{16,20},{20,16},{24,28},{28,24},{1,5},{5... | collective-permute-start | bytes 4718600 | tf_op jit(solution)/shard_map/ppermute | solution.py:113
  104.3 114.4 %reduce-scatter.5.cloned.1.call-start = ((), (), s32[]{:S(2)}) async-start(), calls=%async_computation.6 | async-start | bytes 1966080 | tf_op jit(solution)/shard_map/reduce_scatter | solution.py:108
  130.0 13.1 %collective-permute-start.10 = (bf16[4,8,48,512]{3,2,1,0:T(8,128)(2,1)}, bf16[4,8,48,512]{3,2,1,0:T(8,128)(2,1)S(1)}, u32[]{:S(2)}, u32[]{:S(2)}) collective-permute-start(bf16[4,8,48,512]{3,2,1,0:T(8,128)(2,1)} %bitcast.19), channel_id=1, source_target_pairs={{0,4},{4,0},{8,12},{12,8},{16,20},{20,16},{24,28},{28,24},{1,5},{5... | collective-permute-start | bytes 4718600 | tf_op jit(solution)/shard_map/ppermute | solution.py:113
  131.3 11.8 %collective-permute-start.11 = (f32[4,8,8,128]{3,2,1,0:T(8,128)}, f32[4,8,8,128]{3,2,1,0:T(8,128)}, u32[]{:S(2)}, u32[]{:S(2)}) collective-permute-start(f32[4,8,8,128]{3,2,1,0:T(8,128)} %bitcast.21), channel_id=1, source_target_pairs={{0,4},{4,0},{8,12},{12,8},{16,20},{20,16},{24,28},{28,24},{1,5},{5... | collective-permute-start | bytes 393224 | tf_op jit(solution)/shard_map/ppermute | solution.py:113
  152.0 10.6 %collective-permute-start.16 = (bf16[2,4,48,512]{3,2,1,0:T(8,128)(2,1)S(1)}, bf16[2,4,48,512]{3,2,1,0:T(8,128)(2,1)S(1)}, u32[]{:S(2)}, u32[]{:S(2)}) collective-permute-start(bf16[2,4,48,512]{3,2,1,0:T(8,128)(2,1)S(1)} %get-tuple-element.190), channel_id=1, source_target_pairs={{0,16},{4,20},{8,24},{12,28},{16,0},{20,4},{24,8},{28,12},{1,17},{... | collective-permute-start | bytes 1179656 | tf_op jit(solution)/shard_map/ppermute | solution.py:113
  153.3 9.3 %collective-permute-start.17 = (f32[2,4,8,128]{3,2,1,0:T(8,128)S(1)}, f32[2,4,8,128]{3,2,1,0:T(8,128)S(1)}, u32[]{:S(2)}, u32[]{:S(2)}) collective-permute-start(f32[2,4,8,128]{3,2,1,0:T(8,128)S(1)} %get-tuple-element.240), channel_id=1, source_target_pairs={{0,16},{4,20},{8,24},{12,28},{16,0},{20,4},{24,8},{28,12},{1,17},{... | collective-permute-start | bytes 98312 | tf_op jit(solution)/shard_map/ppermute | solution.py:113
  153.6 11.7 %collective-permute-start.12 = (bf16[2,4,48,512]{3,2,1,0:T(8,128)(2,1)S(1)}, bf16[2,4,48,512]{3,2,1,0:T(8,128)(2,1)S(1)}, u32[]{:S(2)}, u32[]{:S(2)}) collective-permute-start(bf16[2,4,48,512]{3,2,1,0:T(8,128)(2,1)S(1)} %pad_maximum_fusion.8), channel_id=1, source_target_pairs={{0,8},{4,12},{8,0},{12,4},{16,24},{20,28},{24,16},{28,20},{1,9},{5... | collective-permute-start | bytes 1179656 | tf_op jit(solution)/shard_map/ppermute | solution.py:113
  154.9 10.3 %collective-permute-start.13 = (f32[2,4,8,128]{3,2,1,0:T(8,128)S(1)}, f32[2,4,8,128]{3,2,1,0:T(8,128)S(1)}, u32[]{:S(2)}, u32[]{:S(2)}) collective-permute-start(f32[2,4,8,128]{3,2,1,0:T(8,128)S(1)} %pad_maximum_fusion.22), channel_id=1, source_target_pairs={{0,8},{4,12},{8,0},{12,4},{16,24},{20,28},{24,16},{28,20},{1,9},{5... | collective-permute-start | bytes 98312 | tf_op jit(solution)/shard_map/ppermute | solution.py:113
  179.7 83.4 %all-gather.9.cloned.1.call-start = ((), (), s32[]{:S(2)}) async-start(), calls=%async_computation.9 | async-start | bytes 1966080 | tf_op jit(solution)/shard_map/all_gather | solution.py:90
  210.8 14.3 %collective-permute-start.30 = (bf16[4,8,48,512]{3,2,1,0:T(8,128)(2,1)}, bf16[4,8,48,512]{3,2,1,0:T(8,128)(2,1)}, u32[]{:S(2)}, u32[]{:S(2)}) collective-permute-start(bf16[4,8,48,512]{3,2,1,0:T(8,128)(2,1)} %bitcast.51), channel_id=1, source_target_pairs={{0,4},{4,0},{8,12},{12,8},{16,20},{20,16},{24,28},{28,24},{1,5},{5... | collective-permute-start | bytes 4718600 | tf_op jit(solution)/shard_map/ppermute | solution.py:113
  212.1 13.1 %collective-permute-start.31 = (f32[4,8,8,128]{3,2,1,0:T(8,128)S(1)}, f32[4,8,8,128]{3,2,1,0:T(8,128)S(1)}, u32[]{:S(2)}, u32[]{:S(2)}) collective-permute-start(f32[4,8,8,128]{3,2,1,0:T(8,128)S(1)} %bitcast.318), channel_id=1, source_target_pairs={{0,4},{4,0},{8,12},{12,8},{16,20},{20,16},{24,28},{28,24},{1,5},{5... | collective-permute-start | bytes 393224 | tf_op jit(solution)/shard_map/ppermute | solution.py:113
  225.1 72.7 %reduce-scatter.7.cloned.1.call-start = ((), (), s32[]{:S(2)}) async-start(), calls=%async_computation.8 | async-start | bytes 1966080 | tf_op jit(solution)/shard_map/reduce_scatter | solution.py:108
  232.1 11.3 %collective-permute-start.36 = (bf16[2,4,48,512]{3,2,1,0:T(8,128)(2,1)S(1)}, bf16[2,4,48,512]{3,2,1,0:T(8,128)(2,1)S(1)}, u32[]{:S(2)}, u32[]{:S(2)}) collective-permute-start(bf16[2,4,48,512]{3,2,1,0:T(8,128)(2,1)S(1)} %get-tuple-element.184), channel_id=1, source_target_pairs={{0,16},{4,20},{8,24},{12,28},{16,0},{20,4},{24,8},{28,12},{1,17},{... | collective-permute-start | bytes 1179656 | tf_op jit(solution)/shard_map/ppermute | solution.py:113
  232.8 10.6 %collective-permute-start.37 = (f32[2,4,8,128]{3,2,1,0:T(8,128)S(1)}, f32[2,4,8,128]{3,2,1,0:T(8,128)S(1)}, u32[]{:S(2)}, u32[]{:S(2)}) collective-permute-start(f32[2,4,8,128]{3,2,1,0:T(8,128)S(1)} %get-tuple-element.234), channel_id=1, source_target_pairs={{0,16},{4,20},{8,24},{12,28},{16,0},{20,4},{24,8},{28,12},{1,17},{... | collective-permute-start | bytes 98312 | tf_op jit(solution)/shard_map/ppermute | solution.py:113
  233.8 12.3 %collective-permute-start.32 = (bf16[2,4,48,512]{3,2,1,0:T(8,128)(2,1)S(1)}, bf16[2,4,48,512]{3,2,1,0:T(8,128)(2,1)S(1)}, u32[]{:S(2)}, u32[]{:S(2)}) collective-permute-start(bf16[2,4,48,512]{3,2,1,0:T(8,128)(2,1)S(1)} %pad_maximum_fusion.11), channel_id=1, source_target_pairs={{0,8},{4,12},{8,0},{12,4},{16,24},{20,28},{24,16},{28,20},{1,9},{5... | collective-permute-start | bytes 1179656 | tf_op jit(solution)/shard_map/ppermute | solution.py:113
  234.4 11.6 %collective-permute-start.33 = (f32[2,4,8,128]{3,2,1,0:T(8,128)S(1)}, f32[2,4,8,128]{3,2,1,0:T(8,128)S(1)}, u32[]{:S(2)}, u32[]{:S(2)}) collective-permute-start(f32[2,4,8,128]{3,2,1,0:T(8,128)S(1)} %pad_maximum_fusion.24), channel_id=1, source_target_pairs={{0,8},{4,12},{8,0},{12,4},{16,24},{20,28},{24,16},{28,20},{1,9},{5... | collective-permute-start | bytes 98312 | tf_op jit(solution)/shard_map/ppermute | solution.py:113
  256.4 101.9 %all-gather.11.cloned.1.call-start = ((), (), s32[]{:S(2)}) async-start(), calls=%async_computation.11 | async-start | bytes 1966080 | tf_op jit(solution)/shard_map/all_gather | solution.py:90
  303.3 167.8 %reduce-scatter.9.cloned.1.call-start = ((), (), s32[]{:S(2)}) async-start(), calls=%async_computation.10 | async-start | bytes 1966080 | tf_op jit(solution)/shard_map/reduce_scatter | solution.py:108
  307.5 9.4 %collective-permute-start.45 = (f32[2,384]{1,0:T(2,128)S(1)}, f32[2,384]{1,0:T(2,128)S(1)}, u32[]{:S(2)}, u32[]{:S(2)}) collective-permute-start(f32[2,384]{1,0:T(2,128)S(1)} %get-tuple-element.278), channel_id=1, source_target_pairs={{0,3},{1,0},{2,1},{3,2},{4,7},{5,4},{6,5},{7,6},{8,11},{9,8},{10,9... | collective-permute-start | bytes 9224 | tf_op jit(solution)/shard_map/ppermute | solution.py:55
  309.0 7.9 %collective-permute-start.43 = (f32[2,384]{1,0:T(2,128)S(1)}, f32[2,384]{1,0:T(2,128)S(1)}, u32[]{:S(2)}, u32[]{:S(2)}) collective-permute-start(f32[2,384]{1,0:T(2,128)S(1)} %get-tuple-element.278), channel_id=1, source_target_pairs={{0,1},{1,2},{2,3},{3,0},{4,5},{5,6},{6,7},{7,4},{8,9},{9,10},{10,1... | collective-permute-start | bytes 9224 | tf_op jit(solution)/shard_map/ppermute | solution.py:55
  316.5 154.6 %reduce-scatter.11.cloned.1.call-start = ((), (), s32[]{:S(2)}) async-start(), calls=%async_computation.12 | async-start | bytes 1966080 | tf_op jit(solution)/shard_map/reduce_scatter | solution.py:108
  405.7 10.6 %collective-permute-start.60 = (bf16[4,16,2,2048]{3,1,2,0:T(8,128)(2,1)S(1)}, bf16[4,16,2,2048]{3,1,2,0:T(8,128)(2,1)}, u32[]{:S(2)}, u32[]{:S(2)}) collective-permute-start(bf16[4,16,2,2048]{3,1,2,0:T(8,128)(2,1)S(1)} %pad_maximum_fusion.6), channel_id=1, source_target_pairs={{0,4},{4,0},{8,12},{12,8},{16,20},{20,16},{24,28},{28,24},{1,5},{5... | collective-permute-start | bytes 1572872 | tf_op jit(solution)/shard_map/ppermute | solution.py:113
  426.6 39.3 %all-to-all-start = ((bf16[128,2,1572]{2,1,0:T(2,128)(2,1)}), bf16[128,2,1572]{2,1,0:T(2,128)(2,1)}, u32[]{:S(2)}, u32[]{:S(2)}) async-start(bf16[128,2,1572]{2,1,0:T(2,128)(2,1)} %copy.78), calls=%async_computation.4 | async-start | bytes 1703936 | tf_op jit(solution)/shard_map/all_to_all | solution.py:758
  (91 other events, 493.8 us)
Sparse Core Ops, SparseCore 0:
  28.0 37.8 all-gather.4
  104.5 36.5 all-gather.6
  179.8 38.3 reduce-scatter.4
  225.2 34.7 all-gather.8
  262.8 34.9 reduce-scatter.6
  303.4 39.0 all-gather.10
  344.8 35.6 reduce-scatter.8
  414.7 45.1 reduce-scatter.10

commit v7 on v6

--- a/solution.py
+++ b/solution.py
@@ -91,17 +91,21 @@
     mean = jnp.sum(stats[:, 0], axis=0) / width
     variance = jnp.sum(stats[:, 1], axis=0) / width - mean * mean
     scale = lax.rsqrt(variance + 1e-05)
-    normed = [
-        (
+
+    def finish(gathered):
+        normed = [
             (
-                gathered[:, rank * local : (rank + 1) * local].astype(jnp.float32)
-                + (stats[rank, 0] / local - mean)[:, None]
-            )
-            * scale[:, None]
-        ).astype(jnp.bfloat16)
-        for rank in range(lax.axis_size("head"))
-    ]
-    return jnp.concatenate(normed, axis=1), gathered, sent
+                (
+                    gathered[:, rank * local : (rank + 1) * local].astype(jnp.float32)
+                    + (stats[rank, 0] / local - mean)[:, None]
+                )
+                * scale[:, None]
+            ).astype(jnp.bfloat16)
+            for rank in range(lax.axis_size("head"))
+        ]
+        return jnp.concatenate(normed, axis=1)
+
+    return gathered, finish, sent
 
 
 def scatter_columns(shares):
@@ -491,7 +495,7 @@
         out_specs=pl.BlockSpec((rows, out_tile), lambda i: (0, late(i))),
         out_shape=jax.ShapeDtypeStruct((rows, columns), jnp.bfloat16),
         scratch_shapes=[pltpu.VMEM((rows, hidden), jnp.bfloat16)],
-        compiler_params=params(16),
+        compiler_params=params(56),
         name="mlp",
     )(values, gate_up, gate_up, down)
 
@@ -633,12 +637,8 @@
         rows = slice(chunk * step_tokens, (chunk + 1) * step_tokens)
         stream_vals = streams[rows].astype(jnp.float32)
         mixed_in = blend(stream_vals, hc_in[0])
-        normed, token, sent = gathered_norm(mixed_in, width, token)
-        if chunk == 0:
-            normed, k_heads, v_heads, gate_up = lax.optimization_barrier(
-                (normed, k_heads, v_heads, gate_up)
-            )
-        attended_in.append(normed)
+        token, finish, sent = gathered_norm(mixed_in, width, token)
+        attended_in.append((token, finish))
 
     all_shape = (step_requests, tree_size, heads * size)
     before_queries = None
@@ -646,9 +646,14 @@
     for chunk in range(CHUNKS):
         rows = slice(chunk * step_tokens, (chunk + 1) * step_tokens)
         asked = slice(chunk * step_requests, (chunk + 1) * step_requests)
-        normed = attended_in[chunk]
-        if before_normed is not None:
-            normed, before_normed = lax.optimization_barrier((normed, before_normed))
+        gathered, finish = attended_in[chunk]
+        if before_normed is None:
+            normed, k_heads, v_heads, gate_up = lax.optimization_barrier(
+                (finish(gathered), k_heads, v_heads, gate_up)
+            )
+        else:
+            gathered, before_normed = lax.optimization_barrier((gathered, before_normed))
+            normed = finish(gathered)
         thirds = [
             jnp.dot(normed, qkv_weight[:, third], preferred_element_type=jnp.float32)
             for third in range(3)
@@ -689,7 +694,8 @@
 
         stream_vals = streams[rows].astype(jnp.float32)
         mixed_mid = blend(stream_vals, mid_in) + mid_out * attn_delta
-        normed_mid, gathered, sent_mid = gathered_norm(mixed_mid, width)
+        gathered, finish, sent_mid = gathered_norm(mixed_mid, width)
+        normed_mid = finish(gathered)
         shares = mlp(normed_mid, gate_up, down_weight)
         if first_shares is None:
             first_shares = shares
@@ -724,9 +730,29 @@
     final_local = (
         jnp.sum(both_out) * attn_rows + jnp.sum(hc_out[1]) * mlp_rows
     ) + blend(stream_rows, jnp.sum(both_mix, axis=1))
+    final_local, last_shares = lax.optimization_barrier((final_local, last_shares))
     final_full = jnp.concatenate(list(shift_gather(final_local)), axis=1)
-    final_full, last_shares = lax.optimization_barrier((final_full, last_shares))
     final_norm = layer_norm(final_full)
+    own_columns = lax.dynamic_slice_in_dim(
+        final_norm, lax.axis_index("head") * feature_local, feature_local, 1
+    )
+    branch = jnp.einsum(
+        "jd,kde->jke",
+        final_norm.astype(jnp.bfloat16),
+        draft_weight,
+        preferred_element_type=jnp.float32,
+    )
+    drafted = (own_columns[:, None, :] + jax.nn.silu(branch)).astype(jnp.bfloat16)
+    draft_full = jnp.concatenate(list(shift_gather(drafted)), axis=2)
+    draft_all = gather_small(draft_full)
+    logits_local = jnp.dot(
+        draft_all.reshape(-1, width), lm_head, preferred_element_type=jnp.float32
+    )
+    logits_local = logits_local.reshape(all_requests, draft_count, -1)
+    logits_local, mlp_parts[-1] = lax.optimization_barrier((logits_local, mlp_parts[-1]))
+    logits = lax.all_to_all(
+        logits_local.astype(jnp.bfloat16), ("req", "head"), split_axis=0, concat_axis=2, tiled=True
+    ).astype(logits_local.dtype)
     attn_delta = jnp.concatenate(attn_parts)
     mlp_delta = jnp.concatenate(mlp_parts)
     stream_vals = streams.astype(jnp.float32)
@@ -739,25 +765,6 @@
         )
     new_streams = new_streams.astype(jnp.bfloat16)
 
-    own_columns = lax.dynamic_slice_in_dim(
-        final_norm, lax.axis_index("head") * feature_local, feature_local, 1
-    )
-    branch = jnp.einsum(
-        "jd,kde->jke",
-        final_norm.astype(jnp.bfloat16),
-        draft_weight,
-        preferred_element_type=jnp.float32,
-    )
-    drafted = (own_columns[:, None, :] + jax.nn.silu(branch)).astype(jnp.bfloat16)
-    draft_full = jnp.concatenate(list(shift_gather(drafted)), axis=2)
-    draft_all = gather_small(draft_full)
-    logits_local = jnp.dot(
-        draft_all.reshape(-1, width), lm_head, preferred_element_type=jnp.float32
-    )
-    logits_local = logits_local.reshape(all_requests, draft_count, -1)
-    logits = lax.all_to_all(
-        logits_local.astype(jnp.bfloat16), ("req", "head"), split_axis=0, concat_axis=2, tiled=True
-    ).astype(logits_local.dtype)
     return (new_streams, logits)
 
 

time: 495 us -> 556 us (1.12)
  waiting for transfers between devices: 99.2 us -> 166 us
  local copies, waits for them, and re-layouts: 102 us -> 71 us
  starting transfers between devices: 77.4 us -> 87.5 us
  other arithmetic: 68.3 us -> 76.4 us
  Pallas kernels: 101 us -> 107 us
    all_gather x4, waiting for transfers between devices: 1.88 us -> 59.1 us  [gathered_norm(): gathered = lax.all_gather(sent, 'head', axis=1, tiled=True)]
    reduce_scatter x4, waiting for transfers between devices: 5.7 us -> 33.4 us  [scatter_columns(): lax.psum_scatter(shares, 'head', scatter_dimension=1, tiled=True)]
    all_to_all x1, waiting for transfers between devices: 28.7 us -> 9.03 us  [on_device(): lax.all_to_all(logits_local.astype(jnp.bfloat16), ('req', 'head'), split_...]
    unnamed x120 -> x90, local copies, waits for them, and re-layouts: 63.2 us -> 44.5 us
    pallas_call x3, Pallas kernels: 43.8 us -> 59.2 us  [mlp(): pl.pallas_call(functools.partial(mlp_kernel, steps, tile), grid=(steps +...]
    transpose x1 -> x0, local copies, waits for them, and re-layouts: 11.7 us -> none  [on_device(): v_heads = jnp.transpose(v_pages, (0, 2, 1, 3))]
    ppermute x37, waiting for transfers between devices: 42.8 us -> 52.2 us  [swapped(): return lax.ppermute(values, 'req', [(r, r ^ bit) for r in range(count)])]
    pallas_call x2, Pallas kernels: 21.6 us -> 13.3 us  [page_attention(): pl.pallas_call(functools.partial(page_kernel, heads, size), grid_spec=gri...]
  transfers between devices with their start and end apart: 70 -> 70, of which waited for: 32 -> 34; matrix products, arithmetic and copies ran while one was open for 24% -> 21% of each run, Pallas kernels for 19% -> 12%
where the time goes in v7:
time: 556 us; the launch traced here: 550 us
  waiting for transfers between devices  166 us (30%)
  Pallas kernels  107 us (19%)
  starting transfers between devices  87.5 us (16%)
  other arithmetic  76.4 us (14%)
  local copies, waits for them, and re-layouts  71 us (13%)
  matrix products  24 us (4%)
  between operations  17.5 us (3%)
    pallas_call x3, Pallas kernels, mlp(): pl.pallas_call(functools.partial(mlp_kernel, steps, tile), grid=(steps +...  59.2 us
    all_gather x4, waiting for transfers between devices, gathered_norm(): gathered = lax.all_gather(sent, 'head', axis=1, tiled=True)  59.1 us
    ppermute x37, starting transfers between devices, swapped(): return lax.ppermute(values, 'req', [(r, r ^ bit) for r in range(count)])  52.3 us
    ppermute x37, waiting for transfers between devices, swapped(): return lax.ppermute(values, 'req', [(r, r ^ bit) for r in range(count)])  52.2 us
    unnamed x90, local copies, waits for them, and re-layouts  44.5 us
    reduce_scatter x4, waiting for transfers between devices, scatter_columns(): lax.psum_scatter(shares, 'head', scatter_dimension=1, tiled=True)  33.4 us
    ppermute x21, starting transfers between devices, shift_gather(): lax.ppermute(small, 'head', [(z, (z + step) % count) for z in range(count)])  26.7 us
    pallas_call x10, Pallas kernels, merge_partials(): pl.pallas_call(functools.partial(merge_kernel, heads, size, len(pairs)),...  17.8 us
  transfers between devices with their start and end apart: 70, of which 34 were waited for; matrix products, arithmetic and copies ran while one was open for 21% of the time, Pallas kernels for 12%

profile of v7, /device:TPU:1, one launch (start us, length us, event | category | flops | bytes accessed | tf_op | source)
XLA Modules:
  0.0 549.7 jit_solution(14762682266116617954)
XLA Ops:
  8.7 5.8 %fusion.93 = (bf16[768,4,512]{2,0,1:T(8,128)(2,1)S(1)}, f32[768,4,512]{2,0,1:T(8,128)}) fusion(bf16[768,4,512]{2,1,0:T(4,128)(2,1)} %param.17), kind=kLoop, calls=%fused_computation.368 | loop fusion | flops 1572864 | bytes 12582912 | tf_op args[0]
  35.3 17.9 %copy.82 = bf16[256,8,2,2048]{3,1,2,0:T(8,128)(2,1)} copy(bf16[256,8,2,2048]{3,2,1,0:T(2,128)(2,1)} %bitcast.315) | data formatting | bytes 33554432
  53.2 7.2 %copy.88 = bf16[48,128,4,128]{3,1,2,0:T(8,128)(2,1)} copy(bf16[48,128,4,128]{3,2,1,0:T(4,128)(2,1)} %param.28) | data formatting | bytes 12582912 | tf_op args[11]
  60.4 7.2 %copy.89 = bf16[48,128,4,128]{3,1,2,0:T(8,128)(2,1)} copy(bf16[48,128,4,128]{3,2,1,0:T(4,128)(2,1)} %param.27) | data formatting | bytes 12582912 | tf_op args[10]
  93.6 5.6 %collective-permute-start.9 = (bf16[32,48,512]{2,1,0:T(8,128)(2,1)S(1)}, bf16[32,48,512]{2,1,0:T(8,128)(2,1)S(1)}, u32[]{:S(2)}, u32[]{:S(2)}) collective-permute-start(bf16[32,48,512]{2,1,0:T(8,128)(2,1)S(1)} %constant_dynamic-update-slice_fusion.even_ref), channel_id=1, source_target_pairs={{0,4},{4,0},{8,12},{12,8},{16,20},{20,16},{24,28},{28,24},{1,5},{5... | collective-permute-start | bytes 4718600 | tf_op jit(solution)/shard_map/ppermute | solution.py:117
  109.5 6.6 %page_attention.2 = (bf16[64,48,512]{2,1,0:T(8,128)(2,1)S(1)}, f32[64,8,128]{2,1,0:T(8,128)S(1)}) custom-call(s32[48]{0:T(128)S(1)} %get-tuple-element.139.page_ref, s32[48]{0:T(128)S(1)} %get-tuple-element.140.place_ref, s32[48]{0:T(128)S(1)} %get-tuple-element.141.fill_ref, s32[48]{0:T(128)S(1)} %get-tuple-element.341.first_ref, ...), custom_call_target="tpu_custom_call" | custom-call | tf_op jit(solution)/shard_map/page_attention/pallas_call | solution.py:425
  118.0 5.9 %tree_attention.2 = (f32[8,48,512]{2,1,0:T(8,128)S(1)}, f32[8,8,128]{2,1,0:T(8,128)S(1)}) custom-call(bf16[8,48,512]{2,1,0:T(8,128)(2,1)S(1)} %bitcast.271, bf16[8,48,512]{2,1,0:T(8,128)(2,1)S(1)} %bitcast.279, bf16[8,48,512]{2,1,0:T(8,128)(2,1)S(1)} %bitcast.280, f32[8,48,48]{2,1,0:T(8,128)S(1)} %get-tuple-element.211.reach_ref), custom_call_target="tpu_custom_call" | custom-call | tf_op jit(solution)/shard_map/tree_attention/pallas_call | solution.py:242
  124.1 4.6 merge_partials.10
  128.9 10.2 %collective-permute-start.13 = (f32[2,4,8,128]{3,2,1,0:T(8,128)S(1)}, f32[2,4,8,128]{3,2,1,0:T(8,128)S(1)}, u32[]{:S(2)}, u32[]{:S(2)}) collective-permute-start(f32[2,4,8,128]{3,2,1,0:T(8,128)S(1)} %pad_maximum_fusion.23), channel_id=1, source_target_pairs={{0,8},{4,12},{8,0},{12,4},{16,24},{20,28},{24,16},{28,20},{1,9},{5... | collective-permute-start | bytes 98312 | tf_op jit(solution)/shard_map/ppermute | solution.py:117
  140.9 8.5 %collective-permute-done.12 = bf16[2,4,48,512]{3,2,1,0:T(8,128)(2,1)S(1)} collective-permute-done((bf16[2,4,48,512]{3,2,1,0:T(8,128)(2,1)S(1)}, bf16[2,4,48,512]{3,2,1,0:T(8,128)(2,1)S(1)}, u32[]{:S(2)}, u32[]{:S(2)}) %collective-permute-start.12) | collective-permute-done | bytes 393248 | tf_op jit(solution)/shard_map/ppermute | solution.py:117
  161.8 4.6 fusion.90
  173.6 23.2 %reduce-scatter.5.cloned.1.call-done = bf16[384,512]{1,0:T(8,128)(2,1)} async-done(((bf16[384,2048]{1,0:T(8,128)(2,1)}), bf16[384,512]{1,0:T(8,128)(2,1)}) %reduce-scatter.5.cloned.1.call-update) | async-done | bytes 393232 | tf_op jit(solution)/shard_map/reduce_scatter | solution.py:112
  196.7 6.2 %multiply_reduce_fusion.1 = (f32[384]{0:T(512)S(1)}, f32[384]{0:T(512)S(1)}, f32[384,512]{1,0:T(8,128)}) fusion(bf16[384,512]{1,0:T(8,128)(2,1)} %reduce-scatter.5.cloned.1.call-done, f32[]{:T(128)} %multiply_reduce_fusion.7, f32[384,4,512]{2,0,1:T(8,128)} %copy-done.13, f32[]{:T(128)} %bitcast.80, f32[]{:T(128)} %bitcast.79, f32[]{:T(128)} %bitcast.78, ...), kind=kLoop, calls=%fused_computation.67 | loop fusion | flops 2555136 | bytes 4328468 | tf_op jit(solution)/shard_map/reduce_sum | solution.py:84
  206.8 27.8 %all-gather.7.cloned.1.call-done = bf16[384,2048]{1,0:T(8,128)(2,1)} async-done(((bf16[384,512]{1,0:T(8,128)(2,1)}), bf16[384,2048]{1,0:T(8,128)(2,1)}) %all-gather.7.cloned.1.call-update) | async-done | bytes 1572880 | tf_op jit(solution)/shard_map/all_gather | solution.py:90
  253.8 4.2 collective-permute-done.27
  263.0 6.7 %page_attention.3 = (bf16[64,48,512]{2,1,0:T(8,128)(2,1)S(1)}, f32[64,8,128]{2,1,0:T(8,128)S(1)}) custom-call(s32[48]{0:T(128)S(1)} %get-tuple-element.135.page_ref, s32[48]{0:T(128)S(1)} %get-tuple-element.134.place_ref, s32[48]{0:T(128)S(1)} %get-tuple-element.133.fill_ref, s32[48]{0:T(128)S(1)} %get-tuple-element.339.first_ref, ...), custom_call_target="tpu_custom_call" | custom-call | tf_op jit(solution)/shard_map/page_attention/pallas_call | solution.py:425
  274.2 6.1 %tree_attention.3 = (f32[8,48,512]{2,1,0:T(8,128)S(1)}, f32[8,8,128]{2,1,0:T(8,128)S(1)}) custom-call(bf16[8,48,512]{2,1,0:T(8,128)(2,1)S(1)} %bitcast.266, bf16[8,48,512]{2,1,0:T(8,128)(2,1)S(1)} %bitcast.281, bf16[8,48,512]{2,1,0:T(8,128)(2,1)S(1)} %bitcast.282, f32[8,48,48]{2,1,0:T(8,128)S(1)} %get-tuple-element.210.reach_ref), custom_call_target="tpu_custom_call" | custom-call | tf_op jit(solution)/shard_map/tree_attention/pallas_call | solution.py:242
  280.5 5.4 merge_partials.15
  289.3 8.2 %collective-permute-done.32 = bf16[2,4,48,512]{3,2,1,0:T(8,128)(2,1)S(1)} collective-permute-done((bf16[2,4,48,512]{3,2,1,0:T(8,128)(2,1)S(1)}, bf16[2,4,48,512]{3,2,1,0:T(8,128)(2,1)S(1)}, u32[]{:S(2)}, u32[]{:S(2)}) %collective-permute-start.32) | collective-permute-done | bytes 393248 | tf_op jit(solution)/shard_map/ppermute | solution.py:117
  314.2 21.4 %mlp.3 = bf16[384,2048]{1,0:T(8,128)(2,1)} custom-call(bf16[384,2048]{1,0:T(8,128)(2,1)} %pad_maximum_fusion.2.x_ref, bf16[2048,4096]{1,0:T(8,128)(2,1)} %bitcast.309, bf16[2048,4096]{1,0:T(8,128)(2,1)} %bitcast.310, bf16[2048,2048]{1,0:T(8,128)(2,1)} %down_ref.5), custom_call_target="tpu_custom_call" | custom-call | tf_op jit(solution)/shard_map/mlp/pallas_call | solution.py:486
  335.6 10.2 %reduce-scatter.7.cloned.1.call-done = bf16[384,512]{1,0:T(8,128)(2,1)} async-done(((bf16[384,2048]{1,0:T(8,128)(2,1)}), bf16[384,512]{1,0:T(8,128)(2,1)}) %reduce-scatter.7.cloned.1.call-update) | async-done | bytes 393232 | tf_op jit(solution)/shard_map/reduce_scatter | solution.py:112
  356.2 31.3 %all-gather.11.cloned.1.call-done = bf16[384,2048]{1,0:T(8,128)(2,1)} async-done(((bf16[384,512]{1,0:T(8,128)(2,1)}), bf16[384,2048]{1,0:T(8,128)(2,1)}) %all-gather.11.cloned.1.call-update) | async-done | bytes 1572880 | tf_op jit(solution)/shard_map/all_gather | solution.py:90
  390.6 21.2 %mlp.5 = bf16[384,2048]{1,0:T(8,128)(2,1)} custom-call(bf16[384,2048]{1,0:T(8,128)(2,1)} %pad_maximum_fusion.4.x_ref, bf16[2048,4096]{1,0:T(8,128)(2,1)} %bitcast.311, bf16[2048,4096]{1,0:T(8,128)(2,1)} %bitcast.312, bf16[2048,2048]{1,0:T(8,128)(2,1)} %down_ref.5), custom_call_target="tpu_custom_call" | custom-call | tf_op jit(solution)/shard_map/mlp/pallas_call | solution.py:486
  427.6 16.6 %mlp.4 = bf16[16,2048]{1,0:T(8,128)(2,1)} custom-call(bf16[16,2048]{1,0:T(8,128)(2,1)} %multiply_convert_fusion.16.x_ref, bf16[2048,4096]{1,0:T(8,128)(2,1)} %bitcast.313, bf16[2048,4096]{1,0:T(8,128)(2,1)} %bitcast.314, bf16[2048,2048]{1,0:T(8,128)(2,1)} %down_ref.5), custom_call_target="tpu_custom_call" | custom-call | tf_op jit(solution)/shard_map/mlp/pallas_call | solution.py:486
  451.0 4.6 bitcast_add_fusion.2
  476.6 4.4 collective-permute-done.59
  481.1 8.6 %collective-permute-start.60 = (bf16[4,16,2,2048]{3,1,2,0:T(8,128)(2,1)S(1)}, bf16[4,16,2,2048]{3,1,2,0:T(8,128)(2,1)S(1)}, u32[]{:S(2)}, u32[]{:S(2)}) collective-permute-start(bf16[4,16,2,2048]{3,1,2,0:T(8,128)(2,1)S(1)} %pad_maximum_fusion.7), channel_id=1, source_target_pairs={{0,4},{4,0},{8,12},{12,8},{16,20},{20,16},{24,28},{28,24},{1,5},{5... | collective-permute-start | bytes 1572872 | tf_op jit(solution)/shard_map/ppermute | solution.py:117
  489.7 5.2 slice_bitcast_fusion.3
  500.1 5.0 fusion
  510.6 4.4 all-to-all-start
  519.4 8.8 %add_convert_fusion = bf16[768,4,512]{2,1,0:T(4,128)(2,1)} fusion(f32[768,512]{1,0:T(8,128)S(1)} %copy-done.17, f32[4]{0:T(128)S(1)} %get-tuple-element.318, f32[768,512]{1,0:T(8,128)S(1)} %copy-done.18, f32[4]{0:T(128)S(1)} %get-tuple-element.319, f32[768,512]{1,0:T(8,128)} %get-tuple-element.163, f32[4]{0:T(128)S(1)} %get-tuple-element.320, ...), kind=kLoop, calls=%fused_computation.6 | loop fusion | flops 18874368 | bytes 12583008 | tf_op jit(solution)/shard_map/convert_element_type | solution.py:766
  528.2 9.0 %all-to-all-done = bf16[128,2,1572]{2,1,0:T(2,128)(2,1)} async-done(((bf16[128,2,1572]{2,1,0:T(2,128)(2,1)}), bf16[128,2,1572]{2,1,0:T(2,128)(2,1)}, u32[]{:S(2)}, u32[]{:S(2)}) %all-to-all-start) | async-done | bytes 804896 | tf_op jit(solution)/shard_map/all_to_all | solution.py:753
  (431 shorter events, 209.5 us)
Async XLA Ops:
  7.2 60.6 %all-gather.5.cloned.1.call-start = ((), (), s32[]{:S(2)}) async-start(), calls=%async_computation.5 | async-start | bytes 1966080 | tf_op jit(solution)/shard_map/all_gather | solution.py:90
  21.6 45.9 %collective-permute-start = (f32[2,384]{1,0:T(2,128)S(1)}, f32[2,384]{1,0:T(2,128)S(1)}, u32[]{:S(2)}, u32[]{:S(2)}) collective-permute-start(f32[2,384]{1,0:T(2,128)S(1)} %get-tuple-element.292), channel_id=1, source_target_pairs={{0,1},{1,2},{2,3},{3,0},{4,5},{5,6},{6,7},{7,4},{8,9},{9,10},{10,1... | collective-permute-start | bytes 9224 | tf_op jit(solution)/shard_map/ppermute | solution.py:55
  23.8 43.8 %collective-permute-start.1 = (f32[2,384]{1,0:T(2,128)S(1)}, f32[2,384]{1,0:T(2,128)S(1)}, u32[]{:S(2)}, u32[]{:S(2)}) collective-permute-start(f32[2,384]{1,0:T(2,128)S(1)} %get-tuple-element.292), channel_id=1, source_target_pairs={{0,2},{1,3},{2,0},{3,1},{4,6},{5,7},{6,4},{7,5},{8,10},{9,11},{10,... | collective-permute-start | bytes 9224 | tf_op jit(solution)/shard_map/ppermute | solution.py:55
  26.1 41.5 %collective-permute-start.2 = (f32[2,384]{1,0:T(2,128)S(1)}, f32[2,384]{1,0:T(2,128)S(1)}, u32[]{:S(2)}, u32[]{:S(2)}) collective-permute-start(f32[2,384]{1,0:T(2,128)S(1)} %get-tuple-element.292), channel_id=1, source_target_pairs={{0,3},{1,0},{2,1},{3,2},{4,7},{5,4},{6,5},{7,6},{8,11},{9,8},{10,9... | collective-permute-start | bytes 9224 | tf_op jit(solution)/shard_map/ppermute | solution.py:55
  28.1 168.7 %reduce-scatter.5.cloned.1.call-start = ((), (), s32[]{:S(2)}) async-start(), calls=%async_computation.6 | async-start | bytes 1966080 | tf_op jit(solution)/shard_map/reduce_scatter | solution.py:112
  79.8 9.6 %collective-permute-start.5 = (bf16[4,48,512]{2,1,0:T(8,128)(2,1)S(1)}, bf16[4,48,512]{2,1,0:T(8,128)(2,1)S(1)}, u32[]{:S(2)}, u32[]{:S(2)}) collective-permute-start(bf16[4,48,512]{2,1,0:T(8,128)(2,1)S(1)} %bitcast.321), channel_id=1, source_target_pairs={{0,16},{4,20},{8,24},{12,28},{16,0},{20,4},{24,8},{28,12},{1,17},{... | collective-permute-start | bytes 589832 | tf_op jit(solution)/shard_map/ppermute | solution.py:117
  81.0 8.3 %collective-permute-start.4 = (bf16[4,48,512]{2,1,0:T(8,128)(2,1)S(1)}, bf16[4,48,512]{2,1,0:T(8,128)(2,1)S(1)}, u32[]{:S(2)}, u32[]{:S(2)}) collective-permute-start(bf16[4,48,512]{2,1,0:T(8,128)(2,1)S(1)} %bitcast.323), channel_id=1, source_target_pairs={{0,8},{4,12},{8,0},{12,4},{16,24},{20,28},{24,16},{28,20},{1,9},{5... | collective-permute-start | bytes 589832 | tf_op jit(solution)/shard_map/ppermute | solution.py:117
  83.5 9.4 %collective-permute-start.7 = (bf16[4,48,512]{2,1,0:T(8,128)(2,1)S(1)}, bf16[4,48,512]{2,1,0:T(8,128)(2,1)S(1)}, u32[]{:S(2)}, u32[]{:S(2)}) collective-permute-start(bf16[4,48,512]{2,1,0:T(8,128)(2,1)S(1)} %collective-permute-done.3), channel_id=1, source_target_pairs={{0,16},{4,20},{8,24},{12,28},{16,0},{20,4},{24,8},{28,12},{1,17},{... | collective-permute-start | bytes 589832 | tf_op jit(solution)/shard_map/ppermute | solution.py:117
  93.6 10.3 %collective-permute-start.9 = (bf16[32,48,512]{2,1,0:T(8,128)(2,1)S(1)}, bf16[32,48,512]{2,1,0:T(8,128)(2,1)S(1)}, u32[]{:S(2)}, u32[]{:S(2)}) collective-permute-start(bf16[32,48,512]{2,1,0:T(8,128)(2,1)S(1)} %constant_dynamic-update-slice_fusion.even_ref), channel_id=1, source_target_pairs={{0,4},{4,0},{8,12},{12,8},{16,20},{20,16},{24,28},{28,24},{1,5},{5... | collective-permute-start | bytes 4718600 | tf_op jit(solution)/shard_map/ppermute | solution.py:117
  116.3 7.8 %collective-permute-start.10 = (bf16[4,8,48,512]{3,2,1,0:T(8,128)(2,1)S(1)}, bf16[4,8,48,512]{3,2,1,0:T(8,128)(2,1)S(1)}, u32[]{:S(2)}, u32[]{:S(2)}) collective-permute-start(bf16[4,8,48,512]{3,2,1,0:T(8,128)(2,1)S(1)} %bitcast.318), channel_id=1, source_target_pairs={{0,4},{4,0},{8,12},{12,8},{16,20},{20,16},{24,28},{28,24},{1,5},{5... | collective-permute-start | bytes 4718600 | tf_op jit(solution)/shard_map/ppermute | solution.py:117
  128.9 12.0 %collective-permute-start.13 = (f32[2,4,8,128]{3,2,1,0:T(8,128)S(1)}, f32[2,4,8,128]{3,2,1,0:T(8,128)S(1)}, u32[]{:S(2)}, u32[]{:S(2)}) collective-permute-start(f32[2,4,8,128]{3,2,1,0:T(8,128)S(1)} %pad_maximum_fusion.23), channel_id=1, source_target_pairs={{0,8},{4,12},{8,0},{12,4},{16,24},{20,28},{24,16},{28,20},{1,9},{5... | collective-permute-start | bytes 98312 | tf_op jit(solution)/shard_map/ppermute | solution.py:117
  139.2 10.2 %collective-permute-start.12 = (bf16[2,4,48,512]{3,2,1,0:T(8,128)(2,1)S(1)}, bf16[2,4,48,512]{3,2,1,0:T(8,128)(2,1)S(1)}, u32[]{:S(2)}, u32[]{:S(2)}) collective-permute-start(bf16[2,4,48,512]{3,2,1,0:T(8,128)(2,1)S(1)} %pad_maximum_fusion.9), channel_id=1, source_target_pairs={{0,8},{4,12},{8,0},{12,4},{16,24},{20,28},{24,16},{28,20},{1,9},{5... | collective-permute-start | bytes 1179656 | tf_op jit(solution)/shard_map/ppermute | solution.py:117
  139.3 12.8 %collective-permute-start.16 = (bf16[2,4,48,512]{3,2,1,0:T(8,128)(2,1)S(1)}, bf16[2,4,48,512]{3,2,1,0:T(8,128)(2,1)S(1)}, u32[]{:S(2)}, u32[]{:S(2)}) collective-permute-start(bf16[2,4,48,512]{3,2,1,0:T(8,128)(2,1)S(1)} %get-tuple-element.198), channel_id=1, source_target_pairs={{0,16},{4,20},{8,24},{12,28},{16,0},{20,4},{24,8},{28,12},{1,17},{... | collective-permute-start | bytes 1179656 | tf_op jit(solution)/shard_map/ppermute | solution.py:117
  140.5 11.6 %collective-permute-start.17 = (f32[2,4,8,128]{3,2,1,0:T(8,128)S(1)}, f32[2,4,8,128]{3,2,1,0:T(8,128)S(1)}, u32[]{:S(2)}, u32[]{:S(2)}) collective-permute-start(f32[2,4,8,128]{3,2,1,0:T(8,128)S(1)} %get-tuple-element.250), channel_id=1, source_target_pairs={{0,16},{4,20},{8,24},{12,28},{16,0},{20,4},{24,8},{28,12},{1,17},{... | collective-permute-start | bytes 98312 | tf_op jit(solution)/shard_map/ppermute | solution.py:117
  161.8 72.8 %all-gather.7.cloned.1.call-start = ((), (), s32[]{:S(2)}) async-start(), calls=%async_computation.7 | async-start | bytes 1966080 | tf_op jit(solution)/shard_map/all_gather | solution.py:90
  167.4 143.5 %all-gather.9.cloned.1.call-start = ((), (), s32[]{:S(2)}) async-start(), calls=%async_computation.9 | async-start | bytes 1966080 | tf_op jit(solution)/shard_map/all_gather | solution.py:90
  203.0 31.6 %collective-permute-start.40 = (f32[2,384]{1,0:T(2,128)S(1)}, f32[2,384]{1,0:T(2,128)S(1)}, u32[]{:S(2)}, u32[]{:S(2)}) collective-permute-start(f32[2,384]{1,0:T(2,128)S(1)} %get-tuple-element.290), channel_id=1, source_target_pairs={{0,1},{1,2},{2,3},{3,0},{4,5},{5,6},{6,7},{7,4},{8,9},{9,10},{10,1... | collective-permute-start | bytes 9224 | tf_op jit(solution)/shard_map/ppermute | solution.py:55
  203.1 31.5 %collective-permute-start.41 = (f32[2,384]{1,0:T(2,128)S(1)}, f32[2,384]{1,0:T(2,128)S(1)}, u32[]{:S(2)}, u32[]{:S(2)}) collective-permute-start(f32[2,384]{1,0:T(2,128)S(1)} %get-tuple-element.290), channel_id=1, source_target_pairs={{0,2},{1,3},{2,0},{3,1},{4,6},{5,7},{6,4},{7,5},{8,10},{9,11},{10,... | collective-permute-start | bytes 9224 | tf_op jit(solution)/shard_map/ppermute | solution.py:55
  204.6 30.0 %collective-permute-start.42 = (f32[2,384]{1,0:T(2,128)S(1)}, f32[2,384]{1,0:T(2,128)S(1)}, u32[]{:S(2)}, u32[]{:S(2)}) collective-permute-start(f32[2,384]{1,0:T(2,128)S(1)} %get-tuple-element.290), channel_id=1, source_target_pairs={{0,3},{1,0},{2,1},{3,2},{4,7},{5,4},{6,5},{7,6},{8,11},{9,8},{10,9... | collective-permute-start | bytes 9224 | tf_op jit(solution)/shard_map/ppermute | solution.py:55
  245.6 8.2 %collective-permute-start.25 = (bf16[4,48,512]{2,1,0:T(8,128)(2,1)S(1)}, bf16[4,48,512]{2,1,0:T(8,128)(2,1)S(1)}, u32[]{:S(2)}, u32[]{:S(2)}) collective-permute-start(bf16[4,48,512]{2,1,0:T(8,128)(2,1)S(1)} %get-tuple-element.215), channel_id=1, source_target_pairs={{0,16},{4,20},{8,24},{12,28},{16,0},{20,4},{24,8},{28,12},{1,17},{... | collective-permute-start | bytes 589832 | tf_op jit(solution)/shard_map/ppermute | solution.py:117
  248.7 9.3 %collective-permute-start.27 = (bf16[4,48,512]{2,1,0:T(8,128)(2,1)S(1)}, bf16[4,48,512]{2,1,0:T(8,128)(2,1)S(1)}, u32[]{:S(2)}, u32[]{:S(2)}) collective-permute-start(bf16[4,48,512]{2,1,0:T(8,128)(2,1)S(1)} %collective-permute-done.23), channel_id=1, source_target_pairs={{0,16},{4,20},{8,24},{12,28},{16,0},{20,4},{24,8},{28,12},{1,17},{... | collective-permute-start | bytes 589832 | tf_op jit(solution)/shard_map/ppermute | solution.py:117
  249.9 8.1 %collective-permute-start.28 = (bf16[4,48,512]{2,1,0:T(8,128)(2,1)S(1)}, bf16[4,48,512]{2,1,0:T(8,128)(2,1)S(1)}, u32[]{:S(2)}, u32[]{:S(2)}) collective-permute-start(bf16[4,48,512]{2,1,0:T(8,128)(2,1)S(1)} %collective-permute-done.26), channel_id=1, source_target_pairs={{0,8},{4,12},{8,0},{12,4},{16,24},{20,28},{24,16},{28,20},{1,9},{5... | collective-permute-start | bytes 589832 | tf_op jit(solution)/shard_map/ppermute | solution.py:117
  271.7 8.8 %collective-permute-start.30 = (bf16[4,8,48,512]{3,2,1,0:T(8,128)(2,1)}, bf16[4,8,48,512]{3,2,1,0:T(8,128)(2,1)}, u32[]{:S(2)}, u32[]{:S(2)}) collective-permute-start(bf16[4,8,48,512]{3,2,1,0:T(8,128)(2,1)} %bitcast.51), channel_id=1, source_target_pairs={{0,4},{4,0},{8,12},{12,8},{16,20},{20,16},{24,28},{28,24},{1,5},{5... | collective-permute-start | bytes 4718600 | tf_op jit(solution)/shard_map/ppermute | solution.py:117
  272.6 73.2 %reduce-scatter.7.cloned.1.call-start = ((), (), s32[]{:S(2)}) async-start(), calls=%async_computation.8 | async-start | bytes 1966080 | tf_op jit(solution)/shard_map/reduce_scatter | solution.py:112
  286.1 11.4 %collective-permute-start.32 = (bf16[2,4,48,512]{3,2,1,0:T(8,128)(2,1)S(1)}, bf16[2,4,48,512]{3,2,1,0:T(8,128)(2,1)S(1)}, u32[]{:S(2)}, u32[]{:S(2)}) collective-permute-start(bf16[2,4,48,512]{3,2,1,0:T(8,128)(2,1)S(1)} %pad_maximum_fusion.12), channel_id=1, source_target_pairs={{0,8},{4,12},{8,0},{12,4},{16,24},{20,28},{24,16},{28,20},{1,9},{5... | collective-permute-start | bytes 1179656 | tf_op jit(solution)/shard_map/ppermute | solution.py:117
  287.7 12.5 %collective-permute-start.36 = (bf16[2,4,48,512]{3,2,1,0:T(8,128)(2,1)S(1)}, bf16[2,4,48,512]{3,2,1,0:T(8,128)(2,1)S(1)}, u32[]{:S(2)}, u32[]{:S(2)}) collective-permute-start(bf16[2,4,48,512]{3,2,1,0:T(8,128)(2,1)S(1)} %get-tuple-element.192), channel_id=1, source_target_pairs={{0,16},{4,20},{8,24},{12,28},{16,0},{20,4},{24,8},{28,12},{1,17},{... | collective-permute-start | bytes 1179656 | tf_op jit(solution)/shard_map/ppermute | solution.py:117
  288.9 11.3 %collective-permute-start.37 = (f32[2,4,8,128]{3,2,1,0:T(8,128)S(1)}, f32[2,4,8,128]{3,2,1,0:T(8,128)S(1)}, u32[]{:S(2)}, u32[]{:S(2)}) collective-permute-start(f32[2,4,8,128]{3,2,1,0:T(8,128)S(1)} %get-tuple-element.244), channel_id=1, source_target_pairs={{0,16},{4,20},{8,24},{12,28},{16,0},{20,4},{24,8},{28,12},{1,17},{... | collective-permute-start | bytes 98312 | tf_op jit(solution)/shard_map/ppermute | solution.py:117
  310.8 76.7 %all-gather.11.cloned.1.call-start = ((), (), s32[]{:S(2)}) async-start(), calls=%async_computation.11 | async-start | bytes 1966080 | tf_op jit(solution)/shard_map/all_gather | solution.py:90
  351.3 153.8 %reduce-scatter.11.cloned.1.call-start = ((), (), s32[]{:S(2)}) async-start(), calls=%async_computation.12 | async-start | bytes 1966080 | tf_op jit(solution)/shard_map/reduce_scatter | solution.py:112
  411.8 104.4 %reduce-scatter.9.cloned.1.call-start = ((), (), s32[]{:S(2)}) async-start(), calls=%async_computation.10 | async-start | bytes 1966080 | tf_op jit(solution)/shard_map/reduce_scatter | solution.py:112
  481.1 13.8 %collective-permute-start.60 = (bf16[4,16,2,2048]{3,1,2,0:T(8,128)(2,1)S(1)}, bf16[4,16,2,2048]{3,1,2,0:T(8,128)(2,1)S(1)}, u32[]{:S(2)}, u32[]{:S(2)}) collective-permute-start(bf16[4,16,2,2048]{3,1,2,0:T(8,128)(2,1)S(1)} %pad_maximum_fusion.7), channel_id=1, source_target_pairs={{0,4},{4,0},{8,12},{12,8},{16,20},{20,16},{24,28},{28,24},{1,5},{5... | collective-permute-start | bytes 1572872 | tf_op jit(solution)/shard_map/ppermute | solution.py:117
  510.6 26.6 %all-to-all-start = ((bf16[128,2,1572]{2,1,0:T(2,128)(2,1)}), bf16[128,2,1572]{2,1,0:T(2,128)(2,1)}, u32[]{:S(2)}, u32[]{:S(2)}) async-start(bf16[128,2,1572]{2,1,0:T(2,128)(2,1)} %copy.78), calls=%async_computation.4 | async-start | bytes 1703936 | tf_op jit(solution)/shard_map/all_to_all | solution.py:753
  (75 other events, 420.0 us)
Sparse Core Ops, SparseCore 0:
  28.2 36.1 all-gather.4
  161.9 34.8 reduce-scatter.4
  198.3 36.2 all-gather.6
  272.7 35.1 all-gather.8
  310.9 34.8 reduce-scatter.6
  351.4 36.0 all-gather.10
  412.0 36.2 reduce-scatter.10
  459.1 38.3 reduce-scatter.8

commit v8 on v7

--- a/solution.py
+++ b/solution.py
@@ -158,7 +158,7 @@
     state = []
     mine = [sums[:far], logs[:far]]
     theirs = [swapped(sums[far:], near), swapped(logs[far:], near)]
-    merged = first_merged = merge(mine, theirs)
+    merged = merge(mine, theirs)
     half = sums.shape[1] // 2
     done = []
     for part, order in enumerate(orders):
@@ -173,7 +173,7 @@
             places = [places[at] for at in stay]
             kept = merge(ours, got) if place < len(order) - 1 else (ours, got)
         done.append(kept)
-    return done, first_merged[1]
+    return done
 
 
 def rotate_kernel(heads, size, scale, x_ref, y_ref, z_ref, cos_ref, sin_ref, q_ref, k_ref, v_ref):
@@ -495,7 +495,7 @@
         out_specs=pl.BlockSpec((rows, out_tile), lambda i: (0, late(i))),
         out_shape=jax.ShapeDtypeStruct((rows, columns), jnp.bfloat16),
         scratch_shapes=[pltpu.VMEM((rows, hidden), jnp.bfloat16)],
-        compiler_params=params(56),
+        compiler_params=params(40),
         name="mlp",
     )(values, gate_up, gate_up, down)
 
@@ -631,7 +631,6 @@
     gate_up = up_gate.reshape(width, -1)
     token = None
     first_shares = None
-    before_normed = None
     attended_in = []
     for chunk in range(CHUNKS):
         rows = slice(chunk * step_tokens, (chunk + 1) * step_tokens)
@@ -641,18 +640,16 @@
         attended_in.append((token, finish))
 
     all_shape = (step_requests, tree_size, heads * size)
-    before_queries = None
     attn_parts, mlp_parts = [], []
     for chunk in range(CHUNKS):
         rows = slice(chunk * step_tokens, (chunk + 1) * step_tokens)
         asked = slice(chunk * step_requests, (chunk + 1) * step_requests)
         gathered, finish = attended_in[chunk]
-        if before_normed is None:
+        if chunk == 0:
             normed, k_heads, v_heads, gate_up = lax.optimization_barrier(
                 (finish(gathered), k_heads, v_heads, gate_up)
             )
         else:
-            gathered, before_normed = lax.optimization_barrier((gathered, before_normed))
             normed = finish(gathered)
         thirds = [
             jnp.dot(normed, qkv_weight[:, third], preferred_element_type=jnp.float32)
@@ -662,8 +659,6 @@
             thirds, cosine[rows], sine[rows], heads, size, 2 * tree_size
         )
         queries, keys, values = (item.reshape(all_shape) for item in (queries, keys, values))
-        if before_queries is not None:
-            queries, before_queries = lax.optimization_barrier((queries, before_queries))
         even, odd = gather_requests(queries)
         plan = page_plan(
             page_owner, page_fill, chunk * step_requests, step_requests, req_local, parts
@@ -671,7 +666,7 @@
         sums, logs = page_attention(even, odd, k_heads, v_heads, plan, heads, size)
         keys, sums, logs = lax.optimization_barrier((keys, sums, logs))
         tree_pair = tree_attention(queries, keys, values, reach[asked], heads, size)
-        done, before_normed = scatter_requests(
+        done = scatter_requests(
             sums.reshape((parts,) + all_shape),
             logs.reshape(parts, step_requests, 8, LANES),
             merge,
@@ -686,7 +681,10 @@
             ] + [(tree_pair[0][own], tree_pair[1][own])]
             attended.append(merge_partials(pairs, heads, size, with_logs=False)[0])
         attended = jnp.concatenate(attended).reshape(step_tokens, heads * size)
-        before_queries = attended
+        if chunk + 1 < CHUNKS:
+            later, later_finish = attended_in[chunk + 1]
+            attended, later = lax.optimization_barrier((attended, later))
+            attended_in[chunk + 1] = (later, later_finish)
         attn_delta = scatter_columns(project(attended, out_weight))
         if first_shares is not None:
             attn_delta, first_shares = lax.optimization_barrier((attn_delta, first_shares))
@@ -695,6 +693,27 @@
         stream_vals = streams[rows].astype(jnp.float32)
         mixed_mid = blend(stream_vals, mid_in) + mid_out * attn_delta
         gathered, finish, sent_mid = gathered_norm(mixed_mid, width)
+        if chunk == CHUNKS - 1:
+            rows_taken = jnp.arange(req_local, dtype=jnp.int32) * tree_size + accepted_index
+            stream_rows = streams[rows_taken].astype(jnp.float32)
+            is_taken = jnp.arange(tree_size, dtype=jnp.int32)[None, :] == accepted_index[:, None]
+            attn_rows = jnp.concatenate(
+                [
+                    jnp.sum(
+                        jnp.where(
+                            is_taken[piece * step_requests : (piece + 1) * step_requests, :, None],
+                            part.reshape(step_requests, tree_size, feature_local),
+                            0.0,
+                        ),
+                        axis=1,
+                    )
+                    for piece, part in enumerate(attn_parts)
+                ]
+            )
+            mid_rows = blend(stream_rows, mid_in) + mid_out * attn_rows
+            mid_full = jnp.concatenate(list(shift_gather(mid_rows)), axis=1)
+            row_shares = mlp(layer_norm(mid_full).astype(jnp.bfloat16), gate_up, down_weight)
+            gathered, row_shares = lax.optimization_barrier((gathered, row_shares))
         normed_mid = finish(gathered)
         shares = mlp(normed_mid, gate_up, down_weight)
         if first_shares is None:
@@ -705,28 +724,7 @@
             last_shares = shares
             mlp_parts.append(scatter_columns(shares))
 
-    rows_taken = jnp.arange(req_local, dtype=jnp.int32) * tree_size + accepted_index
-    stream_rows = streams[rows_taken].astype(jnp.float32)
-    is_taken = jnp.arange(tree_size, dtype=jnp.int32)[None, :] == accepted_index[:, None]
-    attn_rows = jnp.concatenate(
-        [
-            jnp.sum(
-                jnp.where(
-                    is_taken[chunk * step_requests : (chunk + 1) * step_requests, :, None],
-                    part.reshape(step_requests, tree_size, feature_local),
-                    0.0,
-                ),
-                axis=1,
-            )
-            for chunk, part in enumerate(attn_parts)
-        ]
-    )
-    mid_rows = blend(stream_rows, mid_in) + mid_out * attn_rows
-    mid_full = jnp.concatenate(list(shift_gather(mid_rows)), axis=1)
-    mid_full, first_shares = lax.optimization_barrier((mid_full, first_shares))
-    mlp_rows = shift_scatter(
-        mlp(layer_norm(mid_full).astype(jnp.bfloat16), gate_up, down_weight)
-    )
+    mlp_rows = shift_scatter(row_shares)
     final_local = (
         jnp.sum(both_out) * attn_rows + jnp.sum(hc_out[1]) * mlp_rows
     ) + blend(stream_rows, jnp.sum(both_mix, axis=1))

time: 556 us -> 514 us (0.924)
  waiting for transfers between devices: 166 us -> 119 us
  local copies, waits for them, and re-layouts: 71 us -> 88.9 us
  Pallas kernels: 107 us -> 100 us
  other arithmetic: 76.4 us -> 69.6 us
    all_gather x4, waiting for transfers between devices: 59.1 us -> 7.03 us  [gathered_norm(): gathered = lax.all_gather(sent, 'head', axis=1, tiled=True)]
    unnamed x90 -> x107, local copies, waits for them, and re-layouts: 44.5 us -> 60.1 us
    pallas_call x3, Pallas kernels: 59.2 us -> 49.7 us  [mlp(): pl.pallas_call(functools.partial(mlp_kernel, steps, tile), grid=(steps +...]
    reduce_scatter x4, waiting for transfers between devices: 33.4 us -> 41.5 us  [scatter_columns(): lax.psum_scatter(shares, 'head', scatter_dimension=1, tiled=True)]
where the time goes in v8:
time: 514 us; the launch traced here: 507 us
  waiting for transfers between devices  119 us (23%)
  Pallas kernels  100 us (19%)
  local copies, waits for them, and re-layouts  88.9 us (17%)
  starting transfers between devices  87.8 us (17%)
  other arithmetic  69.6 us (14%)
  matrix products  24.2 us (5%)
  between operations  17.5 us (3%)
    unnamed x107, local copies, waits for them, and re-layouts  60.1 us
    ppermute x37, starting transfers between devices, swapped(): return lax.ppermute(values, 'req', [(r, r ^ bit) for r in range(count)])  51.2 us
    ppermute x37, waiting for transfers between devices, swapped(): return lax.ppermute(values, 'req', [(r, r ^ bit) for r in range(count)])  50.4 us
    pallas_call x3, Pallas kernels, mlp(): pl.pallas_call(functools.partial(mlp_kernel, steps, tile), grid=(steps +...  49.7 us
    reduce_scatter x4, waiting for transfers between devices, scatter_columns(): lax.psum_scatter(shares, 'head', scatter_dimension=1, tiled=True)  41.5 us
    ppermute x21, starting transfers between devices, shift_gather(): lax.ppermute(small, 'head', [(z, (z + step) % count) for z in range(count)])  28.4 us
    pallas_call x10, Pallas kernels, merge_partials(): pl.pallas_call(functools.partial(merge_kernel, heads, size, len(pairs)),...  17.6 us
    pallas_call x2, Pallas kernels, page_attention(): pl.pallas_call(functools.partial(page_kernel, heads, size), grid_spec=gri...  15.5 us
  transfers between devices with their start and end apart: 70, of which 34 were waited for; matrix products, arithmetic and copies ran while one was open for 21% of the time, Pallas kernels for 12%

profile of v8, /device:TPU:1, one launch (start us, length us, event | category | flops | bytes accessed | tf_op | source)
XLA Modules:
  0.0 506.9 jit_solution(2488878903961867619)
XLA Ops:
  8.7 5.8 %fusion.92 = (bf16[768,4,512]{2,0,1:T(8,128)(2,1)S(1)}, f32[768,4,512]{2,0,1:T(8,128)}) fusion(bf16[768,4,512]{2,1,0:T(4,128)(2,1)} %param.17), kind=kLoop, calls=%fused_computation.372 | loop fusion | flops 1572864 | bytes 12582912 | tf_op args[0]
  35.3 17.9 %copy.82 = bf16[256,8,2,2048]{3,1,2,0:T(8,128)(2,1)} copy(bf16[256,8,2,2048]{3,2,1,0:T(2,128)(2,1)} %bitcast.315) | data formatting | bytes 33554432
  53.1 7.2 %copy.88 = bf16[48,128,4,128]{3,1,2,0:T(8,128)(2,1)} copy(bf16[48,128,4,128]{3,2,1,0:T(4,128)(2,1)} %param.28) | data formatting | bytes 12582912 | tf_op args[11]
  60.4 7.2 %copy.89 = bf16[48,128,4,128]{3,1,2,0:T(8,128)(2,1)} copy(bf16[48,128,4,128]{3,2,1,0:T(4,128)(2,1)} %param.27) | data formatting | bytes 12582912 | tf_op args[10]
  84.8 3.9 collective-permute-done.6
  93.5 5.6 %collective-permute-start.9 = (bf16[32,48,512]{2,1,0:T(8,128)(2,1)S(1)}, bf16[32,48,512]{2,1,0:T(8,128)(2,1)S(1)}, u32[]{:S(2)}, u32[]{:S(2)}) collective-permute-start(bf16[32,48,512]{2,1,0:T(8,128)(2,1)S(1)} %constant_dynamic-update-slice_fusion.even_ref), channel_id=1, source_target_pairs={{0,4},{4,0},{8,12},{12,8},{16,20},{20,16},{24,28},{28,24},{1,5},{5... | collective-permute-start | bytes 4718600 | tf_op jit(solution)/shard_map/ppermute | solution.py:117
  109.4 5.9 %page_attention.2 = (bf16[64,48,512]{2,1,0:T(8,128)(2,1)S(1)}, f32[64,8,128]{2,1,0:T(8,128)S(1)}) custom-call(s32[48]{0:T(128)S(1)} %get-tuple-element.143.page_ref, s32[48]{0:T(128)S(1)} %get-tuple-element.144.place_ref, s32[48]{0:T(128)S(1)} %get-tuple-element.145.fill_ref, s32[48]{0:T(128)S(1)} %get-tuple-element.345.first_ref, ...), custom_call_target="tpu_custom_call" | custom-call | tf_op jit(solution)/shard_map/page_attention/pallas_call | solution.py:425
  126.9 6.1 %tree_attention.2 = (f32[8,48,512]{2,1,0:T(8,128)S(1)}, f32[8,8,128]{2,1,0:T(8,128)S(1)}) custom-call(bf16[8,48,512]{2,1,0:T(8,128)(2,1)S(1)} %bitcast.270, bf16[8,48,512]{2,1,0:T(8,128)(2,1)S(1)} %bitcast.279, bf16[8,48,512]{2,1,0:T(8,128)(2,1)S(1)} %bitcast.280, f32[8,48,48]{2,1,0:T(8,128)S(1)} %copy-done.10), custom_call_target="tpu_custom_call" | custom-call | tf_op jit(solution)/shard_map/tree_attention/pallas_call | solution.py:242
  133.1 4.4 merge_partials.10
  141.0 8.2 %collective-permute-done.12 = bf16[2,4,48,512]{3,2,1,0:T(8,128)(2,1)S(1)} collective-permute-done((bf16[2,4,48,512]{3,2,1,0:T(8,128)(2,1)S(1)}, bf16[2,4,48,512]{3,2,1,0:T(8,128)(2,1)S(1)}, u32[]{:S(2)}, u32[]{:S(2)}) %collective-permute-start.12) | collective-permute-done | bytes 393248 | tf_op jit(solution)/shard_map/ppermute | solution.py:117
  168.4 28.2 %reduce-scatter.5.cloned.1.call-done = bf16[384,512]{1,0:T(8,128)(2,1)} async-done(((bf16[384,2048]{1,0:T(8,128)(2,1)}), bf16[384,512]{1,0:T(8,128)(2,1)}) %reduce-scatter.5.cloned.1.call-update) | async-done | bytes 393232 | tf_op jit(solution)/shard_map/reduce_scatter | solution.py:112
  196.6 5.6 %multiply_reduce_fusion.1 = (f32[384]{0:T(512)S(1)}, f32[384]{0:T(512)S(1)}, f32[384,512]{1,0:T(8,128)S(1)}) fusion(bf16[384,512]{1,0:T(8,128)(2,1)} %reduce-scatter.5.cloned.1.call-done, f32[]{:T(128)} %multiply_reduce_fusion.7, f32[384,4,512]{2,0,1:T(8,128)} %copy-done.19, f32[]{:T(128)} %bitcast.82, f32[]{:T(128)} %bitcast.81, f32[]{:T(128)} %bitcast.80, ...), kind=kLoop, calls=%fused_computation.67 | loop fusion | flops 2555136 | bytes 4328468 | tf_op jit(solution)/shard_map/reduce_sum | solution.py:84
  219.7 3.5 collective-permute-done.26
  228.1 6.5 %collective-permute-start.29 = (bf16[32,48,512]{2,1,0:T(8,128)(2,1)S(1)}, bf16[32,48,512]{2,1,0:T(8,128)(2,1)S(1)}, u32[]{:S(2)}, u32[]{:S(2)}) collective-permute-start(bf16[32,48,512]{2,1,0:T(8,128)(2,1)S(1)} %constant_dynamic-update-slice_fusion.8.even_ref), channel_id=1, source_target_pairs={{0,4},{4,0},{8,12},{12,8},{16,20},{20,16},{24,28},{28,24},{1,5},{5... | collective-permute-start | bytes 4718600 | tf_op jit(solution)/shard_map/ppermute | solution.py:117
  237.7 9.6 %page_attention.3 = (bf16[64,48,512]{2,1,0:T(8,128)(2,1)S(1)}, f32[64,8,128]{2,1,0:T(8,128)S(1)}) custom-call(s32[48]{0:T(128)S(1)} %get-tuple-element.139.page_ref, s32[48]{0:T(128)S(1)} %get-tuple-element.138.place_ref, s32[48]{0:T(128)S(1)} %get-tuple-element.137.fill_ref, s32[48]{0:T(128)S(1)} %get-tuple-element.343.first_ref, ...), custom_call_target="tpu_custom_call" | custom-call | tf_op jit(solution)/shard_map/page_attention/pallas_call | solution.py:425
  249.4 6.7 %collective-permute-start.30 = (bf16[4,8,48,512]{3,2,1,0:T(8,128)(2,1)}, bf16[4,8,48,512]{3,2,1,0:T(8,128)(2,1)}, u32[]{:S(2)}, u32[]{:S(2)}) collective-permute-start(bf16[4,8,48,512]{3,2,1,0:T(8,128)(2,1)} %bitcast.52), channel_id=1, source_target_pairs={{0,4},{4,0},{8,12},{12,8},{16,20},{20,16},{24,28},{28,24},{1,5},{5... | collective-permute-start | bytes 4718600 | tf_op jit(solution)/shard_map/ppermute | solution.py:117
  258.1 6.2 %tree_attention.3 = (f32[8,48,512]{2,1,0:T(8,128)S(1)}, f32[8,8,128]{2,1,0:T(8,128)S(1)}) custom-call(bf16[8,48,512]{2,1,0:T(8,128)(2,1)S(1)} %bitcast.271, bf16[8,48,512]{2,1,0:T(8,128)(2,1)S(1)} %bitcast.281, bf16[8,48,512]{2,1,0:T(8,128)(2,1)S(1)} %bitcast.282, f32[8,48,48]{2,1,0:T(8,128)S(1)} %copy-done.9), custom_call_target="tpu_custom_call" | custom-call | tf_op jit(solution)/shard_map/tree_attention/pallas_call | solution.py:242
  264.4 5.5 %merge_partials.15 = (bf16[32,48,512]{2,1,0:T(8,128)(2,1)S(1)}, f32[32,8,128]{2,1,0:T(8,128)S(1)}) custom-call(bf16[32,48,512]{2,1,0:T(8,128)(2,1)S(1)} %copy-done.8, bf16[32,48,512]{2,1,0:T(8,128)(2,1)} %bitcast.53.refs_1_, f32[32,8,128]{2,1,0:T(8,128)S(1)} %get-tuple-element.231.refs_2_, f32[32,8,128]{2,1,0:T(8,128)S(1)} %bitcast.299), custom_call_target="tpu_custom_call" | custom-call | tf_op jit(solution)/shard_map/merge_partials/pallas_call | solution.py:538
  273.3 7.7 %collective-permute-done.32 = bf16[2,4,48,512]{3,2,1,0:T(8,128)(2,1)S(1)} collective-permute-done((bf16[2,4,48,512]{3,2,1,0:T(8,128)(2,1)S(1)}, bf16[2,4,48,512]{3,2,1,0:T(8,128)(2,1)S(1)}, u32[]{:S(2)}, u32[]{:S(2)}) %collective-permute-start.32) | collective-permute-done | bytes 393248 | tf_op jit(solution)/shard_map/ppermute | solution.py:117
  303.4 18.7 %mlp.3 = bf16[384,2048]{1,0:T(8,128)(2,1)} custom-call(bf16[384,2048]{1,0:T(8,128)(2,1)S(1)} %pad_maximum_fusion.2.x_ref, bf16[2048,4096]{1,0:T(8,128)(2,1)} %bitcast.309, bf16[2048,4096]{1,0:T(8,128)(2,1)} %bitcast.310, bf16[2048,2048]{1,0:T(8,128)(2,1)S(1)} %copy-done.2), custom_call_target="tpu_custom_call" | custom-call | tf_op jit(solution)/shard_map/mlp/pallas_call | solution.py:486
  322.1 10.2 %reduce-scatter.7.cloned.1.call-done = bf16[384,512]{1,0:T(8,128)(2,1)} async-done(((bf16[384,2048]{1,0:T(8,128)(2,1)}), bf16[384,512]{1,0:T(8,128)(2,1)}) %reduce-scatter.7.cloned.1.call-update) | async-done | bytes 393232 | tf_op jit(solution)/shard_map/reduce_scatter | solution.py:112
  357.5 12.5 %mlp.4 = bf16[16,2048]{1,0:T(8,128)(2,1)S(1)} custom-call(bf16[16,2048]{1,0:T(8,128)(2,1)S(1)} %multiply_convert_fusion.16.x_ref, bf16[2048,4096]{1,0:T(8,128)(2,1)} %bitcast.311, bf16[2048,4096]{1,0:T(8,128)(2,1)} %bitcast.312, bf16[2048,2048]{1,0:T(8,128)(2,1)S(1)} %copy-done.3), custom_call_target="tpu_custom_call" | custom-call | tf_op jit(solution)/shard_map/mlp/pallas_call | solution.py:486
  370.1 7.0 %all-gather.11.cloned.1.call-done = bf16[384,2048]{1,0:T(8,128)(2,1)} async-done(((bf16[384,512]{1,0:T(8,128)(2,1)}), bf16[384,2048]{1,0:T(8,128)(2,1)}) %all-gather.11.cloned.1.call-update) | async-done | bytes 1572880 | tf_op jit(solution)/shard_map/all_gather | solution.py:90
  382.4 18.5 %mlp.5 = bf16[384,2048]{1,0:T(8,128)(2,1)} custom-call(bf16[384,2048]{1,0:T(8,128)(2,1)S(1)} %pad_maximum_fusion.4.x_ref, bf16[2048,4096]{1,0:T(8,128)(2,1)} %bitcast.313, bf16[2048,4096]{1,0:T(8,128)(2,1)} %bitcast.314, bf16[2048,2048]{1,0:T(8,128)(2,1)S(1)} %copy-done.4), custom_call_target="tpu_custom_call" | custom-call | tf_op jit(solution)/shard_map/mlp/pallas_call | solution.py:486
  406.4 3.9 bitcast_add_fusion.2
  435.2 4.1 collective-permute-done.59
  439.4 6.9 %collective-permute-start.60 = (bf16[4,16,2,2048]{3,1,2,0:T(8,128)(2,1)S(1)}, bf16[4,16,2,2048]{3,1,2,0:T(8,128)(2,1)S(1)}, u32[]{:S(2)}, u32[]{:S(2)}) collective-permute-start(bf16[4,16,2,2048]{3,1,2,0:T(8,128)(2,1)S(1)} %pad_maximum_fusion.7), channel_id=1, source_target_pairs={{0,4},{4,0},{8,12},{12,8},{16,20},{20,16},{24,28},{28,24},{1,5},{5... | collective-permute-start | bytes 1572872 | tf_op jit(solution)/shard_map/ppermute | solution.py:117
  446.3 5.5 %slice_bitcast_fusion.3 = (f32[768,512]{1,0:T(8,128)S(1)}, f32[768,512]{1,0:T(8,128)}, f32[768,512]{1,0:T(8,128)}, f32[768,512]{1,0:T(8,128)}) fusion(f32[768,4,512]{2,0,1:T(8,128)} %get-tuple-element.177), kind=kLoop, calls=%fused_computation.29 | loop fusion | bytes 12582912 | tf_op jit(solution)/shard_map/mul | solution.py:762
  457.0 5.1 %fusion = bf16[128,2,1572]{0,2,1:T(8,128)(2,1)} fusion(bf16[128,2,2048]{2,0,1:T(8,128)(2,1)S(1)} %bitcast.318, bf16[2048,1572]{0,1:T(8,128)(2,1)} %param.26), kind=kOutput, calls=%fused_computation.2 | convolution fusion | flops 1648361472 | bytes 8292352 | tf_op jit(solution)/shard_map/dot_general | solution.py:746
  467.5 4.6 all-to-all-start
  479.4 8.8 %add_convert_fusion = bf16[768,4,512]{2,1,0:T(4,128)(2,1)} fusion(f32[768,512]{1,0:T(8,128)S(1)} %copy-done.24, f32[4]{0:T(128)S(1)} %get-tuple-element.324, f32[768,512]{1,0:T(8,128)S(1)} %copy-done.25, f32[4]{0:T(128)S(1)} %get-tuple-element.325, f32[768,512]{1,0:T(8,128)} %get-tuple-element.169, f32[4]{0:T(128)S(1)} %get-tuple-element.326, ...), kind=kLoop, calls=%fused_computation.6 | loop fusion | flops 18874368 | bytes 12583008 | tf_op jit(solution)/shard_map/convert_element_type | solution.py:764
  488.3 6.2 %all-to-all-done = bf16[128,2,1572]{2,1,0:T(2,128)(2,1)} async-done(((bf16[128,2,1572]{2,1,0:T(2,128)(2,1)}), bf16[128,2,1572]{2,1,0:T(2,128)(2,1)}, u32[]{:S(2)}, u32[]{:S(2)}) %all-to-all-start) | async-done | bytes 804896 | tf_op jit(solution)/shard_map/all_to_all | solution.py:751
  (447 shorter events, 225.6 us)
Async XLA Ops:
  7.2 60.6 %all-gather.5.cloned.1.call-start = ((), (), s32[]{:S(2)}) async-start(), calls=%async_computation.5 | async-start | bytes 1966080 | tf_op jit(solution)/shard_map/all_gather | solution.py:90
  21.6 45.9 %collective-permute-start = (f32[2,384]{1,0:T(2,128)S(1)}, f32[2,384]{1,0:T(2,128)S(1)}, u32[]{:S(2)}, u32[]{:S(2)}) collective-permute-start(f32[2,384]{1,0:T(2,128)S(1)} %get-tuple-element.298), channel_id=1, source_target_pairs={{0,1},{1,2},{2,3},{3,0},{4,5},{5,6},{6,7},{7,4},{8,9},{9,10},{10,1... | collective-permute-start | bytes 9224 | tf_op jit(solution)/shard_map/ppermute | solution.py:55
  23.8 43.8 %collective-permute-start.1 = (f32[2,384]{1,0:T(2,128)S(1)}, f32[2,384]{1,0:T(2,128)S(1)}, u32[]{:S(2)}, u32[]{:S(2)}) collective-permute-start(f32[2,384]{1,0:T(2,128)S(1)} %get-tuple-element.298), channel_id=1, source_target_pairs={{0,2},{1,3},{2,0},{3,1},{4,6},{5,7},{6,4},{7,5},{8,10},{9,11},{10,... | collective-permute-start | bytes 9224 | tf_op jit(solution)/shard_map/ppermute | solution.py:55
  26.1 41.5 %collective-permute-start.2 = (f32[2,384]{1,0:T(2,128)S(1)}, f32[2,384]{1,0:T(2,128)S(1)}, u32[]{:S(2)}, u32[]{:S(2)}) collective-permute-start(f32[2,384]{1,0:T(2,128)S(1)} %get-tuple-element.298), channel_id=1, source_target_pairs={{0,3},{1,0},{2,1},{3,2},{4,7},{5,4},{6,5},{7,6},{8,11},{9,8},{10,9... | collective-permute-start | bytes 9224 | tf_op jit(solution)/shard_map/ppermute | solution.py:55
  28.1 130.7 %all-gather.7.cloned.1.call-start = ((), (), s32[]{:S(2)}) async-start(), calls=%async_computation.6 | async-start | bytes 1966080 | tf_op jit(solution)/shard_map/all_gather | solution.py:90
  79.8 9.6 %collective-permute-start.5 = (bf16[4,48,512]{2,1,0:T(8,128)(2,1)S(1)}, bf16[4,48,512]{2,1,0:T(8,128)(2,1)S(1)}, u32[]{:S(2)}, u32[]{:S(2)}) collective-permute-start(bf16[4,48,512]{2,1,0:T(8,128)(2,1)S(1)} %bitcast.320), channel_id=1, source_target_pairs={{0,16},{4,20},{8,24},{12,28},{16,0},{20,4},{24,8},{28,12},{1,17},{... | collective-permute-start | bytes 589832 | tf_op jit(solution)/shard_map/ppermute | solution.py:117
  81.0 8.4 %collective-permute-start.4 = (bf16[4,48,512]{2,1,0:T(8,128)(2,1)S(1)}, bf16[4,48,512]{2,1,0:T(8,128)(2,1)S(1)}, u32[]{:S(2)}, u32[]{:S(2)}) collective-permute-start(bf16[4,48,512]{2,1,0:T(8,128)(2,1)S(1)} %bitcast.325), channel_id=1, source_target_pairs={{0,8},{4,12},{8,0},{12,4},{16,24},{20,28},{24,16},{28,20},{1,9},{5... | collective-permute-start | bytes 589832 | tf_op jit(solution)/shard_map/ppermute | solution.py:117
  83.5 9.4 %collective-permute-start.7 = (bf16[4,48,512]{2,1,0:T(8,128)(2,1)S(1)}, bf16[4,48,512]{2,1,0:T(8,128)(2,1)S(1)}, u32[]{:S(2)}, u32[]{:S(2)}) collective-permute-start(bf16[4,48,512]{2,1,0:T(8,128)(2,1)S(1)} %collective-permute-done.3), channel_id=1, source_target_pairs={{0,16},{4,20},{8,24},{12,28},{16,0},{20,4},{24,8},{28,12},{1,17},{... | collective-permute-start | bytes 589832 | tf_op jit(solution)/shard_map/ppermute | solution.py:117
  93.5 10.2 %collective-permute-start.9 = (bf16[32,48,512]{2,1,0:T(8,128)(2,1)S(1)}, bf16[32,48,512]{2,1,0:T(8,128)(2,1)S(1)}, u32[]{:S(2)}, u32[]{:S(2)}) collective-permute-start(bf16[32,48,512]{2,1,0:T(8,128)(2,1)S(1)} %constant_dynamic-update-slice_fusion.even_ref), channel_id=1, source_target_pairs={{0,4},{4,0},{8,12},{12,8},{16,20},{20,16},{24,28},{28,24},{1,5},{5... | collective-permute-start | bytes 4718600 | tf_op jit(solution)/shard_map/ppermute | solution.py:117
  116.6 16.5 %collective-permute-start.10 = (bf16[4,8,48,512]{3,2,1,0:T(8,128)(2,1)}, bf16[4,8,48,512]{3,2,1,0:T(8,128)(2,1)S(1)}, u32[]{:S(2)}, u32[]{:S(2)}) collective-permute-start(bf16[4,8,48,512]{3,2,1,0:T(8,128)(2,1)} %bitcast.19), channel_id=1, source_target_pairs={{0,4},{4,0},{8,12},{12,8},{16,20},{20,16},{24,28},{28,24},{1,5},{5... | collective-permute-start | bytes 4718600 | tf_op jit(solution)/shard_map/ppermute | solution.py:117
  122.9 73.7 %reduce-scatter.5.cloned.1.call-start = ((), (), s32[]{:S(2)}) async-start(), calls=%async_computation.7 | async-start | bytes 1966080 | tf_op jit(solution)/shard_map/reduce_scatter | solution.py:112
  123.9 9.2 %collective-permute-start.11 = (f32[4,8,8,128]{3,2,1,0:T(8,128)S(1)}, f32[4,8,8,128]{3,2,1,0:T(8,128)S(1)}, u32[]{:S(2)}, u32[]{:S(2)}) collective-permute-start(f32[4,8,8,128]{3,2,1,0:T(8,128)S(1)} %bitcast.335), channel_id=1, source_target_pairs={{0,4},{4,0},{8,12},{12,8},{16,20},{20,16},{24,28},{28,24},{1,5},{5... | collective-permute-start | bytes 393224 | tf_op jit(solution)/shard_map/ppermute | solution.py:117
  138.5 10.7 %collective-permute-start.12 = (bf16[2,4,48,512]{3,2,1,0:T(8,128)(2,1)S(1)}, bf16[2,4,48,512]{3,2,1,0:T(8,128)(2,1)S(1)}, u32[]{:S(2)}, u32[]{:S(2)}) collective-permute-start(bf16[2,4,48,512]{3,2,1,0:T(8,128)(2,1)S(1)} %pad_maximum_fusion.9), channel_id=1, source_target_pairs={{0,8},{4,12},{8,0},{12,4},{16,24},{20,28},{24,16},{28,20},{1,9},{5... | collective-permute-start | bytes 1179656 | tf_op jit(solution)/shard_map/ppermute | solution.py:117
  139.4 12.5 %collective-permute-start.16 = (bf16[2,4,48,512]{3,2,1,0:T(8,128)(2,1)S(1)}, bf16[2,4,48,512]{3,2,1,0:T(8,128)(2,1)S(1)}, u32[]{:S(2)}, u32[]{:S(2)}) collective-permute-start(bf16[2,4,48,512]{3,2,1,0:T(8,128)(2,1)S(1)} %get-tuple-element.204), channel_id=1, source_target_pairs={{0,16},{4,20},{8,24},{12,28},{16,0},{20,4},{24,8},{28,12},{1,17},{... | collective-permute-start | bytes 1179656 | tf_op jit(solution)/shard_map/ppermute | solution.py:117
  140.2 11.7 %collective-permute-start.17 = (f32[2,4,8,128]{3,2,1,0:T(8,128)S(1)}, f32[2,4,8,128]{3,2,1,0:T(8,128)S(1)}, u32[]{:S(2)}, u32[]{:S(2)}) collective-permute-start(f32[2,4,8,128]{3,2,1,0:T(8,128)S(1)} %get-tuple-element.256), channel_id=1, source_target_pairs={{0,16},{4,20},{8,24},{12,28},{16,0},{20,4},{24,8},{28,12},{1,17},{... | collective-permute-start | bytes 98312 | tf_op jit(solution)/shard_map/ppermute | solution.py:117
  161.7 136.3 %all-gather.9.cloned.1.call-start = ((), (), s32[]{:S(2)}) async-start(), calls=%async_computation.9 | async-start | bytes 1966080 | tf_op jit(solution)/shard_map/all_gather | solution.py:90
  215.2 9.1 %collective-permute-start.25 = (bf16[4,48,512]{2,1,0:T(8,128)(2,1)S(1)}, bf16[4,48,512]{2,1,0:T(8,128)(2,1)S(1)}, u32[]{:S(2)}, u32[]{:S(2)}) collective-permute-start(bf16[4,48,512]{2,1,0:T(8,128)(2,1)S(1)} %bitcast.323), channel_id=1, source_target_pairs={{0,16},{4,20},{8,24},{12,28},{16,0},{20,4},{24,8},{28,12},{1,17},{... | collective-permute-start | bytes 589832 | tf_op jit(solution)/shard_map/ppermute | solution.py:117
  218.6 8.9 %collective-permute-start.27 = (bf16[4,48,512]{2,1,0:T(8,128)(2,1)S(1)}, bf16[4,48,512]{2,1,0:T(8,128)(2,1)S(1)}, u32[]{:S(2)}, u32[]{:S(2)}) collective-permute-start(bf16[4,48,512]{2,1,0:T(8,128)(2,1)S(1)} %collective-permute-done.23), channel_id=1, source_target_pairs={{0,16},{4,20},{8,24},{12,28},{16,0},{20,4},{24,8},{28,12},{1,17},{... | collective-permute-start | bytes 589832 | tf_op jit(solution)/shard_map/ppermute | solution.py:117
  228.1 9.5 %collective-permute-start.29 = (bf16[32,48,512]{2,1,0:T(8,128)(2,1)S(1)}, bf16[32,48,512]{2,1,0:T(8,128)(2,1)S(1)}, u32[]{:S(2)}, u32[]{:S(2)}) collective-permute-start(bf16[32,48,512]{2,1,0:T(8,128)(2,1)S(1)} %constant_dynamic-update-slice_fusion.8.even_ref), channel_id=1, source_target_pairs={{0,4},{4,0},{8,12},{12,8},{16,20},{20,16},{24,28},{28,24},{1,5},{5... | collective-permute-start | bytes 4718600 | tf_op jit(solution)/shard_map/ppermute | solution.py:117
  249.4 15.1 %collective-permute-start.30 = (bf16[4,8,48,512]{3,2,1,0:T(8,128)(2,1)}, bf16[4,8,48,512]{3,2,1,0:T(8,128)(2,1)}, u32[]{:S(2)}, u32[]{:S(2)}) collective-permute-start(bf16[4,8,48,512]{3,2,1,0:T(8,128)(2,1)} %bitcast.52), channel_id=1, source_target_pairs={{0,4},{4,0},{8,12},{12,8},{16,20},{20,16},{24,28},{28,24},{1,5},{5... | collective-permute-start | bytes 4718600 | tf_op jit(solution)/shard_map/ppermute | solution.py:117
  257.0 75.3 %reduce-scatter.7.cloned.1.call-start = ((), (), s32[]{:S(2)}) async-start(), calls=%async_computation.8 | async-start | bytes 1966080 | tf_op jit(solution)/shard_map/reduce_scatter | solution.py:112
  270.1 10.9 %collective-permute-start.32 = (bf16[2,4,48,512]{3,2,1,0:T(8,128)(2,1)S(1)}, bf16[2,4,48,512]{3,2,1,0:T(8,128)(2,1)S(1)}, u32[]{:S(2)}, u32[]{:S(2)}) collective-permute-start(bf16[2,4,48,512]{3,2,1,0:T(8,128)(2,1)S(1)} %pad_maximum_fusion.12), channel_id=1, source_target_pairs={{0,8},{4,12},{8,0},{12,4},{16,24},{20,28},{24,16},{28,20},{1,9},{5... | collective-permute-start | bytes 1179656 | tf_op jit(solution)/shard_map/ppermute | solution.py:117
  271.7 12.4 %collective-permute-start.36 = (bf16[2,4,48,512]{3,2,1,0:T(8,128)(2,1)S(1)}, bf16[2,4,48,512]{3,2,1,0:T(8,128)(2,1)S(1)}, u32[]{:S(2)}, u32[]{:S(2)}) collective-permute-start(bf16[2,4,48,512]{3,2,1,0:T(8,128)(2,1)S(1)} %get-tuple-element.198), channel_id=1, source_target_pairs={{0,16},{4,20},{8,24},{12,28},{16,0},{20,4},{24,8},{28,12},{1,17},{... | collective-permute-start | bytes 1179656 | tf_op jit(solution)/shard_map/ppermute | solution.py:117
  273.1 11.0 %collective-permute-start.37 = (f32[2,4,8,128]{3,2,1,0:T(8,128)S(1)}, f32[2,4,8,128]{3,2,1,0:T(8,128)S(1)}, u32[]{:S(2)}, u32[]{:S(2)}) collective-permute-start(f32[2,4,8,128]{3,2,1,0:T(8,128)S(1)} %get-tuple-element.250), channel_id=1, source_target_pairs={{0,16},{4,20},{8,24},{12,28},{16,0},{20,4},{24,8},{28,12},{1,17},{... | collective-permute-start | bytes 98312 | tf_op jit(solution)/shard_map/ppermute | solution.py:117
  294.7 82.4 %all-gather.11.cloned.1.call-start = ((), (), s32[]{:S(2)}) async-start(), calls=%async_computation.11 | async-start | bytes 1966080 | tf_op jit(solution)/shard_map/all_gather | solution.py:90
  337.9 124.2 %reduce-scatter.11.cloned.1.call-start = ((), (), s32[]{:S(2)}) async-start(), calls=%async_computation.12 | async-start | bytes 1966080 | tf_op jit(solution)/shard_map/reduce_scatter | solution.py:112
  338.3 8.9 %collective-permute-start.49 = (f32[2,384]{1,0:T(2,128)S(1)}, f32[2,384]{1,0:T(2,128)S(1)}, u32[]{:S(2)}, u32[]{:S(2)}) collective-permute-start(f32[2,384]{1,0:T(2,128)S(1)} %get-tuple-element.294), channel_id=1, source_target_pairs={{0,1},{1,2},{2,3},{3,0},{4,5},{5,6},{6,7},{7,4},{8,9},{9,10},{10,1... | collective-permute-start | bytes 9224 | tf_op jit(solution)/shard_map/ppermute | solution.py:55
  338.3 11.2 %collective-permute-start.50 = (f32[2,384]{1,0:T(2,128)S(1)}, f32[2,384]{1,0:T(2,128)S(1)}, u32[]{:S(2)}, u32[]{:S(2)}) collective-permute-start(f32[2,384]{1,0:T(2,128)S(1)} %get-tuple-element.294), channel_id=1, source_target_pairs={{0,2},{1,3},{2,0},{3,1},{4,6},{5,7},{6,4},{7,5},{8,10},{9,11},{10,... | collective-permute-start | bytes 9224 | tf_op jit(solution)/shard_map/ppermute | solution.py:55
  339.8 9.7 %collective-permute-start.51 = (f32[2,384]{1,0:T(2,128)S(1)}, f32[2,384]{1,0:T(2,128)S(1)}, u32[]{:S(2)}, u32[]{:S(2)}) collective-permute-start(f32[2,384]{1,0:T(2,128)S(1)} %get-tuple-element.294), channel_id=1, source_target_pairs={{0,3},{1,0},{2,1},{3,2},{4,7},{5,4},{6,5},{7,6},{8,11},{9,8},{10,9... | collective-permute-start | bytes 9224 | tf_op jit(solution)/shard_map/ppermute | solution.py:55
  400.9 75.6 %reduce-scatter.9.cloned.1.call-start = ((), (), s32[]{:S(2)}) async-start(), calls=%async_computation.10 | async-start | bytes 1966080 | tf_op jit(solution)/shard_map/reduce_scatter | solution.py:112
  439.4 12.4 %collective-permute-start.60 = (bf16[4,16,2,2048]{3,1,2,0:T(8,128)(2,1)S(1)}, bf16[4,16,2,2048]{3,1,2,0:T(8,128)(2,1)S(1)}, u32[]{:S(2)}, u32[]{:S(2)}) collective-permute-start(bf16[4,16,2,2048]{3,1,2,0:T(8,128)(2,1)S(1)} %pad_maximum_fusion.7), channel_id=1, source_target_pairs={{0,4},{4,0},{8,12},{12,8},{16,20},{20,16},{24,28},{28,24},{1,5},{5... | collective-permute-start | bytes 1572872 | tf_op jit(solution)/shard_map/ppermute | solution.py:117
  467.5 26.9 %all-to-all-start = ((bf16[128,2,1572]{2,1,0:T(2,128)(2,1)}), bf16[128,2,1572]{2,1,0:T(2,128)(2,1)}, u32[]{:S(2)}, u32[]{:S(2)}) async-start(bf16[128,2,1572]{2,1,0:T(2,128)(2,1)} %copy.78), calls=%async_computation.4 | async-start | bytes 1703936 | tf_op jit(solution)/shard_map/all_to_all | solution.py:751
  (83 other events, 474.0 us)
Sparse Core Ops, SparseCore 0:
  28.2 36.1 all-gather.4
  123.0 33.3 all-gather.6
  161.8 34.7 reduce-scatter.4
  257.1 36.1 all-gather.8
  296.0 36.2 reduce-scatter.6
  338.0 38.9 all-gather.10
  401.0 38.1 reduce-scatter.10
  441.5 34.8 reduce-scatter.8
